TPU v7x, 32 devices: a whole 2x2x4 slice. The times are simulated.
32 devices in a mesh: section: 2 (over core), dp: 4 (over z), mp: 4 (over y, x).
Axes of the slice: x: 2, y: 2, z: 4, core: 2. Of those that a mesh axis runs over, the one named last changes fastest.
Arguments:
- events: bfloat16 [32, 1024, 512], P(('section', 'dp', 'mp')), may hold values from -6 to 6
- hist_len: int32 [32], P(('section', 'dp', 'mp')), may hold values from 256 to 1024, as said below
- sess_len: int32 [32, 32], P(('section', 'dp', 'mp')), may hold values from 1 to 64, 1024 in all within a row
- w_uvqk: bfloat16 [512, 2048], P('dp'), may hold values from -0.25 to 0.25
- w_out: bfloat16 [512, 512], P('dp'), may hold values from -0.25 to 0.25
- attn_gain: float32 [512], replicated, may hold values from 0.1 to 1.9
- w_in: bfloat16 [512, 4096], P(None, ('section', 'mp')), may hold values from -2 to 2
- ffn_gain: bfloat16 [1, 4096], P(None, ('section', 'mp')), may hold values from 0.099609375 to 1.8984375
- w_up: bfloat16 [4096, 8192], P('section', 'mp'), may hold values from -0.09375 to 0.09375
- w_down: bfloat16 [8192, 4096], P('mp', 'section'), may hold values from -0.0625 to 0.0625
Outputs:
- pooled: bfloat16 [1024, 512], P(('section', 'dp', 'mp'))
- cross_out: bfloat16 [256, 4096], P(('section', 'dp', 'mp'))
Inputs may be any that keep to these rules, and one draw needn't show every extreme that they name: `hist_len`: some user has all 1024 events valid. `sess_len`: a user's 32 sessions cover all 1024 positions; some session has exactly 64 events.
All inputs are finite; a program needn't handle non-finite values.
Results may differ from a plain program's by a relative error of at most 0.015.
Values may be sent and summed in bfloat16 or wider, within the bound.
No kernel may reach another device: no remote copies, remote signals or barrier semaphores. Data moves between devices by JAX's collectives and lax.ppermute only.
A program may use at most 64 MiB of HBM per device.

v0:
```python
import jax
import jax.numpy as jnp
from jax import lax
from jax.sharding import PartitionSpec as P

HEADS = 4
DM = 4096
MICRO = 4


EPSILON = 1e-06


def encode_user(tokens, valid_len, w_uvqk, w_out, norm_gain):
    length, model_width = tokens.shape
    head_dim = model_width // HEADS
    projected = jnp.dot(tokens, w_uvqk, preferred_element_type=jnp.float32)
    activated = jax.nn.silu(projected)
    gate_part = activated[:, :model_width]
    values = activated[:, model_width : 2 * model_width].astype(jnp.bfloat16)
    queries = activated[:, 2 * model_width : 3 * model_width].astype(jnp.bfloat16)
    key_vecs = activated[:, 3 * model_width :].astype(jnp.bfloat16)
    key_heads = key_vecs.reshape(length, HEADS, head_dim)
    value_heads = values.reshape(length, HEADS, head_dim)
    block_rows = min(length, 512)
    columns = jnp.arange(length, dtype=jnp.int32)
    outputs = []
    for block_index in range(length // block_rows):
        query_heads = queries[block_index * block_rows : (block_index + 1) * block_rows]
        query_heads = query_heads.reshape(block_rows, HEADS, head_dim)
        scores = jnp.einsum(
            "ihd,jhd->hij", query_heads, key_heads, preferred_element_type=jnp.float32
        ) * head_dim ** (-0.5)
        rows_at = block_index * block_rows + jnp.arange(block_rows, dtype=jnp.int32)
        visible = (columns[None, :] <= rows_at[:, None]) & (columns[None, :] < valid_len)
        weights = jnp.where(visible[None], jax.nn.silu(scores), 0.0).astype(jnp.bfloat16)
        mixed_heads = jnp.einsum(
            "hij,jhd->ihd", weights, value_heads, preferred_element_type=jnp.float32
        )
        outputs.append(mixed_heads.reshape(block_rows, model_width))
    attended = jnp.concatenate(outputs, axis=0)
    inv_rms = lax.rsqrt(jnp.mean(attended * attended, axis=1, keepdims=True) + EPSILON)
    gated_out = (attended * inv_rms * norm_gain * gate_part).astype(jnp.bfloat16)
    return tokens.astype(jnp.float32) + jnp.dot(
        gated_out, w_out, preferred_element_type=jnp.float32
    )


def pool_sessions(enc_state, valid_len, sess_lens):
    length = enc_state.shape[0]
    sess_ends = jnp.cumsum(sess_lens)
    sess_starts = sess_ends - sess_lens
    positions = jnp.arange(length, dtype=jnp.int32)
    membership = (
        (positions[None, :] >= sess_starts[:, None])
        & (positions[None, :] < sess_ends[:, None])
        & (positions[None, :] < valid_len)
    ).astype(jnp.float32)
    sess_sums = jnp.dot(membership, enc_state, precision=lax.Precision.HIGHEST)
    sess_counts = jnp.sum(membership, axis=1, keepdims=True)
    return (sess_sums / jnp.maximum(sess_counts, 1.0)).astype(jnp.bfloat16)


def per_device(events, hist_len, sess_len, w_uvqk, w_out, attn_gain, w_in, ffn_gain, w_up, w_down):
    full_uvqk, full_out = (
        lax.all_gather(w_uvqk, "dp", axis=0, tiled=True),
        lax.all_gather(w_out, "dp", axis=0, tiled=True),
    )
    enc_state = encode_user(events[0], hist_len[0], full_uvqk, full_out, attn_gain)
    pooled = pool_sessions(enc_state, hist_len[0], sess_len[0])
    micro_count = pooled.shape[0] // MICRO
    group_rows = lax.all_gather(pooled[:micro_count], ("section", "mp"), axis=0, tiled=True)
    section_count = lax.axis_size("section")
    model_count = lax.axis_size("mp")
    total_rows = group_rows.shape[0]
    model_index = lax.axis_index("mp")
    local_in = jnp.dot(group_rows, w_in, preferred_element_type=jnp.float32)
    col_width = local_in.shape[1]
    square_sum = lax.psum(jnp.sum(local_in * local_in, axis=1), ("section", "mp"))
    inv_rms = lax.rsqrt(square_sum / DM + EPSILON)
    normed_part = (local_in * inv_rms[:, None] * ffn_gain.astype(jnp.float32)).astype(jnp.bfloat16)
    half_up = jnp.dot(
        lax.all_gather(normed_part, "mp", axis=1, tiled=True),
        w_up,
        preferred_element_type=jnp.float32,
    )
    up_proj = lax.psum(half_up.astype(jnp.bfloat16), "section").astype(jnp.float32)
    hidden = jax.nn.gelu(up_proj, approximate=True).astype(jnp.bfloat16)
    unit_count = hidden.shape[1]
    hidden_order = hidden.reshape(section_count, model_count, micro_count, unit_count)
    hidden_order = hidden_order.transpose(1, 0, 2, 3).reshape(total_rows, unit_count)
    carry_order = local_in.reshape(section_count, model_count, micro_count, col_width)
    carry_order = carry_order.transpose(1, 0, 2, 3).reshape(total_rows, col_width)
    part_sum = jnp.dot(hidden_order, w_down, preferred_element_type=jnp.float32)
    target = lax.dynamic_slice_in_dim(part_sum, model_index * col_width, col_width, 1) + carry_order
    summed = lax.psum_scatter(
        lax.dynamic_update_slice_in_dim(part_sum, target, model_index * col_width, 1).astype(
            jnp.bfloat16
        ),
        "mp",
        scatter_dimension=0,
        tiled=True,
    ).astype(jnp.float32)
    full_rows = lax.all_to_all(
        summed.astype(jnp.bfloat16), "section", split_axis=0, concat_axis=1, tiled=True
    ).astype(summed.dtype)
    cross_out = full_rows.astype(jnp.bfloat16)
    return (pooled, cross_out)


def solution(mesh):
    return jax.shard_map(
        per_device,
        mesh=mesh,
        in_specs=(
            P(("section", "dp", "mp"), None, None),
            P(("section", "dp", "mp")),
            P(("section", "dp", "mp"), None),
            P("dp", None),
            P("dp", None),
            P(),
            P(None, ("section", "mp")),
            P(None, ("section", "mp")),
            P("section", "mp"),
            P("mp", "section"),
        ),
        out_specs=(P(("section", "dp", "mp"), None), P(("section", "dp", "mp"), None)),
        check_vma=False,
    )
```

profile of v0, /device:TPU:0, one launch (start us, length us, event | category | flops | bytes accessed | tf_op | source)
XLA Modules:
  0.0 207.9 jit_solution(5347029944572468762)
XLA Ops:
  7.2 0.7 all-gather.2.cloned.1.call-update
  8.6 0.7 copy.33
  9.4 0.1 reduce
  9.5 0.7 mul.114
  10.2 0.7 bitcast_subtract_fusion
  10.9 0.2 convert_reduce_fusion
  11.1 22.8 %all_gather.13 = bf16[512,512]{1,0:T(8,128)(2,1)S(1)} all-gather(bf16[128,512]{1,0:T(8,128)(2,1)} %param.14), channel_id=1, replica_groups=mesh['section'=2,'dp'=4,'mp'=4] {'dp'}, dimensions={0}, use_global_device_ids=true | all-gather | bytes 655360 | tf_op jit(solution)/shard_map/all_gather | solution.py:67
  33.9 1.5 fusion.10
  35.4 26.6 %all-gather.2.cloned.1.call-done = bf16[512,2048]{1,0:T(8,128)(2,1)} async-done(((bf16[128,2048]{1,0:T(8,128)(2,1)}), bf16[512,2048]{1,0:T(8,128)(2,1)}) %all-gather.2.cloned.1.call-update) | async-done | bytes 2097168 | tf_op jit(solution)/shard_map/all_gather | solution.py:66
  62.0 8.2 %fusion.59 = (bf16[1024,2048]{1,0:T(8,128)(2,1)S(1)}, f32[1024,2048]{1,0:T(8,128)}) fusion(bf16[512,2048]{1,0:T(8,128)(2,1)} %all-gather.2.cloned.1.call-done, bf16[1,1024,512]{2,1,0:T(8,128)(2,1)} %param.10), kind=kOutput, calls=%fused_computation.72 | convolution fusion | flops 2157969408 | bytes 15728640 | tf_op jit(solution)/shard_map/dot_general | solution.py:17
  70.2 1.5 slice_bitcast_fusion
  71.6 1.1 slice_bitcast_fusion.2
  72.7 0.5 copy.46
  73.2 6.6 %fusion = f32[4,128,512]{2,1,0:T(8,128)} fusion(bf16[1024,4,128]{0,2,1:T(8,128)(2,1)S(1)} %bitcast.68, pred[512,1024]{1,0:T(8,128)(4,1)} %get-tuple-element.6, bf16[128,4,8,128]{3,2,1,0:T(8,128)(2,1)} %get-tuple-element.4, bf16[64,4,8,128]{3,2,1,0:T(8,128)(2,1)} %get-tuple-element.2), kind=kOutput, calls=%fused_computation.3 | convolution fusion | flops 1088421888 | bytes 4194304 | tf_op jit(solution)/shard_map/hij,jhd->ihd/dot_general | solution.py:37
  79.8 1.6 copy.44
  81.4 6.6 %fusion.1 = f32[4,128,512]{2,1,0:T(8,128)} fusion(bf16[1024,4,128]{0,2,1:T(8,128)(2,1)S(1)} %bitcast.69, pred[512,1024]{1,0:T(8,128)(4,1)} %get-tuple-element.7, bf16[128,4,8,128]{3,2,1,0:T(8,128)(2,1)} %get-tuple-element.4, bf16[64,4,8,128]{3,2,1,0:T(8,128)(2,1)} %get-tuple-element.3), kind=kOutput, calls=%fused_computation.4 | convolution fusion | flops 1088421888 | bytes 4194304 | tf_op jit(solution)/shard_map/hij,jhd->ihd/dot_general | solution.py:37
  87.9 1.6 copy.45
  89.5 0.2 multiply_reduce_fusion
  89.8 2.4 %fusion.18 = f32[1024,512]{1,0:T(8,128)S(1)} fusion(bf16[512,512]{1,0:T(8,128)(2,1)S(1)} %all_gather.13, f32[1024,2048]{1,0:T(8,128)} %get-tuple-element.9, f32[512,512]{1,0:T(8,128)S(1)} %copy.45, f32[512,512]{1,0:T(8,128)S(1)} %copy.44, f32[512]{0:T(512)S(1)} %copy-done.3, f32[1024]{0:T(1024)S(1)} %add_rsqrt_fusion), kind=kOutput, calls=%fused_computation.21 | convolution fusion | flops 539492352 | bytes 6821888 | tf_op jit(solution)/shard_map/dot_general | solution.py:44
  92.2 1.0 fusion.15
  93.2 23.4 %all_gather.14 = bf16[64,512]{1,0:T(8,128)(2,1)S(1)} all-gather(bf16[8,512]{1,0:T(8,128)(2,1)S(1)} %slice.35), channel_id=1, replica_groups=mesh['section'=2,'dp'=4,'mp'=4] {'section','mp'}, dimensions={0}, use_global_device_ids=true | all-gather | bytes 73728 | tf_op jit(solution)/shard_map/all_gather | solution.py:72
  116.7 0.3 multiply_reduce_fusion.1
  117.0 14.3 %psum.14 = f32[64]{0:T(128)S(1)} all-reduce(f32[64]{0:T(128)S(1)} %get-tuple-element.10), channel_id=1, replica_groups=mesh['section'=2,'dp'=4,'mp'=4] {'section','mp'}, use_global_device_ids=true, to_apply=%region_4.5 | all-reduce | flops 64 | bytes 512 | tf_op jit(solution)/shard_map/psum | solution.py:79
  131.4 9.8 %all_gather.15 = bf16[64,2048]{1,0:T(8,128)(2,1)S(1)} all-gather(bf16[64,512]{1,0:T(8,128)(2,1)S(1)} %multiply_convert_fusion), channel_id=1, replica_groups=mesh['section'=2,'dp'=4,'mp'=4] {'mp'}, dimensions={1}, use_global_device_ids=true | all-gather | bytes 327680 | tf_op jit(solution)/shard_map/all_gather | solution.py:83
  141.1 5.7 %convolution_convert_fusion = bf16[64,2048]{1,0:T(8,128)(2,1)} fusion(bf16[64,2048]{1,0:T(8,128)(2,1)S(1)} %all_gather.15, bf16[2048,2048]{1,0:T(8,128)(2,1)} %param.18), kind=kOutput, calls=%fused_computation.7 | convolution fusion | flops 537001984 | bytes 8912896 | tf_op jit(solution)/shard_map/dot_general | solution.py:82
  146.9 16.9 %all-reduce.2.cloned.1.call-done = bf16[64,2048]{1,0:T(8,128)(2,1)} async-done(((bf16[64,2048]{1,0:T(8,128)(2,1)}), bf16[64,2048]{1,0:T(8,128)(2,1)}) %all-reduce.2.cloned.1.call-update) | async-done | bytes 262160 | tf_op jit(solution)/shard_map/psum | solution.py:87
  163.8 1.1 fusion.37
  165.0 5.0 %fusion.60 = f32[64,2048]{1,0:T(8,128)S(1)} fusion(bf16[64,2048]{1,0:T(8,128)(2,1)S(1)} %bitcast.66, bf16[2048,2048]{1,0:T(8,128)(2,1)} %param.19), kind=kOutput, calls=%fused_computation.73 | convolution fusion | flops 536870912 | bytes 9175040 | tf_op jit(solution)/shard_map/dot_general | solution.py:94
  170.0 0.7 convert_element_type.51
  170.7 25.4 %reduce-scatter.2.cloned.1.call-done = bf16[16,2048]{1,0:T(8,128)(2,1)} async-done(((bf16[64,2048]{1,0:T(8,128)(2,1)}), bf16[16,2048]{1,0:T(8,128)(2,1)}) %reduce-scatter.2.cloned.1.call-update) | async-done | bytes 65552 | tf_op jit(solution)/shard_map/reduce_scatter | solution.py:96
  196.1 4.7 %all_to_all.19 = bf16[2,8,2048]{2,1,0:T(8,128)(2,1)S(1)} all-to-all(bf16[2,8,2048]{2,1,0:T(8,128)(2,1)} %bitcast.74), channel_id=1, replica_groups=mesh['section'=2,'dp'=4,'mp'=4] {'section'}, dimensions={0} | all-to-all | bytes 131072 | tf_op jit(solution)/shard_map/all_to_all | solution.py:104
  200.8 0.6 copy.74
  (24 shorter events, 0.4 us)
Async XLA Ops:
  7.2 109.5 %copy-start = (bf16[512,512]{1,0:T(8,128)(2,1)S(1)}, bf16[512,512]{1,0:T(8,128)(2,1)}, u32[]{:S(2)}) copy-start(bf16[512,512]{1,0:T(8,128)(2,1)} %param.16) | copy-start | bytes 1572868
  7.2 54.8 %all-gather.2.cloned.1.call-start = ((), (), s32[]{:S(2)}) async-start(), calls=%async_computation.2 | async-start | bytes 2621440 | tf_op jit(solution)/shard_map/all_gather | solution.py:66
  7.9 155.9 %all-reduce.2.cloned.1.call-start = ((), (), s32[]{:S(2)}) async-start(), calls=%async_computation.3 | async-start | bytes 524288 | tf_op jit(solution)/shard_map/psum | solution.py:87
  81.4 8.4 %copy-start.3 = (f32[512]{0:T(512)S(1)}, f32[512]{0:T(512)}, u32[]{:S(2)}) copy-start(f32[512]{0:T(512)} %param.15) | copy-start | bytes 6148
  89.5 2.7 %copy-start.1 = (bf16[1,1024,512]{2,1,0:T(8,128)(2,1)S(1)}, bf16[1,1024,512]{2,1,0:T(8,128)(2,1)}, u32[]{:S(2)}) copy-start(bf16[1,1024,512]{2,1,0:T(8,128)(2,1)} %param.10) | copy-start | bytes 3145732
  93.2 53.6 %copy-start.2 = (bf16[32,512]{1,0:T(8,128)(2,1)}, bf16[32,512]{1,0:T(8,128)(2,1)S(1)}, u32[]{:S(2)}) copy-start(bf16[32,512]{1,0:T(8,128)(2,1)S(1)} %fusion.15) | copy-start | bytes 98308
  146.8 49.3 %reduce-scatter.2.cloned.1.call-start = ((), (), s32[]{:S(2)}) async-start(), calls=%async_computation.4 | async-start | bytes 327680 | tf_op jit(solution)/shard_map/reduce_scatter | solution.py:96
Sparse Core Ops, SparseCore 0:
  9.6 52.3 all-gather.1
  146.9 16.8 all-reduce.1
  170.8 25.2 reduce-scatter.1
where the time goes:
time: 209 us; the launch traced here: 208 us
  blocking collectives  75 us (36%)
  waiting for transfers between devices  69.6 us (33%)
  matrix products  35.6 us (17%)
  between operations  14.6 us (7%)
  local copies, waits for them, and re-layouts  7.6 us (4%)
  other arithmetic  5.41 us (3%)
    all_gather x1, waiting for transfers between devices, per_device(): lax.all_gather(w_uvqk, 'dp', axis=0, tiled=True)  26.6 us
    reduce_scatter x1, waiting for transfers between devices, per_device(): lax.psum_scatter(lax.dynamic_update_slice_in_dim(part_sum, target, model_...  25.4 us
    all_gather x1, blocking collectives, per_device(): lax.all_gather(pooled[:micro_count], ('section', 'mp'), axis=0, tiled=True)  23.4 us
    all_gather x1, blocking collectives, per_device(): lax.all_gather(w_out, 'dp', axis=0, tiled=True)  22.8 us
    psum x1, waiting for transfers between devices, per_device(): lax.psum(half_up.astype(jnp.bfloat16), 'section').astype(jnp.float32)  16.9 us
    psum x1, blocking collectives, per_device(): lax.psum(jnp.sum(local_in * local_in, axis=1), ('section', 'mp'))  14.3 us
    dot_general x2, matrix products, encode_user(): jnp.einsum('hij,jhd->ihd', weights, value_heads, preferred_element_type=j...  13.1 us
    all_gather x1, blocking collectives, per_device(): lax.all_gather(normed_part, 'mp', axis=1, tiled=True)  9.77 us
  transfers between devices with their start and end apart: 3, of which 3 were waited for; matrix products, arithmetic and copies ran while one was open for 2% of the time, Pallas kernels for 0%

commit v1 on v0

v1 whole, which is shorter than its diff:
```python
import functools

import jax
import jax.numpy as jnp
from jax import lax
from jax.experimental import pallas as pl
from jax.experimental.pallas import tpu as pltpu
from jax.sharding import PartitionSpec as P

HEADS = 4
DM = 4096
MICRO = 4
SESS_MAX = 64
EPSILON = 1e-06
F32 = jnp.float32
BF16 = jnp.bfloat16

VMEM = pl.BlockSpec(memory_space=pltpu.VMEM)
SMEM = pl.BlockSpec(memory_space=pltpu.SMEM)
ANY = pl.BlockSpec(memory_space=pl.ANY)


def params(mib):
    return pltpu.CompilerParams(vmem_limit_bytes=mib * 1024 * 1024)


def swap(x, axis, size, flip):
    return lax.ppermute(x, axis, [(i, i ^ flip) for i in range(size)])


def silu_half(h):
    return h + h * jnp.tanh(h)


def encoder_rows(place, counts, row0, first_out, *refs):
    refs = list(refs)
    hist_ref, sess_ref, ev_ref, gain_ref = refs[:4]
    refs = refs[4:]
    n_w, n_wout, n_kv = counts
    w_in_refs, refs = refs[:n_w], refs[n_w:]
    wout_in_refs, refs = refs[:n_wout], refs[n_wout:]
    kv_refs, refs = refs[:n_kv], refs[n_kv:]
    if n_kv:
        sums_ref, refs = refs[0], refs[1:]
    pooled_ref, kv_out, sums_out = refs[:3]
    w_ref, wout_ref, q_ref, gate_ref, att_ref, sems = refs[3:]
    rows, width = ev_ref.shape
    head = width // HEADS
    hist = hist_ref[0]
    copies = place(w_in_refs, wout_in_refs, w_ref, wout_ref, sems)
    for c in copies:
        c.start()

    sess = sess_ref.shape[1]
    lens = jnp.broadcast_to(sess_ref[...], (sess, sess))
    at_row = lax.broadcasted_iota(jnp.int32, (sess, sess), 0)
    at_col = lax.broadcasted_iota(jnp.int32, (sess, sess), 1)
    ends = jnp.sum(jnp.where(at_col <= at_row, lens, 0).astype(F32), axis=1, keepdims=True)
    starts = jnp.sum(jnp.where(at_col < at_row, lens, 0).astype(F32), axis=1, keepdims=True)
    ends = jnp.minimum(ends, hist.astype(F32))
    pos = (lax.broadcasted_iota(jnp.int32, (sess, rows), 1) + row0).astype(F32)
    member = jnp.where((pos >= starts) & (pos < ends), 1.0, 0.0).astype(BF16)
    n_valid = jnp.maximum(ends - starts, 0.0)

    for c in copies:
        c.wait()

    step = min(rows, 256)
    for r in range(0, rows, step):
        x = ev_ref[r : r + step, :]
        at = slice(r, r + step)
        row_pos = lax.broadcasted_iota(jnp.int32, (step, 1), 0) + (row0 + r)

        def act(n):
            part = jnp.dot(x, w_ref[:, n * width : (n + 1) * width], preferred_element_type=F32)
            return silu_half(part * 0.5)

        gate_ref[at, :] = act(0)
        kv_out[at, :width] = jnp.where(row_pos < hist, act(1), 0.0).astype(BF16)
        q_ref[at, :] = act(2).astype(BF16)
        kv_out[at, width:] = act(3).astype(BF16)

    blocks = []
    for ref in list(kv_refs) + [kv_out]:
        for r in range(0, ref.shape[0], step):
            blocks.append((ref, r))
    tri = lax.broadcasted_iota(jnp.int32, (step, step), 1) <= lax.broadcasted_iota(
        jnp.int32, (step, step), 0
    )
    before = len(blocks) - rows // step
    for i in range(rows // step):
        at = slice(i * step, (i + 1) * step)
        for h in range(HEADS):
            q = q_ref[at, h * head : (h + 1) * head]
            total = None
            for j in range(before + i + 1):
                ref, r = blocks[j]
                k = ref[r : r + step, width + h * head : width + (h + 1) * head]
                v = ref[r : r + step, h * head : (h + 1) * head]
                s = lax.dot_general(q, k, (((1,), (1,)), ((), ())), preferred_element_type=F32)
                wts = silu_half(s * (0.5 * head**-0.5))
                if j == before + i:
                    wts = jnp.where(tri, wts, 0.0)
                mixed = jnp.dot(wts.astype(BF16), v, preferred_element_type=F32)
                total = mixed if total is None else total + mixed
            att_ref[at, h * head : (h + 1) * head] = total

    sums_ev = jnp.dot(member, ev_ref[...], preferred_element_type=F32)
    att = att_ref[...]
    inv = lax.rsqrt(jnp.mean(att * att, axis=1, keepdims=True) + EPSILON)
    gated = (att * inv * gain_ref[...] * gate_ref[...]).astype(BF16)
    sums_g = jnp.dot(member, gated, preferred_element_type=F32)
    if n_kv:
        sums_ev = sums_ev + sums_ref[:, :width]
        sums_g = sums_g + sums_ref[:, width:]
    sums_out[:, :width] = sums_ev
    sums_out[:, width:] = sums_g

    hi = sums_g.astype(BF16)
    rest = sums_g - hi.astype(F32)
    mid = rest.astype(BF16)
    low = (rest - mid.astype(F32)).astype(BF16)
    terms = jnp.dot(jnp.concatenate([low, mid, hi], axis=0), wout_ref[...], preferred_element_type=F32)
    out = terms[:sess] + terms[sess : 2 * sess] + terms[2 * sess :] + sums_ev
    out = out / jnp.maximum(n_valid, 1.0)
    out = out.astype(BF16).astype(pooled_ref.dtype)
    pooled_ref[...] = out[:first_out]


def encoder_call(events, hist_len, sess_len, gain, place, weights, wouts, kvs, sums, row0, rows, take, dtype):
    width = events.shape[1]
    sess = sess_len.shape[1]
    block = row0 // rows
    prior = list(kvs) + ([sums] if kvs else [])
    specs = (
        [SMEM, VMEM, pl.BlockSpec((rows, width), lambda i: (block, 0)), VMEM]
        + [ANY] * (len(weights) + len(wouts))
        + [VMEM] * len(prior)
    )
    n_sems = 64
    return pl.pallas_call(
        functools.partial(encoder_rows, place, (len(weights), len(wouts), len(kvs)), row0, take),
        grid=(1,),
        in_specs=specs,
        out_specs=[VMEM, VMEM, VMEM],
        out_shape=[
            jax.ShapeDtypeStruct((take, width), dtype),
            jax.ShapeDtypeStruct((rows, 2 * width), BF16),
            jax.ShapeDtypeStruct((sess, 2 * width), F32),
        ],
        scratch_shapes=[
            pltpu.VMEM((width, 4 * width), BF16),
            pltpu.VMEM((width, width), BF16),
            pltpu.VMEM((rows, width), BF16),
            pltpu.VMEM((rows, width), F32),
            pltpu.VMEM((rows, width), F32),
            pltpu.SemaphoreType.DMA((n_sems,)),
        ],
        compiler_params=params(40),
        cost_estimate=pl.CostEstimate(
            flops=2 * rows * width * 4 * width + 4 * rows * (row0 + rows) * width,
            bytes_accessed=6 * 1024 * 1024,
            transcendentals=4 * rows * width + HEADS * rows * (row0 + rows),
        ),
        name=f"encode_rows_{row0}",
    )(hist_len, sess_len, events, gain, *weights, *wouts, *prior)


def gather_weights(w_uvqk, w_out, sections, dps, mps):
    depth, wide = w_uvqk.shape
    peers = sections * mps
    piece = wide // peers
    if wide % (128 * peers) or depth % 16:
        full = lax.all_gather(w_uvqk, "dp", axis=0, tiled=True)
        full_out = lax.all_gather(w_out, "dp", axis=0, tiled=True)

        def place_whole(ws, wouts, w_ref, wout_ref, sems):
            return [
                pltpu.make_async_copy(ws[0], w_ref, sems.at[0]),
                pltpu.make_async_copy(wouts[0], wout_ref, sems.at[1]),
            ]

        return [full], [full_out], place_whole

    s, m = lax.axis_index("section"), lax.axis_index("mp")
    mine = lax.dynamic_slice_in_dim(w_uvqk, (s * mps + m) * piece, piece, 1)
    got = jnp.stack([swap(mine, "dp", dps, k) for k in range(1, dps)])
    plane = [got] + [swap(got, "mp", mps, k) for k in range(1, mps)]
    across = [swap(p, "section", sections, 1) for p in plane] if sections == 2 else []
    wouts = [w_out] + [swap(w_out, "dp", dps, k) for k in range(1, dps)]

    def place(ws, wouts, w_ref, wout_ref, sems):
        z = lax.axis_index("dp")
        sec, col = lax.axis_index("section"), lax.axis_index("mp")
        copies = [pltpu.make_async_copy(ws[0], w_ref.at[pl.ds(pl.multiple_of(z * depth, depth), depth)], sems.at[0])]
        for a, half in enumerate(ws[1 : 1 + mps] and [ws[1 : 1 + mps], ws[1 + mps :]]):
            for j, ref in enumerate(half):
                spot = ((sec ^ a) * mps + (col ^ j)) * piece
                for k in range(1, dps):
                    dst = w_ref.at[
                        pl.ds(pl.multiple_of((z ^ k) * depth, depth), depth),
                        pl.ds(pl.multiple_of(spot, piece), piece),
                    ]
                    copies.append(pltpu.make_async_copy(ref.at[k - 1], dst, sems.at[len(copies)]))
        for k, ref in enumerate(wouts):
            dst = wout_ref.at[pl.ds(pl.multiple_of((z ^ k) * depth, depth), depth)]
            copies.append(pltpu.make_async_copy(ref, dst, sems.at[len(copies)]))
        return copies

    return [w_uvqk] + plane + across, wouts, place


def hidden_in_kernel(peers, mps, *refs):
    parts, (w_ref, gain_ref, local_ref, send_ref, x_ref) = refs[:peers], refs[peers:]
    me = lax.axis_index("section") * mps + lax.axis_index("mp")
    take = parts[0].shape[0]
    for k, ref in enumerate(parts):
        x_ref[pl.ds(pl.multiple_of((me ^ k) * take, take), take), :] = ref[...]
    local = jnp.dot(x_ref[...].astype(BF16), w_ref[...], preferred_element_type=F32)
    local_ref[...] = local
    cols = local.shape[1]
    send_ref[:, :cols] = (local * gain_ref[...].astype(F32)).astype(BF16)
    square = jnp.sum(local * local, axis=1, keepdims=True)
    hi = square.astype(BF16)
    lo = (square - hi.astype(F32)).astype(BF16)
    lane = lax.broadcasted_iota(jnp.int32, (local.shape[0], 128), 1)
    both = jnp.where(lane == 0, hi.astype(F32), jnp.where(lane == 1, lo.astype(F32), 0.0))
    send_ref[:, cols:] = both.astype(BF16)


def up_kernel(mps, chunks, *refs):
    parts, (w_any, half_ref, send_ref, x_ref, w_ref, sems) = refs[:mps], refs[mps:]
    wide = w_ref.shape[1]
    each = wide // chunks
    copies = [
        pltpu.make_async_copy(
            w_any.at[:, c * each : (c + 1) * each], w_ref.at[:, c * each : (c + 1) * each], sems.at[c]
        )
        for c in range(chunks)
    ]
    for c in copies:
        c.start()
    m = lax.axis_index("mp")
    cols = parts[0].shape[1] - 128
    square = None
    for k, ref in enumerate(parts):
        x_ref[:, pl.ds(pl.multiple_of((m ^ k) * cols, cols), cols)] = ref[:, :cols]
        tail = jnp.sum(ref[:, cols:].astype(F32), axis=1, keepdims=True)
        square = tail if square is None else square + tail
    x = x_ref[...]
    for c in range(chunks):
        copies[c].wait()
        at = slice(c * each, (c + 1) * each)
        half = jnp.dot(x, w_ref[:, at], preferred_element_type=F32)
        half_ref[:, at] = half
        send_ref[:, at] = half.astype(BF16)
    hi = square.astype(BF16)
    lo = (square - hi.astype(F32)).astype(BF16)
    lane = lax.broadcasted_iota(jnp.int32, (square.shape[0], 128), 1)
    half_ref[:, wide:] = jnp.broadcast_to(square, (square.shape[0], 128))
    both = jnp.where(lane == 0, hi.astype(F32), jnp.where(lane == 1, lo.astype(F32), 0.0))
    send_ref[:, wide:] = both.astype(BF16)


def down_kernel(chunks, half_ref, other_ref, local_ref, w_any, out_ref, part_ref, w_ref, sems):
    wide = w_ref.shape[1]
    each = wide // chunks
    copies = [
        pltpu.make_async_copy(
            w_any.at[:, c * each : (c + 1) * each], w_ref.at[:, c * each : (c + 1) * each], sems.at[c]
        )
        for c in range(chunks)
    ]
    for c in copies:
        c.start()
    units = w_ref.shape[0]
    square = half_ref[:, units : units + 1] + jnp.sum(other_ref[:, units:].astype(F32), axis=1, keepdims=True)
    inv = lax.rsqrt(square / DM + EPSILON)
    up = (half_ref[:, :units] + other_ref[:, :units].astype(F32)) * inv
    hidden = jax.nn.gelu(up, approximate=True).astype(BF16)
    for c in range(chunks):
        copies[c].wait()
        at = slice(c * each, (c + 1) * each)
        part_ref[:, at] = jnp.dot(hidden, w_ref[:, at], preferred_element_type=F32)
    m = lax.axis_index("mp")
    cols = local_ref.shape[1]
    own = pl.ds(pl.multiple_of(m * cols, cols), cols)
    part_ref[:, own] = part_ref[:, own] + local_ref[...]
    out_ref[...] = part_ref[...].astype(BF16)


def sum_kernel(sections, mps, got_ref, out_ref):
    got = got_ref[...].astype(F32)
    take, wide = out_ref.shape[0], got.shape[1]
    for s in range(sections):
        total = got[s * mps * take : (s * mps + 1) * take]
        for k in range(s * mps + 1, (s + 1) * mps):
            total = total + got[k * take : (k + 1) * take]
        out_ref[:, s * wide : (s + 1) * wide] = total.astype(BF16)


def cross_block(micro_rows, w_in, ffn_gain, w_up, w_down, sections, mps):
    peers = sections * mps
    take, width = micro_rows.shape
    rows = take * peers
    cols = w_in.shape[1]
    units = w_up.shape[1]
    half_width = w_down.shape[1]
    group = ("section", "mp")

    parts = [micro_rows] + [swap(micro_rows, group, peers, k) for k in range(1, peers)]
    local, send = pl.pallas_call(
        functools.partial(hidden_in_kernel, peers, mps),
        out_shape=[
            jax.ShapeDtypeStruct((rows, cols), F32),
            jax.ShapeDtypeStruct((rows, cols + 128), BF16),
        ],
        in_specs=[VMEM] * (peers + 2),
        out_specs=[VMEM] * 2,
        scratch_shapes=[pltpu.VMEM((rows, width), F32)],
        compiler_params=params(16),
        cost_estimate=pl.CostEstimate(
            flops=2 * rows * width * cols, bytes_accessed=2 * width * cols, transcendentals=0
        ),
        name="hidden_in",
    )(*parts, w_in, ffn_gain)

    got = [send] + [swap(send, "mp", mps, k) for k in range(1, mps)]
    chunks = 4
    half, half_send = pl.pallas_call(
        functools.partial(up_kernel, mps, chunks),
        out_shape=[
            jax.ShapeDtypeStruct((rows, units + 128), F32),
            jax.ShapeDtypeStruct((rows, units + 128), BF16),
        ],
        in_specs=[VMEM] * mps + [ANY],
        out_specs=[VMEM] * 2,
        scratch_shapes=[
            pltpu.VMEM((rows, cols * mps), BF16),
            pltpu.VMEM(w_up.shape, BF16),
            pltpu.SemaphoreType.DMA((chunks,)),
        ],
        compiler_params=params(32),
        cost_estimate=pl.CostEstimate(
            flops=2 * rows * w_up.size, bytes_accessed=2 * w_up.size, transcendentals=0
        ),
        name="up_half",
    )(*got, w_up)

    other = swap(half_send, "section", sections, 1)
    partial = pl.pallas_call(
        functools.partial(down_kernel, chunks),
        out_shape=jax.ShapeDtypeStruct((rows, half_width), BF16),
        in_specs=[VMEM] * 3 + [ANY],
        out_specs=VMEM,
        scratch_shapes=[
            pltpu.VMEM((rows, half_width), F32),
            pltpu.VMEM(w_down.shape, BF16),
            pltpu.SemaphoreType.DMA((chunks,)),
        ],
        compiler_params=params(32),
        cost_estimate=pl.CostEstimate(
            flops=2 * rows * w_down.size, bytes_accessed=2 * w_down.size, transcendentals=rows * units
        ),
        name="down_part",
    )(half, other, local, w_down)

    arrived = lax.all_to_all(partial.reshape(peers, take, half_width), group, split_axis=0, concat_axis=0, tiled=True)
    return pl.pallas_call(
        functools.partial(sum_kernel, sections, mps),
        out_shape=jax.ShapeDtypeStruct((take, half_width * sections), BF16),
        in_specs=[VMEM],
        out_specs=VMEM,
        compiler_params=params(16),
        name="sum_rows",
    )(arrived.reshape(rows, half_width))


def per_device(sections, dps, mps, events, hist_len, sess_len, w_uvqk, w_out, attn_gain, w_in, ffn_gain, w_up, w_down):
    events = events[0]
    length, width = events.shape
    sess = sess_len.shape[1]
    micro_count = sess // MICRO
    gain = attn_gain.reshape(1, width)
    weights, wouts, place = gather_weights(w_uvqk, w_out, sections, dps, mps)
    encode = functools.partial(encoder_call, events, hist_len, sess_len, gain, place, weights, wouts)

    first = min(length, micro_count * SESS_MAX)
    micro_rows, kv, sums = encode([], None, 0, first, micro_count, F32)
    cross_out = cross_block(micro_rows, w_in, ffn_gain, w_up, w_down, sections, mps)

    kvs, row0, step = [kv], first, 256
    pooled = None
    while row0 < length:
        pooled, kv, sums = encode(kvs, sums, row0, step, sess, BF16)
        kvs.append(kv)
        row0 += step
    return (pooled, cross_out)


def solution(mesh):
    sizes = [mesh.shape[name] for name in ("section", "dp", "mp")]
    return jax.shard_map(
        functools.partial(per_device, *sizes),
        mesh=mesh,
        in_specs=(
            P(("section", "dp", "mp"), None, None),
            P(("section", "dp", "mp")),
            P(("section", "dp", "mp"), None),
            P("dp", None),
            P("dp", None),
            P(),
            P(None, ("section", "mp")),
            P(None, ("section", "mp")),
            P("section", "mp"),
            P("mp", "section"),
        ),
        out_specs=(P(("section", "dp", "mp"), None), P(("section", "dp", "mp"), None)),
        check_vma=False,
    )
```

time: 209 us -> 100 us (0.48)
  blocking collectives: 75 us -> 0 us
  waiting for transfers between devices: 69.6 us -> 23.6 us
  matrix products: 35.6 us -> 0 us
  starting transfers between devices: 0.12 us -> 29.1 us
  Pallas kernels: 0 us -> 25.2 us
  between operations: 14.6 us -> 1.59 us
  local copies, waits for them, and re-layouts: 7.6 us -> 20.1 us
  other arithmetic: 5.41 us -> 0.02 us
    all_gather x3 -> x0, blocking collectives: 56 us -> none  [the longest x1 23.4 us: per_device(): lax.all_gather(pooled[:micro_count], ('section', 'mp'), axis=0, tiled=True)]
    dot_general x8 -> x0, matrix products: 35.6 us -> none  [the longest x2 13.1 us: encode_user(): jnp.einsum('hij,jhd->ihd', weights, value_heads, preferred_element_type=j...]
    all_gather x1 -> x0, waiting for transfers between devices: 26.6 us -> none  [per_device(): lax.all_gather(w_uvqk, 'dp', axis=0, tiled=True)]
    ppermute x0 -> x24, starting transfers between devices: none -> 25.5 us  [swap(): return lax.ppermute(x, axis, [(i, i ^ flip) for i in range(size)])]
    reduce_scatter x1 -> x0, waiting for transfers between devices: 25.4 us -> none  [per_device(): lax.psum_scatter(lax.dynamic_update_slice_in_dim(part_sum, target, model_...]
    pallas_call x0 -> x7, Pallas kernels: none -> 25.2 us  [the longest x3 15.9 us: encoder_call(): pl.pallas_call(functools.partial(encoder_rows, place, (len(weights), len(...]
    ppermute x0 -> x24, waiting for transfers between devices: none -> 23.6 us  [swap(): return lax.ppermute(x, axis, [(i, i ^ flip) for i in range(size)])]
    psum x1 -> x0, waiting for transfers between devices: 16.9 us -> none  [per_device(): lax.psum(half_up.astype(jnp.bfloat16), 'section').astype(jnp.float32)]
  transfers between devices with their start and end apart: 3 -> 25, of which waited for: 3 -> 10; matrix products, arithmetic and copies ran while one was open for 2% -> 0% of each run, Pallas kernels for 0% -> 11%
where the time goes in v1:
time: 100 us; the launch traced here: 99.7 us
  starting transfers between devices  29.1 us (29%)
  Pallas kernels  25.2 us (25%)
  waiting for transfers between devices  23.6 us (24%)
  local copies, waits for them, and re-layouts  20.1 us (20%)
  between operations  1.59 us (2%)
    ppermute x24, starting transfers between devices, swap(): return lax.ppermute(x, axis, [(i, i ^ flip) for i in range(size)])  25.5 us
    ppermute x24, waiting for transfers between devices, swap(): return lax.ppermute(x, axis, [(i, i ^ flip) for i in range(size)])  23.6 us
    unnamed x66, local copies, waits for them, and re-layouts  19.1 us
    pallas_call x3, Pallas kernels, encoder_call(): pl.pallas_call(functools.partial(encoder_rows, place, (len(weights), len(...  15.9 us
    pallas_call x1, Pallas kernels, cross_block(): pl.pallas_call(functools.partial(up_kernel, mps, chunks), out_shape=[jax....  4.2 us
    pallas_call x1, Pallas kernels, cross_block(): pl.pallas_call(functools.partial(down_kernel, chunks), out_shape=jax.Shap...  4.18 us
    all_to_all x1, starting transfers between devices, cross_block(): lax.all_to_all(partial.reshape(peers, take, half_width), group, split_axi...  3.6 us
  transfers between devices with their start and end apart: 25, of which 10 were waited for; matrix products, arithmetic and copies ran while one was open for 0% of the time, Pallas kernels for 11%

profile of v1, /device:TPU:0, one launch (start us, length us, event | category | flops | bytes accessed | tf_op | source)
XLA Modules:
  0.0 99.7 jit_solution(17275944334866385317)
XLA Ops:
  1.6 5.0 %collective-permute-start.2 = (bf16[128,256]{1,0:T(8,128)(2,1)S(1)}, bf16[128,256]{1,0:T(8,128)(2,1)S(1)}, u32[]{:S(2)}, u32[]{:S(2)}) collective-permute-start(bf16[128,256]{1,0:T(8,128)(2,1)S(1)} %constant_dynamic-slice_fusion), channel_id=1, source_target_pairs={{0,12},{4,8},{8,4},{12,0},{1,13},{5,9},{9,5},{13,1},{2,14},{6,10},... | collective-permute-start | bytes 196616 | tf_op jit(solution)/shard_map/ppermute | solution.py:28
  7.3 2.0 %collective-permute-done.2 = bf16[128,256]{1,0:T(8,128)(2,1)S(1)} collective-permute-done((bf16[128,256]{1,0:T(8,128)(2,1)S(1)}, bf16[128,256]{1,0:T(8,128)(2,1)S(1)}, u32[]{:S(2)}, u32[]{:S(2)}) %collective-permute-start.2) | collective-permute-done | bytes 65568 | tf_op jit(solution)/shard_map/ppermute | solution.py:28
  9.3 3.0 %collective-permute-done.1 = bf16[128,256]{1,0:T(8,128)(2,1)S(1)} collective-permute-done((bf16[128,256]{1,0:T(8,128)(2,1)S(1)}, bf16[128,256]{1,0:T(8,128)(2,1)S(1)}, u32[]{:S(2)}, u32[]{:S(2)}) %collective-permute-start.1) | collective-permute-done | bytes 65568 | tf_op jit(solution)/shard_map/ppermute | solution.py:28
  12.3 1.6 %collective-permute-start.3 = (bf16[3,128,256]{2,1,0:T(8,128)(2,1)S(1)}, bf16[3,128,256]{2,1,0:T(8,128)(2,1)S(1)}, u32[]{:S(2)}, u32[]{:S(2)}) collective-permute-start(bf16[3,128,256]{2,1,0:T(8,128)(2,1)S(1)} %pad_maximum_fusion.refs_5_), channel_id=1, source_target_pairs={{0,1},{1,0},{2,3},{3,2},{4,5},{5,4},{6,7},{7,6},{8,9},{9,8},{10,11... | collective-permute-start | bytes 589832 | tf_op jit(solution)/shard_map/ppermute | solution.py:28
  13.9 1.5 %collective-permute-start.4 = (bf16[3,128,256]{2,1,0:T(8,128)(2,1)S(1)}, bf16[3,128,256]{2,1,0:T(8,128)(2,1)S(1)}, u32[]{:S(2)}, u32[]{:S(2)}) collective-permute-start(bf16[3,128,256]{2,1,0:T(8,128)(2,1)S(1)} %pad_maximum_fusion.refs_5_), channel_id=1, source_target_pairs={{0,2},{1,3},{2,0},{3,1},{4,6},{5,7},{6,4},{7,5},{8,10},{9,11},{10,... | collective-permute-start | bytes 589832 | tf_op jit(solution)/shard_map/ppermute | solution.py:28
  15.9 1.1 %collective-permute-start.10 = (bf16[128,512]{1,0:T(8,128)(2,1)}, bf16[128,512]{1,0:T(8,128)(2,1)S(1)}, u32[]{:S(2)}, u32[]{:S(2)}) collective-permute-start(bf16[128,512]{1,0:T(8,128)(2,1)} %refs_13_.5), channel_id=1, source_target_pairs={{0,4},{4,0},{8,12},{12,8},{1,5},{5,1},{9,13},{13,9},{2,6},{6,2},{1... | collective-permute-start | bytes 393224 | tf_op jit(solution)/shard_map/ppermute | solution.py:28
  17.0 2.1 %collective-permute-start.11 = (bf16[128,512]{1,0:T(8,128)(2,1)}, bf16[128,512]{1,0:T(8,128)(2,1)S(1)}, u32[]{:S(2)}, u32[]{:S(2)}) collective-permute-start(bf16[128,512]{1,0:T(8,128)(2,1)} %refs_13_.5), channel_id=1, source_target_pairs={{0,8},{4,12},{8,0},{12,4},{1,9},{5,13},{9,1},{13,5},{2,10},{6,14},... | collective-permute-start | bytes 393224 | tf_op jit(solution)/shard_map/ppermute | solution.py:28
  19.1 2.6 %collective-permute-done.10.refs_14_ = bf16[128,512]{1,0:T(8,128)(2,1)S(1)} collective-permute-done((bf16[128,512]{1,0:T(8,128)(2,1)}, bf16[128,512]{1,0:T(8,128)(2,1)S(1)}, u32[]{:S(2)}, u32[]{:S(2)}) %collective-permute-start.10) | collective-permute-done | bytes 131104 | tf_op jit(solution)/shard_map/ppermute | solution.py:28
  22.3 2.2 %collective-permute-done.4.refs_7_ = bf16[3,128,256]{2,1,0:T(8,128)(2,1)S(1)} collective-permute-done((bf16[3,128,256]{2,1,0:T(8,128)(2,1)S(1)}, bf16[3,128,256]{2,1,0:T(8,128)(2,1)S(1)}, u32[]{:S(2)}, u32[]{:S(2)}) %collective-permute-start.4) | collective-permute-done | bytes 196640 | tf_op jit(solution)/shard_map/ppermute | solution.py:28
  25.0 1.6 %collective-permute-start.12 = (bf16[128,512]{1,0:T(8,128)(2,1)}, bf16[128,512]{1,0:T(8,128)(2,1)S(1)}, u32[]{:S(2)}, u32[]{:S(2)}) collective-permute-start(bf16[128,512]{1,0:T(8,128)(2,1)} %refs_13_.5), channel_id=1, source_target_pairs={{0,12},{4,8},{8,4},{12,0},{1,13},{5,9},{9,5},{13,1},{2,14},{6,10},... | collective-permute-start | bytes 393224 | tf_op jit(solution)/shard_map/ppermute | solution.py:28
  27.3 5.3 %collective-permute-done.12.refs_16_ = bf16[128,512]{1,0:T(8,128)(2,1)S(1)} collective-permute-done((bf16[128,512]{1,0:T(8,128)(2,1)}, bf16[128,512]{1,0:T(8,128)(2,1)S(1)}, u32[]{:S(2)}, u32[]{:S(2)}) %collective-permute-start.12) | collective-permute-done | bytes 131104 | tf_op jit(solution)/shard_map/ppermute | solution.py:28
  32.7 1.5 %copy-done.1 = bf16[1,1024,512]{2,1,0:T(8,128)(2,1)S(1)} copy-done((bf16[1,1024,512]{2,1,0:T(8,128)(2,1)S(1)}, bf16[1,1024,512]{2,1,0:T(8,128)(2,1)}, u32[]{:S(2)}) %copy-start.1) | copy-done | bytes 1048600
  34.2 1.0 %copy-done.3 = bf16[128,2048]{1,0:T(8,128)(2,1)S(1)} copy-done((bf16[128,2048]{1,0:T(8,128)(2,1)S(1)}, bf16[128,2048]{1,0:T(8,128)(2,1)}, u32[]{:S(2)}) %copy-start.3) | copy-done | bytes 524312
  37.5 5.0 %encode_rows_0.1 = (f32[8,512]{1,0:T(8,128)S(1)}, bf16[512,1024]{1,0:T(8,128)(2,1)S(1)}, f32[32,1024]{1,0:T(8,128)S(1)}) custom-call(s32[1]{0:T(128)S(6)} %copy.12.refs_0_, s32[1,32]{1,0:T(1,128)S(1)} %copy-done.29, bf16[1024,512]{1,0:T(8,128)(2,1)S(1)} %bitcast.9, f32[1,512]{1,0:T(1,128)S(1)} %bitcast.13, bf16[128,2048]{1,0:T(8,128)(2,1)S(1)} %copy-done.3, ...), custom_call_target="tpu_custom_call" | custom-call | flops 1610612736 | bytes 6291456 | tf_op jit(solution)/shard_map/encode_rows_0/pallas_call | solution.py:141
  42.4 1.2 %collective-permute-start.13 = (f32[8,512]{1,0:T(8,128)S(1)}, f32[8,512]{1,0:T(8,128)S(1)}, u32[]{:S(2)}, u32[]{:S(2)}) collective-permute-start(f32[8,512]{1,0:T(8,128)S(1)} %get-tuple-element.17.refs_0_), channel_id=1, source_target_pairs={{0,1},{1,0},{2,3},{3,2},{16,17},{17,16},{18,19},{19,18},{4,5},{5,4... | collective-permute-start | bytes 49160 | tf_op jit(solution)/shard_map/ppermute | solution.py:28
  44.5 1.4 %collective-permute-start.15 = (f32[8,512]{1,0:T(8,128)S(1)}, f32[8,512]{1,0:T(8,128)S(1)}, u32[]{:S(2)}, u32[]{:S(2)}) collective-permute-start(f32[8,512]{1,0:T(8,128)S(1)} %get-tuple-element.17.refs_0_), channel_id=1, source_target_pairs={{0,3},{1,2},{2,1},{3,0},{16,19},{17,18},{18,17},{19,16},{4,7},{5,6... | collective-permute-start | bytes 49160 | tf_op jit(solution)/shard_map/ppermute | solution.py:28
  46.0 1.3 %collective-permute-start.17 = (f32[8,512]{1,0:T(8,128)S(1)}, f32[8,512]{1,0:T(8,128)S(1)}, u32[]{:S(2)}, u32[]{:S(2)}) collective-permute-start(f32[8,512]{1,0:T(8,128)S(1)} %get-tuple-element.17.refs_0_), channel_id=1, source_target_pairs={{0,17},{1,16},{2,19},{3,18},{16,1},{17,0},{18,3},{19,2},{4,21},{5,... | collective-permute-start | bytes 49160 | tf_op jit(solution)/shard_map/ppermute | solution.py:28
  47.8 1.6 %collective-permute-start.19 = (f32[8,512]{1,0:T(8,128)S(1)}, f32[8,512]{1,0:T(8,128)S(1)}, u32[]{:S(2)}, u32[]{:S(2)}) collective-permute-start(f32[8,512]{1,0:T(8,128)S(1)} %get-tuple-element.17.refs_0_), channel_id=1, source_target_pairs={{0,19},{1,18},{2,17},{3,16},{16,3},{17,2},{18,1},{19,0},{4,23},{5,... | collective-permute-start | bytes 49160 | tf_op jit(solution)/shard_map/ppermute | solution.py:28
  49.3 1.1 %collective-permute-done.18.refs_6_ = f32[8,512]{1,0:T(8,128)S(1)} collective-permute-done((f32[8,512]{1,0:T(8,128)S(1)}, f32[8,512]{1,0:T(8,128)S(1)}, u32[]{:S(2)}, u32[]{:S(2)}) %collective-permute-start.18) | collective-permute-done | bytes 16416 | tf_op jit(solution)/shard_map/ppermute | solution.py:28
  50.4 1.4 %collective-permute-done.19.refs_7_ = f32[8,512]{1,0:T(8,128)S(1)} collective-permute-done((f32[8,512]{1,0:T(8,128)S(1)}, f32[8,512]{1,0:T(8,128)S(1)}, u32[]{:S(2)}, u32[]{:S(2)}) %collective-permute-start.19) | collective-permute-done | bytes 16416 | tf_op jit(solution)/shard_map/ppermute | solution.py:28
  51.8 1.0 %copy-done.23 = bf16[512,512]{1,0:T(8,128)(2,1)S(1)} copy-done((bf16[512,512]{1,0:T(8,128)(2,1)S(1)}, bf16[512,512]{1,0:T(8,128)(2,1)}, u32[]{:S(2)}) %copy-start.23) | copy-done | bytes 524312
  53.9 1.6 %collective-permute-start.20 = (bf16[64,640]{1,0:T(8,128)(2,1)S(1)}, bf16[64,640]{1,0:T(8,128)(2,1)S(1)}, u32[]{:S(2)}, u32[]{:S(2)}) collective-permute-start(bf16[64,640]{1,0:T(8,128)(2,1)S(1)} %get-tuple-element.18.refs_0_), channel_id=1, source_target_pairs={{0,1},{1,0},{2,3},{3,2},{4,5},{5,4},{6,7},{7,6},{8,9},{9,8},{10,11... | collective-permute-start | bytes 245768 | tf_op jit(solution)/shard_map/ppermute | solution.py:28
  56.0 1.5 %collective-permute-start.22 = (bf16[64,640]{1,0:T(8,128)(2,1)S(1)}, bf16[64,640]{1,0:T(8,128)(2,1)S(1)}, u32[]{:S(2)}, u32[]{:S(2)}) collective-permute-start(bf16[64,640]{1,0:T(8,128)(2,1)S(1)} %get-tuple-element.18.refs_0_), channel_id=1, source_target_pairs={{0,3},{1,2},{2,1},{3,0},{4,7},{5,6},{6,5},{7,4},{8,11},{9,10},{10,... | collective-permute-start | bytes 245768 | tf_op jit(solution)/shard_map/ppermute | solution.py:28
  57.5 1.4 %collective-permute-done.20.refs_1_ = bf16[64,640]{1,0:T(8,128)(2,1)S(1)} collective-permute-done((bf16[64,640]{1,0:T(8,128)(2,1)S(1)}, bf16[64,640]{1,0:T(8,128)(2,1)S(1)}, u32[]{:S(2)}, u32[]{:S(2)}) %collective-permute-start.20) | collective-permute-done | bytes 81952 | tf_op jit(solution)/shard_map/ppermute | solution.py:28
  58.9 3.0 %collective-permute-done.21.refs_2_ = bf16[64,640]{1,0:T(8,128)(2,1)S(1)} collective-permute-done((bf16[64,640]{1,0:T(8,128)(2,1)S(1)}, bf16[64,640]{1,0:T(8,128)(2,1)S(1)}, u32[]{:S(2)}, u32[]{:S(2)}) %collective-permute-start.21) | collective-permute-done | bytes 81952 | tf_op jit(solution)/shard_map/ppermute | solution.py:28
  61.8 3.4 %copy-done = bf16[2048,2048]{1,0:T(8,128)(2,1)S(1)} copy-done((bf16[2048,2048]{1,0:T(8,128)(2,1)S(1)}, bf16[2048,2048]{1,0:T(8,128)(2,1)}, u32[]{:S(2)}) %copy-start) | copy-done | bytes 8388632
  65.2 4.2 %up_half.1 = (f32[64,2176]{1,0:T(8,128)S(1)}, bf16[64,2176]{1,0:T(8,128)(2,1)S(1)}) custom-call(bf16[64,640]{1,0:T(8,128)(2,1)S(1)} %get-tuple-element.18.refs_0_, bf16[64,640]{1,0:T(8,128)(2,1)S(1)} %collective-permute-done.20.refs_1_, bf16[64,640]{1,0:T(8,128)(2,1)S(1)} %collective-permute-done.21.refs_2_, ...), custom_call_target="tpu_custom_call" | custom-call | flops 536870912 | bytes 8388608 | tf_op jit(solution)/shard_map/up_half/pallas_call | solution.py:330
  69.5 1.5 %collective-permute-done.23.other_ref = bf16[64,2176]{1,0:T(8,128)(2,1)S(1)} collective-permute-done((bf16[64,2176]{1,0:T(8,128)(2,1)S(1)}, bf16[64,2176]{1,0:T(8,128)(2,1)S(1)}, u32[]{:S(2)}, u32[]{:S(2)}) %collective-permute-start.23) | collective-permute-done | bytes 278560 | tf_op jit(solution)/shard_map/ppermute | solution.py:28
  71.0 4.2 %down_part.1 = bf16[64,2048]{1,0:T(8,128)(2,1)} custom-call(f32[64,2176]{1,0:T(8,128)S(1)} %get-tuple-element.19.half_ref, bf16[64,2176]{1,0:T(8,128)(2,1)S(1)} %collective-permute-done.23.other_ref, f32[64,512]{1,0:T(8,128)S(1)} %get-tuple-element.21.local_ref, bf16[2048,2048]{1,0:T(8,128)(2,1)S(1)} %bitcast.8), custom_call_target="tpu_custom_call" | custom-call | flops 536870912 | bytes 8388608 | tf_op jit(solution)/shard_map/down_part/pallas_call | solution.py:351
  75.2 3.6 %all-to-all-start = ((bf16[8,8,2048]{2,1,0:T(8,128)(2,1)}), bf16[8,8,2048]{2,1,0:T(8,128)(2,1)S(1)}, u32[]{:S(2)}, u32[]{:S(2)}) async-start(bf16[8,8,2048]{2,1,0:T(8,128)(2,1)} %bitcast.5), calls=%async_computation | async-start | bytes 524288 | tf_op jit(solution)/shard_map/all_to_all | solution.py:368
  88.1 5.3 %encode_rows_512.1 = (bf16[32,512]{1,0:T(8,128)(2,1)}, bf16[256,1024]{1,0:T(8,128)(2,1)S(1)}, f32[32,1024]{1,0:T(8,128)S(1)}) custom-call(s32[1]{0:T(128)S(6)} %copy.12.refs_0_, s32[1,32]{1,0:T(1,128)S(1)} %copy-done.30, bf16[1024,512]{1,0:T(8,128)(2,1)S(1)} %bitcast.10, f32[1,512]{1,0:T(1,128)S(1)} %bitcast.14, bf16[128,2048]{1,0:T(8,128)(2,1)S(1)} %copy-done.4, ...), custom_call_target="tpu_custom_call" | custom-call | flops 939524096 | bytes 6291456 | tf_op jit(solution)/shard_map/encode_rows_512/pallas_call | solution.py:141
  93.3 5.7 %encode_rows_768.1 = (bf16[32,512]{1,0:T(8,128)(2,1)}, bf16[256,1024]{1,0:T(8,128)(2,1)}, f32[32,1024]{1,0:T(8,128)}) custom-call(s32[1]{0:T(128)S(6)} %copy.12.refs_0_, s32[1,32]{1,0:T(1,128)S(1)} %copy-done.30, bf16[1024,512]{1,0:T(8,128)(2,1)S(1)} %bitcast.11, f32[1,512]{1,0:T(1,128)S(1)} %bitcast.15, bf16[128,2048]{1,0:T(8,128)(2,1)S(1)} %copy-done.4, ...), custom_call_target="tpu_custom_call" | custom-call | flops 1073741824 | bytes 6291456 | tf_op jit(solution)/shard_map/encode_rows_768/pallas_call | solution.py:141
  (94 shorter events, 18.2 us)
Async XLA Ops:
  0.6 70.4 %slice-start = ((s8[8388608]{0:T(1024)(128)(4,1)}), s8[4194304]{0:T(1024)(128)(4,1)S(1)}, s32[]{:S(2)}) async-start(s8[8388608]{0:T(1024)(128)(4,1)} %bitcast.7), calls=%async_computation.1 | async-start | bytes 8388608
  1.6 7.6 %collective-permute-start.2 = (bf16[128,256]{1,0:T(8,128)(2,1)S(1)}, bf16[128,256]{1,0:T(8,128)(2,1)S(1)}, u32[]{:S(2)}, u32[]{:S(2)}) collective-permute-start(bf16[128,256]{1,0:T(8,128)(2,1)S(1)} %constant_dynamic-slice_fusion), channel_id=1, source_target_pairs={{0,12},{4,8},{8,4},{12,0},{1,13},{5,9},{9,5},{13,1},{2,14},{6,10},... | collective-permute-start | bytes 196616 | tf_op jit(solution)/shard_map/ppermute | solution.py:28
  6.7 5.6 %collective-permute-start.1 = (bf16[128,256]{1,0:T(8,128)(2,1)S(1)}, bf16[128,256]{1,0:T(8,128)(2,1)S(1)}, u32[]{:S(2)}, u32[]{:S(2)}) collective-permute-start(bf16[128,256]{1,0:T(8,128)(2,1)S(1)} %constant_dynamic-slice_fusion), channel_id=1, source_target_pairs={{0,8},{4,12},{8,0},{12,4},{1,9},{5,13},{9,1},{13,5},{2,10},{6,14},... | collective-permute-start | bytes 196616 | tf_op jit(solution)/shard_map/ppermute | solution.py:28
  6.7 5.6 %collective-permute-start = (bf16[128,256]{1,0:T(8,128)(2,1)S(1)}, bf16[128,256]{1,0:T(8,128)(2,1)S(1)}, u32[]{:S(2)}, u32[]{:S(2)}) collective-permute-start(bf16[128,256]{1,0:T(8,128)(2,1)S(1)} %constant_dynamic-slice_fusion), channel_id=1, source_target_pairs={{0,4},{4,0},{8,12},{12,8},{1,5},{5,1},{9,13},{13,9},{2,6},{6,2},{1... | collective-permute-start | bytes 196616 | tf_op jit(solution)/shard_map/ppermute | solution.py:28
  12.3 9.4 %collective-permute-start.3 = (bf16[3,128,256]{2,1,0:T(8,128)(2,1)S(1)}, bf16[3,128,256]{2,1,0:T(8,128)(2,1)S(1)}, u32[]{:S(2)}, u32[]{:S(2)}) collective-permute-start(bf16[3,128,256]{2,1,0:T(8,128)(2,1)S(1)} %pad_maximum_fusion.refs_5_), channel_id=1, source_target_pairs={{0,1},{1,0},{2,3},{3,2},{4,5},{5,4},{6,7},{7,6},{8,9},{9,8},{10,11... | collective-permute-start | bytes 589832 | tf_op jit(solution)/shard_map/ppermute | solution.py:28
  13.9 10.6 %collective-permute-start.4 = (bf16[3,128,256]{2,1,0:T(8,128)(2,1)S(1)}, bf16[3,128,256]{2,1,0:T(8,128)(2,1)S(1)}, u32[]{:S(2)}, u32[]{:S(2)}) collective-permute-start(bf16[3,128,256]{2,1,0:T(8,128)(2,1)S(1)} %pad_maximum_fusion.refs_5_), channel_id=1, source_target_pairs={{0,2},{1,3},{2,0},{3,1},{4,6},{5,7},{6,4},{7,5},{8,10},{9,11},{10,... | collective-permute-start | bytes 589832 | tf_op jit(solution)/shard_map/ppermute | solution.py:28
  15.4 9.1 %collective-permute-start.5 = (bf16[3,128,256]{2,1,0:T(8,128)(2,1)S(1)}, bf16[3,128,256]{2,1,0:T(8,128)(2,1)S(1)}, u32[]{:S(2)}, u32[]{:S(2)}) collective-permute-start(bf16[3,128,256]{2,1,0:T(8,128)(2,1)S(1)} %pad_maximum_fusion.refs_5_), channel_id=1, source_target_pairs={{0,3},{1,2},{2,1},{3,0},{4,7},{5,6},{6,5},{7,4},{8,11},{9,10},{10,... | collective-permute-start | bytes 589832 | tf_op jit(solution)/shard_map/ppermute | solution.py:28
  15.9 5.9 %collective-permute-start.10 = (bf16[128,512]{1,0:T(8,128)(2,1)}, bf16[128,512]{1,0:T(8,128)(2,1)S(1)}, u32[]{:S(2)}, u32[]{:S(2)}) collective-permute-start(bf16[128,512]{1,0:T(8,128)(2,1)} %refs_13_.5), channel_id=1, source_target_pairs={{0,4},{4,0},{8,12},{12,8},{1,5},{5,1},{9,13},{13,9},{2,6},{6,2},{1... | collective-permute-start | bytes 393224 | tf_op jit(solution)/shard_map/ppermute | solution.py:28
  17.0 8.0 %collective-permute-start.11 = (bf16[128,512]{1,0:T(8,128)(2,1)}, bf16[128,512]{1,0:T(8,128)(2,1)S(1)}, u32[]{:S(2)}, u32[]{:S(2)}) collective-permute-start(bf16[128,512]{1,0:T(8,128)(2,1)} %refs_13_.5), channel_id=1, source_target_pairs={{0,8},{4,12},{8,0},{12,4},{1,9},{5,13},{9,1},{13,5},{2,10},{6,14},... | collective-permute-start | bytes 393224 | tf_op jit(solution)/shard_map/ppermute | solution.py:28
  21.7 32.1 %copy-start.17 = (bf16[128,512]{1,0:T(8,128)(2,1)}, bf16[128,512]{1,0:T(8,128)(2,1)S(1)}, u32[]{:S(2)}) copy-start(bf16[128,512]{1,0:T(8,128)(2,1)S(1)} %collective-permute-done.10.refs_14_) | copy-start | bytes 393220
  21.7 10.9 %collective-permute-start.6 = (bf16[3,128,256]{2,1,0:T(8,128)(2,1)S(1)}, bf16[3,128,256]{2,1,0:T(8,128)(2,1)S(1)}, u32[]{:S(2)}, u32[]{:S(2)}) collective-permute-start(bf16[3,128,256]{2,1,0:T(8,128)(2,1)S(1)} %pad_maximum_fusion.refs_5_), channel_id=1, source_target_pairs={{0,16},{16,0},{1,17},{17,1},{2,18},{18,2},{3,19},{19,3},{4,20},{20... | collective-permute-start | bytes 589832 | tf_op jit(solution)/shard_map/ppermute | solution.py:28
  21.8 10.9 %collective-permute-start.7 = (bf16[3,128,256]{2,1,0:T(8,128)(2,1)S(1)}, bf16[3,128,256]{2,1,0:T(8,128)(2,1)S(1)}, u32[]{:S(2)}, u32[]{:S(2)}) collective-permute-start(bf16[3,128,256]{2,1,0:T(8,128)(2,1)S(1)} %collective-permute-done.3.refs_6_), channel_id=1, source_target_pairs={{0,16},{16,0},{1,17},{17,1},{2,18},{18,2},{3,19},{19,3},{4,20},{20... | collective-permute-start | bytes 589832 | tf_op jit(solution)/shard_map/ppermute | solution.py:28
  24.5 8.2 %collective-permute-start.8 = (bf16[3,128,256]{2,1,0:T(8,128)(2,1)S(1)}, bf16[3,128,256]{2,1,0:T(8,128)(2,1)S(1)}, u32[]{:S(2)}, u32[]{:S(2)}) collective-permute-start(bf16[3,128,256]{2,1,0:T(8,128)(2,1)S(1)} %collective-permute-done.4.refs_7_), channel_id=1, source_target_pairs={{0,16},{16,0},{1,17},{17,1},{2,18},{18,2},{3,19},{19,3},{4,20},{20... | collective-permute-start | bytes 589832 | tf_op jit(solution)/shard_map/ppermute | solution.py:28
  24.5 50.8 %copy-start.5 = (bf16[3,128,256]{2,1,0:T(8,128)(2,1)}, bf16[3,128,256]{2,1,0:T(8,128)(2,1)S(1)}, u32[]{:S(2)}) copy-start(bf16[3,128,256]{2,1,0:T(8,128)(2,1)S(1)} %collective-permute-done.5.refs_8_) | copy-start | bytes 589828
  24.5 8.2 %collective-permute-start.9 = (bf16[3,128,256]{2,1,0:T(8,128)(2,1)S(1)}, bf16[3,128,256]{2,1,0:T(8,128)(2,1)S(1)}, u32[]{:S(2)}, u32[]{:S(2)}) collective-permute-start(bf16[3,128,256]{2,1,0:T(8,128)(2,1)S(1)} %collective-permute-done.5.refs_8_), channel_id=1, source_target_pairs={{0,16},{16,0},{1,17},{17,1},{2,18},{18,2},{3,19},{19,3},{4,20},{20... | collective-permute-start | bytes 589832 | tf_op jit(solution)/shard_map/ppermute | solution.py:28
  25.0 28.9 %copy-start.19 = (bf16[128,512]{1,0:T(8,128)(2,1)}, bf16[128,512]{1,0:T(8,128)(2,1)S(1)}, u32[]{:S(2)}) copy-start(bf16[128,512]{1,0:T(8,128)(2,1)S(1)} %collective-permute-done.11.refs_15_) | copy-start | bytes 393220
  25.0 7.6 %collective-permute-start.12 = (bf16[128,512]{1,0:T(8,128)(2,1)}, bf16[128,512]{1,0:T(8,128)(2,1)S(1)}, u32[]{:S(2)}, u32[]{:S(2)}) collective-permute-start(bf16[128,512]{1,0:T(8,128)(2,1)} %refs_13_.5), channel_id=1, source_target_pairs={{0,12},{4,8},{8,4},{12,0},{1,13},{5,9},{9,5},{13,1},{2,14},{6,10},... | collective-permute-start | bytes 393224 | tf_op jit(solution)/shard_map/ppermute | solution.py:28
  42.4 4.8 %collective-permute-start.13 = (f32[8,512]{1,0:T(8,128)S(1)}, f32[8,512]{1,0:T(8,128)S(1)}, u32[]{:S(2)}, u32[]{:S(2)}) collective-permute-start(f32[8,512]{1,0:T(8,128)S(1)} %get-tuple-element.17.refs_0_), channel_id=1, source_target_pairs={{0,1},{1,0},{2,3},{3,2},{16,17},{17,16},{18,19},{19,18},{4,5},{5,4... | collective-permute-start | bytes 49160 | tf_op jit(solution)/shard_map/ppermute | solution.py:28
  43.6 4.1 %collective-permute-start.14 = (f32[8,512]{1,0:T(8,128)S(1)}, f32[8,512]{1,0:T(8,128)S(1)}, u32[]{:S(2)}, u32[]{:S(2)}) collective-permute-start(f32[8,512]{1,0:T(8,128)S(1)} %get-tuple-element.17.refs_0_), channel_id=1, source_target_pairs={{0,2},{1,3},{2,0},{3,1},{16,18},{17,19},{18,16},{19,17},{4,6},{5,7... | collective-permute-start | bytes 49160 | tf_op jit(solution)/shard_map/ppermute | solution.py:28
  44.5 4.8 %collective-permute-start.15 = (f32[8,512]{1,0:T(8,128)S(1)}, f32[8,512]{1,0:T(8,128)S(1)}, u32[]{:S(2)}, u32[]{:S(2)}) collective-permute-start(f32[8,512]{1,0:T(8,128)S(1)} %get-tuple-element.17.refs_0_), channel_id=1, source_target_pairs={{0,3},{1,2},{2,1},{3,0},{16,19},{17,18},{18,17},{19,16},{4,7},{5,6... | collective-permute-start | bytes 49160 | tf_op jit(solution)/shard_map/ppermute | solution.py:28
  46.0 3.3 %collective-permute-start.16 = (f32[8,512]{1,0:T(8,128)S(1)}, f32[8,512]{1,0:T(8,128)S(1)}, u32[]{:S(2)}, u32[]{:S(2)}) collective-permute-start(f32[8,512]{1,0:T(8,128)S(1)} %get-tuple-element.17.refs_0_), channel_id=1, source_target_pairs={{0,16},{1,17},{2,18},{3,19},{16,0},{17,1},{18,2},{19,3},{4,20},{5,... | collective-permute-start | bytes 49160 | tf_op jit(solution)/shard_map/ppermute | solution.py:28
  46.0 3.3 %collective-permute-start.17 = (f32[8,512]{1,0:T(8,128)S(1)}, f32[8,512]{1,0:T(8,128)S(1)}, u32[]{:S(2)}, u32[]{:S(2)}) collective-permute-start(f32[8,512]{1,0:T(8,128)S(1)} %get-tuple-element.17.refs_0_), channel_id=1, source_target_pairs={{0,17},{1,16},{2,19},{3,18},{16,1},{17,0},{18,3},{19,2},{4,21},{5,... | collective-permute-start | bytes 49160 | tf_op jit(solution)/shard_map/ppermute | solution.py:28
  47.2 3.2 %collective-permute-start.18 = (f32[8,512]{1,0:T(8,128)S(1)}, f32[8,512]{1,0:T(8,128)S(1)}, u32[]{:S(2)}, u32[]{:S(2)}) collective-permute-start(f32[8,512]{1,0:T(8,128)S(1)} %get-tuple-element.17.refs_0_), channel_id=1, source_target_pairs={{0,18},{1,19},{2,16},{3,17},{16,2},{17,3},{18,0},{19,1},{4,22},{5,... | collective-permute-start | bytes 49160 | tf_op jit(solution)/shard_map/ppermute | solution.py:28
  47.8 4.1 %collective-permute-start.19 = (f32[8,512]{1,0:T(8,128)S(1)}, f32[8,512]{1,0:T(8,128)S(1)}, u32[]{:S(2)}, u32[]{:S(2)}) collective-permute-start(f32[8,512]{1,0:T(8,128)S(1)} %get-tuple-element.17.refs_0_), channel_id=1, source_target_pairs={{0,19},{1,18},{2,17},{3,16},{16,3},{17,2},{18,1},{19,0},{4,23},{5,... | collective-permute-start | bytes 49160 | tf_op jit(solution)/shard_map/ppermute | solution.py:28
  53.6 25.3 %copy-start.4 = (bf16[128,2048]{1,0:T(8,128)(2,1)S(1)}, bf16[128,2048]{1,0:T(8,128)(2,1)}, u32[]{:S(2)}) copy-start(bf16[128,2048]{1,0:T(8,128)(2,1)} %refs_4_.6) | copy-start | bytes 1572868
  53.6 25.3 %copy-start.27 = (f32[512]{0:T(512)S(1)}, f32[512]{0:T(512)}, u32[]{:S(2)}) copy-start(f32[512]{0:T(512)} %param.15) | copy-start | bytes 6148
  53.9 25.0 %copy-start.30 = (s32[1,32]{1,0:T(1,128)S(1)}, s32[1,32]{1,0:T(1,128)}, u32[]{:S(2)}) copy-start(s32[1,32]{1,0:T(1,128)} %refs_1_.5) | copy-start | bytes 388
  53.9 4.9 %collective-permute-start.20 = (bf16[64,640]{1,0:T(8,128)(2,1)S(1)}, bf16[64,640]{1,0:T(8,128)(2,1)S(1)}, u32[]{:S(2)}, u32[]{:S(2)}) collective-permute-start(bf16[64,640]{1,0:T(8,128)(2,1)S(1)} %get-tuple-element.18.refs_0_), channel_id=1, source_target_pairs={{0,1},{1,0},{2,3},{3,2},{4,5},{5,4},{6,7},{7,6},{8,9},{9,8},{10,11... | collective-permute-start | bytes 245768 | tf_op jit(solution)/shard_map/ppermute | solution.py:28
  55.5 6.3 %collective-permute-start.21 = (bf16[64,640]{1,0:T(8,128)(2,1)S(1)}, bf16[64,640]{1,0:T(8,128)(2,1)S(1)}, u32[]{:S(2)}, u32[]{:S(2)}) collective-permute-start(bf16[64,640]{1,0:T(8,128)(2,1)S(1)} %get-tuple-element.18.refs_0_), channel_id=1, source_target_pairs={{0,2},{1,3},{2,0},{3,1},{4,6},{5,7},{6,4},{7,5},{8,10},{9,11},{10,... | collective-permute-start | bytes 245768 | tf_op jit(solution)/shard_map/ppermute | solution.py:28
  56.0 5.8 %collective-permute-start.22 = (bf16[64,640]{1,0:T(8,128)(2,1)S(1)}, bf16[64,640]{1,0:T(8,128)(2,1)S(1)}, u32[]{:S(2)}, u32[]{:S(2)}) collective-permute-start(bf16[64,640]{1,0:T(8,128)(2,1)S(1)} %get-tuple-element.18.refs_0_), channel_id=1, source_target_pairs={{0,3},{1,2},{2,1},{3,0},{4,7},{5,6},{6,5},{7,4},{8,11},{9,10},{10,... | collective-permute-start | bytes 245768 | tf_op jit(solution)/shard_map/ppermute | solution.py:28
  69.4 1.6 %collective-permute-start.23 = (bf16[64,2176]{1,0:T(8,128)(2,1)S(1)}, bf16[64,2176]{1,0:T(8,128)(2,1)S(1)}, u32[]{:S(2)}, u32[]{:S(2)}) collective-permute-start(bf16[64,2176]{1,0:T(8,128)(2,1)S(1)} %get-tuple-element.20), channel_id=1, source_target_pairs={{0,16},{16,0},{1,17},{17,1},{2,18},{18,2},{3,19},{19,3},{4,20},{20... | collective-permute-start | bytes 835592 | tf_op jit(solution)/shard_map/ppermute | solution.py:28
  75.2 23.8 %all-to-all-start = ((bf16[8,8,2048]{2,1,0:T(8,128)(2,1)}), bf16[8,8,2048]{2,1,0:T(8,128)(2,1)S(1)}, u32[]{:S(2)}, u32[]{:S(2)}) async-start(bf16[8,8,2048]{2,1,0:T(8,128)(2,1)} %bitcast.5), calls=%async_computation | async-start | bytes 524288 | tf_op jit(solution)/shard_map/all_to_all | solution.py:368
  (26 other events, 158.6 us)

commit v2 on v1

v2 whole, which is shorter than its diff:
```python
import functools

import jax
import jax.numpy as jnp
from jax import lax
from jax.experimental import pallas as pl
from jax.experimental.pallas import tpu as pltpu
from jax.sharding import PartitionSpec as P

HEADS = 4
DM = 4096
MICRO = 4
SESS_MAX = 64
EPSILON = 1e-06
F32 = jnp.float32
BF16 = jnp.bfloat16

VMEM = pl.BlockSpec(memory_space=pltpu.VMEM)
SMEM = pl.BlockSpec(memory_space=pltpu.SMEM)
HBM = pl.BlockSpec(memory_space=pltpu.HBM)


def params(mib):
    return pltpu.CompilerParams(vmem_limit_bytes=mib * 1024 * 1024)


def swap(x, axis, size, flip):
    return lax.ppermute(x, axis, [(i, i ^ flip) for i in range(size)])


def silu_half(h):
    return h + h * jnp.tanh(h)


def encoder_rows(place, n_w, n_wout, row0, rows, copies_out, *refs):
    refs = list(refs)
    hist_ref, sess_ref, ev_ref, gain_ref = refs[:4]
    refs = refs[4:]
    copies = []
    if place is not None:
        w_parts, wout_parts, refs = refs[:n_w], refs[n_w : n_w + n_wout], refs[n_w + n_wout :]
        pooled_ref, w_ref, wout_ref, kv_out, sums_out = refs[:5]
        q_ref, gate_ref, att_ref, sems = refs[5:]
        prior = []
        copies = place(w_parts, wout_parts, w_ref, wout_ref, sems)
    else:
        w_ref, wout_ref, kv_ref, sums_ref, pooled_ref = refs[:5]
        q_ref, gate_ref, att_ref, kv_out = refs[5:]
        prior = [kv_ref]
    for c in copies:
        c.start()
    for c in copies:
        c.wait()
    width = ev_ref.shape[1]
    head = width // HEADS
    hist = hist_ref[0]

    sess = sess_ref.shape[1]
    lens = jnp.broadcast_to(sess_ref[...], (sess, sess))
    at_row = lax.broadcasted_iota(jnp.int32, (sess, sess), 0)
    at_col = lax.broadcasted_iota(jnp.int32, (sess, sess), 1)
    ends = jnp.sum(jnp.where(at_col <= at_row, lens, 0).astype(F32), axis=1, keepdims=True)
    starts = jnp.sum(jnp.where(at_col < at_row, lens, 0).astype(F32), axis=1, keepdims=True)
    ends = jnp.minimum(ends, hist.astype(F32))
    pos = (lax.broadcasted_iota(jnp.int32, (sess, rows), 1) + row0).astype(F32)
    member = jnp.where((pos >= starts) & (pos < ends), 1.0, 0.0).astype(BF16)
    n_valid = jnp.maximum(ends - starts, 0.0)

    step = min(rows, 256)
    for r in range(0, rows, step):
        x = ev_ref[row0 + r : row0 + r + step, :]
        at = slice(r, r + step)
        row_pos = lax.broadcasted_iota(jnp.int32, (step, 1), 0) + (row0 + r)

        def act(n):
            part = jnp.dot(x, w_ref[:, n * width : (n + 1) * width], preferred_element_type=F32)
            return silu_half(part * 0.5)

        gate_ref[at, :] = act(0)
        kv_out[at, :width] = jnp.where(row_pos < hist, act(1), 0.0).astype(BF16)
        q_ref[at, :] = act(2).astype(BF16)
        kv_out[at, width:] = act(3).astype(BF16)

    blocks = []
    for ref in prior + [kv_out]:
        for r in range(0, ref.shape[0], step):
            blocks.append((ref, r))
    tri = lax.broadcasted_iota(jnp.int32, (step, step), 1) <= lax.broadcasted_iota(
        jnp.int32, (step, step), 0
    )
    before = len(blocks) - rows // step
    for i in range(rows // step):
        at = slice(i * step, (i + 1) * step)
        for h in range(HEADS):
            q = q_ref[at, h * head : (h + 1) * head]
            total = None
            for j in range(before + i + 1):
                ref, r = blocks[j]
                k = ref[r : r + step, width + h * head : width + (h + 1) * head]
                v = ref[r : r + step, h * head : (h + 1) * head]
                s = lax.dot_general(q, k, (((1,), (1,)), ((), ())), preferred_element_type=F32)
                wts = silu_half(s * (0.5 * head**-0.5))
                if j == before + i:
                    wts = jnp.where(tri, wts, 0.0)
                mixed = jnp.dot(wts.astype(BF16), v, preferred_element_type=F32)
                total = mixed if total is None else total + mixed
            att_ref[at, h * head : (h + 1) * head] = total

    sums_ev = jnp.dot(member, ev_ref[row0 : row0 + rows, :], preferred_element_type=F32)
    att = att_ref[...]
    inv = lax.rsqrt(jnp.mean(att * att, axis=1, keepdims=True) + EPSILON)
    gated = (att * inv * gain_ref[...] * gate_ref[...]).astype(BF16)
    sums_g = jnp.dot(member, gated, preferred_element_type=F32)
    if place is not None:
        sums_out[:, :width] = sums_ev
        sums_out[:, width:] = sums_g
    else:
        sums_ev = sums_ev + sums_ref[:, :width]
        sums_g = sums_g + sums_ref[:, width:]

    hi = sums_g.astype(BF16)
    rest = sums_g - hi.astype(F32)
    mid = rest.astype(BF16)
    low = (rest - mid.astype(F32)).astype(BF16)
    terms = jnp.dot(jnp.concatenate([low, mid, hi], axis=0), wout_ref[...], preferred_element_type=F32)
    out = terms[:sess] + terms[sess : 2 * sess] + terms[2 * sess :] + sums_ev
    out = out / jnp.maximum(n_valid, 1.0)
    if copies_out:
        peers, take = copies_out
        out = jnp.concatenate([out[:take]] * peers, axis=0)
    pooled_ref[...] = out.astype(BF16)


def encoder_call(hist_len, sess_len, events, gain, row0, rows, weights, copies_out=None, carried=None):
    width = events.shape[1]
    sess = sess_len.shape[1]
    place, w_parts, wout_parts = weights if carried is None else (None, [], [])
    scratch = [
        pltpu.VMEM((rows, width), BF16),
        pltpu.VMEM((rows, width), F32),
        pltpu.VMEM((rows, width), F32),
    ]
    if carried is None:
        operands = [*w_parts, *wout_parts]
        peers, take = copies_out
        out_shape = [
            jax.ShapeDtypeStruct((peers * take, width), BF16),
            jax.ShapeDtypeStruct((width, 4 * width), BF16),
            jax.ShapeDtypeStruct((width, width), BF16),
            jax.ShapeDtypeStruct((rows, 2 * width), BF16),
            jax.ShapeDtypeStruct((sess, 2 * width), F32),
        ]
        scratch.append(pltpu.SemaphoreType.DMA((64,)))
    else:
        operands = carried
        out_shape = [jax.ShapeDtypeStruct((sess, width), BF16)]
        scratch.append(pltpu.VMEM((rows, 2 * width), BF16))
    return pl.pallas_call(
        functools.partial(encoder_rows, place, len(w_parts), len(wout_parts), row0, rows, copies_out),
        in_specs=[SMEM] + [VMEM] * (3 + len(operands)),
        out_specs=[VMEM] * len(out_shape),
        out_shape=out_shape,
        scratch_shapes=scratch,
        compiler_params=params(16),
        cost_estimate=pl.CostEstimate(
            flops=2 * rows * width * 4 * width + 4 * rows * (row0 + rows) * width,
            bytes_accessed=6 * 1024 * 1024,
            transcendentals=4 * rows * width + HEADS * rows * (row0 + rows),
        ),
        name=f"encode_rows_{row0}",
    )(hist_len, sess_len, events, gain, *operands)


def load_kernel(n_parts, n_load, *refs):
    parts, refs = refs[:n_parts], refs[n_parts:]
    from_refs, refs = refs[:n_load], refs[n_load:]
    to_refs, refs = refs[:n_load], refs[n_load:]
    sems = refs[-1]
    copies = [pltpu.make_async_copy(a, b, sems.at[i]) for i, (a, b) in enumerate(zip(from_refs, to_refs))]
    for c in copies:
        c.start()
    for k, part in enumerate(parts):
        refs[0][k] = part[...]
    for c in copies:
        c.wait()


def load_call(parts, loads):
    out_shape = [jax.ShapeDtypeStruct(x.shape, x.dtype) for x in loads]
    if parts:
        out_shape.append(jax.ShapeDtypeStruct((len(parts), *parts[0].shape), parts[0].dtype))
    out = pl.pallas_call(
        functools.partial(load_kernel, len(parts), len(loads)),
        in_specs=[VMEM] * len(parts) + [HBM] * len(loads),
        out_specs=[VMEM] * len(out_shape),
        out_shape=out_shape,
        scratch_shapes=[pltpu.SemaphoreType.DMA((len(loads),))],
        compiler_params=params(8),
        name="load",
    )(*parts, *loads)
    return (out[:-1], out[-1]) if parts else (out, None)


def gather_weights(w_uvqk, w_out, loads, sections, dps, mps):
    depth, wide = w_uvqk.shape
    peers = sections * mps
    piece = wide // peers
    part = depth // sections
    if wide % (128 * peers) or part % 16:
        full = lax.all_gather(w_uvqk, "dp", axis=0, tiled=True)
        full_out = lax.all_gather(w_out, "dp", axis=0, tiled=True)

        def place_whole(ws, wouts, w_ref, wout_ref, sems):
            return [
                pltpu.make_async_copy(ws[0], w_ref, sems.at[0]),
                pltpu.make_async_copy(wouts[0], wout_ref, sems.at[1]),
            ]

        return (place_whole, [full], [full_out]), load_call([], loads)[0]

    s, m = lax.axis_index("section"), lax.axis_index("mp")
    mine = lax.dynamic_slice_in_dim(w_uvqk, (s * mps + m) * piece, piece, 1)
    got = jnp.stack([swap(mine, "dp", dps, k) for k in range(1, dps)])
    plane = [got] + [swap(got, "mp", mps, k) for k in range(1, mps)]
    half = lax.dynamic_slice_in_dim(w_out, s * part, part, 0)
    parts = [swap(half, "dp", dps, k) for k in range(1, dps)]
    (w_uvqk, w_out, *loads), got_out = load_call(parts, [w_uvqk, w_out, *loads])
    ws, wouts = [w_uvqk] + plane, [w_out, got_out]
    if sections == 2:
        ws = ws + [swap(p, "section", sections, 1) for p in plane]
        wouts = wouts + [swap(got_out, "section", sections, 1)]

    def place(ws, wouts, w_ref, wout_ref, sems):
        z = lax.axis_index("dp")
        sec, col = lax.axis_index("section"), lax.axis_index("mp")
        copies = []

        def add(src, dst):
            copies.append(pltpu.make_async_copy(src, dst, sems.at[len(copies)]))

        own = pl.ds(pl.multiple_of(z * depth, depth), depth)
        add(ws[0], w_ref.at[own])
        add(wouts[0], wout_ref.at[own])
        for i, ref in enumerate(ws[1:]):
            spot = ((sec ^ (i // mps)) * mps + (col ^ (i % mps))) * piece
            for k in range(1, dps):
                at = pl.ds(pl.multiple_of((z ^ k) * depth, depth), depth)
                add(ref.at[k - 1], w_ref.at[at, pl.ds(pl.multiple_of(spot, piece), piece)])
        for i, ref in enumerate(wouts[1:]):
            for k in range(1, dps):
                at = pl.ds(pl.multiple_of((z ^ k) * depth + (sec ^ i) * part, part), part)
                add(ref.at[k - 1], wout_ref.at[at])
        return copies

    return (place, ws, wouts), loads


def hidden_in_kernel(copies_out, x_ref, w_ref, gain_ref, local_ref, send_ref):
    local = jnp.dot(x_ref[...], w_ref[...], preferred_element_type=F32)
    local_ref[...] = local
    rows, cols = local.shape
    scaled = (local * gain_ref[...].astype(F32)).astype(BF16)
    tail = two_terms(jnp.sum(local * local, axis=1, keepdims=True))
    for k in range(copies_out):
        send_ref[k, :, :cols] = scaled
        send_ref[k, :, cols:] = tail


def two_terms(square):
    hi = square.astype(BF16).astype(F32)
    lane = lax.broadcasted_iota(jnp.int32, (square.shape[0], 128), 1)
    return jnp.where(lane == 0, hi, jnp.where(lane == 1, square - hi, 0.0)).astype(BF16)


def up_kernel(chunks, got_ref, w_ref, half_ref, send_ref):
    mps, rows, cols = got_ref.shape
    cols = cols - 128
    wide = w_ref.shape[1]
    each = wide // chunks
    square = None
    for k in range(mps):
        tail = jnp.sum(got_ref[k, :, cols:].astype(F32), axis=1, keepdims=True)
        square = tail if square is None else square + tail
    x = jnp.concatenate([got_ref[k, :, :cols] for k in range(mps)], axis=1)
    for c in range(chunks):
        at = slice(c * each, (c + 1) * each)
        half = jnp.dot(x, w_ref[:, at], preferred_element_type=F32)
        half_ref[:, at] = half
        send_ref[:, at] = half.astype(BF16)
    half_ref[:, wide:] = jnp.broadcast_to(square, (rows, 128))
    send_ref[:, wide:] = two_terms(square)


def down_kernel(chunks, half_ref, other_ref, local_ref, w_ref, out_ref, part_ref):
    units, wide = w_ref.shape
    each = wide // chunks
    square = half_ref[:, units : units + 1] + jnp.sum(other_ref[:, units:].astype(F32), axis=1, keepdims=True)
    inv = lax.rsqrt(square / DM + EPSILON)
    up = (half_ref[:, :units] + other_ref[:, :units].astype(F32)) * inv
    hidden = jax.nn.gelu(up, approximate=True).astype(BF16)
    for c in range(chunks):
        at = slice(c * each, (c + 1) * each)
        part_ref[:, at] = jnp.dot(hidden, w_ref[:, at], preferred_element_type=F32)
    m = lax.axis_index("mp")
    cols = local_ref.shape[1]
    own = pl.ds(pl.multiple_of(m * cols, cols), cols)
    part_ref[:, own] = part_ref[:, own] + local_ref[...]
    out_ref[...] = part_ref[...].astype(BF16)


def sum_kernel(sections, mps, got_ref, out_ref):
    got = got_ref[...].astype(F32)
    take, wide = out_ref.shape[0], got.shape[1]
    for s in range(sections):
        total = got[s * mps * take : (s * mps + 1) * take]
        for k in range(s * mps + 1, (s + 1) * mps):
            total = total + got[k * take : (k + 1) * take]
        out_ref[:, s * wide : (s + 1) * wide] = total.astype(BF16)


def cross_block(micro_rows, take, w_in, ffn_gain, w_up, w_down, sections, mps):
    peers = sections * mps
    rows, width = micro_rows.shape
    cols = w_in.shape[1]
    units = w_up.shape[1]
    half_width = w_down.shape[1]
    group = ("section", "mp")
    chunks = 4

    arrived = lax.all_to_all(
        micro_rows.reshape(peers, take, width), group, split_axis=0, concat_axis=0, tiled=True
    ).reshape(rows, width)
    local, send = pl.pallas_call(
        functools.partial(hidden_in_kernel, mps),
        out_shape=[
            jax.ShapeDtypeStruct((rows, cols), F32),
            jax.ShapeDtypeStruct((mps, rows, cols + 128), BF16),
        ],
        in_specs=[VMEM] * 3,
        out_specs=[VMEM] * 2,
        compiler_params=params(8),
        cost_estimate=pl.CostEstimate(
            flops=2 * rows * width * cols, bytes_accessed=2 * width * cols, transcendentals=0
        ),
        name="hidden_in",
    )(arrived, w_in, ffn_gain)

    got = lax.all_to_all(send, "mp", split_axis=0, concat_axis=0, tiled=True)
    half, half_send = pl.pallas_call(
        functools.partial(up_kernel, chunks),
        out_shape=[
            jax.ShapeDtypeStruct((rows, units + 128), F32),
            jax.ShapeDtypeStruct((rows, units + 128), BF16),
        ],
        in_specs=[VMEM] * 2,
        out_specs=[VMEM] * 2,
        compiler_params=params(8),
        cost_estimate=pl.CostEstimate(
            flops=2 * rows * w_up.size, bytes_accessed=2 * w_up.size, transcendentals=0
        ),
        name="up_half",
    )(got, w_up)

    other = swap(half_send, "section", sections, 1)
    partial = pl.pallas_call(
        functools.partial(down_kernel, chunks),
        out_shape=jax.ShapeDtypeStruct((rows, half_width), BF16),
        in_specs=[VMEM] * 4,
        out_specs=VMEM,
        scratch_shapes=[pltpu.VMEM((rows, half_width), F32)],
        compiler_params=params(8),
        cost_estimate=pl.CostEstimate(
            flops=2 * rows * w_down.size, bytes_accessed=2 * w_down.size, transcendentals=rows * units
        ),
        name="down_part",
    )(half, other, local, w_down)

    arrived = lax.all_to_all(
        partial.reshape(peers, take, half_width), group, split_axis=0, concat_axis=0, tiled=True
    ).reshape(rows, half_width)
    return pl.pallas_call(
        functools.partial(sum_kernel, sections, mps),
        out_shape=jax.ShapeDtypeStruct((take, half_width * sections), BF16),
        in_specs=[VMEM],
        out_specs=VMEM,
        compiler_params=params(8),
        name="sum_rows",
    )(arrived)


def per_device(sections, dps, mps, events, hist_len, sess_len, w_uvqk, w_out, attn_gain, w_in, ffn_gain, w_up, w_down):
    events = events[0]
    length, width = events.shape
    sess = sess_len.shape[1]
    take = sess // MICRO
    loads = [sess_len, events, attn_gain.reshape(1, width), w_in, ffn_gain]
    weights, loads = gather_weights(w_uvqk, w_out, loads, sections, dps, mps)
    sess_len, events, gain, w_in, ffn_gain = loads
    encode = functools.partial(encoder_call, hist_len, sess_len, events, gain)

    first = take * SESS_MAX
    micro_rows, *carried = encode(0, first, weights, copies_out=(sections * mps, take))
    cross_out = cross_block(micro_rows, take, w_in, ffn_gain, w_up, w_down, sections, mps)
    (pooled,) = encode(first, length - first, weights, carried=carried)
    return (pooled, cross_out)


def solution(mesh):
    sizes = [mesh.shape[name] for name in ("section", "dp", "mp")]
    return jax.shard_map(
        functools.partial(per_device, *sizes),
        mesh=mesh,
        in_specs=(
            P(("section", "dp", "mp"), None, None),
            P(("section", "dp", "mp")),
            P(("section", "dp", "mp"), None),
            P("dp", None),
            P("dp", None),
            P(),
            P(None, ("section", "mp")),
            P(None, ("section", "mp")),
            P("section", "mp"),
            P("mp", "section"),
        ),
        out_specs=(P(("section", "dp", "mp"), None), P(("section", "dp", "mp"), None)),
        check_vma=False,
    )
```

time: 100 us -> 79.2 us (0.79)
  blocking collectives: 0 us -> 18 us
  starting transfers between devices: 29.1 us -> 18.4 us
  waiting for transfers between devices: 23.6 us -> 12.9 us
  local copies, waits for them, and re-layouts: 20.1 us -> 11.2 us
  Pallas kernels: 25.2 us -> 16.4 us
    all_to_all x0 -> x2, blocking collectives: none -> 18 us  [the longest x1 9.52 us: cross_block(): got = lax.all_to_all(send, 'mp', split_axis=0, concat_axis=0, tiled=True)]
    ppermute x24 -> x15, waiting for transfers between devices: 23.6 us -> 12.9 us  [swap(): return lax.ppermute(x, axis, [(i, i ^ flip) for i in range(size)])]
    ppermute x24 -> x15, starting transfers between devices: 25.5 us -> 14.9 us  [swap(): return lax.ppermute(x, axis, [(i, i ^ flip) for i in range(size)])]
    unnamed x66 -> x28, local copies, waits for them, and re-layouts: 19.1 us -> 9.48 us
    pallas_call x5, Pallas kernels: 20.4 us -> 13.2 us  [the longest x2 10.9 us: encoder_call(): pl.pallas_call(functools.partial(encoder_rows, place, len(w_parts), len(w...]
    pallas_call x1, Pallas kernels: 4.18 us -> 2.56 us  [cross_block(): pl.pallas_call(functools.partial(down_kernel, chunks), out_shape=jax.Shap...]
  transfers between devices with their start and end apart: 25 -> 16, of which waited for: 10 -> 8; matrix products, arithmetic and copies ran while one was open for 0% -> 1% of each run, Pallas kernels for 11% -> 8%
where the time goes in v2:
time: 79.2 us; the launch traced here: 78.5 us
  starting transfers between devices  18.4 us (23%)
  blocking collectives  18 us (23%)
  Pallas kernels  16.4 us (21%)
  waiting for transfers between devices  12.9 us (16%)
  local copies, waits for them, and re-layouts  11.2 us (14%)
  between operations  1.59 us (2%)
    ppermute x15, starting transfers between devices, swap(): return lax.ppermute(x, axis, [(i, i ^ flip) for i in range(size)])  14.9 us
    ppermute x15, waiting for transfers between devices, swap(): return lax.ppermute(x, axis, [(i, i ^ flip) for i in range(size)])  12.9 us
    pallas_call x2, Pallas kernels, encoder_call(): pl.pallas_call(functools.partial(encoder_rows, place, len(w_parts), len(w...  10.9 us
    all_to_all x1, blocking collectives, cross_block(): got = lax.all_to_all(send, 'mp', split_axis=0, concat_axis=0, tiled=True)  9.52 us
    unnamed x28, local copies, waits for them, and re-layouts  9.48 us
    all_to_all x1, blocking collectives, cross_block(): lax.all_to_all(micro_rows.reshape(peers, take, width), group, split_axis=...  8.44 us
    all_to_all x1, starting transfers between devices, cross_block(): lax.all_to_all(partial.reshape(peers, take, half_width), group, split_axi...  3.59 us
    pallas_call x1, Pallas kernels, cross_block(): pl.pallas_call(functools.partial(down_kernel, chunks), out_shape=jax.Shap...  2.56 us
  transfers between devices with their start and end apart: 16, of which 8 were waited for; matrix products, arithmetic and copies ran while one was open for 1% of the time, Pallas kernels for 8%

profile of v2, /device:TPU:0, one launch (start us, length us, event | category | flops | bytes accessed | tf_op | source)
XLA Modules:
  0.0 78.5 jit_solution(4619307529520045652)
XLA Ops:
  0.6 0.8 %constant_dynamic-slice_fusion = bf16[128,256]{1,0:T(8,128)(2,1)S(1)} fusion(bf16[128,2048]{1,0:T(8,128)(2,1)} %refs_3_.1, s32[]{:T(128)S(6)} %select_n.7), kind=kLoop, calls=%fused_computation.1 | loop fusion | bytes 131076 | tf_op jit(solution)/shard_map/dynamic_slice | solution.py:222
  1.5 5.0 %collective-permute-start.5 = (bf16[128,256]{1,0:T(8,128)(2,1)S(1)}, bf16[128,256]{1,0:T(8,128)(2,1)S(1)}, u32[]{:S(2)}, u32[]{:S(2)}) collective-permute-start(bf16[128,256]{1,0:T(8,128)(2,1)S(1)} %constant_dynamic-slice_fusion), channel_id=1, source_target_pairs={{0,12},{4,8},{8,4},{12,0},{1,13},{5,9},{9,5},{13,1},{2,14},{6,10},... | collective-permute-start | bytes 196616 | tf_op jit(solution)/shard_map/ppermute | solution.py:28
  6.5 0.6 collective-permute-start.3
  7.1 2.0 %collective-permute-done.5 = bf16[128,256]{1,0:T(8,128)(2,1)S(1)} collective-permute-done((bf16[128,256]{1,0:T(8,128)(2,1)S(1)}, bf16[128,256]{1,0:T(8,128)(2,1)S(1)}, u32[]{:S(2)}, u32[]{:S(2)}) %collective-permute-start.5) | collective-permute-done | bytes 65568 | tf_op jit(solution)/shard_map/ppermute | solution.py:28
  9.1 3.0 %collective-permute-done.4 = bf16[128,256]{1,0:T(8,128)(2,1)S(1)} collective-permute-done((bf16[128,256]{1,0:T(8,128)(2,1)S(1)}, bf16[128,256]{1,0:T(8,128)(2,1)S(1)}, u32[]{:S(2)}, u32[]{:S(2)}) %collective-permute-start.4) | collective-permute-done | bytes 65568 | tf_op jit(solution)/shard_map/ppermute | solution.py:28
  12.2 2.5 %collective-permute-start.8 = (bf16[3,128,256]{2,1,0:T(8,128)(2,1)S(1)}, bf16[3,128,256]{2,1,0:T(8,128)(2,1)S(1)}, u32[]{:S(2)}, u32[]{:S(2)}) collective-permute-start(bf16[3,128,256]{2,1,0:T(8,128)(2,1)S(1)} %pad_maximum_fusion.refs_5_), channel_id=1, source_target_pairs={{0,3},{1,2},{2,1},{3,0},{4,7},{5,6},{6,5},{7,4},{8,11},{9,10},{10,... | collective-permute-start | bytes 589832 | tf_op jit(solution)/shard_map/ppermute | solution.py:28
  14.7 0.5 collective-permute-start.7
  15.2 0.5 collective-permute-start.6
  15.7 0.8 %constant_dynamic-slice_fusion.1 = bf16[64,512]{1,0:T(8,128)(2,1)S(1)} fusion(bf16[128,512]{1,0:T(8,128)(2,1)} %refs_4_.1, s32[]{:T(128)S(6)} %select_n.6), kind=kLoop, calls=%fused_computation.2 | loop fusion | bytes 131076 | tf_op jit(solution)/shard_map/dynamic_slice | solution.py:225
  16.6 2.6 %collective-permute-start.2 = (bf16[64,512]{1,0:T(8,128)(2,1)S(1)}, bf16[64,512]{1,0:T(8,128)(2,1)S(1)}, u32[]{:S(2)}, u32[]{:S(2)}) collective-permute-start(bf16[64,512]{1,0:T(8,128)(2,1)S(1)} %constant_dynamic-slice_fusion.1), channel_id=1, source_target_pairs={{0,12},{4,8},{8,4},{12,0},{1,13},{5,9},{9,5},{13,1},{2,14},{6,10},... | collective-permute-start | bytes 196616 | tf_op jit(solution)/shard_map/ppermute | solution.py:28
  19.2 3.5 %collective-permute-done.2.refs_2_ = bf16[64,512]{1,0:T(8,128)(2,1)S(1)} collective-permute-done((bf16[64,512]{1,0:T(8,128)(2,1)S(1)}, bf16[64,512]{1,0:T(8,128)(2,1)S(1)}, u32[]{:S(2)}, u32[]{:S(2)}) %collective-permute-start.2) | collective-permute-done | bytes 65568 | tf_op jit(solution)/shard_map/ppermute | solution.py:28
  22.7 1.9 %collective-permute-start = (bf16[64,512]{1,0:T(8,128)(2,1)S(1)}, bf16[64,512]{1,0:T(8,128)(2,1)S(1)}, u32[]{:S(2)}, u32[]{:S(2)}) collective-permute-start(bf16[64,512]{1,0:T(8,128)(2,1)S(1)} %constant_dynamic-slice_fusion.1), channel_id=1, source_target_pairs={{0,4},{4,0},{8,12},{12,8},{1,5},{5,1},{9,13},{13,9},{2,6},{6,2},{1... | collective-permute-start | bytes 196616 | tf_op jit(solution)/shard_map/ppermute | solution.py:28
  24.8 2.2 %collective-permute-done.refs_0_ = bf16[64,512]{1,0:T(8,128)(2,1)S(1)} collective-permute-done((bf16[64,512]{1,0:T(8,128)(2,1)S(1)}, bf16[64,512]{1,0:T(8,128)(2,1)S(1)}, u32[]{:S(2)}, u32[]{:S(2)}) %collective-permute-start) | collective-permute-done | bytes 65568 | tf_op jit(solution)/shard_map/ppermute | solution.py:28
  27.0 1.2 %copy-done.1 = bf16[1,1024,512]{2,1,0:T(8,128)(2,1)S(1)} copy-done((bf16[1,1024,512]{2,1,0:T(8,128)(2,1)S(1)}, bf16[1,1024,512]{2,1,0:T(8,128)(2,1)}, u32[]{:S(2)}) %copy-start.1) | copy-done | bytes 1048600
  28.2 1.0 %copy-done.2 = bf16[128,2048]{1,0:T(8,128)(2,1)S(1)} copy-done((bf16[128,2048]{1,0:T(8,128)(2,1)S(1)}, bf16[128,2048]{1,0:T(8,128)(2,1)}, u32[]{:S(2)}) %copy-start.2) | copy-done | bytes 524312
  29.3 1.0 %copy-done.3 = bf16[512,512]{1,0:T(8,128)(2,1)S(1)} copy-done((bf16[512,512]{1,0:T(8,128)(2,1)S(1)}, bf16[512,512]{1,0:T(8,128)(2,1)}, u32[]{:S(2)}) %copy-start.3) | copy-done | bytes 524312
  30.3 0.9 %copy-done.4 = bf16[128,512]{1,0:T(8,128)(2,1)S(1)} copy-done((bf16[128,512]{1,0:T(8,128)(2,1)S(1)}, bf16[128,512]{1,0:T(8,128)(2,1)}, u32[]{:S(2)}) %copy-start.4) | copy-done | bytes 131096
  31.2 0.7 copy-done.5
  31.9 0.7 copy-done.6
  32.6 0.7 copy-done.7
  36.0 4.8 %encode_rows_0.1 = (bf16[64,512]{1,0:T(8,128)(2,1)S(1)}, bf16[512,2048]{1,0:T(8,128)(2,1)S(1)}, bf16[512,512]{1,0:T(8,128)(2,1)S(1)}, bf16[512,1024]{1,0:T(8,128)(2,1)S(1)}, f32[32,1024]{1,0:T(8,128)S(1)}) custom-call(s32[1]{0:T(128)S(6)} %copy.12.refs_0_, s32[1,32]{1,0:T(1,128)S(1)} %get-tuple-element.19.refs_1_, ...), custom_call_target="tpu_custom_call" | custom-call | flops 1610612736 | bytes 6291456 | tf_op jit(solution)/shard_map/encode_rows_0/pallas_call | solution.py:158
  40.9 1.0 %copy-done.8 = bf16[512,1024]{1,0:T(8,128)(2,1)} copy-done((bf16[512,1024]{1,0:T(8,128)(2,1)}, bf16[512,1024]{1,0:T(8,128)(2,1)S(1)}, u32[]{:S(2)}) %copy-start.8) | copy-done | bytes 1048600
  41.8 8.4 %all_to_all.15 = bf16[8,8,512]{2,1,0:T(8,128)(2,1)S(1)} all-to-all(bf16[8,8,512]{2,1,0:T(8,128)(2,1)S(1)} %bitcast.14), channel_id=1, replica_groups=mesh['section'=2,'dp'=4,'mp'=4] {'section','mp'}, dimensions={0} | all-to-all | bytes 131072 | tf_op jit(solution)/shard_map/all_to_all | solution.py:330
  50.6 9.5 %all_to_all.16.got_ref = bf16[4,64,640]{2,1,0:T(8,128)(2,1)S(1)} all-to-all(bf16[4,64,640]{2,1,0:T(8,128)(2,1)S(1)} %get-tuple-element.32), channel_id=1, replica_groups=mesh['section'=2,'dp'=4,'mp'=4] {'mp'}, dimensions={0} | all-to-all | bytes 655360 | tf_op jit(solution)/shard_map/all_to_all | solution.py:348
  60.1 1.6 %up_half.1 = (f32[64,2176]{1,0:T(8,128)S(1)}, bf16[64,2176]{1,0:T(8,128)(2,1)S(1)}) custom-call(bf16[4,64,640]{2,1,0:T(8,128)(2,1)S(1)} %all_to_all.16.got_ref, bf16[2048,2048]{1,0:T(8,128)(2,1)S(1)} %copy-done), custom_call_target="tpu_custom_call" | custom-call | flops 536870912 | bytes 8388608 | tf_op jit(solution)/shard_map/up_half/pallas_call | solution.py:349
  61.8 1.5 %collective-permute-done.14.other_ref = bf16[64,2176]{1,0:T(8,128)(2,1)S(1)} collective-permute-done((bf16[64,2176]{1,0:T(8,128)(2,1)S(1)}, bf16[64,2176]{1,0:T(8,128)(2,1)S(1)}, u32[]{:S(2)}, u32[]{:S(2)}) %collective-permute-start.14) | collective-permute-done | bytes 278560 | tf_op jit(solution)/shard_map/ppermute | solution.py:28
  63.3 2.6 %down_part.1 = bf16[64,2048]{1,0:T(8,128)(2,1)} custom-call(f32[64,2176]{1,0:T(8,128)S(1)} %get-tuple-element.33.half_ref, bf16[64,2176]{1,0:T(8,128)(2,1)S(1)} %collective-permute-done.14.other_ref, f32[64,512]{1,0:T(8,128)S(1)} %get-tuple-element.35.local_ref, bf16[2048,2048]{1,0:T(8,128)(2,1)S(1)} %bitcast.10), custom_call_target="tpu_custom_call" | custom-call | flops 536870912 | bytes 8388608 | tf_op jit(solution)/shard_map/down_part/pallas_call | solution.py:365
  65.9 3.6 %all-to-all-start.2 = ((bf16[8,8,2048]{2,1,0:T(8,128)(2,1)}), bf16[8,8,2048]{2,1,0:T(8,128)(2,1)S(1)}, u32[]{:S(2)}, u32[]{:S(2)}) async-start(bf16[8,8,2048]{2,1,0:T(8,128)(2,1)} %bitcast.7), calls=%async_computation.2 | async-start | bytes 524288 | tf_op jit(solution)/shard_map/all_to_all | solution.py:378
  69.5 1.2 %copy-done.9 = bf16[512,1024]{1,0:T(8,128)(2,1)S(1)} copy-done((bf16[512,1024]{1,0:T(8,128)(2,1)S(1)}, bf16[512,1024]{1,0:T(8,128)(2,1)}, u32[]{:S(2)}) %copy-start.9) | copy-done | bytes 1048600
  70.7 1.0 %copy-done.11 = bf16[512,512]{1,0:T(8,128)(2,1)S(1)} copy-done((bf16[512,512]{1,0:T(8,128)(2,1)S(1)}, bf16[512,512]{1,0:T(8,128)(2,1)}, u32[]{:S(2)}) %copy-start.11) | copy-done | bytes 524312
  71.8 6.1 %encode_rows_512.1 = bf16[32,512]{1,0:T(8,128)(2,1)} custom-call(s32[1]{0:T(128)S(6)} %copy.12.refs_0_, s32[1,32]{1,0:T(1,128)S(1)} %get-tuple-element.19.refs_1_, bf16[1024,512]{1,0:T(8,128)(2,1)S(1)} %get-tuple-element.20.refs_2_, f32[1,512]{1,0:T(1,128)S(1)} %get-tuple-element.21.refs_3_, bf16[512,2048]{1,0:T(8,128)(2,1)S(1)} %get-tuple-element.25.refs_4_, ...), custom_call_target="tpu_custom_call" | custom-call | flops 2147483648 | bytes 6291456 | tf_op jit(solution)/shard_map/encode_rows_512/pallas_call | solution.py:158
  77.8 0.7 sum_rows.1
  (41 shorter events, 2.5 us)
Async XLA Ops:
  1.5 7.6 %collective-permute-start.5 = (bf16[128,256]{1,0:T(8,128)(2,1)S(1)}, bf16[128,256]{1,0:T(8,128)(2,1)S(1)}, u32[]{:S(2)}, u32[]{:S(2)}) collective-permute-start(bf16[128,256]{1,0:T(8,128)(2,1)S(1)} %constant_dynamic-slice_fusion), channel_id=1, source_target_pairs={{0,12},{4,8},{8,4},{12,0},{1,13},{5,9},{9,5},{13,1},{2,14},{6,10},... | collective-permute-start | bytes 196616 | tf_op jit(solution)/shard_map/ppermute | solution.py:28
  6.5 5.6 %collective-permute-start.4 = (bf16[128,256]{1,0:T(8,128)(2,1)S(1)}, bf16[128,256]{1,0:T(8,128)(2,1)S(1)}, u32[]{:S(2)}, u32[]{:S(2)}) collective-permute-start(bf16[128,256]{1,0:T(8,128)(2,1)S(1)} %constant_dynamic-slice_fusion), channel_id=1, source_target_pairs={{0,8},{4,12},{8,0},{12,4},{1,9},{5,13},{9,1},{13,5},{2,10},{6,14},... | collective-permute-start | bytes 196616 | tf_op jit(solution)/shard_map/ppermute | solution.py:28
  6.5 5.6 %collective-permute-start.3 = (bf16[128,256]{1,0:T(8,128)(2,1)S(1)}, bf16[128,256]{1,0:T(8,128)(2,1)S(1)}, u32[]{:S(2)}, u32[]{:S(2)}) collective-permute-start(bf16[128,256]{1,0:T(8,128)(2,1)S(1)} %constant_dynamic-slice_fusion), channel_id=1, source_target_pairs={{0,4},{4,0},{8,12},{12,8},{1,5},{5,1},{9,13},{13,9},{2,6},{6,2},{1... | collective-permute-start | bytes 196616 | tf_op jit(solution)/shard_map/ppermute | solution.py:28
  7.1 53.0 %copy-start = (bf16[2048,2048]{1,0:T(8,128)(2,1)S(1)}, bf16[2048,2048]{1,0:T(8,128)(2,1)}, u32[]{:S(2)}) copy-start(bf16[2048,2048]{1,0:T(8,128)(2,1)} %w_ref.2) | copy-start | bytes 25165828
  12.2 21.6 %collective-permute-start.8 = (bf16[3,128,256]{2,1,0:T(8,128)(2,1)S(1)}, bf16[3,128,256]{2,1,0:T(8,128)(2,1)S(1)}, u32[]{:S(2)}, u32[]{:S(2)}) collective-permute-start(bf16[3,128,256]{2,1,0:T(8,128)(2,1)S(1)} %pad_maximum_fusion.refs_5_), channel_id=1, source_target_pairs={{0,3},{1,2},{2,1},{3,0},{4,7},{5,6},{6,5},{7,4},{8,11},{9,10},{10,... | collective-permute-start | bytes 589832 | tf_op jit(solution)/shard_map/ppermute | solution.py:28
  14.7 19.6 %collective-permute-start.7 = (bf16[3,128,256]{2,1,0:T(8,128)(2,1)S(1)}, bf16[3,128,256]{2,1,0:T(8,128)(2,1)S(1)}, u32[]{:S(2)}, u32[]{:S(2)}) collective-permute-start(bf16[3,128,256]{2,1,0:T(8,128)(2,1)S(1)} %pad_maximum_fusion.refs_5_), channel_id=1, source_target_pairs={{0,2},{1,3},{2,0},{3,1},{4,6},{5,7},{6,4},{7,5},{8,10},{9,11},{10,... | collective-permute-start | bytes 589832 | tf_op jit(solution)/shard_map/ppermute | solution.py:28
  15.2 19.1 %collective-permute-start.6 = (bf16[3,128,256]{2,1,0:T(8,128)(2,1)S(1)}, bf16[3,128,256]{2,1,0:T(8,128)(2,1)S(1)}, u32[]{:S(2)}, u32[]{:S(2)}) collective-permute-start(bf16[3,128,256]{2,1,0:T(8,128)(2,1)S(1)} %pad_maximum_fusion.refs_5_), channel_id=1, source_target_pairs={{0,1},{1,0},{2,3},{3,2},{4,5},{5,4},{6,7},{7,6},{8,9},{9,8},{10,11... | collective-permute-start | bytes 589832 | tf_op jit(solution)/shard_map/ppermute | solution.py:28
  16.6 6.2 %collective-permute-start.2 = (bf16[64,512]{1,0:T(8,128)(2,1)S(1)}, bf16[64,512]{1,0:T(8,128)(2,1)S(1)}, u32[]{:S(2)}, u32[]{:S(2)}) collective-permute-start(bf16[64,512]{1,0:T(8,128)(2,1)S(1)} %constant_dynamic-slice_fusion.1), channel_id=1, source_target_pairs={{0,12},{4,8},{8,4},{12,0},{1,13},{5,9},{9,5},{13,1},{2,14},{6,10},... | collective-permute-start | bytes 196616 | tf_op jit(solution)/shard_map/ppermute | solution.py:28
  19.2 5.5 %collective-permute-start.1 = (bf16[64,512]{1,0:T(8,128)(2,1)S(1)}, bf16[64,512]{1,0:T(8,128)(2,1)S(1)}, u32[]{:S(2)}, u32[]{:S(2)}) collective-permute-start(bf16[64,512]{1,0:T(8,128)(2,1)S(1)} %constant_dynamic-slice_fusion.1), channel_id=1, source_target_pairs={{0,8},{4,12},{8,0},{12,4},{1,9},{5,13},{9,1},{13,5},{2,10},{6,14},... | collective-permute-start | bytes 196616 | tf_op jit(solution)/shard_map/ppermute | solution.py:28
  22.7 4.3 %collective-permute-start = (bf16[64,512]{1,0:T(8,128)(2,1)S(1)}, bf16[64,512]{1,0:T(8,128)(2,1)S(1)}, u32[]{:S(2)}, u32[]{:S(2)}) collective-permute-start(bf16[64,512]{1,0:T(8,128)(2,1)S(1)} %constant_dynamic-slice_fusion.1), channel_id=1, source_target_pairs={{0,4},{4,0},{8,12},{12,8},{1,5},{5,1},{9,13},{13,9},{2,6},{6,2},{1... | collective-permute-start | bytes 196616 | tf_op jit(solution)/shard_map/ppermute | solution.py:28
  24.8 10.8 %collective-permute-start.9 = (bf16[3,128,256]{2,1,0:T(8,128)(2,1)S(1)}, bf16[3,128,256]{2,1,0:T(8,128)(2,1)S(1)}, u32[]{:S(2)}, u32[]{:S(2)}) collective-permute-start(bf16[3,128,256]{2,1,0:T(8,128)(2,1)S(1)} %pad_maximum_fusion.refs_5_), channel_id=1, source_target_pairs={{0,16},{16,0},{1,17},{17,1},{2,18},{18,2},{3,19},{19,3},{4,20},{20... | collective-permute-start | bytes 589832 | tf_op jit(solution)/shard_map/ppermute | solution.py:28
  27.0 1.2 %copy-start.1 = (bf16[1,1024,512]{2,1,0:T(8,128)(2,1)S(1)}, bf16[1,1024,512]{2,1,0:T(8,128)(2,1)}, u32[]{:S(2)}) copy-start(bf16[1,1024,512]{2,1,0:T(8,128)(2,1)} %param.10) | copy-start | bytes 3145732
  28.2 1.0 %copy-start.2 = (bf16[128,2048]{1,0:T(8,128)(2,1)S(1)}, bf16[128,2048]{1,0:T(8,128)(2,1)}, u32[]{:S(2)}) copy-start(bf16[128,2048]{1,0:T(8,128)(2,1)} %refs_3_.1) | copy-start | bytes 1572868
  29.3 1.0 %copy-start.3 = (bf16[512,512]{1,0:T(8,128)(2,1)S(1)}, bf16[512,512]{1,0:T(8,128)(2,1)}, u32[]{:S(2)}) copy-start(bf16[512,512]{1,0:T(8,128)(2,1)} %refs_8_.1) | copy-start | bytes 1572868
  30.3 0.9 %copy-start.4 = (bf16[128,512]{1,0:T(8,128)(2,1)S(1)}, bf16[128,512]{1,0:T(8,128)(2,1)}, u32[]{:S(2)}) copy-start(bf16[128,512]{1,0:T(8,128)(2,1)} %refs_4_.1) | copy-start | bytes 393220
  31.2 0.7 copy-start.5
  31.9 0.7 copy-start.6
  32.6 0.7 copy-start.7
  33.6 29.7 %slice-start = ((s8[8388608]{0:T(1024)(128)(4,1)}), s8[4194304]{0:T(1024)(128)(4,1)S(1)}, s32[]{:S(2)}) async-start(s8[8388608]{0:T(1024)(128)(4,1)} %bitcast.9), calls=%async_computation.3 | async-start | bytes 8388608
  33.6 1.9 %collective-permute-start.13 = (bf16[3,64,512]{2,1,0:T(8,128)(2,1)S(1)}, bf16[3,64,512]{2,1,0:T(8,128)(2,1)S(1)}, u32[]{:S(2)}, u32[]{:S(2)}) collective-permute-start(bf16[3,64,512]{2,1,0:T(8,128)(2,1)S(1)} %get-tuple-element.24.refs_14_), channel_id=1, source_target_pairs={{0,16},{16,0},{1,17},{17,1},{2,18},{18,2},{3,19},{19,3},{4,20},{20... | collective-permute-start | bytes 589832 | tf_op jit(solution)/shard_map/ppermute | solution.py:28
  33.7 1.8 %collective-permute-start.12 = (bf16[3,128,256]{2,1,0:T(8,128)(2,1)S(1)}, bf16[3,128,256]{2,1,0:T(8,128)(2,1)S(1)}, u32[]{:S(2)}, u32[]{:S(2)}) collective-permute-start(bf16[3,128,256]{2,1,0:T(8,128)(2,1)S(1)} %collective-permute-done.8.refs_8_), channel_id=1, source_target_pairs={{0,16},{16,0},{1,17},{17,1},{2,18},{18,2},{3,19},{19,3},{4,20},{20... | collective-permute-start | bytes 589832 | tf_op jit(solution)/shard_map/ppermute | solution.py:28
  34.2 1.5 %collective-permute-start.11 = (bf16[3,128,256]{2,1,0:T(8,128)(2,1)S(1)}, bf16[3,128,256]{2,1,0:T(8,128)(2,1)S(1)}, u32[]{:S(2)}, u32[]{:S(2)}) collective-permute-start(bf16[3,128,256]{2,1,0:T(8,128)(2,1)S(1)} %collective-permute-done.7.refs_7_), channel_id=1, source_target_pairs={{0,16},{16,0},{1,17},{17,1},{2,18},{18,2},{3,19},{19,3},{4,20},{20... | collective-permute-start | bytes 589832 | tf_op jit(solution)/shard_map/ppermute | solution.py:28
  34.3 1.7 %collective-permute-start.10 = (bf16[3,128,256]{2,1,0:T(8,128)(2,1)S(1)}, bf16[3,128,256]{2,1,0:T(8,128)(2,1)S(1)}, u32[]{:S(2)}, u32[]{:S(2)}) collective-permute-start(bf16[3,128,256]{2,1,0:T(8,128)(2,1)S(1)} %collective-permute-done.6.refs_6_), channel_id=1, source_target_pairs={{0,16},{16,0},{1,17},{17,1},{2,18},{18,2},{3,19},{19,3},{4,20},{20... | collective-permute-start | bytes 589832 | tf_op jit(solution)/shard_map/ppermute | solution.py:28
  40.8 1.0 %copy-start.8 = (bf16[512,1024]{1,0:T(8,128)(2,1)}, bf16[512,1024]{1,0:T(8,128)(2,1)S(1)}, u32[]{:S(2)}) copy-start(bf16[512,1024]{1,0:T(8,128)(2,1)S(1)} %get-tuple-element.27.refs_6_) | copy-start | bytes 3145732
  41.8 8.7 %copy-start.10 = (bf16[512,512]{1,0:T(8,128)(2,1)}, bf16[512,512]{1,0:T(8,128)(2,1)S(1)}, u32[]{:S(2)}) copy-start(bf16[512,512]{1,0:T(8,128)(2,1)S(1)} %get-tuple-element.26.refs_5_) | copy-start | bytes 1572868
  60.1 3.2 %slice-start.1 = ((s8[8388608]{0:T(1024)(128)(4,1)}), s8[4194304]{0:T(1024)(128)(4,1)S(1)}, s32[]{:S(2)}) async-start(s8[8388608]{0:T(1024)(128)(4,1)} %bitcast.9), calls=%async_computation.4 | async-start | bytes 8388608
  61.7 1.6 %collective-permute-start.14 = (bf16[64,2176]{1,0:T(8,128)(2,1)S(1)}, bf16[64,2176]{1,0:T(8,128)(2,1)S(1)}, u32[]{:S(2)}, u32[]{:S(2)}) collective-permute-start(bf16[64,2176]{1,0:T(8,128)(2,1)S(1)} %get-tuple-element.34), channel_id=1, source_target_pairs={{0,16},{16,0},{1,17},{17,1},{2,18},{18,2},{3,19},{19,3},{4,20},{20... | collective-permute-start | bytes 835592 | tf_op jit(solution)/shard_map/ppermute | solution.py:28
  65.9 11.9 %all-to-all-start.2 = ((bf16[8,8,2048]{2,1,0:T(8,128)(2,1)}), bf16[8,8,2048]{2,1,0:T(8,128)(2,1)S(1)}, u32[]{:S(2)}, u32[]{:S(2)}) async-start(bf16[8,8,2048]{2,1,0:T(8,128)(2,1)} %bitcast.7), calls=%async_computation.2 | async-start | bytes 524288 | tf_op jit(solution)/shard_map/all_to_all | solution.py:378
  69.5 1.2 %copy-start.9 = (bf16[512,1024]{1,0:T(8,128)(2,1)S(1)}, bf16[512,1024]{1,0:T(8,128)(2,1)}, u32[]{:S(2)}) copy-start(bf16[512,1024]{1,0:T(8,128)(2,1)} %copy-done.8) | copy-start | bytes 3145732
  70.7 1.0 %copy-start.11 = (bf16[512,512]{1,0:T(8,128)(2,1)S(1)}, bf16[512,512]{1,0:T(8,128)(2,1)}, u32[]{:S(2)}) copy-start(bf16[512,512]{1,0:T(8,128)(2,1)} %copy-done.10) | copy-start | bytes 1572868

commit v3 on v2

v3 whole, which is shorter than its diff:
```python
import functools

import jax
import jax.numpy as jnp
from jax import lax
from jax.experimental import pallas as pl
from jax.experimental.pallas import tpu as pltpu
from jax.sharding import PartitionSpec as P

HEADS = 4
DM = 4096
MICRO = 4
SESS_MAX = 64
EPSILON = 1e-06
F32 = jnp.float32
BF16 = jnp.bfloat16

VMEM = pl.BlockSpec(memory_space=pltpu.VMEM)
HBM = pl.BlockSpec(memory_space=pltpu.HBM)


def params(mib):
    return pltpu.CompilerParams(vmem_limit_bytes=mib * 1024 * 1024)


def swap(x, axis, size, flip):
    return lax.ppermute(x, axis, [(i, i ^ flip) for i in range(size)])


def silu_half(h):
    return h + h * jnp.tanh(h)


def encoder_rows(place, n_w, n_wout, row0, rows, copies_out, *refs):
    refs = list(refs)
    bounds_ref, ev_ref, gain_ref = refs[:3]
    refs = refs[3:]
    copies = []
    if place is not None:
        w_parts, wout_parts, refs = refs[:n_w], refs[n_w : n_w + n_wout], refs[n_w + n_wout :]
        pooled_ref, w_ref, wout_ref, kv_out, sums_out = refs[:5]
        q_ref, gate_ref, att_ref, sems = refs[5:]
        prior = []
        copies = place(w_parts, wout_parts, w_ref, wout_ref, sems)
    else:
        w_ref, wout_ref, kv_ref, sums_ref, pooled_ref = refs[:5]
        q_ref, gate_ref, att_ref, kv_out = refs[5:]
        prior = [kv_ref]
    for c in copies:
        c.start()
    for c in copies:
        c.wait()
    width = ev_ref.shape[1]
    head = width // HEADS
    starts, ends, hist = bounds_ref[0, :, :1], bounds_ref[1, :, :1], bounds_ref[2, :1, :1]
    sess = starts.shape[0]

    pos = (lax.broadcasted_iota(jnp.int32, (sess, rows), 1) + row0).astype(F32)
    member = jnp.where((pos >= starts) & (pos < ends), 1.0, 0.0).astype(BF16)
    n_valid = jnp.maximum(ends - starts, 0.0)

    step = min(rows, 256)
    for r in range(0, rows, step):
        x = ev_ref[r : r + step, :]
        at = slice(r, r + step)
        row_pos = lax.broadcasted_iota(jnp.int32, (step, 1), 0).astype(F32) + (row0 + r)

        def act(n):
            part = jnp.dot(x, w_ref[:, n * width : (n + 1) * width], preferred_element_type=F32)
            return silu_half(part * 0.5)

        gate_ref[at, :] = act(0)
        kv_out[at, :width] = jnp.where(row_pos < hist, act(1), 0.0).astype(BF16)
        q_ref[at, :] = act(2).astype(BF16)
        kv_out[at, width:] = act(3).astype(BF16)

    blocks = []
    for ref in prior + [kv_out]:
        for r in range(0, ref.shape[0], step):
            blocks.append((ref, r))
    tri = lax.broadcasted_iota(jnp.int32, (step, step), 1) <= lax.broadcasted_iota(
        jnp.int32, (step, step), 0
    )
    before = len(blocks) - rows // step
    for i in range(rows // step):
        at = slice(i * step, (i + 1) * step)
        for h in range(HEADS):
            q = q_ref[at, h * head : (h + 1) * head]
            total = None
            for j in range(before + i + 1):
                ref, r = blocks[j]
                k = ref[r : r + step, width + h * head : width + (h + 1) * head]
                v = ref[r : r + step, h * head : (h + 1) * head]
                s = lax.dot_general(q, k, (((1,), (1,)), ((), ())), preferred_element_type=F32)
                wts = silu_half(s * (0.5 * head**-0.5))
                if j == before + i:
                    wts = jnp.where(tri, wts, 0.0)
                mixed = jnp.dot(wts.astype(BF16), v, preferred_element_type=F32)
                total = mixed if total is None else total + mixed
            att_ref[at, h * head : (h + 1) * head] = total

    sums_ev = jnp.dot(member, ev_ref[...], preferred_element_type=F32)
    att = att_ref[...]
    inv = lax.rsqrt(jnp.mean(att * att, axis=1, keepdims=True) + EPSILON)
    gated = (att * inv * gain_ref[:1] * gate_ref[...]).astype(BF16)
    sums_g = jnp.dot(member, gated, preferred_element_type=F32)
    if place is not None:
        sums_out[:, :width] = sums_ev
        sums_out[:, width:] = sums_g
    else:
        sums_ev = sums_ev + sums_ref[:, :width]
        sums_g = sums_g + sums_ref[:, width:]

    hi = sums_g.astype(BF16)
    rest = sums_g - hi.astype(F32)
    mid = rest.astype(BF16)
    low = (rest - mid.astype(F32)).astype(BF16)
    terms = jnp.dot(jnp.concatenate([low, mid, hi], axis=0), wout_ref[...], preferred_element_type=F32)
    out = terms[:sess] + terms[sess : 2 * sess] + terms[2 * sess :] + sums_ev
    out = out / jnp.maximum(n_valid, 1.0)
    if copies_out:
        peers, take = copies_out
        out = jnp.concatenate([out[:take]] * peers, axis=0)
    pooled_ref[...] = out.astype(pooled_ref.dtype)


def encoder_call(bounds, gain, events, row0, weights, copies_out=None, carried=None):
    rows, width = events.shape
    sess = bounds.shape[1]
    place, w_parts, wout_parts = weights if carried is None else (None, [], [])
    scratch = [
        pltpu.VMEM((rows, width), BF16),
        pltpu.VMEM((rows, width), F32),
        pltpu.VMEM((rows, width), F32),
    ]
    if carried is None:
        operands = [*w_parts, *wout_parts]
        peers, take = copies_out
        out_shape = [
            jax.ShapeDtypeStruct((peers * take, width), BF16),
            jax.ShapeDtypeStruct((width, 4 * width), BF16),
            jax.ShapeDtypeStruct((width, width), BF16),
            jax.ShapeDtypeStruct((rows, 2 * width), BF16),
            jax.ShapeDtypeStruct((sess, 2 * width), F32),
        ]
        scratch.append(pltpu.SemaphoreType.DMA((64,)))
    else:
        operands = carried
        out_shape = [jax.ShapeDtypeStruct((sess, width), F32)]
        scratch.append(pltpu.VMEM((rows, 2 * width), BF16))
    return pl.pallas_call(
        functools.partial(encoder_rows, place, len(w_parts), len(wout_parts), row0, rows, copies_out),
        in_specs=[VMEM] * (3 + len(operands)),
        out_specs=[VMEM] * len(out_shape),
        out_shape=out_shape,
        scratch_shapes=scratch,
        compiler_params=params(16),
        cost_estimate=pl.CostEstimate(
            flops=2 * rows * width * 4 * width + 4 * rows * (row0 + rows) * width,
            bytes_accessed=6 * 1024 * 1024,
            transcendentals=4 * rows * width + HEADS * rows * (row0 + rows),
        ),
        name=f"encode_rows_{row0}",
    )(bounds, events, gain, *operands)


def parity(m):
    return (m & 1) ^ ((m >> 1) & 1)


def split_kernel(*refs):
    *parts, next_ref, left_ref, right_ref, next_out = refs
    next_out[...] = next_ref[...]
    half = left_ref.shape[2]
    for k, part in enumerate(parts):
        left_ref[k] = part[:, :half]
        right_ref[k] = part[:, half:]


def gather_weights(w_uvqk, w_out, w_in, ffn_gain, sections, dps, mps):
    depth, wide = w_uvqk.shape
    gains = [ffn_gain] + [swap(ffn_gain, "mp", mps, k) for k in range(1, mps)]
    if (sections, mps) != (2, 4) or wide % 1024 or depth % 32:
        full = lax.all_gather(w_uvqk, "dp", axis=0, tiled=True)
        full_out = lax.all_gather(w_out, "dp", axis=0, tiled=True)
        blocks = [[w_in]] + [[swap(w_in, "mp", mps, k)] for k in range(1, mps)]

        def place_whole(ws, wouts, w_ref, wout_ref, sems):
            return [
                pltpu.make_async_copy(ws[0], w_ref, sems.at[0]),
                pltpu.make_async_copy(wouts[0], wout_ref, sems.at[1]),
            ]

        return (place_whole, [full], [full_out]), blocks, gains

    quarter, part = wide // 4, depth // 2
    sec, m = lax.axis_index("section"), lax.axis_index("mp")
    mine = lax.dynamic_slice_in_dim(w_uvqk, (sec * 2 + parity(m)) * quarter, quarter, 1)
    half = lax.dynamic_slice_in_dim(w_out, sec * part, part, 0)
    got = [swap(mine, "dp", dps, k) for k in range(1, dps)]
    left, right, half = pl.pallas_call(
        split_kernel,
        in_specs=[VMEM] * (len(got) + 1),
        out_specs=[VMEM] * 3,
        out_shape=[
            *[jax.ShapeDtypeStruct((len(got), depth, quarter // 2), BF16)] * 2,
            jax.ShapeDtypeStruct(half.shape, BF16),
        ],
        compiler_params=params(8),
        cost_estimate=pl.CostEstimate(flops=0, bytes_accessed=16 * 1024 * 1024, transcendentals=0),
        name="split",
    )(*got, half)
    plane = [left, right, swap(left, "mp", mps, 1), swap(right, "mp", mps, 2)]
    ws = [w_uvqk[:, : wide // 2], w_uvqk[:, wide // 2 :]] + plane + [swap(p, "section", sections, 1) for p in plane]
    got_out = [swap(half, "dp", dps, k) for k in range(1, dps)]
    wouts = [w_out[:part], w_out[part:]] + got_out + [swap(p, "section", sections, 1) for p in got_out]

    from_x, from_y = swap(w_in, "mp", mps, 1), swap(w_in, "mp", mps, 2)
    cut = w_in.shape[0] // 32 * 16
    diagonal = [swap(from_x[:cut], "mp", mps, 2), swap(from_y[cut:], "mp", mps, 1)]

    def place(ws, wouts, w_ref, wout_ref, sems):
        z = lax.axis_index("dp")
        sec, m = lax.axis_index("section"), lax.axis_index("mp")
        copies = []

        def add(src, dst):
            copies.append(pltpu.make_async_copy(src, dst, sems.at[len(copies)]))

        def rows_of(k):
            return (z ^ k) * depth

        own = pl.ds(pl.multiple_of(rows_of(0), depth), depth)
        for i in range(2):
            add(ws[i], w_ref.at[own, pl.ds(i * (wide // 2), wide // 2)])
            add(wouts[i], wout_ref.at[pl.ds(pl.multiple_of(rows_of(0) + i * part, part), part)])
        for i, ref in enumerate(ws[2:]):
            spot = (sec ^ (i // 4)) * 2 * quarter + (parity(m) ^ (i // 2 % 2)) * quarter + (i % 2) * (quarter // 2)
            cols = pl.ds(pl.multiple_of(spot, quarter // 2), quarter // 2)
            for k in range(1, dps):
                add(ref.at[k - 1], w_ref.at[pl.ds(pl.multiple_of(rows_of(k), depth), depth), cols])
        for i, ref in enumerate(wouts[2:]):
            k = i % (dps - 1) + 1
            at = rows_of(k) + (sec ^ (i // (dps - 1))) * part
            add(ref, wout_ref.at[pl.ds(pl.multiple_of(at, part), part)])
        return copies

    return (place, ws, wouts), [[w_in], [from_x], [from_y], diagonal], gains


def two_terms(square):
    hi = square.astype(BF16).astype(F32)
    lane = lax.broadcasted_iota(jnp.int32, (square.shape[0], 128), 1)
    return jnp.where(lane == 0, hi, jnp.where(lane == 1, square - hi, 0.0)).astype(BF16)


def up_kernel(chunks, pieces, x_ref, *refs):
    w_in_refs, refs = refs[: sum(pieces)], refs[sum(pieces) :]
    gain_refs, refs = refs[: len(pieces)], refs[len(pieces) :]
    w_ref, local_ref, half_ref, send_ref, normed_ref = refs
    m = lax.axis_index("mp")
    x = x_ref[...]
    square = None
    at = 0
    for k, n in enumerate(pieces):
        block = jnp.concatenate([r[...] for r in w_in_refs[at : at + n]], axis=0)
        at += n
        hidden = jnp.dot(x, block, preferred_element_type=F32)
        part = jnp.sum(hidden * hidden, axis=1, keepdims=True)
        square = part if square is None else square + part
        gain = gain_refs[k][...].astype(F32)
        cols = hidden.shape[1]
        normed_ref[:, pl.ds(pl.multiple_of((m ^ k) * cols, cols), cols)] = (hidden * gain).astype(BF16)
        if k == 0:
            local_ref[...] = hidden
    normed = normed_ref[...]
    wide = w_ref.shape[1]
    each = wide // chunks
    for c in range(chunks):
        at = slice(c * each, (c + 1) * each)
        half = jnp.dot(normed, w_ref[:, at], preferred_element_type=F32)
        half_ref[:, at] = half
        send_ref[:, at] = half.astype(BF16)
    half_ref[:, wide:] = jnp.broadcast_to(square, (x.shape[0], 128))
    send_ref[:, wide:] = two_terms(square)


def down_kernel(chunks, half_ref, other_ref, local_ref, w_ref, _, out_ref, part_ref):
    units, wide = w_ref.shape
    each = wide // chunks
    square = half_ref[:, units : units + 1] + jnp.sum(other_ref[:, units:].astype(F32), axis=1, keepdims=True)
    inv = lax.rsqrt(square / DM + EPSILON)
    up = (half_ref[:, :units] + other_ref[:, :units].astype(F32)) * inv
    hidden = jax.nn.gelu(up, approximate=True).astype(BF16)
    for c in range(chunks):
        at = slice(c * each, (c + 1) * each)
        part_ref[:, at] = jnp.dot(hidden, w_ref[:, at], preferred_element_type=F32)
    m = lax.axis_index("mp")
    cols = local_ref.shape[1]
    own = pl.ds(pl.multiple_of(m * cols, cols), cols)
    part_ref[:, own] = part_ref[:, own] + local_ref[...]
    out_ref[...] = part_ref[...].astype(BF16)


def sum_kernel(sections, mps, got_ref, out_ref):
    got = got_ref[...].astype(F32)
    take, wide = out_ref.shape[0], got.shape[1]
    for s in range(sections):
        total = got[s * mps * take : (s * mps + 1) * take]
        for k in range(s * mps + 1, (s + 1) * mps):
            total = total + got[k * take : (k + 1) * take]
        out_ref[:, s * wide : (s + 1) * wide] = total.astype(BF16)


def cross_block(micro_rows, take, w_in_blocks, gains, w_up, w_down, encode_rest, sections, mps):
    peers = sections * mps
    rows, width = micro_rows.shape
    cols = w_up.shape[0] // mps
    units = w_up.shape[1]
    half_width = w_down.shape[1]
    group = ("section", "mp")
    chunks = 4

    arrived = lax.all_to_all(
        micro_rows.reshape(peers, take, width), group, split_axis=0, concat_axis=0, tiled=True
    ).reshape(rows, width)
    blocks = [piece for block in w_in_blocks for piece in block]
    local, half, half_send = pl.pallas_call(
        functools.partial(up_kernel, chunks, [len(block) for block in w_in_blocks]),
        out_shape=[
            jax.ShapeDtypeStruct((rows, cols), F32),
            jax.ShapeDtypeStruct((rows, units + 128), F32),
            jax.ShapeDtypeStruct((rows, units + 128), BF16),
        ],
        in_specs=[VMEM] * (len(blocks) + len(gains) + 2),
        out_specs=[VMEM] * 3,
        scratch_shapes=[pltpu.VMEM((rows, w_up.shape[0]), BF16)],
        compiler_params=params(10),
        cost_estimate=pl.CostEstimate(
            flops=2 * rows * w_up.size, bytes_accessed=2 * w_up.size, transcendentals=0
        ),
        name="up_half",
    )(arrived, *blocks, *gains, w_up)

    other = swap(half_send, "section", sections, 1)
    rest = encode_rest()
    partial = pl.pallas_call(
        functools.partial(down_kernel, chunks),
        out_shape=jax.ShapeDtypeStruct((rows, half_width), BF16),
        in_specs=[VMEM] * 4 + [HBM],
        out_specs=VMEM,
        scratch_shapes=[pltpu.VMEM((rows, half_width), F32)],
        compiler_params=params(8),
        cost_estimate=pl.CostEstimate(
            flops=2 * rows * w_down.size, bytes_accessed=2 * w_down.size, transcendentals=rows * units
        ),
        name="down_part",
    )(half, other, local, w_down, rest)

    arrived = lax.all_to_all(
        partial.reshape(peers, take, half_width), group, split_axis=0, concat_axis=0, tiled=True
    ).reshape(rows, half_width)
    cross_out = pl.pallas_call(
        functools.partial(sum_kernel, sections, mps),
        out_shape=jax.ShapeDtypeStruct((take, half_width * sections), BF16),
        in_specs=[VMEM],
        out_specs=VMEM,
        compiler_params=params(8),
        name="sum_rows",
    )(arrived)
    return rest, partial, cross_out


def round_kernel(x_ref, _, out_ref):
    out_ref[...] = x_ref[...].astype(BF16)


def per_device(sections, dps, mps, events, hist_len, sess_len, w_uvqk, w_out, attn_gain, w_in, ffn_gain, w_up, w_down):
    events = events[0]
    length, width = events.shape
    sess = sess_len.shape[1]
    take = sess // MICRO
    gain = jnp.broadcast_to(attn_gain, (8, width))
    weights, w_in_blocks, gains = gather_weights(w_uvqk, w_out, w_in, ffn_gain, sections, dps, mps)
    ends = jnp.sum(jnp.where(jnp.tri(sess, dtype=jnp.bool_), sess_len, 0), axis=1)
    bounds = jnp.stack([ends - sess_len[0], jnp.minimum(ends, hist_len), jnp.broadcast_to(hist_len, ends.shape)])
    bounds = jnp.broadcast_to(bounds.astype(F32)[:, :, None], (3, sess, 128))
    encode = functools.partial(encoder_call, bounds, gain)

    first = take * SESS_MAX
    micro_rows, *carried = encode(events[:first], 0, weights, copies_out=(sections * mps, take))

    def encode_rest():
        return encode(events[first:], first, weights, carried=carried)[0]

    pooled, after, cross_out = cross_block(micro_rows, take, w_in_blocks, gains, w_up, w_down, encode_rest, sections, mps)
    pooled = pl.pallas_call(
        round_kernel,
        out_shape=jax.ShapeDtypeStruct(pooled.shape, BF16),
        in_specs=[VMEM, HBM],
        out_specs=VMEM,
        compiler_params=params(8),
        name="round_pooled",
    )(pooled, after)
    return (pooled, cross_out)


def solution(mesh):
    sizes = [mesh.shape[name] for name in ("section", "dp", "mp")]
    return jax.shard_map(
        functools.partial(per_device, *sizes),
        mesh=mesh,
        in_specs=(
            P(("section", "dp", "mp"), None, None),
            P(("section", "dp", "mp")),
            P(("section", "dp", "mp"), None),
            P("dp", None),
            P("dp", None),
            P(),
            P(None, ("section", "mp")),
            P(None, ("section", "mp")),
            P("section", "mp"),
            P("mp", "section"),
        ),
        out_specs=(P(("section", "dp", "mp"), None), P(("section", "dp", "mp"), None)),
        check_vma=False,
    )
```

time: 79.2 us -> 83.4 us (1.053)
  blocking collectives: 18 us -> 0 us
  starting transfers between devices: 18.4 us -> 31.7 us
  waiting for transfers between devices: 12.9 us -> 17.9 us
  local copies, waits for them, and re-layouts: 11.2 us -> 13.6 us
  other arithmetic: 0.02 us -> 1.44 us
    all_to_all x2 -> x0, blocking collectives: 18 us -> none  [the longest x1 9.52 us: cross_block(): got = lax.all_to_all(send, 'mp', split_axis=0, concat_axis=0, tiled=True)]
    ppermute x15 -> x23, starting transfers between devices: 14.9 us -> 24.8 us  [swap(): return lax.ppermute(x, axis, [(i, i ^ flip) for i in range(size)])]
    all_to_all x1, waiting for transfers between devices: 0.01 us -> 5.88 us  [cross_block(): lax.all_to_all(partial.reshape(peers, take, half_width), group, split_axi...]
    slice x0 -> x5, local copies, waits for them, and re-layouts: none -> 4.7 us  [the longest x1 1.27 us: per_device(): events[:first]]
    all_to_all x0 -> x1, starting transfers between devices: none -> 3.53 us  [cross_block(): lax.all_to_all(micro_rows.reshape(peers, take, width), group, split_axis=...]
    unnamed x28 -> x18, local copies, waits for them, and re-layouts: 9.48 us -> 7.13 us
    ppermute x15 -> x23, waiting for transfers between devices: 12.9 us -> 12 us  [swap(): return lax.ppermute(x, axis, [(i, i ^ flip) for i in range(size)])]
    dynamic_slice x2 -> x1, local copies, waits for them, and re-layouts: 1.69 us -> 0.97 us  [gather_weights(): lax.dynamic_slice_in_dim(w_uvqk, (sec * 2 + parity(m)) * quarter, quarter...]
  transfers between devices with their start and end apart: 16 -> 25, of which waited for: 8 -> 8; matrix products, arithmetic and copies ran while one was open for 1% -> 8% of each run, Pallas kernels for 8% -> 14%
where the time goes in v3:
time: 83.4 us; the launch traced here: 82.9 us
  starting transfers between devices  31.7 us (38%)
  waiting for transfers between devices  17.9 us (21%)
  Pallas kernels  16.8 us (20%)
  local copies, waits for them, and re-layouts  13.6 us (16%)
  between operations  1.53 us (2%)
  other arithmetic  1.44 us (2%)
    ppermute x23, starting transfers between devices, swap(): return lax.ppermute(x, axis, [(i, i ^ flip) for i in range(size)])  24.8 us
    ppermute x23, waiting for transfers between devices, swap(): return lax.ppermute(x, axis, [(i, i ^ flip) for i in range(size)])  12 us
    pallas_call x2, Pallas kernels, encoder_call(): pl.pallas_call(functools.partial(encoder_rows, place, len(w_parts), len(w...  10.9 us
    unnamed x18, local copies, waits for them, and re-layouts  7.13 us
    all_to_all x1, waiting for transfers between devices, cross_block(): lax.all_to_all(partial.reshape(peers, take, half_width), group, split_axi...  5.88 us
    all_to_all x1, starting transfers between devices, cross_block(): lax.all_to_all(micro_rows.reshape(peers, take, width), group, split_axis=...  3.53 us
    all_to_all x1, starting transfers between devices, cross_block(): lax.all_to_all(partial.reshape(peers, take, half_width), group, split_axi...  3.41 us
    pallas_call x1, Pallas kernels, cross_block(): pl.pallas_call(functools.partial(down_kernel, chunks), out_shape=jax.Shap...  2.54 us
  transfers between devices with their start and end apart: 25, of which 8 were waited for; matrix products, arithmetic and copies ran while one was open for 8% of the time, Pallas kernels for 14%

profile of v3, /device:TPU:0, one launch (start us, length us, event | category | flops | bytes accessed | tf_op | source)
XLA Modules:
  0.0 82.9 jit_solution(18071489553710331966)
XLA Ops:
  0.7 1.0 %constant_dynamic-slice_fusion.1 = bf16[128,512]{1,0:T(8,128)(2,1)S(1)} fusion(bf16[128,2048]{1,0:T(8,128)(2,1)} %param.13, s32[]{:T(128)S(6)} %select_n.11), kind=kLoop, calls=%fused_computation.8 | loop fusion | bytes 262148 | tf_op jit(solution)/shard_map/dynamic_slice | solution.py:198
  1.6 3.1 %collective-permute-start = (bf16[128,512]{1,0:T(8,128)(2,1)S(1)}, bf16[128,512]{1,0:T(8,128)(2,1)S(1)}, u32[]{:S(2)}, u32[]{:S(2)}) collective-permute-start(bf16[128,512]{1,0:T(8,128)(2,1)S(1)} %constant_dynamic-slice_fusion.1), channel_id=1, source_target_pairs={{0,4},{4,0},{8,12},{12,8},{1,5},{5,1},{9,13},{13,9},{2,6},{6,2},{1... | collective-permute-start | bytes 393224 | tf_op jit(solution)/shard_map/ppermute | solution.py:27
  4.7 2.6 %collective-permute-start.1 = (bf16[128,512]{1,0:T(8,128)(2,1)S(1)}, bf16[128,512]{1,0:T(8,128)(2,1)S(1)}, u32[]{:S(2)}, u32[]{:S(2)}) collective-permute-start(bf16[128,512]{1,0:T(8,128)(2,1)S(1)} %constant_dynamic-slice_fusion.1), channel_id=1, source_target_pairs={{0,8},{4,12},{8,0},{12,4},{1,9},{5,13},{9,1},{13,5},{2,10},{6,14},... | collective-permute-start | bytes 393224 | tf_op jit(solution)/shard_map/ppermute | solution.py:27
  7.3 1.7 %collective-permute-start.15 = (bf16[512,512]{1,0:T(8,128)(2,1)}, bf16[512,512]{1,0:T(8,128)(2,1)S(1)}, u32[]{:S(2)}, u32[]{:S(2)}) collective-permute-start(bf16[512,512]{1,0:T(8,128)(2,1)} %refs_0_.1), channel_id=1, source_target_pairs={{0,1},{1,0},{2,3},{3,2},{4,5},{5,4},{6,7},{7,6},{8,9},{9,8},{10,11... | collective-permute-start | bytes 1572872 | tf_op jit(solution)/shard_map/ppermute | solution.py:27
  9.0 1.5 %collective-permute-start.16 = (bf16[512,512]{1,0:T(8,128)(2,1)}, bf16[512,512]{1,0:T(8,128)(2,1)S(1)}, u32[]{:S(2)}, u32[]{:S(2)}) collective-permute-start(bf16[512,512]{1,0:T(8,128)(2,1)} %refs_0_.1), channel_id=1, source_target_pairs={{0,2},{1,3},{2,0},{3,1},{4,6},{5,7},{6,4},{7,5},{8,10},{9,11},{10,... | collective-permute-start | bytes 1572872 | tf_op jit(solution)/shard_map/ppermute | solution.py:27
  10.6 0.9 %fusion.1 = (bf16[64,512]{1,0:T(8,128)(2,1)S(1)}, bf16[64,512]{1,0:T(8,128)(2,1)S(1)}, bf16[64,512]{1,0:T(8,128)(2,1)S(1)}) fusion(bf16[128,512]{1,0:T(8,128)(2,1)} %param.14, s32[]{:T(128)S(6)} %select_n.12), kind=kLoop, calls=%fused_computation.10 | loop fusion | bytes 393220 | tf_op jit(solution)/shard_map/slice | solution.py:216
  11.5 6.2 %collective-permute-done.1.refs_1_ = bf16[128,512]{1,0:T(8,128)(2,1)S(1)} collective-permute-done((bf16[128,512]{1,0:T(8,128)(2,1)S(1)}, bf16[128,512]{1,0:T(8,128)(2,1)S(1)}, u32[]{:S(2)}, u32[]{:S(2)}) %collective-permute-start.1) | collective-permute-done | bytes 131104 | tf_op jit(solution)/shard_map/ppermute | solution.py:27
  17.7 2.0 %collective-permute-start.9 = (bf16[64,512]{1,0:T(8,128)(2,1)S(1)}, bf16[64,512]{1,0:T(8,128)(2,1)S(1)}, u32[]{:S(2)}, u32[]{:S(2)}) collective-permute-start(bf16[64,512]{1,0:T(8,128)(2,1)S(1)} %get-tuple-element.15), channel_id=1, source_target_pairs={{0,4},{4,0},{8,12},{12,8},{1,5},{5,1},{9,13},{13,9},{2,6},{6,2},{1... | collective-permute-start | bytes 196616 | tf_op jit(solution)/shard_map/ppermute | solution.py:27
  19.7 1.1 %collective-permute-start.10 = (bf16[64,512]{1,0:T(8,128)(2,1)S(1)}, bf16[64,512]{1,0:T(8,128)(2,1)S(1)}, u32[]{:S(2)}, u32[]{:S(2)}) collective-permute-start(bf16[64,512]{1,0:T(8,128)(2,1)S(1)} %get-tuple-element.15), channel_id=1, source_target_pairs={{0,8},{4,12},{8,0},{12,4},{1,9},{5,13},{9,1},{13,5},{2,10},{6,14},... | collective-permute-start | bytes 196616 | tf_op jit(solution)/shard_map/ppermute | solution.py:27
  20.8 1.4 %collective-permute-start.11 = (bf16[64,512]{1,0:T(8,128)(2,1)S(1)}, bf16[64,512]{1,0:T(8,128)(2,1)S(1)}, u32[]{:S(2)}, u32[]{:S(2)}) collective-permute-start(bf16[64,512]{1,0:T(8,128)(2,1)S(1)} %get-tuple-element.15), channel_id=1, source_target_pairs={{0,12},{4,8},{8,4},{12,0},{1,13},{5,9},{9,5},{13,1},{2,14},{6,10},... | collective-permute-start | bytes 196616 | tf_op jit(solution)/shard_map/ppermute | solution.py:27
  22.2 1.3 %slice_bitcast_fusion = (bf16[512,512]{1,0:T(8,128)(2,1)S(1)}, bf16[512,512]{1,0:T(8,128)(2,1)S(1)}) fusion(bf16[1,1024,512]{2,1,0:T(8,128)(2,1)} %param.10), kind=kLoop, calls=%fused_computation | loop fusion | bytes 2097152 | tf_op jit(solution)/shard_map/slice | solution.py:391
  23.5 1.6 %collective-permute-start.3 = (bf16[3,128,256]{2,1,0:T(8,128)(2,1)S(1)}, bf16[3,128,256]{2,1,0:T(8,128)(2,1)S(1)}, u32[]{:S(2)}, u32[]{:S(2)}) collective-permute-start(bf16[3,128,256]{2,1,0:T(8,128)(2,1)S(1)} %get-tuple-element.13.refs_5_), channel_id=1, source_target_pairs={{0,1},{1,0},{2,3},{3,2},{4,5},{5,4},{6,7},{7,6},{8,9},{9,8},{10,11... | collective-permute-start | bytes 589832 | tf_op jit(solution)/shard_map/ppermute | solution.py:27
  25.0 1.1 %collective-permute-done.10.refs_16_ = bf16[64,512]{1,0:T(8,128)(2,1)S(1)} collective-permute-done((bf16[64,512]{1,0:T(8,128)(2,1)S(1)}, bf16[64,512]{1,0:T(8,128)(2,1)S(1)}, u32[]{:S(2)}, u32[]{:S(2)}) %collective-permute-start.10) | collective-permute-done | bytes 65568 | tf_op jit(solution)/shard_map/ppermute | solution.py:27
  26.1 1.5 %collective-permute-start.4 = (bf16[3,128,256]{2,1,0:T(8,128)(2,1)S(1)}, bf16[3,128,256]{2,1,0:T(8,128)(2,1)S(1)}, u32[]{:S(2)}, u32[]{:S(2)}) collective-permute-start(bf16[3,128,256]{2,1,0:T(8,128)(2,1)S(1)} %get-tuple-element.14.refs_6_), channel_id=1, source_target_pairs={{0,2},{1,3},{2,0},{3,1},{4,6},{5,7},{6,4},{7,5},{8,10},{9,11},{10,... | collective-permute-start | bytes 589832 | tf_op jit(solution)/shard_map/ppermute | solution.py:27
  27.6 1.1 %fusion = (bf16[128,1024]{1,0:T(8,128)(2,1)S(1)}, bf16[128,1024]{1,0:T(8,128)(2,1)S(1)}) fusion(bf16[128,2048]{1,0:T(8,128)(2,1)} %param.13), kind=kLoop, calls=%fused_computation.9 | loop fusion | bytes 1048576 | tf_op jit(solution)/shard_map/slice | solution.py:214
  34.5 1.5 %collective-permute-start.17 = (bf16[256,512]{1,0:T(8,128)(2,1)}, bf16[256,512]{1,0:T(8,128)(2,1)S(1)}, u32[]{:S(2)}, u32[]{:S(2)}) collective-permute-start(bf16[256,512]{1,0:T(8,128)(2,1)} %slice.40), channel_id=1, source_target_pairs={{0,2},{1,3},{2,0},{3,1},{4,6},{5,7},{6,4},{7,5},{8,10},{9,11},{10,... | collective-permute-start | bytes 786440 | tf_op jit(solution)/shard_map/ppermute | solution.py:27
  36.0 1.5 %collective-permute-start.18 = (bf16[256,512]{1,0:T(8,128)(2,1)}, bf16[256,512]{1,0:T(8,128)(2,1)S(1)}, u32[]{:S(2)}, u32[]{:S(2)}) collective-permute-start(bf16[256,512]{1,0:T(8,128)(2,1)} %slice.41), channel_id=1, source_target_pairs={{0,1},{1,0},{2,3},{3,2},{4,5},{5,4},{6,7},{7,6},{8,9},{9,8},{10,11... | collective-permute-start | bytes 786440 | tf_op jit(solution)/shard_map/ppermute | solution.py:27
  38.3 5.5 %encode_rows_0.1 = (bf16[64,512]{1,0:T(8,128)(2,1)}, bf16[512,2048]{1,0:T(8,128)(2,1)S(1)}, bf16[512,512]{1,0:T(8,128)(2,1)S(1)}, bf16[512,1024]{1,0:T(8,128)(2,1)S(1)}, f32[32,1024]{1,0:T(8,128)S(1)}) custom-call(f32[3,32,128]{2,1,0:T(8,128)S(1)} %broadcast_in_dim.26.refs_0_, bf16[512,512]{1,0:T(8,128)(2,1)S(1)} %get-tuple-element.24.refs_1_, ...), custom_call_target="tpu_custom_call" | custom-call | flops 1610612736 | bytes 6291456 | tf_op jit(solution)/shard_map/encode_rows_0/pallas_call | solution.py:151
  43.8 1.4 %copy-done.3 = bf16[512,2048]{1,0:T(8,128)(2,1)} copy-done((bf16[512,2048]{1,0:T(8,128)(2,1)}, bf16[512,2048]{1,0:T(8,128)(2,1)S(1)}, u32[]{:S(2)}) %copy-start.3) | copy-done | bytes 2097176
  45.1 1.0 %copy-done.5 = bf16[512,1024]{1,0:T(8,128)(2,1)} copy-done((bf16[512,1024]{1,0:T(8,128)(2,1)}, bf16[512,1024]{1,0:T(8,128)(2,1)S(1)}, u32[]{:S(2)}) %copy-start.5) | copy-done | bytes 1048600
  46.1 3.5 %all-to-all-start = ((bf16[8,8,512]{2,1,0:T(8,128)(2,1)}), bf16[8,8,512]{2,1,0:T(8,128)(2,1)S(1)}, u32[]{:S(2)}, u32[]{:S(2)}) async-start(bf16[8,8,512]{2,1,0:T(8,128)(2,1)} %bitcast.5), calls=%async_computation | async-start | bytes 131072 | tf_op jit(solution)/shard_map/all_to_all | solution.py:324
  49.7 1.7 %collective-permute-start.19 = (bf16[1,512]{1,0:T(2,128)(2,1)S(1)}, bf16[1,512]{1,0:T(2,128)(2,1)S(1)}, u32[]{:S(2)}, u32[]{:S(2)}) collective-permute-start(bf16[1,512]{1,0:T(2,128)(2,1)S(1)} %copy-done.2), channel_id=1, source_target_pairs={{0,1},{1,0},{2,3},{3,2},{4,5},{5,4},{6,7},{7,6},{8,9},{9,8},{10,11... | collective-permute-start | bytes 3080 | tf_op jit(solution)/shard_map/ppermute | solution.py:27
  51.4 1.5 %collective-permute-start.20 = (bf16[1,512]{1,0:T(2,128)(2,1)S(1)}, bf16[1,512]{1,0:T(2,128)(2,1)S(1)}, u32[]{:S(2)}, u32[]{:S(2)}) collective-permute-start(bf16[1,512]{1,0:T(2,128)(2,1)S(1)} %copy-done.2), channel_id=1, source_target_pairs={{0,2},{1,3},{2,0},{3,1},{4,6},{5,7},{6,4},{7,5},{8,10},{9,11},{10,... | collective-permute-start | bytes 3080 | tf_op jit(solution)/shard_map/ppermute | solution.py:27
  53.5 1.5 %collective-permute-done.20.refs_7_ = bf16[1,512]{1,0:T(2,128)(2,1)S(1)} collective-permute-done((bf16[1,512]{1,0:T(2,128)(2,1)S(1)}, bf16[1,512]{1,0:T(2,128)(2,1)S(1)}, u32[]{:S(2)}, u32[]{:S(2)}) %collective-permute-start.20) | collective-permute-done | bytes 1056 | tf_op jit(solution)/shard_map/ppermute | solution.py:27
  55.0 2.4 %collective-permute-done.21.refs_8_ = bf16[1,512]{1,0:T(2,128)(2,1)S(1)} collective-permute-done((bf16[1,512]{1,0:T(2,128)(2,1)S(1)}, bf16[1,512]{1,0:T(2,128)(2,1)S(1)}, u32[]{:S(2)}, u32[]{:S(2)}) %collective-permute-start.21) | collective-permute-done | bytes 1056 | tf_op jit(solution)/shard_map/ppermute | solution.py:27
  57.4 3.5 %copy-done = bf16[2048,2048]{1,0:T(8,128)(2,1)S(1)} copy-done((bf16[2048,2048]{1,0:T(8,128)(2,1)S(1)}, bf16[2048,2048]{1,0:T(8,128)(2,1)}, u32[]{:S(2)}) %copy-start) | copy-done | bytes 8388632
  61.0 2.0 %up_half.1 = (f32[64,512]{1,0:T(8,128)S(1)}, f32[64,2176]{1,0:T(8,128)S(1)}, bf16[64,2176]{1,0:T(8,128)(2,1)S(1)}) custom-call(bf16[64,512]{1,0:T(8,128)(2,1)S(1)} %bitcast.18, bf16[512,512]{1,0:T(8,128)(2,1)S(1)} %copy-done.1, bf16[512,512]{1,0:T(8,128)(2,1)S(1)} %collective-permute-done.15.refs_1_, bf16[512,512]{1,0:T(8,128)(2,1)S(1)} %collective-permute-done.16.refs_2_, ...), custom_call_target="tpu_custom_call" | custom-call | flops 536870912 | bytes 8388608 | tf_op jit(solution)/shard_map/up_half/pallas_call | solution.py:328
  63.1 1.2 %copy-done.6 = bf16[512,1024]{1,0:T(8,128)(2,1)S(1)} copy-done((bf16[512,1024]{1,0:T(8,128)(2,1)S(1)}, bf16[512,1024]{1,0:T(8,128)(2,1)}, u32[]{:S(2)}) %copy-start.6) | copy-done | bytes 1048600
  64.3 5.4 %encode_rows_512.1._.x_ref = f32[32,512]{1,0:T(8,128)S(1)} custom-call(f32[3,32,128]{2,1,0:T(8,128)S(1)} %broadcast_in_dim.26.refs_0_, bf16[512,512]{1,0:T(8,128)(2,1)S(1)} %get-tuple-element.25.refs_1_, f32[8,512]{1,0:T(8,128)S(1)} %broadcast_in_dim.27.refs_2_, bf16[512,2048]{1,0:T(8,128)(2,1)S(1)} %copy-done.4, ...), custom_call_target="tpu_custom_call" | custom-call | flops 2147483648 | bytes 6291456 | tf_op jit(solution)/shard_map/encode_rows_512/pallas_call | solution.py:151
  69.8 2.5 %down_part.1._ = bf16[64,2048]{1,0:T(8,128)(2,1)} custom-call(f32[64,2176]{1,0:T(8,128)S(1)} %get-tuple-element.21.half_ref, bf16[64,2176]{1,0:T(8,128)(2,1)S(1)} %collective-permute-done.22.other_ref, f32[64,512]{1,0:T(8,128)S(1)} %get-tuple-element.23.local_ref, bf16[2048,2048]{1,0:T(8,128)(2,1)S(1)} %bitcast.16, f32[32,512]{1,0:T(8,128)S(1)} %encode_rows_512.1._.x_ref), custom_call_target="tpu_custom_call" | custom-call | flops 536870912 | bytes 8388608 | tf_op jit(solution)/shard_map/down_part/pallas_call | solution.py:347
  72.3 3.4 %all-to-all-start.1 = ((bf16[8,8,2048]{2,1,0:T(8,128)(2,1)}), bf16[8,8,2048]{2,1,0:T(8,128)(2,1)S(1)}, u32[]{:S(2)}, u32[]{:S(2)}) async-start(bf16[8,8,2048]{2,1,0:T(8,128)(2,1)} %bitcast.7), calls=%async_computation.1 | async-start | bytes 524288 | tf_op jit(solution)/shard_map/all_to_all | solution.py:360
  76.4 5.9 %all-to-all-done.1 = bf16[8,8,2048]{2,1,0:T(8,128)(2,1)S(1)} async-done(((bf16[8,8,2048]{2,1,0:T(8,128)(2,1)}), bf16[8,8,2048]{2,1,0:T(8,128)(2,1)S(1)}, u32[]{:S(2)}, u32[]{:S(2)}) %all-to-all-start.1) | async-done | bytes 262176 | tf_op jit(solution)/shard_map/all_to_all | solution.py:360
  (56 shorter events, 8.0 us)
Async XLA Ops:
  0.6 56.8 %copy-start.1 = (bf16[512,512]{1,0:T(8,128)(2,1)S(1)}, bf16[512,512]{1,0:T(8,128)(2,1)}, u32[]{:S(2)}) copy-start(bf16[512,512]{1,0:T(8,128)(2,1)} %refs_0_.1) | copy-start | bytes 1572868
  0.6 49.0 %copy-start.2 = (bf16[1,512]{1,0:T(2,128)(2,1)S(1)}, bf16[1,512]{1,0:T(2,128)(2,1)}, u32[]{:S(2)}) copy-start(bf16[1,512]{1,0:T(2,128)(2,1)} %refs_5_.1) | copy-start | bytes 3076
  1.6 9.8 %collective-permute-start = (bf16[128,512]{1,0:T(8,128)(2,1)S(1)}, bf16[128,512]{1,0:T(8,128)(2,1)S(1)}, u32[]{:S(2)}, u32[]{:S(2)}) collective-permute-start(bf16[128,512]{1,0:T(8,128)(2,1)S(1)} %constant_dynamic-slice_fusion.1), channel_id=1, source_target_pairs={{0,4},{4,0},{8,12},{12,8},{1,5},{5,1},{9,13},{13,9},{2,6},{6,2},{1... | collective-permute-start | bytes 393224 | tf_op jit(solution)/shard_map/ppermute | solution.py:27
  4.7 12.9 %collective-permute-start.1 = (bf16[128,512]{1,0:T(8,128)(2,1)S(1)}, bf16[128,512]{1,0:T(8,128)(2,1)S(1)}, u32[]{:S(2)}, u32[]{:S(2)}) collective-permute-start(bf16[128,512]{1,0:T(8,128)(2,1)S(1)} %constant_dynamic-slice_fusion.1), channel_id=1, source_target_pairs={{0,8},{4,12},{8,0},{12,4},{1,9},{5,13},{9,1},{13,5},{2,10},{6,14},... | collective-permute-start | bytes 393224 | tf_op jit(solution)/shard_map/ppermute | solution.py:27
  7.3 10.3 %collective-permute-start.2 = (bf16[128,512]{1,0:T(8,128)(2,1)S(1)}, bf16[128,512]{1,0:T(8,128)(2,1)S(1)}, u32[]{:S(2)}, u32[]{:S(2)}) collective-permute-start(bf16[128,512]{1,0:T(8,128)(2,1)S(1)} %constant_dynamic-slice_fusion.1), channel_id=1, source_target_pairs={{0,12},{4,8},{8,4},{12,0},{1,13},{5,9},{9,5},{13,1},{2,14},{6,10},... | collective-permute-start | bytes 393224 | tf_op jit(solution)/shard_map/ppermute | solution.py:27
  7.3 24.5 %collective-permute-start.15 = (bf16[512,512]{1,0:T(8,128)(2,1)}, bf16[512,512]{1,0:T(8,128)(2,1)S(1)}, u32[]{:S(2)}, u32[]{:S(2)}) collective-permute-start(bf16[512,512]{1,0:T(8,128)(2,1)} %refs_0_.1), channel_id=1, source_target_pairs={{0,1},{1,0},{2,3},{3,2},{4,5},{5,4},{6,7},{7,6},{8,9},{9,8},{10,11... | collective-permute-start | bytes 1572872 | tf_op jit(solution)/shard_map/ppermute | solution.py:27
  9.0 23.3 %collective-permute-start.16 = (bf16[512,512]{1,0:T(8,128)(2,1)}, bf16[512,512]{1,0:T(8,128)(2,1)S(1)}, u32[]{:S(2)}, u32[]{:S(2)}) collective-permute-start(bf16[512,512]{1,0:T(8,128)(2,1)} %refs_0_.1), channel_id=1, source_target_pairs={{0,2},{1,3},{2,0},{3,1},{4,6},{5,7},{6,4},{7,5},{8,10},{9,11},{10,... | collective-permute-start | bytes 1572872 | tf_op jit(solution)/shard_map/ppermute | solution.py:27
  17.7 5.8 %collective-permute-start.9 = (bf16[64,512]{1,0:T(8,128)(2,1)S(1)}, bf16[64,512]{1,0:T(8,128)(2,1)S(1)}, u32[]{:S(2)}, u32[]{:S(2)}) collective-permute-start(bf16[64,512]{1,0:T(8,128)(2,1)S(1)} %get-tuple-element.15), channel_id=1, source_target_pairs={{0,4},{4,0},{8,12},{12,8},{1,5},{5,1},{9,13},{13,9},{2,6},{6,2},{1... | collective-permute-start | bytes 196616 | tf_op jit(solution)/shard_map/ppermute | solution.py:27
  19.7 6.4 %collective-permute-start.10 = (bf16[64,512]{1,0:T(8,128)(2,1)S(1)}, bf16[64,512]{1,0:T(8,128)(2,1)S(1)}, u32[]{:S(2)}, u32[]{:S(2)}) collective-permute-start(bf16[64,512]{1,0:T(8,128)(2,1)S(1)} %get-tuple-element.15), channel_id=1, source_target_pairs={{0,8},{4,12},{8,0},{12,4},{1,9},{5,13},{9,1},{13,5},{2,10},{6,14},... | collective-permute-start | bytes 196616 | tf_op jit(solution)/shard_map/ppermute | solution.py:27
  20.8 6.8 %collective-permute-start.11 = (bf16[64,512]{1,0:T(8,128)(2,1)S(1)}, bf16[64,512]{1,0:T(8,128)(2,1)S(1)}, u32[]{:S(2)}, u32[]{:S(2)}) collective-permute-start(bf16[64,512]{1,0:T(8,128)(2,1)S(1)} %get-tuple-element.15), channel_id=1, source_target_pairs={{0,12},{4,8},{8,4},{12,0},{1,13},{5,9},{9,5},{13,1},{2,14},{6,10},... | collective-permute-start | bytes 196616 | tf_op jit(solution)/shard_map/ppermute | solution.py:27
  23.5 7.7 %collective-permute-start.3 = (bf16[3,128,256]{2,1,0:T(8,128)(2,1)S(1)}, bf16[3,128,256]{2,1,0:T(8,128)(2,1)S(1)}, u32[]{:S(2)}, u32[]{:S(2)}) collective-permute-start(bf16[3,128,256]{2,1,0:T(8,128)(2,1)S(1)} %get-tuple-element.13.refs_5_), channel_id=1, source_target_pairs={{0,1},{1,0},{2,3},{3,2},{4,5},{5,4},{6,7},{7,6},{8,9},{9,8},{10,11... | collective-permute-start | bytes 589832 | tf_op jit(solution)/shard_map/ppermute | solution.py:27
  26.1 5.7 %collective-permute-start.4 = (bf16[3,128,256]{2,1,0:T(8,128)(2,1)S(1)}, bf16[3,128,256]{2,1,0:T(8,128)(2,1)S(1)}, u32[]{:S(2)}, u32[]{:S(2)}) collective-permute-start(bf16[3,128,256]{2,1,0:T(8,128)(2,1)S(1)} %get-tuple-element.14.refs_6_), channel_id=1, source_target_pairs={{0,2},{1,3},{2,0},{3,1},{4,6},{5,7},{6,4},{7,5},{8,10},{9,11},{10,... | collective-permute-start | bytes 589832 | tf_op jit(solution)/shard_map/ppermute | solution.py:27
  27.6 1.7 %collective-permute-start.12 = (bf16[64,512]{1,0:T(8,128)(2,1)S(1)}, bf16[64,512]{1,0:T(8,128)(2,1)S(1)}, u32[]{:S(2)}, u32[]{:S(2)}) collective-permute-start(bf16[64,512]{1,0:T(8,128)(2,1)S(1)} %collective-permute-done.9.refs_15_), channel_id=1, source_target_pairs={{0,16},{16,0},{1,17},{17,1},{2,18},{18,2},{3,19},{19,3},{4,20},{20... | collective-permute-start | bytes 196616 | tf_op jit(solution)/shard_map/ppermute | solution.py:27
  29.4 1.5 %collective-permute-start.13 = (bf16[64,512]{1,0:T(8,128)(2,1)S(1)}, bf16[64,512]{1,0:T(8,128)(2,1)S(1)}, u32[]{:S(2)}, u32[]{:S(2)}) collective-permute-start(bf16[64,512]{1,0:T(8,128)(2,1)S(1)} %collective-permute-done.10.refs_16_), channel_id=1, source_target_pairs={{0,16},{16,0},{1,17},{17,1},{2,18},{18,2},{3,19},{19,3},{4,20},{20... | collective-permute-start | bytes 196616 | tf_op jit(solution)/shard_map/ppermute | solution.py:27
  30.8 5.2 %collective-permute-start.5 = (bf16[3,128,256]{2,1,0:T(8,128)(2,1)S(1)}, bf16[3,128,256]{2,1,0:T(8,128)(2,1)S(1)}, u32[]{:S(2)}, u32[]{:S(2)}) collective-permute-start(bf16[3,128,256]{2,1,0:T(8,128)(2,1)S(1)} %get-tuple-element.13.refs_5_), channel_id=1, source_target_pairs={{0,16},{16,0},{1,17},{17,1},{2,18},{18,2},{3,19},{19,3},{4,20},{20... | collective-permute-start | bytes 589832 | tf_op jit(solution)/shard_map/ppermute | solution.py:27
  31.2 6.3 %collective-permute-start.6 = (bf16[3,128,256]{2,1,0:T(8,128)(2,1)S(1)}, bf16[3,128,256]{2,1,0:T(8,128)(2,1)S(1)}, u32[]{:S(2)}, u32[]{:S(2)}) collective-permute-start(bf16[3,128,256]{2,1,0:T(8,128)(2,1)S(1)} %get-tuple-element.14.refs_6_), channel_id=1, source_target_pairs={{0,16},{16,0},{1,17},{17,1},{2,18},{18,2},{3,19},{19,3},{4,20},{20... | collective-permute-start | bytes 589832 | tf_op jit(solution)/shard_map/ppermute | solution.py:27
  31.8 2.7 %collective-permute-start.14 = (bf16[64,512]{1,0:T(8,128)(2,1)S(1)}, bf16[64,512]{1,0:T(8,128)(2,1)S(1)}, u32[]{:S(2)}, u32[]{:S(2)}) collective-permute-start(bf16[64,512]{1,0:T(8,128)(2,1)S(1)} %collective-permute-done.11.refs_17_), channel_id=1, source_target_pairs={{0,16},{16,0},{1,17},{17,1},{2,18},{18,2},{3,19},{19,3},{4,20},{20... | collective-permute-start | bytes 196616 | tf_op jit(solution)/shard_map/ppermute | solution.py:27
  31.8 5.7 %collective-permute-start.7 = (bf16[3,128,256]{2,1,0:T(8,128)(2,1)S(1)}, bf16[3,128,256]{2,1,0:T(8,128)(2,1)S(1)}, u32[]{:S(2)}, u32[]{:S(2)}) collective-permute-start(bf16[3,128,256]{2,1,0:T(8,128)(2,1)S(1)} %collective-permute-done.3.refs_7_), channel_id=1, source_target_pairs={{0,16},{16,0},{1,17},{17,1},{2,18},{18,2},{3,19},{19,3},{4,20},{20... | collective-permute-start | bytes 589832 | tf_op jit(solution)/shard_map/ppermute | solution.py:27
  32.3 5.2 %collective-permute-start.8 = (bf16[3,128,256]{2,1,0:T(8,128)(2,1)S(1)}, bf16[3,128,256]{2,1,0:T(8,128)(2,1)S(1)}, u32[]{:S(2)}, u32[]{:S(2)}) collective-permute-start(bf16[3,128,256]{2,1,0:T(8,128)(2,1)S(1)} %collective-permute-done.4.refs_8_), channel_id=1, source_target_pairs={{0,16},{16,0},{1,17},{17,1},{2,18},{18,2},{3,19},{19,3},{4,20},{20... | collective-permute-start | bytes 589832 | tf_op jit(solution)/shard_map/ppermute | solution.py:27
  34.5 22.9 %collective-permute-start.17 = (bf16[256,512]{1,0:T(8,128)(2,1)}, bf16[256,512]{1,0:T(8,128)(2,1)S(1)}, u32[]{:S(2)}, u32[]{:S(2)}) collective-permute-start(bf16[256,512]{1,0:T(8,128)(2,1)} %slice.40), channel_id=1, source_target_pairs={{0,2},{1,3},{2,0},{3,1},{4,6},{5,7},{6,4},{7,5},{8,10},{9,11},{10,... | collective-permute-start | bytes 786440 | tf_op jit(solution)/shard_map/ppermute | solution.py:27
  36.0 21.4 %collective-permute-start.18 = (bf16[256,512]{1,0:T(8,128)(2,1)}, bf16[256,512]{1,0:T(8,128)(2,1)S(1)}, u32[]{:S(2)}, u32[]{:S(2)}) collective-permute-start(bf16[256,512]{1,0:T(8,128)(2,1)} %slice.41), channel_id=1, source_target_pairs={{0,1},{1,0},{2,3},{3,2},{4,5},{5,4},{6,7},{7,6},{8,9},{9,8},{10,11... | collective-permute-start | bytes 786440 | tf_op jit(solution)/shard_map/ppermute | solution.py:27
  43.8 1.4 %copy-start.3 = (bf16[512,2048]{1,0:T(8,128)(2,1)}, bf16[512,2048]{1,0:T(8,128)(2,1)S(1)}, u32[]{:S(2)}) copy-start(bf16[512,2048]{1,0:T(8,128)(2,1)S(1)} %get-tuple-element.16.refs_3_) | copy-start | bytes 6291460
  46.1 11.2 %all-to-all-start = ((bf16[8,8,512]{2,1,0:T(8,128)(2,1)}), bf16[8,8,512]{2,1,0:T(8,128)(2,1)S(1)}, u32[]{:S(2)}, u32[]{:S(2)}) async-start(bf16[8,8,512]{2,1,0:T(8,128)(2,1)} %bitcast.5), calls=%async_computation | async-start | bytes 131072 | tf_op jit(solution)/shard_map/all_to_all | solution.py:324
  49.7 3.8 %collective-permute-start.19 = (bf16[1,512]{1,0:T(2,128)(2,1)S(1)}, bf16[1,512]{1,0:T(2,128)(2,1)S(1)}, u32[]{:S(2)}, u32[]{:S(2)}) collective-permute-start(bf16[1,512]{1,0:T(2,128)(2,1)S(1)} %copy-done.2), channel_id=1, source_target_pairs={{0,1},{1,0},{2,3},{3,2},{4,5},{5,4},{6,7},{7,6},{8,9},{9,8},{10,11... | collective-permute-start | bytes 3080 | tf_op jit(solution)/shard_map/ppermute | solution.py:27
  51.4 3.6 %collective-permute-start.20 = (bf16[1,512]{1,0:T(2,128)(2,1)S(1)}, bf16[1,512]{1,0:T(2,128)(2,1)S(1)}, u32[]{:S(2)}, u32[]{:S(2)}) collective-permute-start(bf16[1,512]{1,0:T(2,128)(2,1)S(1)} %copy-done.2), channel_id=1, source_target_pairs={{0,2},{1,3},{2,0},{3,1},{4,6},{5,7},{6,4},{7,5},{8,10},{9,11},{10,... | collective-permute-start | bytes 3080 | tf_op jit(solution)/shard_map/ppermute | solution.py:27
  52.9 4.5 %collective-permute-start.21 = (bf16[1,512]{1,0:T(2,128)(2,1)S(1)}, bf16[1,512]{1,0:T(2,128)(2,1)S(1)}, u32[]{:S(2)}, u32[]{:S(2)}) collective-permute-start(bf16[1,512]{1,0:T(2,128)(2,1)S(1)} %copy-done.2), channel_id=1, source_target_pairs={{0,3},{1,2},{2,1},{3,0},{4,7},{5,6},{6,5},{7,4},{8,11},{9,10},{10,... | collective-permute-start | bytes 3080 | tf_op jit(solution)/shard_map/ppermute | solution.py:27
  57.4 12.4 %slice-start = ((s8[8388608]{0:T(1024)(128)(4,1)}), s8[4194304]{0:T(1024)(128)(4,1)S(1)}, s32[]{:S(2)}) async-start(s8[8388608]{0:T(1024)(128)(4,1)} %bitcast.15), calls=%async_computation.2 | async-start | bytes 8388608
  57.4 3.5 %copy-start = (bf16[2048,2048]{1,0:T(8,128)(2,1)S(1)}, bf16[2048,2048]{1,0:T(8,128)(2,1)}, u32[]{:S(2)}) copy-start(bf16[2048,2048]{1,0:T(8,128)(2,1)} %refs_9_.1) | copy-start | bytes 25165828
  60.9 2.1 %copy-start.4 = (bf16[512,2048]{1,0:T(8,128)(2,1)S(1)}, bf16[512,2048]{1,0:T(8,128)(2,1)}, u32[]{:S(2)}) copy-start(bf16[512,2048]{1,0:T(8,128)(2,1)} %copy-done.3) | copy-start | bytes 6291460
  61.0 8.8 %slice-start.1 = ((s8[8388608]{0:T(1024)(128)(4,1)}), s8[4194304]{0:T(1024)(128)(4,1)S(1)}, s32[]{:S(2)}) async-start(s8[8388608]{0:T(1024)(128)(4,1)} %bitcast.15), calls=%async_computation.3 | async-start | bytes 8388608
  63.0 6.8 %collective-permute-start.22 = (bf16[64,2176]{1,0:T(8,128)(2,1)S(1)}, bf16[64,2176]{1,0:T(8,128)(2,1)S(1)}, u32[]{:S(2)}, u32[]{:S(2)}) collective-permute-start(bf16[64,2176]{1,0:T(8,128)(2,1)S(1)} %get-tuple-element.22), channel_id=1, source_target_pairs={{0,16},{16,0},{1,17},{17,1},{2,18},{18,2},{3,19},{19,3},{4,20},{20... | collective-permute-start | bytes 835592 | tf_op jit(solution)/shard_map/ppermute | solution.py:27
  72.3 9.9 %all-to-all-start.1 = ((bf16[8,8,2048]{2,1,0:T(8,128)(2,1)}), bf16[8,8,2048]{2,1,0:T(8,128)(2,1)S(1)}, u32[]{:S(2)}, u32[]{:S(2)}) async-start(bf16[8,8,2048]{2,1,0:T(8,128)(2,1)} %bitcast.7), calls=%async_computation.1 | async-start | bytes 524288 | tf_op jit(solution)/shard_map/all_to_all | solution.py:360
  (2 other events, 2.2 us)

commit v4 on v3

v4 whole, which is shorter than its diff:
```python
import functools

import jax
import jax.numpy as jnp
from jax import lax
from jax.experimental import pallas as pl
from jax.experimental.pallas import tpu as pltpu
from jax.sharding import PartitionSpec as P

HEADS = 4
DM = 4096
MICRO = 4
SESS_MAX = 64
EPSILON = 1e-06
F32 = jnp.float32
BF16 = jnp.bfloat16

VMEM = pl.BlockSpec(memory_space=pltpu.VMEM)


def swap(x, axis, size, flip):
    return lax.ppermute(x, axis, [(i, i ^ flip) for i in range(size)])


def silu_half(h):
    return h + h * jnp.tanh(h)


def in_order(ref, at, dps):
    if dps == 1:
        return ref[at, :]
    z = lax.axis_index("dp")
    cols = ref.shape[1] // dps
    return jnp.concatenate([ref[at, pl.ds(pl.multiple_of((z ^ k) * cols, cols), cols)] for k in range(dps)], axis=1)


def project(dps, row0, hist, ev_ref, w_ref, gate_ref, q_ref, kv_ref):
    rows, width = ev_ref.shape
    step = min(rows, 256)
    for r in range(0, rows, step):
        at = slice(r, r + step)
        x = in_order(ev_ref, at, dps)
        row_pos = lax.broadcasted_iota(jnp.int32, (step, 1), 0).astype(F32) + (row0 + r)

        def act(n):
            part = jnp.dot(x, w_ref[:, n * width : (n + 1) * width], preferred_element_type=F32)
            return silu_half(part * 0.5)

        gate_ref[at, :] = act(0).astype(gate_ref.dtype)
        kv_ref[at, :width] = jnp.where(row_pos < hist, act(1), 0.0).astype(BF16)
        q_ref[at, :] = act(2).astype(BF16)
        kv_ref[at, width:] = act(3).astype(BF16)


def attend(q_ref, kv_refs, gate_ref, gain_ref, att_ref):
    rows, width = q_ref.shape
    head = width // HEADS
    step = min(rows, 256)
    blocks = [(ref, r) for ref in kv_refs for r in range(0, ref.shape[0], step)]
    tri = lax.broadcasted_iota(jnp.int32, (step, step), 1) <= lax.broadcasted_iota(
        jnp.int32, (step, step), 0
    )
    before = len(blocks) - rows // step
    for i in range(rows // step):
        at = slice(i * step, (i + 1) * step)
        for h in range(HEADS):
            q = q_ref[at, h * head : (h + 1) * head]
            total = None
            for j in range(before + i + 1):
                ref, r = blocks[j]
                k = ref[r : r + step, width + h * head : width + (h + 1) * head]
                v = ref[r : r + step, h * head : (h + 1) * head]
                s = lax.dot_general(q, k, (((1,), (1,)), ((), ())), preferred_element_type=F32)
                wts = silu_half(s * (0.5 * head**-0.5))
                if j == before + i:
                    wts = jnp.where(tri, wts, 0.0)
                mixed = jnp.dot(wts.astype(BF16), v, preferred_element_type=F32)
                total = mixed if total is None else total + mixed
            att_ref[at, h * head : (h + 1) * head] = total
    att = att_ref[...]
    inv = lax.rsqrt(jnp.mean(att * att, axis=1, keepdims=True) + EPSILON)
    return (att * inv * gain_ref[:1] * gate_ref[...].astype(F32)).astype(BF16)


def membership(bounds_ref, row0, rows):
    starts, ends = bounds_ref[0, :, :1], bounds_ref[1, :, :1]
    pos = (lax.broadcasted_iota(jnp.int32, (starts.shape[0], rows), 1) + row0).astype(F32)
    return jnp.where((pos >= starts) & (pos < ends), 1.0, 0.0).astype(BF16)


def pool(dps, bounds_ref, sums_ev, sums_ref, wout_ref):
    n_valid = jnp.maximum(bounds_ref[1, :, :1] - bounds_ref[0, :, :1], 1.0)
    sess = sums_ev.shape[0]
    sums_g = in_order(sums_ref, slice(None), dps)
    hi = sums_g.astype(BF16)
    rest = sums_g - hi.astype(F32)
    mid = rest.astype(BF16)
    low = (rest - mid.astype(F32)).astype(BF16)
    terms = jnp.dot(jnp.concatenate([low, mid, hi], axis=0), wout_ref[...], preferred_element_type=F32)
    return (terms[:sess] + terms[sess : 2 * sess] + terms[2 * sess :] + sums_ev) / n_valid


def first_kernel(place, dps, copies_out, n_parts, bounds_ref, ev_ref, gain_ref, *refs):
    parts, refs = refs[:n_parts], refs[n_parts:]
    pooled_ref, w_ref, wout_ref, kv_ref, sums_ev_ref, sums_g_ref, q_ref, gate_ref, att_ref, sems = refs
    copies = place(parts, w_ref, wout_ref, sems)
    for c in copies:
        c.start()
    member = membership(bounds_ref, 0, ev_ref.shape[0])
    sums_ev = jnp.dot(member, ev_ref[...], preferred_element_type=F32)
    sums_ev_ref[...] = sums_ev
    for c in copies:
        c.wait()
    project(dps, 0, bounds_ref[2, :1, :1], ev_ref, w_ref, gate_ref, q_ref, kv_ref)
    gated = attend(q_ref, [kv_ref], gate_ref, gain_ref, att_ref)
    sums_g_ref[...] = jnp.dot(member, gated, preferred_element_type=F32)
    out = pool(dps, bounds_ref, sums_ev, sums_g_ref, wout_ref)
    peers, take = copies_out
    pooled_ref[...] = jnp.concatenate([out[:take]] * peers, axis=0).astype(BF16)


def project_kernel(dps, row0, bounds_ref, ev_ref, w_ref, sums_ev_ref, _, gate_ref, q_ref, kv_ref, out_ref):
    project(dps, row0, bounds_ref[2, :1, :1], ev_ref, w_ref, gate_ref, q_ref, kv_ref)
    member = membership(bounds_ref, row0, ev_ref.shape[0])
    out_ref[...] = sums_ev_ref[...] + jnp.dot(member, ev_ref[...], preferred_element_type=F32)


def attend_kernel(row0, bounds_ref, gain_ref, gate_ref, q_ref, kv_first, kv_ref, sums_ref, _, out_ref, att_ref):
    member = membership(bounds_ref, row0, q_ref.shape[0])
    gated = attend(q_ref, [kv_first, kv_ref], gate_ref, gain_ref, att_ref)
    out_ref[...] = sums_ref[...] + jnp.dot(member, gated, preferred_element_type=F32)


def call(kernel, name, operands, out_shape, scratch, mib, flops, size, transcendentals=0):
    return pl.pallas_call(
        kernel,
        in_specs=[VMEM] * len(operands),
        out_specs=[VMEM] * len(out_shape),
        out_shape=[jax.ShapeDtypeStruct(shape, kind) for shape, kind in out_shape],
        scratch_shapes=scratch,
        compiler_params=pltpu.CompilerParams(vmem_limit_bytes=mib * 1024 * 1024),
        cost_estimate=pl.CostEstimate(flops=flops, bytes_accessed=size, transcendentals=transcendentals),
        name=name,
    )(*operands)


def parity(m):
    return (m & 1) ^ ((m >> 1) & 1)


def split_kernel(*refs):
    *parts, left_ref, right_ref = refs
    half = left_ref.shape[2]
    for k, part in enumerate(parts):
        left_ref[k] = part[:, :half]
        right_ref[k] = part[:, half:]


def gather_weights(w_uvqk, w_out, w_in, ffn_gain, sections, dps, mps):
    depth, wide = w_uvqk.shape
    width = w_out.shape[1]
    w_in = jnp.concatenate([w_in, jnp.broadcast_to(ffn_gain, (16, w_in.shape[1]))], axis=0)
    if (sections, mps) != (2, 4) or wide != 4 * width or depth % 128:
        ws = [lax.all_gather(x, "dp", axis=0, tiled=True) for x in (w_uvqk, w_out)]
        blocks = [[w_in]] + [[swap(w_in, "mp", mps, k)] for k in range(1, mps)]

        def place_whole(parts, w_ref, wout_ref, sems):
            return [
                pltpu.make_async_copy(parts[0], w_ref, sems.at[0]),
                pltpu.make_async_copy(parts[1], wout_ref, sems.at[1]),
            ]

        return place_whole, ws, blocks, 1

    part = depth // 4
    cut = width // 2
    sec, m = lax.axis_index("section"), lax.axis_index("mp")
    share = sec * 2 + parity(m)
    mine = jnp.concatenate(
        [
            lax.dynamic_slice_in_dim(w_uvqk, share * width, width, 1),
            lax.dynamic_slice_in_dim(w_out, share * part, part, 0),
        ],
        axis=0,
    )
    got = [swap(mine, "dp", dps, k) for k in range(1, dps)]
    left, right = call(
        split_kernel,
        "split",
        got,
        [((len(got), depth + part, cut), BF16)] * 2,
        [],
        8,
        0,
        16 * 1024 * 1024,
    )
    plane = [left, right, swap(left, "mp", mps, 1), swap(right, "mp", mps, 2)]
    parts = [w_uvqk[:, : wide // 2], w_uvqk[:, wide // 2 :], w_out[: depth // 2], w_out[depth // 2 :]]
    parts = parts + plane + [swap(p, "section", sections, 1) for p in plane]

    from_x, from_y = swap(w_in, "mp", mps, 1), swap(w_in, "mp", mps, 2)
    middle = w_in.shape[0] // 32 * 16
    diagonal = [swap(from_x[:middle], "mp", mps, 2), swap(from_y[middle:], "mp", mps, 1)]

    def place(parts, w_ref, wout_ref, sems):
        sec, m = lax.axis_index("section"), lax.axis_index("mp")
        w_ref, wout_ref = w_ref.reshape(dps, depth, wide), wout_ref.reshape(dps, depth, width)
        copies = []

        def add(src, dst):
            copies.append(pltpu.make_async_copy(src, dst, sems.at[len(copies)]))

        for i in range(2):
            add(parts[i], w_ref.at[0, :, i * (wide // 2) : (i + 1) * (wide // 2)])
            add(parts[2 + i], wout_ref.at[0, i * (depth // 2) : (i + 1) * (depth // 2)])
        for i, ref in enumerate(parts[4:]):
            owner = (sec ^ (i // 4)) * 2 + (parity(m) ^ (i // 2 % 2))
            at = (i % 2) * cut
            cols = pl.ds(pl.multiple_of(owner * width + at, cut), cut)
            add(ref.at[:, :depth], w_ref.at[1:, :, cols])
            rows = pl.ds(pl.multiple_of(owner * part, part), part)
            add(ref.at[:, depth:], wout_ref.at[1:, rows, at : at + cut])
        return copies

    return place, parts, [[w_in], [from_x], [from_y], diagonal], dps


def two_terms(square):
    hi = square.astype(BF16).astype(F32)
    lane = lax.broadcasted_iota(jnp.int32, (square.shape[0], 128), 1)
    return jnp.where(lane == 0, hi, jnp.where(lane == 1, square - hi, 0.0)).astype(BF16)


def up_kernel(chunks, pieces, x_ref, *refs):
    w_in_refs, refs = refs[: sum(pieces)], refs[sum(pieces) :]
    w_ref, local_ref, half_ref, send_ref, normed_ref = refs
    m = lax.axis_index("mp")
    depth = x_ref.shape[1]
    x = x_ref[...]
    square = None
    at = 0
    for k, n in enumerate(pieces):
        block = jnp.concatenate([r[...] for r in w_in_refs[at : at + n]], axis=0)
        at += n
        hidden = jnp.dot(x, block[:depth], preferred_element_type=F32)
        part = jnp.sum(hidden * hidden, axis=1, keepdims=True)
        square = part if square is None else square + part
        gain = block[depth:].astype(F32)[:1]
        cols = hidden.shape[1]
        normed_ref[:, pl.ds(pl.multiple_of((m ^ k) * cols, cols), cols)] = (hidden * gain).astype(BF16)
        if k == 0:
            local_ref[...] = hidden
    normed = normed_ref[...]
    wide = w_ref.shape[1]
    each = wide // chunks
    for c in range(chunks):
        at = slice(c * each, (c + 1) * each)
        half = jnp.dot(normed, w_ref[:, at], preferred_element_type=F32)
        half_ref[:, at] = half
        send_ref[:, at] = half.astype(BF16)
    half_ref[:, wide:] = jnp.broadcast_to(square, (x.shape[0], 128))
    send_ref[:, wide:] = two_terms(square)


def down_kernel(chunks, half_ref, other_ref, local_ref, w_ref, _, out_ref, part_ref):
    units, wide = w_ref.shape
    each = wide // chunks
    square = half_ref[:, units : units + 1] + jnp.sum(other_ref[:, units:].astype(F32), axis=1, keepdims=True)
    inv = lax.rsqrt(square / DM + EPSILON)
    up = (half_ref[:, :units] + other_ref[:, :units].astype(F32)) * inv
    hidden = jax.nn.gelu(up, approximate=True).astype(BF16)
    for c in range(chunks):
        at = slice(c * each, (c + 1) * each)
        part_ref[:, at] = jnp.dot(hidden, w_ref[:, at], preferred_element_type=F32)
    m = lax.axis_index("mp")
    cols = local_ref.shape[1]
    own = pl.ds(pl.multiple_of(m * cols, cols), cols)
    part_ref[:, own] = part_ref[:, own] + local_ref[...]
    out_ref[...] = part_ref[...].astype(BF16)


def finish_kernel(sections, mps, dps, got_ref, bounds_ref, sums_ev_ref, sums_g_ref, wout_ref, out_ref, pooled_ref):
    pooled_ref[...] = pool(dps, bounds_ref, sums_ev_ref[...], sums_g_ref, wout_ref).astype(BF16)
    got = got_ref[...].astype(F32)
    take, wide = out_ref.shape[0], got.shape[1]
    for s in range(sections):
        total = got[s * mps * take : (s * mps + 1) * take]
        for k in range(s * mps + 1, (s + 1) * mps):
            total = total + got[k * take : (k + 1) * take]
        out_ref[:, s * wide : (s + 1) * wide] = total.astype(BF16)


def per_device(sections, dps, mps, events, hist_len, sess_len, w_uvqk, w_out, attn_gain, w_in, ffn_gain, w_up, w_down):
    events = events[0]
    length, width = events.shape
    sess = sess_len.shape[1]
    take = sess // MICRO
    peers = sections * mps
    rows = take * peers
    cols = w_in.shape[1]
    units = w_up.shape[1]
    half_width = w_down.shape[1]
    group = ("section", "mp")
    first = take * SESS_MAX
    rest = length - first

    gain = jnp.broadcast_to(attn_gain, (8, width))
    ends = jnp.sum(jnp.where(jnp.tri(sess, dtype=jnp.bool_), sess_len, 0), axis=1)
    bounds = jnp.stack([ends - sess_len[0], jnp.minimum(ends, hist_len), jnp.broadcast_to(hist_len, ends.shape)])
    bounds = jnp.broadcast_to(bounds.astype(F32)[:, :, None], (3, sess, 128))
    place, parts, w_in_blocks, dps = gather_weights(w_uvqk, w_out, w_in, ffn_gain, sections, dps, mps)

    micro_rows, full_w, full_wout, kv_first, sums_ev, sums_g = call(
        functools.partial(first_kernel, place, dps, (peers, take), len(parts)),
        "encode_first",
        [bounds, events[:first], gain, *parts],
        [
            ((rows, width), BF16),
            ((width, 4 * width), BF16),
            ((width, width), BF16),
            ((first, 2 * width), BF16),
            ((sess, width), F32),
            ((sess, width), F32),
        ],
        [
            pltpu.VMEM((first, width), BF16),
            pltpu.VMEM((first, width), F32),
            pltpu.VMEM((first, width), F32),
            pltpu.SemaphoreType.DMA((32,)),
        ],
        16,
        8 * first * width * width + 2 * first * first * width,
        6 * 1024 * 1024,
        4 * first * width + HEADS * first * first,
    )
    arrived = lax.all_to_all(
        micro_rows.reshape(peers, take, width), group, split_axis=0, concat_axis=0, tiled=True
    ).reshape(rows, width)
    blocks = [piece for block in w_in_blocks for piece in block]
    local, half, half_send = call(
        functools.partial(up_kernel, 4, [len(block) for block in w_in_blocks]),
        "up_half",
        [arrived, *blocks, w_up],
        [((rows, cols), F32), ((rows, units + 128), F32), ((rows, units + 128), BF16)],
        [pltpu.VMEM((rows, w_up.shape[0]), BF16)],
        10,
        2 * rows * w_up.size,
        2 * w_up.size,
    )
    other = swap(half_send, "section", sections, 1)
    gate, queries, kv_rest, sums_ev = call(
        functools.partial(project_kernel, dps, first),
        "project_rest",
        [bounds, events[first:], full_w, sums_ev, local],
        [((rest, width), BF16), ((rest, width), BF16), ((rest, 2 * width), BF16), ((sess, width), F32)],
        [],
        10,
        8 * rest * width * width,
        6 * 1024 * 1024,
        4 * rest * width,
    )
    (partial,) = call(
        functools.partial(down_kernel, 4),
        "down_part",
        [half, other, local, w_down, sums_ev],
        [((rows, half_width), BF16)],
        [pltpu.VMEM((rows, half_width), F32)],
        8,
        2 * rows * w_down.size,
        2 * w_down.size,
        rows * units,
    )
    arrived = lax.all_to_all(
        partial.reshape(peers, take, half_width), group, split_axis=0, concat_axis=0, tiled=True
    ).reshape(rows, half_width)
    (sums_g,) = call(
        functools.partial(attend_kernel, first),
        "attend_rest",
        [bounds, gain, gate, queries, kv_first, kv_rest, sums_g, partial],
        [((sess, width), F32)],
        [pltpu.VMEM((rest, width), F32)],
        10,
        4 * rest * length * width,
        6 * 1024 * 1024,
        HEADS * rest * length,
    )
    cross_out, pooled = call(
        functools.partial(finish_kernel, sections, mps, dps),
        "finish",
        [arrived, bounds, sums_ev, sums_g, full_wout],
        [((take, half_width * sections), BF16), ((sess, width), BF16)],
        [],
        8,
        6 * sess * width * width,
        2 * 1024 * 1024,
    )
    return (pooled, cross_out)


def solution(mesh):
    sizes = [mesh.shape[name] for name in ("section", "dp", "mp")]
    return jax.shard_map(
        functools.partial(per_device, *sizes),
        mesh=mesh,
        in_specs=(
            P(("section", "dp", "mp"), None, None),
            P(("section", "dp", "mp")),
            P(("section", "dp", "mp"), None),
            P("dp", None),
            P("dp", None),
            P(),
            P(None, ("section", "mp")),
            P(None, ("section", "mp")),
            P("section", "mp"),
            P("mp", "section"),
        ),
        out_specs=(P(("section", "dp", "mp"), None), P(("section", "dp", "mp"), None)),
        check_vma=False,
    )
```

time: 83.4 us -> 63 us (0.76)
  starting transfers between devices: 31.7 us -> 18.6 us
  local copies, waits for them, and re-layouts: 13.6 us -> 4.16 us
  blocking collectives: 0 us -> 7.52 us
  waiting for transfers between devices: 17.9 us -> 12.6 us
    ppermute x23 -> x14, starting transfers between devices: 24.8 us -> 15 us  [swap(): return lax.ppermute(x, axis, [(i, i ^ flip) for i in range(size)])]
    all_to_all x0 -> x1, blocking collectives: none -> 7.52 us  [per_device(): lax.all_to_all(micro_rows.reshape(peers, take, width), group, split_axis=...]
    all_to_all x2 -> x1, waiting for transfers between devices: 5.88 us -> 0.01 us  [per_device(): lax.all_to_all(partial.reshape(peers, take, half_width), group, split_axi...]
    unnamed x18 -> x24, local copies, waits for them, and re-layouts: 7.13 us -> 2.13 us
    slice x4, local copies, waits for them, and re-layouts: 3.63 us -> 0.11 us  [the longest x1 0.07 us: per_device(): events[first:]]
    all_to_all x2 -> x1, starting transfers between devices: 6.94 us -> 3.59 us  [per_device(): lax.all_to_all(partial.reshape(peers, take, half_width), group, split_axi...]
    concatenate x0 -> x2, other arithmetic: none -> 1.13 us  [the longest x1 1.11 us: gather_weights(): jnp.concatenate([w_in, jnp.broadcast_to(ffn_gain, (16, w_in.shape[1]))],...]
    slice x1, local copies, waits for them, and re-layouts: 1.06 us -> 0.04 us  [gather_weights(): w_uvqk[:, wide // 2:]]
  transfers between devices with their start and end apart: 25 -> 15, of which waited for: 8 -> 2; matrix products, arithmetic and copies ran while one was open for 8% -> 3% of each run, Pallas kernels for 14% -> 17%
where the time goes in v4:
time: 63 us; the launch traced here: 62.5 us
  starting transfers between devices  18.6 us (30%)
  Pallas kernels  16.1 us (26%)
  waiting for transfers between devices  12.6 us (20%)
  blocking collectives  7.52 us (12%)
  local copies, waits for them, and re-layouts  4.16 us (7%)
  other arithmetic  1.96 us (3%)
  between operations  1.59 us (3%)
    pallas_call x7, Pallas kernels, call(): pl.pallas_call(kernel, in_specs=[VMEM] * len(operands), out_specs=[VMEM]...  16.1 us
    ppermute x14, starting transfers between devices, swap(): return lax.ppermute(x, axis, [(i, i ^ flip) for i in range(size)])  15 us
    ppermute x14, waiting for transfers between devices, swap(): return lax.ppermute(x, axis, [(i, i ^ flip) for i in range(size)])  12.6 us
    all_to_all x1, blocking collectives, per_device(): lax.all_to_all(micro_rows.reshape(peers, take, width), group, split_axis=...  7.52 us
    all_to_all x1, starting transfers between devices, per_device(): lax.all_to_all(partial.reshape(peers, take, half_width), group, split_axi...  3.59 us
    unnamed x24, local copies, waits for them, and re-layouts  2.13 us
  transfers between devices with their start and end apart: 15, of which 2 were waited for; matrix products, arithmetic and copies ran while one was open for 3% of the time, Pallas kernels for 17%

profile of v4, /device:TPU:0, one launch (start us, length us, event | category | flops | bytes accessed | tf_op | source)
XLA Modules:
  0.0 62.5 jit_solution(15482564253943588244)
XLA Ops:
  0.7 1.0 %constant_dynamic-slice_fusion.1 = bf16[128,512]{1,0:T(8,128)(2,1)S(1)} fusion(bf16[128,2048]{1,0:T(8,128)(2,1)} %param.13, s32[]{:T(128)S(6)} %select_n.11), kind=kLoop, calls=%fused_computation.10 | loop fusion | bytes 262148 | tf_op jit(solution)/shard_map/dynamic_slice | solution.py:181
  1.7 0.8 %constant_dynamic-slice_fusion = bf16[32,512]{1,0:T(8,128)(2,1)S(1)} fusion(bf16[128,512]{1,0:T(8,128)(2,1)} %param.14, s32[]{:T(128)S(6)} %select_n.12), kind=kLoop, calls=%fused_computation.9 | loop fusion | bytes 65540 | tf_op jit(solution)/shard_map/dynamic_slice | solution.py:182
  2.5 3.1 %collective-permute-start = (bf16[160,512]{1,0:T(8,128)(2,1)S(1)}, bf16[160,512]{1,0:T(8,128)(2,1)S(1)}, u32[]{:S(2)}, u32[]{:S(2)}) collective-permute-start(bf16[160,512]{1,0:T(8,128)(2,1)S(1)} %pad_maximum_fusion.1), channel_id=1, source_target_pairs={{0,4},{4,0},{8,12},{12,8},{1,5},{5,1},{9,13},{13,9},{2,6},{6,2},{1... | collective-permute-start | bytes 491528 | tf_op jit(solution)/shard_map/ppermute | solution.py:22
  5.6 2.6 %collective-permute-start.1 = (bf16[160,512]{1,0:T(8,128)(2,1)S(1)}, bf16[160,512]{1,0:T(8,128)(2,1)S(1)}, u32[]{:S(2)}, u32[]{:S(2)}) collective-permute-start(bf16[160,512]{1,0:T(8,128)(2,1)S(1)} %pad_maximum_fusion.1), channel_id=1, source_target_pairs={{0,8},{4,12},{8,0},{12,4},{1,9},{5,13},{9,1},{13,5},{2,10},{6,14},... | collective-permute-start | bytes 491528 | tf_op jit(solution)/shard_map/ppermute | solution.py:22
  8.2 0.7 %reduce = bf16[512]{0:T(512)(128)(2,1)S(1)} reduce(bf16[1,512]{1,0:T(2,128)(2,1)} %param.17, bf16[]{:T(256)} %constant.27), dimensions={0}, to_apply=%param.17.reduce_sub_computation | reduce | bytes 2050 | tf_op args[7]
  8.9 1.1 %pad_maximum_fusion.refs_0_ = bf16[528,512]{1,0:T(8,128)(2,1)S(1)} fusion(bf16[16,512]{1,0:T(8,128)(2,1)S(1)} %broadcast_in_dim.36, bf16[512,512]{1,0:T(8,128)(2,1)} %param.16), kind=kLoop, calls=%fused_computation | loop fusion | flops 1081344 | bytes 1081344 | tf_op jit(solution)/shard_map/concatenate | solution.py:162
  10.0 1.8 %collective-permute-start.10 = (bf16[528,512]{1,0:T(8,128)(2,1)S(1)}, bf16[528,512]{1,0:T(8,128)(2,1)S(1)}, u32[]{:S(2)}, u32[]{:S(2)}) collective-permute-start(bf16[528,512]{1,0:T(8,128)(2,1)S(1)} %pad_maximum_fusion.refs_0_), channel_id=1, source_target_pairs={{0,2},{1,3},{2,0},{3,1},{4,6},{5,7},{6,4},{7,5},{8,10},{9,11},{10,... | collective-permute-start | bytes 1622024 | tf_op jit(solution)/shard_map/ppermute | solution.py:22
  11.8 1.5 %collective-permute-start.9 = (bf16[528,512]{1,0:T(8,128)(2,1)S(1)}, bf16[528,512]{1,0:T(8,128)(2,1)S(1)}, u32[]{:S(2)}, u32[]{:S(2)}) collective-permute-start(bf16[528,512]{1,0:T(8,128)(2,1)S(1)} %pad_maximum_fusion.refs_0_), channel_id=1, source_target_pairs={{0,1},{1,0},{2,3},{3,2},{4,5},{5,4},{6,7},{7,6},{8,9},{9,8},{10,11... | collective-permute-start | bytes 1622024 | tf_op jit(solution)/shard_map/ppermute | solution.py:22
  13.3 0.1 slice_bitcast_fusion
  13.5 7.2 %collective-permute-done.1.refs_1_ = bf16[160,512]{1,0:T(8,128)(2,1)S(1)} collective-permute-done((bf16[160,512]{1,0:T(8,128)(2,1)S(1)}, bf16[160,512]{1,0:T(8,128)(2,1)S(1)}, u32[]{:S(2)}, u32[]{:S(2)}) %collective-permute-start.1) | collective-permute-done | bytes 163872 | tf_op jit(solution)/shard_map/ppermute | solution.py:22
  20.7 1.6 %collective-permute-start.3 = (bf16[3,160,256]{2,1,0:T(8,128)(2,1)S(1)}, bf16[3,160,256]{2,1,0:T(8,128)(2,1)S(1)}, u32[]{:S(2)}, u32[]{:S(2)}) collective-permute-start(bf16[3,160,256]{2,1,0:T(8,128)(2,1)S(1)} %get-tuple-element.19.refs_4_), channel_id=1, source_target_pairs={{0,1},{1,0},{2,3},{3,2},{4,5},{5,4},{6,7},{7,6},{8,9},{9,8},{10,11... | collective-permute-start | bytes 737288 | tf_op jit(solution)/shard_map/ppermute | solution.py:22
  22.2 1.5 %collective-permute-start.4 = (bf16[3,160,256]{2,1,0:T(8,128)(2,1)S(1)}, bf16[3,160,256]{2,1,0:T(8,128)(2,1)S(1)}, u32[]{:S(2)}, u32[]{:S(2)}) collective-permute-start(bf16[3,160,256]{2,1,0:T(8,128)(2,1)S(1)} %get-tuple-element.20.refs_5_), channel_id=1, source_target_pairs={{0,2},{1,3},{2,0},{3,1},{4,6},{5,7},{6,4},{7,5},{8,10},{9,11},{10,... | collective-permute-start | bytes 737288 | tf_op jit(solution)/shard_map/ppermute | solution.py:22
  23.8 0.1 collective-permute-start.5
  23.8 0.1 select_reduce_fusion
  24.6 5.4 %collective-permute-done.3.refs_6_ = bf16[3,160,256]{2,1,0:T(8,128)(2,1)S(1)} collective-permute-done((bf16[3,160,256]{2,1,0:T(8,128)(2,1)S(1)}, bf16[3,160,256]{2,1,0:T(8,128)(2,1)S(1)}, u32[]{:S(2)}, u32[]{:S(2)}) %collective-permute-start.3) | collective-permute-done | bytes 245792 | tf_op jit(solution)/shard_map/ppermute | solution.py:22
  30.1 0.5 collective-permute-start.7
  30.6 0.1 collective-permute-start.8
  30.7 1.6 %collective-permute-start.12 = (bf16[272,512]{1,0:T(8,128)(2,1)S(1)}, bf16[272,512]{1,0:T(8,128)(2,1)S(1)}, u32[]{:S(2)}, u32[]{:S(2)}) collective-permute-start(bf16[272,512]{1,0:T(8,128)(2,1)S(1)} %slice.41), channel_id=1, source_target_pairs={{0,1},{1,0},{2,3},{3,2},{4,5},{5,4},{6,7},{7,6},{8,9},{9,8},{10,11... | collective-permute-start | bytes 835592 | tf_op jit(solution)/shard_map/ppermute | solution.py:22
  32.3 0.6 collective-permute-start.11
  32.9 0.1 broadcast_in_dim.33.bounds_ref
  33.0 0.0 slice-start
  33.0 4.2 %encode_first.1 = (bf16[64,512]{1,0:T(8,128)(2,1)S(1)}, bf16[512,2048]{1,0:T(8,128)(2,1)S(1)}, bf16[512,512]{1,0:T(8,128)(2,1)S(1)}, bf16[512,1024]{1,0:T(8,128)...) custom-call(f32[3,32,128]{2,1,0:T(8,128)S(1)} %broadcast_in_dim.33.bounds_ref, ...), custom_call_target="tpu_custom_call" | custom-call | flops 1342177280 | bytes 6291456 | tf_op jit(solution)/shard_map/encode_first/pallas_call | solution.py:135
  37.2 7.5 %all_to_all.10 = bf16[8,8,512]{2,1,0:T(8,128)(2,1)S(1)} all-to-all(bf16[8,8,512]{2,1,0:T(8,128)(2,1)S(1)} %bitcast.19), channel_id=1, replica_groups=mesh['section'=2,'dp'=4,'mp'=4] {'section','mp'}, dimensions={0} | all-to-all | bytes 131072 | tf_op jit(solution)/shard_map/all_to_all | solution.py:336
  44.7 2.0 %up_half.1 = (f32[64,512]{1,0:T(8,128)S(1)}, f32[64,2176]{1,0:T(8,128)S(1)}, bf16[64,2176]{1,0:T(8,128)(2,1)S(1)}) custom-call(bf16[64,512]{1,0:T(8,128)(2,1)S(1)} %bitcast.18, bf16[528,512]{1,0:T(8,128)(2,1)S(1)} %pad_maximum_fusion.refs_0_, bf16[528,512]{1,0:T(8,128)(2,1)S(1)} %collective-permute-done.9.refs_1_, ...), custom_call_target="tpu_custom_call" | custom-call | flops 536870912 | bytes 8388608 | tf_op jit(solution)/shard_map/up_half/pallas_call | solution.py:135
  46.7 0.2 collective-permute-start.13
  46.9 1.6 %project_rest.1 = (bf16[512,512]{1,0:T(8,128)(2,1)S(1)}, bf16[512,512]{1,0:T(8,128)(2,1)S(1)}, bf16[512,1024]{1,0:T(8,128)(2,1)S(1)}, f32[32,512]{1,0:T(8,128)S(1)}) custom-call(f32[3,32,128]{2,1,0:T(8,128)S(1)} %broadcast_in_dim.33.bounds_ref, bf16[512,512]{1,0:T(8,128)(2,1)S(1)} %get-tuple-element.36.ev_ref, ...), custom_call_target="tpu_custom_call" | custom-call | flops 1073741824 | bytes 6291456 | tf_op jit(solution)/shard_map/project_rest/pallas_call | solution.py:135
  48.5 2.5 %down_part.1._ = bf16[64,2048]{1,0:T(8,128)(2,1)} custom-call(f32[64,2176]{1,0:T(8,128)S(1)} %get-tuple-element.22.half_ref, bf16[64,2176]{1,0:T(8,128)(2,1)S(1)} %collective-permute-done.13.other_ref, f32[64,512]{1,0:T(8,128)S(1)} %get-tuple-element.24._.local_ref, bf16[2048,2048]{1,0:T(8,128)(2,1)S(1)} %bitcast.16, ...), custom_call_target="tpu_custom_call" | custom-call | flops 536870912 | bytes 8388608 | tf_op jit(solution)/shard_map/down_part/pallas_call | solution.py:135
  51.1 3.6 %all-to-all-start.1 = ((bf16[8,8,2048]{2,1,0:T(8,128)(2,1)}), bf16[8,8,2048]{2,1,0:T(8,128)(2,1)S(1)}, u32[]{:S(2)}, u32[]{:S(2)}) async-start(bf16[8,8,2048]{2,1,0:T(8,128)(2,1)} %bitcast.7), calls=%async_computation.1 | async-start | bytes 524288 | tf_op jit(solution)/shard_map/all_to_all | solution.py:373
  54.7 1.0 %copy-done.2 = bf16[512,512]{1,0:T(8,128)(2,1)S(1)} copy-done((bf16[512,512]{1,0:T(8,128)(2,1)S(1)}, bf16[512,512]{1,0:T(8,128)(2,1)}, u32[]{:S(2)}) %copy-start.2) | copy-done | bytes 524312
  55.7 1.0 %copy-done.4 = bf16[512,512]{1,0:T(8,128)(2,1)S(1)} copy-done((bf16[512,512]{1,0:T(8,128)(2,1)S(1)}, bf16[512,512]{1,0:T(8,128)(2,1)}, u32[]{:S(2)}) %copy-start.4) | copy-done | bytes 524312
  56.8 4.9 %attend_rest.1.sums_g_ref = f32[32,512]{1,0:T(8,128)S(1)} custom-call(f32[3,32,128]{2,1,0:T(8,128)S(1)} %broadcast_in_dim.33.bounds_ref, f32[8,512]{1,0:T(8,128)S(1)} %broadcast_in_dim.34.gain_ref, bf16[512,512]{1,0:T(8,128)(2,1)S(1)} %copy-done.2, bf16[512,512]{1,0:T(8,128)(2,1)S(1)} %copy-done.4, bf16[512,1024]{1,0:T(8,128)(2,1)S(1)} %get-tuple-element.30.kv_first, ...), custom_call_target="tpu_custom_call" | custom-call | flops 1073741824 | bytes 6291456 | tf_op jit(solution)/shard_map/attend_rest/pallas_call | solution.py:135
  61.7 0.8 %finish.1 = (bf16[8,4096]{1,0:T(8,128)(2,1)}, bf16[32,512]{1,0:T(8,128)(2,1)}) custom-call(bf16[64,2048]{1,0:T(8,128)(2,1)S(1)} %bitcast.17, f32[3,32,128]{2,1,0:T(8,128)S(1)} %broadcast_in_dim.33.bounds_ref, f32[32,512]{1,0:T(8,128)S(1)} %get-tuple-element.27._.sums_ev_ref, f32[32,512]{1,0:T(8,128)S(1)} %attend_rest.1.sums_g_ref, ...), custom_call_target="tpu_custom_call" | custom-call | flops 50331648 | bytes 2097152 | tf_op jit(solution)/shard_map/finish/pallas_call | solution.py:135
  (48 shorter events, 0.2 us)
Async XLA Ops:
  0.6 12.8 %copy-start.6 = (bf16[128,2048]{1,0:T(8,128)(2,1)S(1)}, bf16[128,2048]{1,0:T(8,128)(2,1)}, u32[]{:S(2)}) copy-start(bf16[128,2048]{1,0:T(8,128)(2,1)} %param.13) | copy-start | bytes 1572868
  0.6 12.7 %copy-start.5 = (bf16[1,1024,512]{2,1,0:T(8,128)(2,1)S(1)}, bf16[1,1024,512]{2,1,0:T(8,128)(2,1)}, u32[]{:S(2)}) copy-start(bf16[1,1024,512]{2,1,0:T(8,128)(2,1)} %param.10) | copy-start | bytes 3145732
  2.5 11.0 %collective-permute-start = (bf16[160,512]{1,0:T(8,128)(2,1)S(1)}, bf16[160,512]{1,0:T(8,128)(2,1)S(1)}, u32[]{:S(2)}, u32[]{:S(2)}) collective-permute-start(bf16[160,512]{1,0:T(8,128)(2,1)S(1)} %pad_maximum_fusion.1), channel_id=1, source_target_pairs={{0,4},{4,0},{8,12},{12,8},{1,5},{5,1},{9,13},{13,9},{2,6},{6,2},{1... | collective-permute-start | bytes 491528 | tf_op jit(solution)/shard_map/ppermute | solution.py:22
  5.6 15.0 %collective-permute-start.1 = (bf16[160,512]{1,0:T(8,128)(2,1)S(1)}, bf16[160,512]{1,0:T(8,128)(2,1)S(1)}, u32[]{:S(2)}, u32[]{:S(2)}) collective-permute-start(bf16[160,512]{1,0:T(8,128)(2,1)S(1)} %pad_maximum_fusion.1), channel_id=1, source_target_pairs={{0,8},{4,12},{8,0},{12,4},{1,9},{5,13},{9,1},{13,5},{2,10},{6,14},... | collective-permute-start | bytes 491528 | tf_op jit(solution)/shard_map/ppermute | solution.py:22
  8.2 12.5 %collective-permute-start.2 = (bf16[160,512]{1,0:T(8,128)(2,1)S(1)}, bf16[160,512]{1,0:T(8,128)(2,1)S(1)}, u32[]{:S(2)}, u32[]{:S(2)}) collective-permute-start(bf16[160,512]{1,0:T(8,128)(2,1)S(1)} %pad_maximum_fusion.1), channel_id=1, source_target_pairs={{0,12},{4,8},{8,4},{12,0},{1,13},{5,9},{9,5},{13,1},{2,14},{6,10},... | collective-permute-start | bytes 491528 | tf_op jit(solution)/shard_map/ppermute | solution.py:22
  8.9 14.9 %copy-start.7 = (bf16[128,512]{1,0:T(8,128)(2,1)S(1)}, bf16[128,512]{1,0:T(8,128)(2,1)}, u32[]{:S(2)}) copy-start(bf16[128,512]{1,0:T(8,128)(2,1)} %param.14) | copy-start | bytes 393220
  10.0 13.8 %copy-start.9 = (s32[1,32]{1,0:T(1,128)S(1)}, s32[1,32]{1,0:T(1,128)}, u32[]{:S(2)}) copy-start(s32[1,32]{1,0:T(1,128)} %param.12) | copy-start | bytes 388
  10.0 22.9 %copy-start.8 = (f32[512]{0:T(512)S(1)}, f32[512]{0:T(512)}, u32[]{:S(2)}) copy-start(f32[512]{0:T(512)} %param.15) | copy-start | bytes 6148
  10.0 20.5 %collective-permute-start.10 = (bf16[528,512]{1,0:T(8,128)(2,1)S(1)}, bf16[528,512]{1,0:T(8,128)(2,1)S(1)}, u32[]{:S(2)}, u32[]{:S(2)}) collective-permute-start(bf16[528,512]{1,0:T(8,128)(2,1)S(1)} %pad_maximum_fusion.refs_0_), channel_id=1, source_target_pairs={{0,2},{1,3},{2,0},{3,1},{4,6},{5,7},{6,4},{7,5},{8,10},{9,11},{10,... | collective-permute-start | bytes 1622024 | tf_op jit(solution)/shard_map/ppermute | solution.py:22
  11.8 18.8 %collective-permute-start.9 = (bf16[528,512]{1,0:T(8,128)(2,1)S(1)}, bf16[528,512]{1,0:T(8,128)(2,1)S(1)}, u32[]{:S(2)}, u32[]{:S(2)}) collective-permute-start(bf16[528,512]{1,0:T(8,128)(2,1)S(1)} %pad_maximum_fusion.refs_0_), channel_id=1, source_target_pairs={{0,1},{1,0},{2,3},{3,2},{4,5},{5,4},{6,7},{7,6},{8,9},{9,8},{10,11... | collective-permute-start | bytes 1622024 | tf_op jit(solution)/shard_map/ppermute | solution.py:22
  13.3 31.4 %copy-start = (bf16[2048,2048]{1,0:T(8,128)(2,1)S(1)}, bf16[2048,2048]{1,0:T(8,128)(2,1)}, u32[]{:S(2)}) copy-start(bf16[2048,2048]{1,0:T(8,128)(2,1)} %refs_5_.1) | copy-start | bytes 25165828
  20.7 9.4 %collective-permute-start.3 = (bf16[3,160,256]{2,1,0:T(8,128)(2,1)S(1)}, bf16[3,160,256]{2,1,0:T(8,128)(2,1)S(1)}, u32[]{:S(2)}, u32[]{:S(2)}) collective-permute-start(bf16[3,160,256]{2,1,0:T(8,128)(2,1)S(1)} %get-tuple-element.19.refs_4_), channel_id=1, source_target_pairs={{0,1},{1,0},{2,3},{3,2},{4,5},{5,4},{6,7},{7,6},{8,9},{9,8},{10,11... | collective-permute-start | bytes 737288 | tf_op jit(solution)/shard_map/ppermute | solution.py:22
  22.2 7.8 %collective-permute-start.4 = (bf16[3,160,256]{2,1,0:T(8,128)(2,1)S(1)}, bf16[3,160,256]{2,1,0:T(8,128)(2,1)S(1)}, u32[]{:S(2)}, u32[]{:S(2)}) collective-permute-start(bf16[3,160,256]{2,1,0:T(8,128)(2,1)S(1)} %get-tuple-element.20.refs_5_), channel_id=1, source_target_pairs={{0,2},{1,3},{2,0},{3,1},{4,6},{5,7},{6,4},{7,5},{8,10},{9,11},{10,... | collective-permute-start | bytes 737288 | tf_op jit(solution)/shard_map/ppermute | solution.py:22
  23.8 8.5 %collective-permute-start.5 = (bf16[3,160,256]{2,1,0:T(8,128)(2,1)S(1)}, bf16[3,160,256]{2,1,0:T(8,128)(2,1)S(1)}, u32[]{:S(2)}, u32[]{:S(2)}) collective-permute-start(bf16[3,160,256]{2,1,0:T(8,128)(2,1)S(1)} %get-tuple-element.19.refs_4_), channel_id=1, source_target_pairs={{0,16},{16,0},{1,17},{17,1},{2,18},{18,2},{3,19},{19,3},{4,20},{20... | collective-permute-start | bytes 737288 | tf_op jit(solution)/shard_map/ppermute | solution.py:22
  30.1 2.8 %collective-permute-start.6 = (bf16[3,160,256]{2,1,0:T(8,128)(2,1)S(1)}, bf16[3,160,256]{2,1,0:T(8,128)(2,1)S(1)}, u32[]{:S(2)}, u32[]{:S(2)}) collective-permute-start(bf16[3,160,256]{2,1,0:T(8,128)(2,1)S(1)} %get-tuple-element.20.refs_5_), channel_id=1, source_target_pairs={{0,16},{16,0},{1,17},{17,1},{2,18},{18,2},{3,19},{19,3},{4,20},{20... | collective-permute-start | bytes 737288 | tf_op jit(solution)/shard_map/ppermute | solution.py:22
  30.1 2.8 %collective-permute-start.7 = (bf16[3,160,256]{2,1,0:T(8,128)(2,1)S(1)}, bf16[3,160,256]{2,1,0:T(8,128)(2,1)S(1)}, u32[]{:S(2)}, u32[]{:S(2)}) collective-permute-start(bf16[3,160,256]{2,1,0:T(8,128)(2,1)S(1)} %collective-permute-done.3.refs_6_), channel_id=1, source_target_pairs={{0,16},{16,0},{1,17},{17,1},{2,18},{18,2},{3,19},{19,3},{4,20},{20... | collective-permute-start | bytes 737288 | tf_op jit(solution)/shard_map/ppermute | solution.py:22
  30.6 2.3 %collective-permute-start.8 = (bf16[3,160,256]{2,1,0:T(8,128)(2,1)S(1)}, bf16[3,160,256]{2,1,0:T(8,128)(2,1)S(1)}, u32[]{:S(2)}, u32[]{:S(2)}) collective-permute-start(bf16[3,160,256]{2,1,0:T(8,128)(2,1)S(1)} %collective-permute-done.4.refs_7_), channel_id=1, source_target_pairs={{0,16},{16,0},{1,17},{17,1},{2,18},{18,2},{3,19},{19,3},{4,20},{20... | collective-permute-start | bytes 737288 | tf_op jit(solution)/shard_map/ppermute | solution.py:22
  30.7 14.0 %collective-permute-start.12 = (bf16[272,512]{1,0:T(8,128)(2,1)S(1)}, bf16[272,512]{1,0:T(8,128)(2,1)S(1)}, u32[]{:S(2)}, u32[]{:S(2)}) collective-permute-start(bf16[272,512]{1,0:T(8,128)(2,1)S(1)} %slice.41), channel_id=1, source_target_pairs={{0,1},{1,0},{2,3},{3,2},{4,5},{5,4},{6,7},{7,6},{8,9},{9,8},{10,11... | collective-permute-start | bytes 835592 | tf_op jit(solution)/shard_map/ppermute | solution.py:22
  32.3 12.4 %collective-permute-start.11 = (bf16[256,512]{1,0:T(8,128)(2,1)S(1)}, bf16[256,512]{1,0:T(8,128)(2,1)S(1)}, u32[]{:S(2)}, u32[]{:S(2)}) collective-permute-start(bf16[256,512]{1,0:T(8,128)(2,1)S(1)} %slice.40), channel_id=1, source_target_pairs={{0,2},{1,3},{2,0},{3,1},{4,6},{5,7},{6,4},{7,5},{8,10},{9,11},{10,... | collective-permute-start | bytes 786440 | tf_op jit(solution)/shard_map/ppermute | solution.py:22
  33.0 15.6 %slice-start = ((s8[8388608]{0:T(1024)(128)(4,1)}), s8[4194304]{0:T(1024)(128)(4,1)S(1)}, s32[]{:S(2)}) async-start(s8[8388608]{0:T(1024)(128)(4,1)} %bitcast.15), calls=%async_computation.2 | async-start | bytes 8388608
  44.7 3.8 %slice-start.1 = ((s8[8388608]{0:T(1024)(128)(4,1)}), s8[4194304]{0:T(1024)(128)(4,1)S(1)}, s32[]{:S(2)}) async-start(s8[8388608]{0:T(1024)(128)(4,1)} %bitcast.15), calls=%async_computation.3 | async-start | bytes 8388608
  46.7 1.8 %collective-permute-start.13 = (bf16[64,2176]{1,0:T(8,128)(2,1)S(1)}, bf16[64,2176]{1,0:T(8,128)(2,1)S(1)}, u32[]{:S(2)}, u32[]{:S(2)}) collective-permute-start(bf16[64,2176]{1,0:T(8,128)(2,1)S(1)} %get-tuple-element.23), channel_id=1, source_target_pairs={{0,16},{16,0},{1,17},{17,1},{2,18},{18,2},{3,19},{19,3},{4,20},{20... | collective-permute-start | bytes 835592 | tf_op jit(solution)/shard_map/ppermute | solution.py:22
  48.5 2.6 %copy-start.1 = (bf16[512,512]{1,0:T(8,128)(2,1)}, bf16[512,512]{1,0:T(8,128)(2,1)S(1)}, u32[]{:S(2)}) copy-start(bf16[512,512]{1,0:T(8,128)(2,1)S(1)} %get-tuple-element.28.gate_ref) | copy-start | bytes 1572868
  48.5 2.6 %copy-start.3 = (bf16[512,512]{1,0:T(8,128)(2,1)}, bf16[512,512]{1,0:T(8,128)(2,1)S(1)}, u32[]{:S(2)}) copy-start(bf16[512,512]{1,0:T(8,128)(2,1)S(1)} %get-tuple-element.29.q_ref) | copy-start | bytes 1572868
  51.1 10.6 %all-to-all-start.1 = ((bf16[8,8,2048]{2,1,0:T(8,128)(2,1)}), bf16[8,8,2048]{2,1,0:T(8,128)(2,1)S(1)}, u32[]{:S(2)}, u32[]{:S(2)}) async-start(bf16[8,8,2048]{2,1,0:T(8,128)(2,1)} %bitcast.7), calls=%async_computation.1 | async-start | bytes 524288 | tf_op jit(solution)/shard_map/all_to_all | solution.py:373
  54.7 1.0 %copy-start.2 = (bf16[512,512]{1,0:T(8,128)(2,1)S(1)}, bf16[512,512]{1,0:T(8,128)(2,1)}, u32[]{:S(2)}) copy-start(bf16[512,512]{1,0:T(8,128)(2,1)} %copy-done.1) | copy-start | bytes 1572868
  55.7 1.0 %copy-start.4 = (bf16[512,512]{1,0:T(8,128)(2,1)S(1)}, bf16[512,512]{1,0:T(8,128)(2,1)}, u32[]{:S(2)}) copy-start(bf16[512,512]{1,0:T(8,128)(2,1)} %copy-done.3) | copy-start | bytes 1572868

commit v5 on v4

--- a/solution.py
+++ b/solution.py
@@ -102,15 +102,11 @@
 
 def first_kernel(place, dps, copies_out, n_parts, bounds_ref, ev_ref, gain_ref, *refs):
     parts, refs = refs[:n_parts], refs[n_parts:]
-    pooled_ref, w_ref, wout_ref, kv_ref, sums_ev_ref, sums_g_ref, q_ref, gate_ref, att_ref, sems = refs
-    copies = place(parts, w_ref, wout_ref, sems)
-    for c in copies:
-        c.start()
+    pooled_ref, w_ref, wout_ref, kv_ref, sums_ev_ref, sums_g_ref, q_ref, gate_ref, att_ref = refs
+    place(parts, w_ref, wout_ref)
     member = membership(bounds_ref, 0, ev_ref.shape[0])
     sums_ev = jnp.dot(member, ev_ref[...], preferred_element_type=F32)
     sums_ev_ref[...] = sums_ev
-    for c in copies:
-        c.wait()
     project(dps, 0, bounds_ref[2, :1, :1], ev_ref, w_ref, gate_ref, q_ref, kv_ref)
     gated = attend(q_ref, [kv_ref], gate_ref, gain_ref, att_ref)
     sums_g_ref[...] = jnp.dot(member, gated, preferred_element_type=F32)
@@ -119,13 +115,20 @@
     pooled_ref[...] = jnp.concatenate([out[:take]] * peers, axis=0).astype(BF16)
 
 
-def project_kernel(dps, row0, bounds_ref, ev_ref, w_ref, sums_ev_ref, _, gate_ref, q_ref, kv_ref, out_ref):
+def halves(ref):
+    cols = ref.shape[1] // 2
+    return ref.at[:, :cols], ref.at[:, cols:]
+
+
+def project_kernel(dps, row0, bounds_ref, ev_ref, w_ref, sums_ev_ref, _, qg_ref, kv_ref, out_ref):
+    q_ref, gate_ref = halves(qg_ref)
     project(dps, row0, bounds_ref[2, :1, :1], ev_ref, w_ref, gate_ref, q_ref, kv_ref)
     member = membership(bounds_ref, row0, ev_ref.shape[0])
     out_ref[...] = sums_ev_ref[...] + jnp.dot(member, ev_ref[...], preferred_element_type=F32)
 
 
-def attend_kernel(row0, bounds_ref, gain_ref, gate_ref, q_ref, kv_first, kv_ref, sums_ref, _, out_ref, att_ref):
+def attend_kernel(row0, bounds_ref, gain_ref, qg_ref, kv_first, kv_ref, sums_ref, _, out_ref, att_ref):
+    q_ref, gate_ref = halves(qg_ref)
     member = membership(bounds_ref, row0, q_ref.shape[0])
     gated = attend(q_ref, [kv_first, kv_ref], gate_ref, gain_ref, att_ref)
     out_ref[...] = sums_ref[...] + jnp.dot(member, gated, preferred_element_type=F32)
@@ -160,15 +163,13 @@
     depth, wide = w_uvqk.shape
     width = w_out.shape[1]
     w_in = jnp.concatenate([w_in, jnp.broadcast_to(ffn_gain, (16, w_in.shape[1]))], axis=0)
-    if (sections, mps) != (2, 4) or wide != 4 * width or depth % 128:
+    if (sections, dps, mps) != (2, 4, 4) or wide != 4 * width or depth % 128:
         ws = [lax.all_gather(x, "dp", axis=0, tiled=True) for x in (w_uvqk, w_out)]
         blocks = [[w_in]] + [[swap(w_in, "mp", mps, k)] for k in range(1, mps)]
 
-        def place_whole(parts, w_ref, wout_ref, sems):
-            return [
-                pltpu.make_async_copy(parts[0], w_ref, sems.at[0]),
-                pltpu.make_async_copy(parts[1], wout_ref, sems.at[1]),
-            ]
+        def place_whole(parts, w_ref, wout_ref):
+            w_ref[...] = parts[0][...]
+            wout_ref[...] = parts[1][...]
 
         return place_whole, ws, blocks, 1
 
@@ -183,44 +184,40 @@
         ],
         axis=0,
     )
-    got = [swap(mine, "dp", dps, k) for k in range(1, dps)]
-    left, right = call(
-        split_kernel,
-        "split",
-        got,
-        [((len(got), depth + part, cut), BF16)] * 2,
-        [],
-        8,
-        0,
-        16 * 1024 * 1024,
-    )
-    plane = [left, right, swap(left, "mp", mps, 1), swap(right, "mp", mps, 2)]
-    parts = [w_uvqk[:, : wide // 2], w_uvqk[:, wide // 2 :], w_out[: depth // 2], w_out[depth // 2 :]]
-    parts = parts + plane + [swap(p, "section", sections, 1) for p in plane]
+    near, far = swap(mine, "dp", dps, 1), swap(mine, "dp", dps, 2)
+    parts, owners = [w_uvqk[:, : wide // 2], w_uvqk[:, wide // 2 :], w_out[: depth // 2], w_out[depth // 2 :]], []
+    for at, got in ((1, [near, far]), (3, [swap(far, "dp", dps, 1)])):
+        left, right = call(
+            split_kernel,
+            f"split_{at}",
+            got,
+            [((len(got), depth + part, cut), BF16)] * 2,
+            [],
+            8,
+            0,
+            16 * 1024 * 1024,
+        )
+        plane = [left, right, swap(left, "mp", mps, 1), swap(right, "mp", mps, 2)]
+        parts = parts + plane + [swap(p, "section", sections, 1) for p in plane]
+        owners = owners + [(at, i // 4, i // 2 % 2, i % 2 * cut) for i in range(8)]
 
     from_x, from_y = swap(w_in, "mp", mps, 1), swap(w_in, "mp", mps, 2)
     middle = w_in.shape[0] // 32 * 16
     diagonal = [swap(from_x[:middle], "mp", mps, 2), swap(from_y[middle:], "mp", mps, 1)]
 
-    def place(parts, w_ref, wout_ref, sems):
+    def place(parts, w_ref, wout_ref):
         sec, m = lax.axis_index("section"), lax.axis_index("mp")
-        w_ref, wout_ref = w_ref.reshape(dps, depth, wide), wout_ref.reshape(dps, depth, width)
-        copies = []
-
-        def add(src, dst):
-            copies.append(pltpu.make_async_copy(src, dst, sems.at[len(copies)]))
-
         for i in range(2):
-            add(parts[i], w_ref.at[0, :, i * (wide // 2) : (i + 1) * (wide // 2)])
-            add(parts[2 + i], wout_ref.at[0, i * (depth // 2) : (i + 1) * (depth // 2)])
-        for i, ref in enumerate(parts[4:]):
-            owner = (sec ^ (i // 4)) * 2 + (parity(m) ^ (i // 2 % 2))
-            at = (i % 2) * cut
+            w_ref[:depth, i * (wide // 2) : (i + 1) * (wide // 2)] = parts[i][...]
+            wout_ref[i * (depth // 2) : (i + 1) * (depth // 2)] = parts[2 + i][...]
+        for ref, (first, other_sec, other_half, at) in zip(parts[4:], owners):
+            owner = (sec ^ other_sec) * 2 + (parity(m) ^ other_half)
             cols = pl.ds(pl.multiple_of(owner * width + at, cut), cut)
-            add(ref.at[:, :depth], w_ref.at[1:, :, cols])
-            rows = pl.ds(pl.multiple_of(owner * part, part), part)
-            add(ref.at[:, depth:], wout_ref.at[1:, rows, at : at + cut])
-        return copies
+            for k in range(ref.shape[0]):
+                row = (first + k) * depth
+                w_ref[row : row + depth, cols] = ref[k, :depth]
+                rows = pl.ds(pl.multiple_of(row + owner * part, part), part)
+                wout_ref[rows, at : at + cut] = ref[k, depth:]
 
     return place, parts, [[w_in], [from_x], [from_y], diagonal], dps
 
@@ -326,7 +323,6 @@
             pltpu.VMEM((first, width), BF16),
             pltpu.VMEM((first, width), F32),
             pltpu.VMEM((first, width), F32),
-            pltpu.SemaphoreType.DMA((32,)),
         ],
         16,
         8 * first * width * width + 2 * first * first * width,
@@ -348,11 +344,11 @@
         2 * w_up.size,
     )
     other = swap(half_send, "section", sections, 1)
-    gate, queries, kv_rest, sums_ev = call(
+    queries_gate, kv_rest, sums_ev = call(
         functools.partial(project_kernel, dps, first),
         "project_rest",
         [bounds, events[first:], full_w, sums_ev, local],
-        [((rest, width), BF16), ((rest, width), BF16), ((rest, 2 * width), BF16), ((sess, width), F32)],
+        [((rest, 2 * width), BF16), ((rest, 2 * width), BF16), ((sess, width), F32)],
         [],
         10,
         8 * rest * width * width,
@@ -376,7 +372,7 @@
     (sums_g,) = call(
         functools.partial(attend_kernel, first),
         "attend_rest",
-        [bounds, gain, gate, queries, kv_first, kv_rest, sums_g, partial],
+        [bounds, gain, queries_gate, kv_first, kv_rest, sums_g, partial],
         [((sess, width), F32)],
         [pltpu.VMEM((rest, width), F32)],
         10,

time: 63 us -> 71.6 us (1.14)
  waiting for transfers between devices: 12.6 us -> 20.4 us
  starting transfers between devices: 18.6 us -> 20 us
  blocking collectives: 7.52 us -> 8.51 us
  local copies, waits for them, and re-layouts: 4.16 us -> 3.3 us
    ppermute x14 -> x20, waiting for transfers between devices: 12.6 us -> 20.2 us  [swap(): return lax.ppermute(x, axis, [(i, i ^ flip) for i in range(size)])]
    ppermute x14 -> x20, starting transfers between devices: 15 us -> 16.4 us  [swap(): return lax.ppermute(x, axis, [(i, i ^ flip) for i in range(size)])]
    all_to_all x1, blocking collectives: 7.52 us -> 8.51 us  [per_device(): lax.all_to_all(micro_rows.reshape(peers, take, width), group, split_axis=...]
    unnamed x24 -> x20, local copies, waits for them, and re-layouts: 2.13 us -> 1.27 us
    pallas_call x7 -> x8, Pallas kernels: 16.1 us -> 15.4 us  [call(): pl.pallas_call(kernel, in_specs=[VMEM] * len(operands), out_specs=[VMEM]...]
  transfers between devices with their start and end apart: 15 -> 21, of which waited for: 2 -> 8; matrix products, arithmetic and copies ran while one was open for 3% -> 3% of each run, Pallas kernels for 17% -> 14%
where the time goes in v5:
time: 71.6 us; the launch traced here: 71.2 us
  waiting for transfers between devices  20.4 us (28%)
  starting transfers between devices  20 us (28%)
  Pallas kernels  15.4 us (22%)
  blocking collectives  8.51 us (12%)
  local copies, waits for them, and re-layouts  3.3 us (5%)
  other arithmetic  1.96 us (3%)
  between operations  1.56 us (2%)
    ppermute x20, waiting for transfers between devices, swap(): return lax.ppermute(x, axis, [(i, i ^ flip) for i in range(size)])  20.2 us
    ppermute x20, starting transfers between devices, swap(): return lax.ppermute(x, axis, [(i, i ^ flip) for i in range(size)])  16.4 us
    pallas_call x8, Pallas kernels, call(): pl.pallas_call(kernel, in_specs=[VMEM] * len(operands), out_specs=[VMEM]...  15.4 us
    all_to_all x1, blocking collectives, per_device(): lax.all_to_all(micro_rows.reshape(peers, take, width), group, split_axis=...  8.51 us
    all_to_all x1, starting transfers between devices, per_device(): lax.all_to_all(partial.reshape(peers, take, half_width), group, split_axi...  3.59 us
  transfers between devices with their start and end apart: 21, of which 8 were waited for; matrix products, arithmetic and copies ran while one was open for 3% of the time, Pallas kernels for 14%

profile of v5, /device:TPU:0, one launch (start us, length us, event | category | flops | bytes accessed | tf_op | source)
XLA Modules:
  0.0 71.2 jit_solution(9342144523944655700)
XLA Ops:
  0.7 1.0 %constant_dynamic-slice_fusion.1 = bf16[128,512]{1,0:T(8,128)(2,1)S(1)} fusion(bf16[128,2048]{1,0:T(8,128)(2,1)} %param.13, s32[]{:T(128)S(6)} %select_n.11), kind=kLoop, calls=%fused_computation.10 | loop fusion | bytes 262148 | tf_op jit(solution)/shard_map/dynamic_slice | solution.py:182
  1.7 0.8 %constant_dynamic-slice_fusion = bf16[32,512]{1,0:T(8,128)(2,1)S(1)} fusion(bf16[128,512]{1,0:T(8,128)(2,1)} %param.14, s32[]{:T(128)S(6)} %select_n.12), kind=kLoop, calls=%fused_computation.9 | loop fusion | bytes 65540 | tf_op jit(solution)/shard_map/dynamic_slice | solution.py:183
  2.5 4.1 %collective-permute-start.1 = (bf16[160,512]{1,0:T(8,128)(2,1)S(1)}, bf16[160,512]{1,0:T(8,128)(2,1)S(1)}, u32[]{:S(2)}, u32[]{:S(2)}) collective-permute-start(bf16[160,512]{1,0:T(8,128)(2,1)S(1)} %pad_maximum_fusion.1), channel_id=1, source_target_pairs={{0,8},{4,12},{8,0},{12,4},{1,9},{5,13},{9,1},{13,5},{2,10},{6,14},... | collective-permute-start | bytes 491528 | tf_op jit(solution)/shard_map/ppermute | solution.py:22
  6.6 1.6 %collective-permute-start = (bf16[160,512]{1,0:T(8,128)(2,1)S(1)}, bf16[160,512]{1,0:T(8,128)(2,1)S(1)}, u32[]{:S(2)}, u32[]{:S(2)}) collective-permute-start(bf16[160,512]{1,0:T(8,128)(2,1)S(1)} %pad_maximum_fusion.1), channel_id=1, source_target_pairs={{0,4},{4,0},{8,12},{12,8},{1,5},{5,1},{9,13},{13,9},{2,6},{6,2},{1... | collective-permute-start | bytes 491528 | tf_op jit(solution)/shard_map/ppermute | solution.py:22
  8.2 0.7 reduce
  8.9 1.1 %pad_maximum_fusion.refs_0_ = bf16[528,512]{1,0:T(8,128)(2,1)S(1)} fusion(bf16[16,512]{1,0:T(8,128)(2,1)S(1)} %broadcast_in_dim.36, bf16[512,512]{1,0:T(8,128)(2,1)} %param.16), kind=kLoop, calls=%fused_computation | loop fusion | flops 1081344 | bytes 1081344 | tf_op jit(solution)/shard_map/concatenate | solution.py:165
  10.0 1.6 %collective-permute-start.16 = (bf16[528,512]{1,0:T(8,128)(2,1)S(1)}, bf16[528,512]{1,0:T(8,128)(2,1)S(1)}, u32[]{:S(2)}, u32[]{:S(2)}) collective-permute-start(bf16[528,512]{1,0:T(8,128)(2,1)S(1)} %pad_maximum_fusion.refs_0_), channel_id=1, source_target_pairs={{0,2},{1,3},{2,0},{3,1},{4,6},{5,7},{6,4},{7,5},{8,10},{9,11},{10,... | collective-permute-start | bytes 1622024 | tf_op jit(solution)/shard_map/ppermute | solution.py:22
  11.6 1.5 %collective-permute-start.15 = (bf16[528,512]{1,0:T(8,128)(2,1)S(1)}, bf16[528,512]{1,0:T(8,128)(2,1)S(1)}, u32[]{:S(2)}, u32[]{:S(2)}) collective-permute-start(bf16[528,512]{1,0:T(8,128)(2,1)S(1)} %pad_maximum_fusion.refs_0_), channel_id=1, source_target_pairs={{0,1},{1,0},{2,3},{3,2},{4,5},{5,4},{6,7},{7,6},{8,9},{9,8},{10,11... | collective-permute-start | bytes 1622024 | tf_op jit(solution)/shard_map/ppermute | solution.py:22
  13.2 1.2 %collective-permute-done.1.refs_1_ = bf16[160,512]{1,0:T(8,128)(2,1)S(1)} collective-permute-done((bf16[160,512]{1,0:T(8,128)(2,1)S(1)}, bf16[160,512]{1,0:T(8,128)(2,1)S(1)}, u32[]{:S(2)}, u32[]{:S(2)}) %collective-permute-start.1) | collective-permute-done | bytes 163872 | tf_op jit(solution)/shard_map/ppermute | solution.py:22
  14.6 1.6 %collective-permute-start.2 = (bf16[2,160,256]{2,1,0:T(8,128)(2,1)S(1)}, bf16[2,160,256]{2,1,0:T(8,128)(2,1)S(1)}, u32[]{:S(2)}, u32[]{:S(2)}) collective-permute-start(bf16[2,160,256]{2,1,0:T(8,128)(2,1)S(1)} %get-tuple-element.20.refs_4_), channel_id=1, source_target_pairs={{0,1},{1,0},{2,3},{3,2},{4,5},{5,4},{6,7},{7,6},{8,9},{9,8},{10,11... | collective-permute-start | bytes 491528 | tf_op jit(solution)/shard_map/ppermute | solution.py:22
  16.2 1.4 %collective-permute-start.8 = (bf16[160,512]{1,0:T(8,128)(2,1)S(1)}, bf16[160,512]{1,0:T(8,128)(2,1)S(1)}, u32[]{:S(2)}, u32[]{:S(2)}) collective-permute-start(bf16[160,512]{1,0:T(8,128)(2,1)S(1)} %collective-permute-done.1.refs_1_), channel_id=1, source_target_pairs={{0,4},{4,0},{8,12},{12,8},{1,5},{5,1},{9,13},{13,9},{2,6},{6,2},{1... | collective-permute-start | bytes 491528 | tf_op jit(solution)/shard_map/ppermute | solution.py:22
  17.8 10.5 %collective-permute-done.2.refs_6_ = bf16[2,160,256]{2,1,0:T(8,128)(2,1)S(1)} collective-permute-done((bf16[2,160,256]{2,1,0:T(8,128)(2,1)S(1)}, bf16[2,160,256]{2,1,0:T(8,128)(2,1)S(1)}, u32[]{:S(2)}, u32[]{:S(2)}) %collective-permute-start.2) | collective-permute-done | bytes 163872 | tf_op jit(solution)/shard_map/ppermute | solution.py:22
  28.3 0.5 collective-permute-start.3
  29.5 4.1 %collective-permute-done.3.refs_7_ = bf16[2,160,256]{2,1,0:T(8,128)(2,1)S(1)} collective-permute-done((bf16[2,160,256]{2,1,0:T(8,128)(2,1)S(1)}, bf16[2,160,256]{2,1,0:T(8,128)(2,1)S(1)}, u32[]{:S(2)}, u32[]{:S(2)}) %collective-permute-start.3) | collective-permute-done | bytes 163872 | tf_op jit(solution)/shard_map/ppermute | solution.py:22
  33.6 1.6 %collective-permute-start.9 = (bf16[1,160,256]{2,1,0:T(8,128)(2,1)S(1)}, bf16[1,160,256]{2,1,0:T(8,128)(2,1)S(1)}, u32[]{:S(2)}, u32[]{:S(2)}) collective-permute-start(bf16[1,160,256]{2,1,0:T(8,128)(2,1)S(1)} %get-tuple-element.22.refs_12_), channel_id=1, source_target_pairs={{0,1},{1,0},{2,3},{3,2},{4,5},{5,4},{6,7},{7,6},{8,9},{9,8},{10,11... | collective-permute-start | bytes 245768 | tf_op jit(solution)/shard_map/ppermute | solution.py:22
  35.3 0.3 collective-permute-start.10
  35.8 2.2 %collective-permute-done.9.refs_14_ = bf16[1,160,256]{2,1,0:T(8,128)(2,1)S(1)} collective-permute-done((bf16[1,160,256]{2,1,0:T(8,128)(2,1)S(1)}, bf16[1,160,256]{2,1,0:T(8,128)(2,1)S(1)}, u32[]{:S(2)}, u32[]{:S(2)}) %collective-permute-start.9) | collective-permute-done | bytes 81952 | tf_op jit(solution)/shard_map/ppermute | solution.py:22
  38.1 1.7 %collective-permute-done.10.refs_15_ = bf16[1,160,256]{2,1,0:T(8,128)(2,1)S(1)} collective-permute-done((bf16[1,160,256]{2,1,0:T(8,128)(2,1)S(1)}, bf16[1,160,256]{2,1,0:T(8,128)(2,1)S(1)}, u32[]{:S(2)}, u32[]{:S(2)}) %collective-permute-start.10) | collective-permute-done | bytes 81952 | tf_op jit(solution)/shard_map/ppermute | solution.py:22
  39.7 0.5 collective-permute-start.7
  40.4 0.5 collective-permute-start.14
  40.9 0.4 collective-permute-start.18
  41.3 0.3 collective-permute-done.13.refs_18_
  41.5 0.3 collective-permute-start.17
  42.0 3.5 %encode_first.1 = (bf16[64,512]{1,0:T(8,128)(2,1)S(1)}, bf16[512,2048]{1,0:T(8,128)(2,1)S(1)}, bf16[512,512]{1,0:T(8,128)(2,1)S(1)}, bf16[512,1024]{1,0:T(8,128)...) custom-call(f32[3,32,128]{2,1,0:T(8,128)S(1)} %broadcast_in_dim.33.bounds_ref, ...), custom_call_target="tpu_custom_call" | custom-call | flops 1342177280 | bytes 6291456 | tf_op jit(solution)/shard_map/encode_first/pallas_call | solution.py:138
  45.5 8.5 %all_to_all.10 = bf16[8,8,512]{2,1,0:T(8,128)(2,1)S(1)} all-to-all(bf16[8,8,512]{2,1,0:T(8,128)(2,1)S(1)} %bitcast.19), channel_id=1, replica_groups=mesh['section'=2,'dp'=4,'mp'=4] {'section','mp'}, dimensions={0} | all-to-all | bytes 131072 | tf_op jit(solution)/shard_map/all_to_all | solution.py:332
  54.1 2.0 %up_half.1 = (f32[64,512]{1,0:T(8,128)S(1)}, f32[64,2176]{1,0:T(8,128)S(1)}, bf16[64,2176]{1,0:T(8,128)(2,1)S(1)}) custom-call(bf16[64,512]{1,0:T(8,128)(2,1)S(1)} %bitcast.18, bf16[528,512]{1,0:T(8,128)(2,1)S(1)} %pad_maximum_fusion.refs_0_, bf16[528,512]{1,0:T(8,128)(2,1)S(1)} %collective-permute-done.15.refs_1_, ...), custom_call_target="tpu_custom_call" | custom-call | flops 536870912 | bytes 8388608 | tf_op jit(solution)/shard_map/up_half/pallas_call | solution.py:138
  56.3 1.6 %project_rest.1 = (bf16[512,1024]{1,0:T(8,128)(2,1)S(1)}, bf16[512,1024]{1,0:T(8,128)(2,1)S(1)}, f32[32,512]{1,0:T(8,128)S(1)}) custom-call(f32[3,32,128]{2,1,0:T(8,128)S(1)} %broadcast_in_dim.33.bounds_ref, bf16[512,512]{1,0:T(8,128)(2,1)S(1)} %get-tuple-element.38.ev_ref, bf16[512,2048]{1,0:T(8,128)(2,1)S(1)} %get-tuple-element.28.w_ref, ...), custom_call_target="tpu_custom_call" | custom-call | flops 1073741824 | bytes 6291456 | tf_op jit(solution)/shard_map/project_rest/pallas_call | solution.py:138
  57.9 2.5 %down_part.1._ = bf16[64,2048]{1,0:T(8,128)(2,1)} custom-call(f32[64,2176]{1,0:T(8,128)S(1)} %get-tuple-element.25.half_ref, bf16[64,2176]{1,0:T(8,128)(2,1)S(1)} %collective-permute-done.19.other_ref, f32[64,512]{1,0:T(8,128)S(1)} %get-tuple-element.27._.local_ref, bf16[2048,2048]{1,0:T(8,128)(2,1)S(1)} %bitcast.16, ...), custom_call_target="tpu_custom_call" | custom-call | flops 536870912 | bytes 8388608 | tf_op jit(solution)/shard_map/down_part/pallas_call | solution.py:138
  60.4 3.6 %all-to-all-start.1 = ((bf16[8,8,2048]{2,1,0:T(8,128)(2,1)}), bf16[8,8,2048]{2,1,0:T(8,128)(2,1)S(1)}, u32[]{:S(2)}, u32[]{:S(2)}) async-start(bf16[8,8,2048]{2,1,0:T(8,128)(2,1)} %bitcast.7), calls=%async_computation.1 | async-start | bytes 524288 | tf_op jit(solution)/shard_map/all_to_all | solution.py:369
  64.0 1.2 %copy-done.2 = bf16[512,1024]{1,0:T(8,128)(2,1)S(1)} copy-done((bf16[512,1024]{1,0:T(8,128)(2,1)S(1)}, bf16[512,1024]{1,0:T(8,128)(2,1)}, u32[]{:S(2)}) %copy-start.2) | copy-done | bytes 1048600
  65.2 4.9 %attend_rest.1.sums_g_ref = f32[32,512]{1,0:T(8,128)S(1)} custom-call(f32[3,32,128]{2,1,0:T(8,128)S(1)} %broadcast_in_dim.33.bounds_ref, f32[8,512]{1,0:T(8,128)S(1)} %broadcast_in_dim.34.gain_ref, bf16[512,1024]{1,0:T(8,128)(2,1)S(1)} %get-tuple-element.31.qg_ref, bf16[512,1024]{1,0:T(8,128)(2,1)S(1)} %get-tuple-element.32.kv_first, ...), custom_call_target="tpu_custom_call" | custom-call | flops 1073741824 | bytes 6291456 | tf_op jit(solution)/shard_map/attend_rest/pallas_call | solution.py:138
  70.3 0.8 %finish.1 = (bf16[8,4096]{1,0:T(8,128)(2,1)}, bf16[32,512]{1,0:T(8,128)(2,1)}) custom-call(bf16[64,2048]{1,0:T(8,128)(2,1)S(1)} %bitcast.17, f32[3,32,128]{2,1,0:T(8,128)S(1)} %broadcast_in_dim.33.bounds_ref, f32[32,512]{1,0:T(8,128)S(1)} %get-tuple-element.30._.sums_ev_ref, f32[32,512]{1,0:T(8,128)S(1)} %attend_rest.1.sums_g_ref, ...), custom_call_target="tpu_custom_call" | custom-call | flops 50331648 | bytes 2097152 | tf_op jit(solution)/shard_map/finish/pallas_call | solution.py:138
  (57 shorter events, 1.3 us)
Async XLA Ops:
  0.6 12.5 %copy-start.3 = (bf16[1,1024,512]{2,1,0:T(8,128)(2,1)S(1)}, bf16[1,1024,512]{2,1,0:T(8,128)(2,1)}, u32[]{:S(2)}) copy-start(bf16[1,1024,512]{2,1,0:T(8,128)(2,1)} %param.10) | copy-start | bytes 3145732
  0.7 17.0 %copy-start.4 = (bf16[128,2048]{1,0:T(8,128)(2,1)S(1)}, bf16[128,2048]{1,0:T(8,128)(2,1)}, u32[]{:S(2)}) copy-start(bf16[128,2048]{1,0:T(8,128)(2,1)} %param.13) | copy-start | bytes 1572868
  2.5 11.9 %collective-permute-start.1 = (bf16[160,512]{1,0:T(8,128)(2,1)S(1)}, bf16[160,512]{1,0:T(8,128)(2,1)S(1)}, u32[]{:S(2)}, u32[]{:S(2)}) collective-permute-start(bf16[160,512]{1,0:T(8,128)(2,1)S(1)} %pad_maximum_fusion.1), channel_id=1, source_target_pairs={{0,8},{4,12},{8,0},{12,4},{1,9},{5,13},{9,1},{13,5},{2,10},{6,14},... | collective-permute-start | bytes 491528 | tf_op jit(solution)/shard_map/ppermute | solution.py:22
  6.6 8.0 %collective-permute-start = (bf16[160,512]{1,0:T(8,128)(2,1)S(1)}, bf16[160,512]{1,0:T(8,128)(2,1)S(1)}, u32[]{:S(2)}, u32[]{:S(2)}) collective-permute-start(bf16[160,512]{1,0:T(8,128)(2,1)S(1)} %pad_maximum_fusion.1), channel_id=1, source_target_pairs={{0,4},{4,0},{8,12},{12,8},{1,5},{5,1},{9,13},{13,9},{2,6},{6,2},{1... | collective-permute-start | bytes 491528 | tf_op jit(solution)/shard_map/ppermute | solution.py:22
  8.9 19.9 %copy-start.5 = (bf16[128,512]{1,0:T(8,128)(2,1)S(1)}, bf16[128,512]{1,0:T(8,128)(2,1)}, u32[]{:S(2)}) copy-start(bf16[128,512]{1,0:T(8,128)(2,1)} %param.14) | copy-start | bytes 393220
  10.0 25.6 %copy-start.7 = (s32[1,32]{1,0:T(1,128)S(1)}, s32[1,32]{1,0:T(1,128)}, u32[]{:S(2)}) copy-start(s32[1,32]{1,0:T(1,128)} %param.12) | copy-start | bytes 388
  10.0 32.0 %copy-start.6 = (f32[512]{0:T(512)S(1)}, f32[512]{0:T(512)}, u32[]{:S(2)}) copy-start(f32[512]{0:T(512)} %param.15) | copy-start | bytes 6148
  10.0 29.7 %collective-permute-start.16 = (bf16[528,512]{1,0:T(8,128)(2,1)S(1)}, bf16[528,512]{1,0:T(8,128)(2,1)S(1)}, u32[]{:S(2)}, u32[]{:S(2)}) collective-permute-start(bf16[528,512]{1,0:T(8,128)(2,1)S(1)} %pad_maximum_fusion.refs_0_), channel_id=1, source_target_pairs={{0,2},{1,3},{2,0},{3,1},{4,6},{5,7},{6,4},{7,5},{8,10},{9,11},{10,... | collective-permute-start | bytes 1622024 | tf_op jit(solution)/shard_map/ppermute | solution.py:22
  11.6 28.6 %collective-permute-start.15 = (bf16[528,512]{1,0:T(8,128)(2,1)S(1)}, bf16[528,512]{1,0:T(8,128)(2,1)S(1)}, u32[]{:S(2)}, u32[]{:S(2)}) collective-permute-start(bf16[528,512]{1,0:T(8,128)(2,1)S(1)} %pad_maximum_fusion.refs_0_), channel_id=1, source_target_pairs={{0,1},{1,0},{2,3},{3,2},{4,5},{5,4},{6,7},{7,6},{8,9},{9,8},{10,11... | collective-permute-start | bytes 1622024 | tf_op jit(solution)/shard_map/ppermute | solution.py:22
  13.1 40.9 %copy-start = (bf16[2048,2048]{1,0:T(8,128)(2,1)S(1)}, bf16[2048,2048]{1,0:T(8,128)(2,1)}, u32[]{:S(2)}) copy-start(bf16[2048,2048]{1,0:T(8,128)(2,1)} %refs_5_.1) | copy-start | bytes 25165828
  14.6 13.7 %collective-permute-start.2 = (bf16[2,160,256]{2,1,0:T(8,128)(2,1)S(1)}, bf16[2,160,256]{2,1,0:T(8,128)(2,1)S(1)}, u32[]{:S(2)}, u32[]{:S(2)}) collective-permute-start(bf16[2,160,256]{2,1,0:T(8,128)(2,1)S(1)} %get-tuple-element.20.refs_4_), channel_id=1, source_target_pairs={{0,1},{1,0},{2,3},{3,2},{4,5},{5,4},{6,7},{7,6},{8,9},{9,8},{10,11... | collective-permute-start | bytes 491528 | tf_op jit(solution)/shard_map/ppermute | solution.py:22
  16.2 12.6 %collective-permute-start.8 = (bf16[160,512]{1,0:T(8,128)(2,1)S(1)}, bf16[160,512]{1,0:T(8,128)(2,1)S(1)}, u32[]{:S(2)}, u32[]{:S(2)}) collective-permute-start(bf16[160,512]{1,0:T(8,128)(2,1)S(1)} %collective-permute-done.1.refs_1_), channel_id=1, source_target_pairs={{0,4},{4,0},{8,12},{12,8},{1,5},{5,1},{9,13},{13,9},{2,6},{6,2},{1... | collective-permute-start | bytes 491528 | tf_op jit(solution)/shard_map/ppermute | solution.py:22
  17.7 17.6 %collective-permute-start.4 = (bf16[2,160,256]{2,1,0:T(8,128)(2,1)S(1)}, bf16[2,160,256]{2,1,0:T(8,128)(2,1)S(1)}, u32[]{:S(2)}, u32[]{:S(2)}) collective-permute-start(bf16[2,160,256]{2,1,0:T(8,128)(2,1)S(1)} %get-tuple-element.20.refs_4_), channel_id=1, source_target_pairs={{0,16},{16,0},{1,17},{17,1},{2,18},{18,2},{3,19},{19,3},{4,20},{20... | collective-permute-start | bytes 491528 | tf_op jit(solution)/shard_map/ppermute | solution.py:22
  28.3 5.3 %collective-permute-start.3 = (bf16[2,160,256]{2,1,0:T(8,128)(2,1)S(1)}, bf16[2,160,256]{2,1,0:T(8,128)(2,1)S(1)}, u32[]{:S(2)}, u32[]{:S(2)}) collective-permute-start(bf16[2,160,256]{2,1,0:T(8,128)(2,1)S(1)} %get-tuple-element.21.refs_5_), channel_id=1, source_target_pairs={{0,2},{1,3},{2,0},{3,1},{4,6},{5,7},{6,4},{7,5},{8,10},{9,11},{10,... | collective-permute-start | bytes 491528 | tf_op jit(solution)/shard_map/ppermute | solution.py:22
  28.8 6.9 %collective-permute-start.5 = (bf16[2,160,256]{2,1,0:T(8,128)(2,1)S(1)}, bf16[2,160,256]{2,1,0:T(8,128)(2,1)S(1)}, u32[]{:S(2)}, u32[]{:S(2)}) collective-permute-start(bf16[2,160,256]{2,1,0:T(8,128)(2,1)S(1)} %get-tuple-element.21.refs_5_), channel_id=1, source_target_pairs={{0,16},{16,0},{1,17},{17,1},{2,18},{18,2},{3,19},{19,3},{4,20},{20... | collective-permute-start | bytes 491528 | tf_op jit(solution)/shard_map/ppermute | solution.py:22
  33.6 4.4 %collective-permute-start.9 = (bf16[1,160,256]{2,1,0:T(8,128)(2,1)S(1)}, bf16[1,160,256]{2,1,0:T(8,128)(2,1)S(1)}, u32[]{:S(2)}, u32[]{:S(2)}) collective-permute-start(bf16[1,160,256]{2,1,0:T(8,128)(2,1)S(1)} %get-tuple-element.22.refs_12_), channel_id=1, source_target_pairs={{0,1},{1,0},{2,3},{3,2},{4,5},{5,4},{6,7},{7,6},{8,9},{9,8},{10,11... | collective-permute-start | bytes 245768 | tf_op jit(solution)/shard_map/ppermute | solution.py:22
  35.3 4.4 %collective-permute-start.10 = (bf16[1,160,256]{2,1,0:T(8,128)(2,1)S(1)}, bf16[1,160,256]{2,1,0:T(8,128)(2,1)S(1)}, u32[]{:S(2)}, u32[]{:S(2)}) collective-permute-start(bf16[1,160,256]{2,1,0:T(8,128)(2,1)S(1)} %get-tuple-element.23.refs_13_), channel_id=1, source_target_pairs={{0,2},{1,3},{2,0},{3,1},{4,6},{5,7},{6,4},{7,5},{8,10},{9,11},{10,... | collective-permute-start | bytes 245768 | tf_op jit(solution)/shard_map/ppermute | solution.py:22
  35.7 4.6 %collective-permute-start.11 = (bf16[1,160,256]{2,1,0:T(8,128)(2,1)S(1)}, bf16[1,160,256]{2,1,0:T(8,128)(2,1)S(1)}, u32[]{:S(2)}, u32[]{:S(2)}) collective-permute-start(bf16[1,160,256]{2,1,0:T(8,128)(2,1)S(1)} %get-tuple-element.22.refs_12_), channel_id=1, source_target_pairs={{0,16},{16,0},{1,17},{17,1},{2,18},{18,2},{3,19},{19,3},{4,20},{20... | collective-permute-start | bytes 245768 | tf_op jit(solution)/shard_map/ppermute | solution.py:22
  38.1 2.8 %collective-permute-start.12 = (bf16[1,160,256]{2,1,0:T(8,128)(2,1)S(1)}, bf16[1,160,256]{2,1,0:T(8,128)(2,1)S(1)}, u32[]{:S(2)}, u32[]{:S(2)}) collective-permute-start(bf16[1,160,256]{2,1,0:T(8,128)(2,1)S(1)} %get-tuple-element.23.refs_13_), channel_id=1, source_target_pairs={{0,16},{16,0},{1,17},{17,1},{2,18},{18,2},{3,19},{19,3},{4,20},{20... | collective-permute-start | bytes 245768 | tf_op jit(solution)/shard_map/ppermute | solution.py:22
  39.7 2.2 %collective-permute-start.6 = (bf16[2,160,256]{2,1,0:T(8,128)(2,1)S(1)}, bf16[2,160,256]{2,1,0:T(8,128)(2,1)S(1)}, u32[]{:S(2)}, u32[]{:S(2)}) collective-permute-start(bf16[2,160,256]{2,1,0:T(8,128)(2,1)S(1)} %collective-permute-done.2.refs_6_), channel_id=1, source_target_pairs={{0,16},{16,0},{1,17},{17,1},{2,18},{18,2},{3,19},{19,3},{4,20},{20... | collective-permute-start | bytes 491528 | tf_op jit(solution)/shard_map/ppermute | solution.py:22
  39.7 2.2 %collective-permute-start.7 = (bf16[2,160,256]{2,1,0:T(8,128)(2,1)S(1)}, bf16[2,160,256]{2,1,0:T(8,128)(2,1)S(1)}, u32[]{:S(2)}, u32[]{:S(2)}) collective-permute-start(bf16[2,160,256]{2,1,0:T(8,128)(2,1)S(1)} %collective-permute-done.3.refs_7_), channel_id=1, source_target_pairs={{0,16},{16,0},{1,17},{17,1},{2,18},{18,2},{3,19},{19,3},{4,20},{20... | collective-permute-start | bytes 491528 | tf_op jit(solution)/shard_map/ppermute | solution.py:22
  40.2 1.3 %collective-permute-start.13 = (bf16[1,160,256]{2,1,0:T(8,128)(2,1)S(1)}, bf16[1,160,256]{2,1,0:T(8,128)(2,1)S(1)}, u32[]{:S(2)}, u32[]{:S(2)}) collective-permute-start(bf16[1,160,256]{2,1,0:T(8,128)(2,1)S(1)} %collective-permute-done.9.refs_14_), channel_id=1, source_target_pairs={{0,16},{16,0},{1,17},{17,1},{2,18},{18,2},{3,19},{19,3},{4,20},{20... | collective-permute-start | bytes 245768 | tf_op jit(solution)/shard_map/ppermute | solution.py:22
  40.4 1.5 %collective-permute-start.14 = (bf16[1,160,256]{2,1,0:T(8,128)(2,1)S(1)}, bf16[1,160,256]{2,1,0:T(8,128)(2,1)S(1)}, u32[]{:S(2)}, u32[]{:S(2)}) collective-permute-start(bf16[1,160,256]{2,1,0:T(8,128)(2,1)S(1)} %collective-permute-done.10.refs_15_), channel_id=1, source_target_pairs={{0,16},{16,0},{1,17},{17,1},{2,18},{18,2},{3,19},{19,3},{4,20},{20... | collective-permute-start | bytes 245768 | tf_op jit(solution)/shard_map/ppermute | solution.py:22
  40.9 13.2 %collective-permute-start.18 = (bf16[272,512]{1,0:T(8,128)(2,1)S(1)}, bf16[272,512]{1,0:T(8,128)(2,1)S(1)}, u32[]{:S(2)}, u32[]{:S(2)}) collective-permute-start(bf16[272,512]{1,0:T(8,128)(2,1)S(1)} %slice.41), channel_id=1, source_target_pairs={{0,1},{1,0},{2,3},{3,2},{4,5},{5,4},{6,7},{7,6},{8,9},{9,8},{10,11... | collective-permute-start | bytes 835592 | tf_op jit(solution)/shard_map/ppermute | solution.py:22
  41.5 12.5 %collective-permute-start.17 = (bf16[256,512]{1,0:T(8,128)(2,1)S(1)}, bf16[256,512]{1,0:T(8,128)(2,1)S(1)}, u32[]{:S(2)}, u32[]{:S(2)}) collective-permute-start(bf16[256,512]{1,0:T(8,128)(2,1)S(1)} %slice.40), channel_id=1, source_target_pairs={{0,2},{1,3},{2,0},{3,1},{4,6},{5,7},{6,4},{7,5},{8,10},{9,11},{10,... | collective-permute-start | bytes 786440 | tf_op jit(solution)/shard_map/ppermute | solution.py:22
  42.0 15.9 %slice-start = ((s8[8388608]{0:T(1024)(128)(4,1)}), s8[4194304]{0:T(1024)(128)(4,1)S(1)}, s32[]{:S(2)}) async-start(s8[8388608]{0:T(1024)(128)(4,1)} %bitcast.15), calls=%async_computation.2 | async-start | bytes 8388608
  54.0 3.8 %slice-start.1 = ((s8[8388608]{0:T(1024)(128)(4,1)}), s8[4194304]{0:T(1024)(128)(4,1)S(1)}, s32[]{:S(2)}) async-start(s8[8388608]{0:T(1024)(128)(4,1)} %bitcast.15), calls=%async_computation.3 | async-start | bytes 8388608
  56.1 1.8 %collective-permute-start.19 = (bf16[64,2176]{1,0:T(8,128)(2,1)S(1)}, bf16[64,2176]{1,0:T(8,128)(2,1)S(1)}, u32[]{:S(2)}, u32[]{:S(2)}) collective-permute-start(bf16[64,2176]{1,0:T(8,128)(2,1)S(1)} %get-tuple-element.26), channel_id=1, source_target_pairs={{0,16},{16,0},{1,17},{17,1},{2,18},{18,2},{3,19},{19,3},{4,20},{20... | collective-permute-start | bytes 835592 | tf_op jit(solution)/shard_map/ppermute | solution.py:22
  57.8 2.6 %copy-start.1 = (bf16[512,1024]{1,0:T(8,128)(2,1)}, bf16[512,1024]{1,0:T(8,128)(2,1)S(1)}, u32[]{:S(2)}) copy-start(bf16[512,1024]{1,0:T(8,128)(2,1)S(1)} %get-tuple-element.33.kv_ref) | copy-start | bytes 3145732
  60.4 9.9 %all-to-all-start.1 = ((bf16[8,8,2048]{2,1,0:T(8,128)(2,1)}), bf16[8,8,2048]{2,1,0:T(8,128)(2,1)S(1)}, u32[]{:S(2)}, u32[]{:S(2)}) async-start(bf16[8,8,2048]{2,1,0:T(8,128)(2,1)} %bitcast.7), calls=%async_computation.1 | async-start | bytes 524288 | tf_op jit(solution)/shard_map/all_to_all | solution.py:369
  64.0 1.2 %copy-start.2 = (bf16[512,1024]{1,0:T(8,128)(2,1)S(1)}, bf16[512,1024]{1,0:T(8,128)(2,1)}, u32[]{:S(2)}) copy-start(bf16[512,1024]{1,0:T(8,128)(2,1)} %copy-done.1) | copy-start | bytes 3145732

commit v6 on v5

--- a/solution.py
+++ b/solution.py
@@ -26,12 +26,16 @@
     return h + h * jnp.tanh(h)
 
 
+def order_of(dps):
+    return [0, *range(2, dps), 1]
+
+
 def in_order(ref, at, dps):
     if dps == 1:
         return ref[at, :]
     z = lax.axis_index("dp")
     cols = ref.shape[1] // dps
-    return jnp.concatenate([ref[at, pl.ds(pl.multiple_of((z ^ k) * cols, cols), cols)] for k in range(dps)], axis=1)
+    return jnp.concatenate([ref[at, pl.ds(pl.multiple_of((z ^ k) * cols, cols), cols)] for k in order_of(dps)], axis=1)
 
 
 def project(dps, row0, hist, ev_ref, w_ref, gate_ref, q_ref, kv_ref):
@@ -152,18 +156,26 @@
 
 
 def split_kernel(*refs):
-    *parts, left_ref, right_ref = refs
+    *parts, left_ref, right_ref, both_ref = refs
     half = left_ref.shape[2]
     for k, part in enumerate(parts):
-        left_ref[k] = part[:, :half]
-        right_ref[k] = part[:, half:]
+        for i, ref in enumerate((left_ref, right_ref)):
+            piece = part[:, i * half : (i + 1) * half]
+            ref[k] = piece
+            both_ref[i, k] = piece
+
+
+def merge_kernel(left_ref, right_ref, next_ref, both_ref, next_out):
+    both_ref[0] = left_ref[...]
+    both_ref[1] = right_ref[...]
+    next_out[...] = next_ref[...]
 
 
 def gather_weights(w_uvqk, w_out, w_in, ffn_gain, sections, dps, mps):
     depth, wide = w_uvqk.shape
     width = w_out.shape[1]
     w_in = jnp.concatenate([w_in, jnp.broadcast_to(ffn_gain, (16, w_in.shape[1]))], axis=0)
-    if (sections, dps, mps) != (2, 4, 4) or wide != 4 * width or depth % 128:
+    if (sections, mps) != (2, 4) or wide != 4 * width or depth % 128:
         ws = [lax.all_gather(x, "dp", axis=0, tiled=True) for x in (w_uvqk, w_out)]
         blocks = [[w_in]] + [[swap(w_in, "mp", mps, k)] for k in range(1, mps)]
 
@@ -184,42 +196,44 @@
         ],
         axis=0,
     )
-    near, far = swap(mine, "dp", dps, 1), swap(mine, "dp", dps, 2)
-    parts, owners = [w_uvqk[:, : wide // 2], w_uvqk[:, wide // 2 :], w_out[: depth // 2], w_out[depth // 2 :]], []
-    for at, got in ((1, [near, far]), (3, [swap(far, "dp", dps, 1)])):
-        left, right = call(
-            split_kernel,
-            f"split_{at}",
-            got,
-            [((len(got), depth + part, cut), BF16)] * 2,
-            [],
-            8,
-            0,
-            16 * 1024 * 1024,
-        )
-        plane = [left, right, swap(left, "mp", mps, 1), swap(right, "mp", mps, 2)]
-        parts = parts + plane + [swap(p, "section", sections, 1) for p in plane]
-        owners = owners + [(at, i // 4, i // 2 % 2, i % 2 * cut) for i in range(8)]
-
+    got = [swap(mine, "dp", dps, k) for k in order_of(dps)[1:]]
+    size = (len(got), depth + part, cut)
+    left, right, both = call(
+        split_kernel, "split", got, [(size, BF16), (size, BF16), ((2, *size), BF16)], [], 8, 0, 16 * 1024 * 1024
+    )
     from_x, from_y = swap(w_in, "mp", mps, 1), swap(w_in, "mp", mps, 2)
-    middle = w_in.shape[0] // 32 * 16
-    diagonal = [swap(from_x[:middle], "mp", mps, 2), swap(from_y[middle:], "mp", mps, 1)]
+    others, w_in_later = call(
+        merge_kernel,
+        "merge",
+        [swap(left, "mp", mps, 1), swap(right, "mp", mps, 2), w_in],
+        [((2, *size), BF16), (w_in.shape, BF16)],
+        [],
+        8,
+        0,
+        1024 * 1024,
+    )
+    plane = [both, others]
+    parts = [w_uvqk[:, : wide // 2], w_uvqk[:, wide // 2 :], w_out[: depth // 2], w_out[depth // 2 :]]
+    parts = parts + plane + [swap(p, "section", sections, 1) for p in plane]
+    blocks = [[w_in], [from_x], [from_y], [swap(w_in_later, "mp", mps, 3)]]
 
     def place(parts, w_ref, wout_ref):
         sec, m = lax.axis_index("section"), lax.axis_index("mp")
         for i in range(2):
             w_ref[:depth, i * (wide // 2) : (i + 1) * (wide // 2)] = parts[i][...]
             wout_ref[i * (depth // 2) : (i + 1) * (depth // 2)] = parts[2 + i][...]
-        for ref, (first, other_sec, other_half, at) in zip(parts[4:], owners):
-            owner = (sec ^ other_sec) * 2 + (parity(m) ^ other_half)
-            cols = pl.ds(pl.multiple_of(owner * width + at, cut), cut)
-            for k in range(ref.shape[0]):
-                row = (first + k) * depth
-                w_ref[row : row + depth, cols] = ref[k, :depth]
-                rows = pl.ds(pl.multiple_of(row + owner * part, part), part)
-                wout_ref[rows, at : at + cut] = ref[k, depth:]
-
-    return place, parts, [[w_in], [from_x], [from_y], diagonal], dps
+        for i, ref in enumerate(parts[4:]):
+            owner = (sec ^ (i // 2)) * 2 + (parity(m) ^ (i % 2))
+            for side in range(2):
+                at = side * cut
+                cols = pl.ds(pl.multiple_of(owner * width + at, cut), cut)
+                for k in range(dps - 1):
+                    row = (k + 1) * depth
+                    w_ref[row : row + depth, cols] = ref[side, k, :depth]
+                    rows = pl.ds(pl.multiple_of(row + owner * part, part), part)
+                    wout_ref[rows, at : at + cut] = ref[side, k, depth:]
+
+    return place, parts, blocks, dps
 
 
 def two_terms(square):

time: 71.6 us -> 75.9 us (1.060)
  local copies, waits for them, and re-layouts: 3.3 us -> 17.5 us
  blocking collectives: 8.51 us -> 0 us
  waiting for transfers between devices: 20.4 us -> 16.8 us
  Pallas kernels: 15.4 us -> 16.9 us
    unnamed x20 -> x26, local copies, waits for them, and re-layouts: 1.27 us -> 13.5 us
    all_to_all x1 -> x0, blocking collectives: 8.51 us -> none  [per_device(): lax.all_to_all(micro_rows.reshape(peers, take, width), group, split_axis=...]
    ppermute x20 -> x11, waiting for transfers between devices: 20.2 us -> 15 us  [swap(): return lax.ppermute(x, axis, [(i, i ^ flip) for i in range(size)])]
    all_to_all x0 -> x1, starting transfers between devices: none -> 3.35 us  [per_device(): lax.all_to_all(micro_rows.reshape(peers, take, width), group, split_axis=...]
    ppermute x20 -> x11, starting transfers between devices: 16.4 us -> 13.6 us  [swap(): return lax.ppermute(x, axis, [(i, i ^ flip) for i in range(size)])]
    all_to_all x0 -> x1, waiting for transfers between devices: none -> 1.8 us  [per_device(): lax.all_to_all(micro_rows.reshape(peers, take, width), group, split_axis=...]
    pallas_call x8, Pallas kernels: 15.4 us -> 16.9 us  [call(): pl.pallas_call(kernel, in_specs=[VMEM] * len(operands), out_specs=[VMEM]...]
    slice x1, local copies, waits for them, and re-layouts: 0.07 us -> 1.27 us  [per_device(): events[first:]]
  transfers between devices with their start and end apart: 21 -> 13, of which waited for: 8 -> 6; matrix products, arithmetic and copies ran while one was open for 3% -> 6% of each run, Pallas kernels for 14% -> 15%
where the time goes in v6:
time: 75.9 us; the launch traced here: 75.2 us
  starting transfers between devices  20.6 us (27%)
  local copies, waits for them, and re-layouts  17.5 us (23%)
  Pallas kernels  16.9 us (22%)
  waiting for transfers between devices  16.8 us (22%)
  other arithmetic  1.92 us (3%)
  between operations  1.5 us (2%)
    pallas_call x8, Pallas kernels, call(): pl.pallas_call(kernel, in_specs=[VMEM] * len(operands), out_specs=[VMEM]...  16.9 us
    ppermute x11, waiting for transfers between devices, swap(): return lax.ppermute(x, axis, [(i, i ^ flip) for i in range(size)])  15 us
    ppermute x11, starting transfers between devices, swap(): return lax.ppermute(x, axis, [(i, i ^ flip) for i in range(size)])  13.6 us
    unnamed x26, local copies, waits for them, and re-layouts  13.5 us
    all_to_all x1, starting transfers between devices, per_device(): lax.all_to_all(partial.reshape(peers, take, half_width), group, split_axi...  3.59 us
    all_to_all x1, starting transfers between devices, per_device(): lax.all_to_all(micro_rows.reshape(peers, take, width), group, split_axis=...  3.35 us
    all_to_all x1, waiting for transfers between devices, per_device(): lax.all_to_all(micro_rows.reshape(peers, take, width), group, split_axis=...  1.8 us
  transfers between devices with their start and end apart: 13, of which 6 were waited for; matrix products, arithmetic and copies ran while one was open for 6% of the time, Pallas kernels for 15%

profile of v6, /device:TPU:0, one launch (start us, length us, event | category | flops | bytes accessed | tf_op | source)
XLA Modules:
  0.0 75.2 jit_solution(4633323920544423434)
XLA Ops:
  0.7 1.0 %constant_dynamic-slice_fusion.1 = bf16[128,512]{1,0:T(8,128)(2,1)S(1)} fusion(bf16[128,2048]{1,0:T(8,128)(2,1)} %param.13, s32[]{:T(128)S(6)} %select_n.11), kind=kLoop, calls=%fused_computation.10 | loop fusion | bytes 262148 | tf_op jit(solution)/shard_map/dynamic_slice | solution.py:194
  2.4 4.1 %collective-permute-start = (bf16[160,512]{1,0:T(8,128)(2,1)S(1)}, bf16[160,512]{1,0:T(8,128)(2,1)S(1)}, u32[]{:S(2)}, u32[]{:S(2)}) collective-permute-start(bf16[160,512]{1,0:T(8,128)(2,1)S(1)} %pad_maximum_fusion.1), channel_id=1, source_target_pairs={{0,8},{4,12},{8,0},{12,4},{1,9},{5,13},{9,1},{13,5},{2,10},{6,14},... | collective-permute-start | bytes 491528 | tf_op jit(solution)/shard_map/ppermute | solution.py:22
  6.5 1.3 %collective-permute-start.1 = (bf16[160,512]{1,0:T(8,128)(2,1)S(1)}, bf16[160,512]{1,0:T(8,128)(2,1)S(1)}, u32[]{:S(2)}, u32[]{:S(2)}) collective-permute-start(bf16[160,512]{1,0:T(8,128)(2,1)S(1)} %pad_maximum_fusion.1), channel_id=1, source_target_pairs={{0,12},{4,8},{8,4},{12,0},{1,13},{5,9},{9,5},{13,1},{2,14},{6,10},... | collective-permute-start | bytes 491528 | tf_op jit(solution)/shard_map/ppermute | solution.py:22
  8.8 1.1 %pad_maximum_fusion.next_ref.refs_0_ = bf16[528,512]{1,0:T(8,128)(2,1)S(1)} fusion(bf16[16,512]{1,0:T(8,128)(2,1)S(1)} %broadcast_in_dim.36, bf16[512,512]{1,0:T(8,128)(2,1)} %param.16), kind=kLoop, calls=%fused_computation | loop fusion | flops 1081344 | bytes 1081344 | tf_op jit(solution)/shard_map/concatenate | solution.py:177
  9.9 1.6 %collective-permute-start.7 = (bf16[528,512]{1,0:T(8,128)(2,1)S(1)}, bf16[528,512]{1,0:T(8,128)(2,1)S(1)}, u32[]{:S(2)}, u32[]{:S(2)}) collective-permute-start(bf16[528,512]{1,0:T(8,128)(2,1)S(1)} %pad_maximum_fusion.next_ref.refs_0_), channel_id=1, source_target_pairs={{0,1},{1,0},{2,3},{3,2},{4,5},{5,4},{6,7},{7,6},{8,9},{9,8},{10,11... | collective-permute-start | bytes 1622024 | tf_op jit(solution)/shard_map/ppermute | solution.py:22
  11.5 1.5 %collective-permute-start.8 = (bf16[528,512]{1,0:T(8,128)(2,1)S(1)}, bf16[528,512]{1,0:T(8,128)(2,1)S(1)}, u32[]{:S(2)}, u32[]{:S(2)}) collective-permute-start(bf16[528,512]{1,0:T(8,128)(2,1)S(1)} %pad_maximum_fusion.next_ref.refs_0_), channel_id=1, source_target_pairs={{0,2},{1,3},{2,0},{3,1},{4,6},{5,7},{6,4},{7,5},{8,10},{9,11},{10,... | collective-permute-start | bytes 1622024 | tf_op jit(solution)/shard_map/ppermute | solution.py:22
  13.0 0.9 %fusion.1 = (bf16[64,512]{1,0:T(8,128)(2,1)S(1)}, bf16[64,512]{1,0:T(8,128)(2,1)S(1)}) fusion(bf16[128,512]{1,0:T(8,128)(2,1)} %param.14), kind=kLoop, calls=%fused_computation.12 | loop fusion | bytes 262144 | tf_op jit(solution)/shard_map/slice | solution.py:216
  13.9 4.8 %collective-permute-done.refs_0_ = bf16[160,512]{1,0:T(8,128)(2,1)S(1)} collective-permute-done((bf16[160,512]{1,0:T(8,128)(2,1)S(1)}, bf16[160,512]{1,0:T(8,128)(2,1)S(1)}, u32[]{:S(2)}, u32[]{:S(2)}) %collective-permute-start) | collective-permute-done | bytes 163872 | tf_op jit(solution)/shard_map/ppermute | solution.py:22
  19.2 1.6 %collective-permute-start.3 = (bf16[3,160,256]{2,1,0:T(8,128)(2,1)S(1)}, bf16[3,160,256]{2,1,0:T(8,128)(2,1)S(1)}, u32[]{:S(2)}, u32[]{:S(2)}) collective-permute-start(bf16[3,160,256]{2,1,0:T(8,128)(2,1)S(1)} %get-tuple-element.22), channel_id=1, source_target_pairs={{0,1},{1,0},{2,3},{3,2},{4,5},{5,4},{6,7},{7,6},{8,9},{9,8},{10,11... | collective-permute-start | bytes 737288 | tf_op jit(solution)/shard_map/ppermute | solution.py:22
  20.8 1.5 %collective-permute-start.4 = (bf16[3,160,256]{2,1,0:T(8,128)(2,1)S(1)}, bf16[3,160,256]{2,1,0:T(8,128)(2,1)S(1)}, u32[]{:S(2)}, u32[]{:S(2)}) collective-permute-start(bf16[3,160,256]{2,1,0:T(8,128)(2,1)S(1)} %get-tuple-element.23), channel_id=1, source_target_pairs={{0,2},{1,3},{2,0},{3,1},{4,6},{5,7},{6,4},{7,5},{8,10},{9,11},{10,... | collective-permute-start | bytes 737288 | tf_op jit(solution)/shard_map/ppermute | solution.py:22
  23.2 5.4 %collective-permute-done.3.left_ref = bf16[3,160,256]{2,1,0:T(8,128)(2,1)S(1)} collective-permute-done((bf16[3,160,256]{2,1,0:T(8,128)(2,1)S(1)}, bf16[3,160,256]{2,1,0:T(8,128)(2,1)S(1)}, u32[]{:S(2)}, u32[]{:S(2)}) %collective-permute-start.3) | collective-permute-done | bytes 245792 | tf_op jit(solution)/shard_map/ppermute | solution.py:22
  28.7 1.2 %collective-permute-done.4.right_ref = bf16[3,160,256]{2,1,0:T(8,128)(2,1)S(1)} collective-permute-done((bf16[3,160,256]{2,1,0:T(8,128)(2,1)S(1)}, bf16[3,160,256]{2,1,0:T(8,128)(2,1)S(1)}, u32[]{:S(2)}, u32[]{:S(2)}) %collective-permute-start.4) | collective-permute-done | bytes 245792 | tf_op jit(solution)/shard_map/ppermute | solution.py:22
  29.9 0.9 %merge.1 = (bf16[2,3,160,256]{3,2,1,0:T(8,128)(2,1)S(1)}, bf16[528,512]{1,0:T(8,128)(2,1)}) custom-call(bf16[3,160,256]{2,1,0:T(8,128)(2,1)S(1)} %collective-permute-done.3.left_ref, bf16[3,160,256]{2,1,0:T(8,128)(2,1)S(1)} %collective-permute-done.4.right_ref, bf16[528,512]{1,0:T(8,128)(2,1)S(1)} %pad_maximum_fusion.next_ref.refs_0_), custom_call_target="tpu_custom_call" | custom-call | bytes 1048576 | tf_op jit(solution)/shard_map/merge/pallas_call | solution.py:142
  30.8 1.5 %collective-permute-start.9 = (bf16[528,512]{1,0:T(8,128)(2,1)}, bf16[528,512]{1,0:T(8,128)(2,1)S(1)}, u32[]{:S(2)}, u32[]{:S(2)}) collective-permute-start(bf16[528,512]{1,0:T(8,128)(2,1)} %get-tuple-element.26), channel_id=1, source_target_pairs={{0,3},{1,2},{2,1},{3,0},{4,7},{5,6},{6,5},{7,4},{8,11},{9,10},{10,... | collective-permute-start | bytes 1622024 | tf_op jit(solution)/shard_map/ppermute | solution.py:22
  32.3 1.3 %slice_bitcast_fusion = (bf16[512,512]{1,0:T(8,128)(2,1)S(1)}, bf16[512,512]{1,0:T(8,128)(2,1)S(1)}) fusion(bf16[1,1024,512]{2,1,0:T(8,128)(2,1)} %param.10), kind=kLoop, calls=%fused_computation.1 | loop fusion | bytes 2097152 | tf_op jit(solution)/shard_map/slice | solution.py:364
  33.7 4.2 %encode_first.1 = (bf16[64,512]{1,0:T(8,128)(2,1)}, bf16[512,2048]{1,0:T(8,128)(2,1)S(1)}, bf16[512,512]{1,0:T(8,128)(2,1)S(1)}, bf16[512,1024]{1,0:T(8,128)(2,1...) custom-call(f32[3,32,128]{2,1,0:T(8,128)S(1)} %broadcast_in_dim.33.bounds_ref, ...), custom_call_target="tpu_custom_call" | custom-call | flops 1342177280 | bytes 6291456 | tf_op jit(solution)/shard_map/encode_first/pallas_call | solution.py:142
  37.8 1.0 %copy-done.2 = bf16[512,1024]{1,0:T(8,128)(2,1)} copy-done((bf16[512,1024]{1,0:T(8,128)(2,1)}, bf16[512,1024]{1,0:T(8,128)(2,1)S(1)}, u32[]{:S(2)}) %copy-start.2) | copy-done | bytes 1048600
  38.8 1.4 %copy-done.8 = bf16[512,2048]{1,0:T(8,128)(2,1)} copy-done((bf16[512,2048]{1,0:T(8,128)(2,1)}, bf16[512,2048]{1,0:T(8,128)(2,1)S(1)}, u32[]{:S(2)}) %copy-start.8) | copy-done | bytes 2097176
  40.2 3.4 %all-to-all-start = ((bf16[8,8,512]{2,1,0:T(8,128)(2,1)}), bf16[8,8,512]{2,1,0:T(8,128)(2,1)S(1)}, u32[]{:S(2)}, u32[]{:S(2)}) async-start(bf16[8,8,512]{2,1,0:T(8,128)(2,1)} %bitcast.4), calls=%async_computation | async-start | bytes 131072 | tf_op jit(solution)/shard_map/all_to_all | solution.py:346
  43.6 3.0 %collective-permute-done.9.refs_3_ = bf16[528,512]{1,0:T(8,128)(2,1)S(1)} collective-permute-done((bf16[528,512]{1,0:T(8,128)(2,1)}, bf16[528,512]{1,0:T(8,128)(2,1)S(1)}, u32[]{:S(2)}, u32[]{:S(2)}) %collective-permute-start.9) | collective-permute-done | bytes 540704 | tf_op jit(solution)/shard_map/ppermute | solution.py:22
  46.6 1.8 %all-to-all-done = bf16[8,8,512]{2,1,0:T(8,128)(2,1)S(1)} async-done(((bf16[8,8,512]{2,1,0:T(8,128)(2,1)}), bf16[8,8,512]{2,1,0:T(8,128)(2,1)S(1)}, u32[]{:S(2)}, u32[]{:S(2)}) %all-to-all-start) | async-done | bytes 65568 | tf_op jit(solution)/shard_map/all_to_all | solution.py:346
  48.4 3.4 %copy-done.1 = bf16[2048,2048]{1,0:T(8,128)(2,1)S(1)} copy-done((bf16[2048,2048]{1,0:T(8,128)(2,1)S(1)}, bf16[2048,2048]{1,0:T(8,128)(2,1)}, u32[]{:S(2)}) %copy-start.1) | copy-done | bytes 8388632
  51.8 2.0 %up_half.1 = (f32[64,512]{1,0:T(8,128)S(1)}, f32[64,2176]{1,0:T(8,128)S(1)}, bf16[64,2176]{1,0:T(8,128)(2,1)S(1)}) custom-call(bf16[64,512]{1,0:T(8,128)(2,1)S(1)} %bitcast.16, bf16[528,512]{1,0:T(8,128)(2,1)S(1)} %pad_maximum_fusion.next_ref.refs_0_, bf16[528,512]{1,0:T(8,128)(2,1)S(1)} %collective-permute-done.7.refs_1_, ...), custom_call_target="tpu_custom_call" | custom-call | flops 536870912 | bytes 8388608 | tf_op jit(solution)/shard_map/up_half/pallas_call | solution.py:142
  54.0 1.6 %project_rest.1 = (bf16[512,1024]{1,0:T(8,128)(2,1)S(1)}, bf16[512,1024]{1,0:T(8,128)(2,1)S(1)}, f32[32,512]{1,0:T(8,128)S(1)}) custom-call(f32[3,32,128]{2,1,0:T(8,128)S(1)} %broadcast_in_dim.33.bounds_ref, bf16[512,512]{1,0:T(8,128)(2,1)S(1)} %get-tuple-element.40.ev_ref, bf16[512,2048]{1,0:T(8,128)(2,1)S(1)} %copy-done.9, ...), custom_call_target="tpu_custom_call" | custom-call | flops 1073741824 | bytes 6291456 | tf_op jit(solution)/shard_map/project_rest/pallas_call | solution.py:142
  55.6 1.0 %copy-done.4 = bf16[512,1024]{1,0:T(8,128)(2,1)} copy-done((bf16[512,1024]{1,0:T(8,128)(2,1)}, bf16[512,1024]{1,0:T(8,128)(2,1)S(1)}, u32[]{:S(2)}) %copy-start.4) | copy-done | bytes 1048600
  56.5 1.0 %copy-done.6 = bf16[512,1024]{1,0:T(8,128)(2,1)} copy-done((bf16[512,1024]{1,0:T(8,128)(2,1)}, bf16[512,1024]{1,0:T(8,128)(2,1)S(1)}, u32[]{:S(2)}) %copy-start.6) | copy-done | bytes 1048600
  57.5 3.4 %copy-done = bf16[2048,2048]{1,0:T(8,128)(2,1)S(1)} copy-done((bf16[2048,2048]{1,0:T(8,128)(2,1)S(1)}, bf16[2048,2048]{1,0:T(8,128)(2,1)}, u32[]{:S(2)}) %copy-start) | copy-done | bytes 8388632
  60.9 2.5 %down_part.1._ = bf16[64,2048]{1,0:T(8,128)(2,1)} custom-call(f32[64,2176]{1,0:T(8,128)S(1)} %get-tuple-element.27.half_ref, bf16[64,2176]{1,0:T(8,128)(2,1)S(1)} %collective-permute-done.10.other_ref, f32[64,512]{1,0:T(8,128)S(1)} %get-tuple-element.29._.local_ref, bf16[2048,2048]{1,0:T(8,128)(2,1)S(1)} %copy-done, ...), custom_call_target="tpu_custom_call" | custom-call | flops 536870912 | bytes 8388608 | tf_op jit(solution)/shard_map/down_part/pallas_call | solution.py:142
  63.4 3.6 %all-to-all-start.1 = ((bf16[8,8,2048]{2,1,0:T(8,128)(2,1)}), bf16[8,8,2048]{2,1,0:T(8,128)(2,1)S(1)}, u32[]{:S(2)}, u32[]{:S(2)}) async-start(bf16[8,8,2048]{2,1,0:T(8,128)(2,1)} %bitcast.7), calls=%async_computation.1 | async-start | bytes 524288 | tf_op jit(solution)/shard_map/all_to_all | solution.py:383
  67.0 1.2 %copy-done.5 = bf16[512,1024]{1,0:T(8,128)(2,1)S(1)} copy-done((bf16[512,1024]{1,0:T(8,128)(2,1)S(1)}, bf16[512,1024]{1,0:T(8,128)(2,1)}, u32[]{:S(2)}) %copy-start.5) | copy-done | bytes 1048600
  68.2 1.2 %copy-done.7 = bf16[512,1024]{1,0:T(8,128)(2,1)S(1)} copy-done((bf16[512,1024]{1,0:T(8,128)(2,1)S(1)}, bf16[512,1024]{1,0:T(8,128)(2,1)}, u32[]{:S(2)}) %copy-start.7) | copy-done | bytes 1048600
  69.5 4.9 %attend_rest.1.sums_g_ref = f32[32,512]{1,0:T(8,128)S(1)} custom-call(f32[3,32,128]{2,1,0:T(8,128)S(1)} %broadcast_in_dim.33.bounds_ref, f32[8,512]{1,0:T(8,128)S(1)} %broadcast_in_dim.34.gain_ref, bf16[512,1024]{1,0:T(8,128)(2,1)S(1)} %copy-done.5, bf16[512,1024]{1,0:T(8,128)(2,1)S(1)} %copy-done.3, bf16[512,1024]{1,0:T(8,128)(2,1)S(1)} %copy-done.7, ...), custom_call_target="tpu_custom_call" | custom-call | flops 1073741824 | bytes 6291456 | tf_op jit(solution)/shard_map/attend_rest/pallas_call | solution.py:142
  (43 shorter events, 3.7 us)
Async XLA Ops:
  0.6 22.5 %copy-start.10 = (bf16[128,2048]{1,0:T(8,128)(2,1)S(1)}, bf16[128,2048]{1,0:T(8,128)(2,1)}, u32[]{:S(2)}) copy-start(bf16[128,2048]{1,0:T(8,128)(2,1)} %param.13) | copy-start | bytes 1572868
  0.6 21.7 %copy-start.12 = (s32[1,32]{1,0:T(1,128)S(1)}, s32[1,32]{1,0:T(1,128)}, u32[]{:S(2)}) copy-start(s32[1,32]{1,0:T(1,128)} %param.12) | copy-start | bytes 388
  2.4 16.2 %collective-permute-start = (bf16[160,512]{1,0:T(8,128)(2,1)S(1)}, bf16[160,512]{1,0:T(8,128)(2,1)S(1)}, u32[]{:S(2)}, u32[]{:S(2)}) collective-permute-start(bf16[160,512]{1,0:T(8,128)(2,1)S(1)} %pad_maximum_fusion.1), channel_id=1, source_target_pairs={{0,8},{4,12},{8,0},{12,4},{1,9},{5,13},{9,1},{13,5},{2,10},{6,14},... | collective-permute-start | bytes 491528 | tf_op jit(solution)/shard_map/ppermute | solution.py:22
  6.5 12.1 %collective-permute-start.1 = (bf16[160,512]{1,0:T(8,128)(2,1)S(1)}, bf16[160,512]{1,0:T(8,128)(2,1)S(1)}, u32[]{:S(2)}, u32[]{:S(2)}) collective-permute-start(bf16[160,512]{1,0:T(8,128)(2,1)S(1)} %pad_maximum_fusion.1), channel_id=1, source_target_pairs={{0,12},{4,8},{8,4},{12,0},{1,13},{5,9},{9,5},{13,1},{2,14},{6,10},... | collective-permute-start | bytes 491528 | tf_op jit(solution)/shard_map/ppermute | solution.py:22
  7.9 11.3 %collective-permute-start.2 = (bf16[160,512]{1,0:T(8,128)(2,1)S(1)}, bf16[160,512]{1,0:T(8,128)(2,1)S(1)}, u32[]{:S(2)}, u32[]{:S(2)}) collective-permute-start(bf16[160,512]{1,0:T(8,128)(2,1)S(1)} %pad_maximum_fusion.1), channel_id=1, source_target_pairs={{0,4},{4,0},{8,12},{12,8},{1,5},{5,1},{9,13},{13,9},{2,6},{6,2},{1... | collective-permute-start | bytes 491528 | tf_op jit(solution)/shard_map/ppermute | solution.py:22
  9.9 33.6 %collective-permute-start.7 = (bf16[528,512]{1,0:T(8,128)(2,1)S(1)}, bf16[528,512]{1,0:T(8,128)(2,1)S(1)}, u32[]{:S(2)}, u32[]{:S(2)}) collective-permute-start(bf16[528,512]{1,0:T(8,128)(2,1)S(1)} %pad_maximum_fusion.next_ref.refs_0_), channel_id=1, source_target_pairs={{0,1},{1,0},{2,3},{3,2},{4,5},{5,4},{6,7},{7,6},{8,9},{9,8},{10,11... | collective-permute-start | bytes 1622024 | tf_op jit(solution)/shard_map/ppermute | solution.py:22
  11.5 32.1 %collective-permute-start.8 = (bf16[528,512]{1,0:T(8,128)(2,1)S(1)}, bf16[528,512]{1,0:T(8,128)(2,1)S(1)}, u32[]{:S(2)}, u32[]{:S(2)}) collective-permute-start(bf16[528,512]{1,0:T(8,128)(2,1)S(1)} %pad_maximum_fusion.next_ref.refs_0_), channel_id=1, source_target_pairs={{0,2},{1,3},{2,0},{3,1},{4,6},{5,7},{6,4},{7,5},{8,10},{9,11},{10,... | collective-permute-start | bytes 1622024 | tf_op jit(solution)/shard_map/ppermute | solution.py:22
  19.2 9.5 %collective-permute-start.3 = (bf16[3,160,256]{2,1,0:T(8,128)(2,1)S(1)}, bf16[3,160,256]{2,1,0:T(8,128)(2,1)S(1)}, u32[]{:S(2)}, u32[]{:S(2)}) collective-permute-start(bf16[3,160,256]{2,1,0:T(8,128)(2,1)S(1)} %get-tuple-element.22), channel_id=1, source_target_pairs={{0,1},{1,0},{2,3},{3,2},{4,5},{5,4},{6,7},{7,6},{8,9},{9,8},{10,11... | collective-permute-start | bytes 737288 | tf_op jit(solution)/shard_map/ppermute | solution.py:22
  20.8 9.1 %collective-permute-start.4 = (bf16[3,160,256]{2,1,0:T(8,128)(2,1)S(1)}, bf16[3,160,256]{2,1,0:T(8,128)(2,1)S(1)}, u32[]{:S(2)}, u32[]{:S(2)}) collective-permute-start(bf16[3,160,256]{2,1,0:T(8,128)(2,1)S(1)} %get-tuple-element.23), channel_id=1, source_target_pairs={{0,2},{1,3},{2,0},{3,1},{4,6},{5,7},{6,4},{7,5},{8,10},{9,11},{10,... | collective-permute-start | bytes 737288 | tf_op jit(solution)/shard_map/ppermute | solution.py:22
  23.1 10.5 %copy-start.11 = (f32[512]{0:T(512)S(1)}, f32[512]{0:T(512)}, u32[]{:S(2)}) copy-start(f32[512]{0:T(512)} %param.15) | copy-start | bytes 6148
  23.2 10.4 %collective-permute-start.5 = (bf16[2,3,160,256]{3,2,1,0:T(8,128)(2,1)S(1)}, bf16[2,3,160,256]{3,2,1,0:T(8,128)(2,1)S(1)}, u32[]{:S(2)}, u32[]{:S(2)}) collective-permute-start(bf16[2,3,160,256]{3,2,1,0:T(8,128)(2,1)S(1)} %get-tuple-element.21.refs_4_), channel_id=1, source_target_pairs={{0,16},{16,0},{1,17},{17,1},{2,18},{18,2},{3,19},{19,3},{4,20},{20... | collective-permute-start | bytes 1474568 | tf_op jit(solution)/shard_map/ppermute | solution.py:22
  30.8 2.8 %collective-permute-start.6 = (bf16[2,3,160,256]{3,2,1,0:T(8,128)(2,1)S(1)}, bf16[2,3,160,256]{3,2,1,0:T(8,128)(2,1)S(1)}, u32[]{:S(2)}, u32[]{:S(2)}) collective-permute-start(bf16[2,3,160,256]{3,2,1,0:T(8,128)(2,1)S(1)} %get-tuple-element.24.refs_5_), channel_id=1, source_target_pairs={{0,16},{16,0},{1,17},{17,1},{2,18},{18,2},{3,19},{19,3},{4,20},{20... | collective-permute-start | bytes 1474568 | tf_op jit(solution)/shard_map/ppermute | solution.py:22
  30.8 15.8 %collective-permute-start.9 = (bf16[528,512]{1,0:T(8,128)(2,1)}, bf16[528,512]{1,0:T(8,128)(2,1)S(1)}, u32[]{:S(2)}, u32[]{:S(2)}) collective-permute-start(bf16[528,512]{1,0:T(8,128)(2,1)} %get-tuple-element.26), channel_id=1, source_target_pairs={{0,3},{1,2},{2,1},{3,0},{4,7},{5,6},{6,5},{7,4},{8,11},{9,10},{10,... | collective-permute-start | bytes 1622024 | tf_op jit(solution)/shard_map/ppermute | solution.py:22
  37.8 1.0 %copy-start.2 = (bf16[512,1024]{1,0:T(8,128)(2,1)}, bf16[512,1024]{1,0:T(8,128)(2,1)S(1)}, u32[]{:S(2)}) copy-start(bf16[512,1024]{1,0:T(8,128)(2,1)S(1)} %get-tuple-element.34.kv_first) | copy-start | bytes 3145732
  38.8 1.4 %copy-start.8 = (bf16[512,2048]{1,0:T(8,128)(2,1)}, bf16[512,2048]{1,0:T(8,128)(2,1)S(1)}, u32[]{:S(2)}) copy-start(bf16[512,2048]{1,0:T(8,128)(2,1)S(1)} %get-tuple-element.30.w_ref) | copy-start | bytes 6291460
  40.2 8.2 %all-to-all-start = ((bf16[8,8,512]{2,1,0:T(8,128)(2,1)}), bf16[8,8,512]{2,1,0:T(8,128)(2,1)S(1)}, u32[]{:S(2)}, u32[]{:S(2)}) async-start(bf16[8,8,512]{2,1,0:T(8,128)(2,1)} %bitcast.4), calls=%async_computation | async-start | bytes 131072 | tf_op jit(solution)/shard_map/all_to_all | solution.py:346
  48.4 3.4 %copy-start.1 = (bf16[2048,2048]{1,0:T(8,128)(2,1)S(1)}, bf16[2048,2048]{1,0:T(8,128)(2,1)}, u32[]{:S(2)}) copy-start(bf16[2048,2048]{1,0:T(8,128)(2,1)} %refs_4_.1) | copy-start | bytes 25165828
  51.8 2.2 %copy-start.9 = (bf16[512,2048]{1,0:T(8,128)(2,1)S(1)}, bf16[512,2048]{1,0:T(8,128)(2,1)}, u32[]{:S(2)}) copy-start(bf16[512,2048]{1,0:T(8,128)(2,1)} %copy-done.8) | copy-start | bytes 6291460
  53.8 3.7 %collective-permute-start.10 = (bf16[64,2176]{1,0:T(8,128)(2,1)S(1)}, bf16[64,2176]{1,0:T(8,128)(2,1)S(1)}, u32[]{:S(2)}, u32[]{:S(2)}) collective-permute-start(bf16[64,2176]{1,0:T(8,128)(2,1)S(1)} %get-tuple-element.28), channel_id=1, source_target_pairs={{0,16},{16,0},{1,17},{17,1},{2,18},{18,2},{3,19},{19,3},{4,20},{20... | collective-permute-start | bytes 835592 | tf_op jit(solution)/shard_map/ppermute | solution.py:22
  55.5 1.0 %copy-start.4 = (bf16[512,1024]{1,0:T(8,128)(2,1)}, bf16[512,1024]{1,0:T(8,128)(2,1)S(1)}, u32[]{:S(2)}) copy-start(bf16[512,1024]{1,0:T(8,128)(2,1)S(1)} %get-tuple-element.33.qg_ref) | copy-start | bytes 3145732
  56.5 1.0 %copy-start.6 = (bf16[512,1024]{1,0:T(8,128)(2,1)}, bf16[512,1024]{1,0:T(8,128)(2,1)S(1)}, u32[]{:S(2)}) copy-start(bf16[512,1024]{1,0:T(8,128)(2,1)S(1)} %get-tuple-element.35.kv_ref) | copy-start | bytes 3145732
  57.5 3.4 %copy-start = (bf16[2048,2048]{1,0:T(8,128)(2,1)S(1)}, bf16[2048,2048]{1,0:T(8,128)(2,1)}, u32[]{:S(2)}) copy-start(bf16[2048,2048]{1,0:T(8,128)(2,1)} %w_ref.1) | copy-start | bytes 25165828
  60.9 6.1 %copy-start.3 = (bf16[512,1024]{1,0:T(8,128)(2,1)S(1)}, bf16[512,1024]{1,0:T(8,128)(2,1)}, u32[]{:S(2)}) copy-start(bf16[512,1024]{1,0:T(8,128)(2,1)} %copy-done.2) | copy-start | bytes 3145732
  63.4 11.0 %all-to-all-start.1 = ((bf16[8,8,2048]{2,1,0:T(8,128)(2,1)}), bf16[8,8,2048]{2,1,0:T(8,128)(2,1)S(1)}, u32[]{:S(2)}, u32[]{:S(2)}) async-start(bf16[8,8,2048]{2,1,0:T(8,128)(2,1)} %bitcast.7), calls=%async_computation.1 | async-start | bytes 524288 | tf_op jit(solution)/shard_map/all_to_all | solution.py:383
  67.0 1.2 %copy-start.5 = (bf16[512,1024]{1,0:T(8,128)(2,1)S(1)}, bf16[512,1024]{1,0:T(8,128)(2,1)}, u32[]{:S(2)}) copy-start(bf16[512,1024]{1,0:T(8,128)(2,1)} %copy-done.4) | copy-start | bytes 3145732
  68.2 1.2 %copy-start.7 = (bf16[512,1024]{1,0:T(8,128)(2,1)S(1)}, bf16[512,1024]{1,0:T(8,128)(2,1)}, u32[]{:S(2)}) copy-start(bf16[512,1024]{1,0:T(8,128)(2,1)} %copy-done.6) | copy-start | bytes 3145732

commit v7 on v5

--- a/solution.py
+++ b/solution.py
@@ -26,12 +26,16 @@
     return h + h * jnp.tanh(h)
 
 
+def order_of(dps):
+    return [0, *range(2, dps), 1]
+
+
 def in_order(ref, at, dps):
     if dps == 1:
         return ref[at, :]
     z = lax.axis_index("dp")
     cols = ref.shape[1] // dps
-    return jnp.concatenate([ref[at, pl.ds(pl.multiple_of((z ^ k) * cols, cols), cols)] for k in range(dps)], axis=1)
+    return jnp.concatenate([ref[at, pl.ds(pl.multiple_of((z ^ k) * cols, cols), cols)] for k in order_of(dps)], axis=1)
 
 
 def project(dps, row0, hist, ev_ref, w_ref, gate_ref, q_ref, kv_ref):
@@ -127,10 +131,12 @@
     out_ref[...] = sums_ev_ref[...] + jnp.dot(member, ev_ref[...], preferred_element_type=F32)
 
 
-def attend_kernel(row0, bounds_ref, gain_ref, qg_ref, kv_first, kv_ref, sums_ref, _, out_ref, att_ref):
+def attend_kernel(row0, at, rows, bounds_ref, gain_ref, qg_ref, kv_first, kv_ref, sums_ref, _, out_ref, att_ref):
+    here = pl.ds(at, rows)
     q_ref, gate_ref = halves(qg_ref)
-    member = membership(bounds_ref, row0, q_ref.shape[0])
-    gated = attend(q_ref, [kv_first, kv_ref], gate_ref, gain_ref, att_ref)
+    member = membership(bounds_ref, row0 + at, rows)
+    kv_refs = [kv_first, kv_ref.at[: at + rows]]
+    gated = attend(q_ref.at[here], kv_refs, gate_ref.at[here], gain_ref, att_ref)
     out_ref[...] = sums_ref[...] + jnp.dot(member, gated, preferred_element_type=F32)
 
 
@@ -163,7 +169,7 @@
     depth, wide = w_uvqk.shape
     width = w_out.shape[1]
     w_in = jnp.concatenate([w_in, jnp.broadcast_to(ffn_gain, (16, w_in.shape[1]))], axis=0)
-    if (sections, dps, mps) != (2, 4, 4) or wide != 4 * width or depth % 128:
+    if (sections, mps) != (2, 4) or wide != 4 * width or depth % 128:
         ws = [lax.all_gather(x, "dp", axis=0, tiled=True) for x in (w_uvqk, w_out)]
         blocks = [[w_in]] + [[swap(w_in, "mp", mps, k)] for k in range(1, mps)]
 
@@ -184,22 +190,20 @@
         ],
         axis=0,
     )
-    near, far = swap(mine, "dp", dps, 1), swap(mine, "dp", dps, 2)
-    parts, owners = [w_uvqk[:, : wide // 2], w_uvqk[:, wide // 2 :], w_out[: depth // 2], w_out[depth // 2 :]], []
-    for at, got in ((1, [near, far]), (3, [swap(far, "dp", dps, 1)])):
-        left, right = call(
-            split_kernel,
-            f"split_{at}",
-            got,
-            [((len(got), depth + part, cut), BF16)] * 2,
-            [],
-            8,
-            0,
-            16 * 1024 * 1024,
-        )
-        plane = [left, right, swap(left, "mp", mps, 1), swap(right, "mp", mps, 2)]
-        parts = parts + plane + [swap(p, "section", sections, 1) for p in plane]
-        owners = owners + [(at, i // 4, i // 2 % 2, i % 2 * cut) for i in range(8)]
+    got = [swap(mine, "dp", dps, k) for k in order_of(dps)[1:]]
+    left, right = call(
+        split_kernel,
+        "split",
+        got,
+        [((len(got), depth + part, cut), BF16)] * 2,
+        [],
+        8,
+        0,
+        16 * 1024 * 1024,
+    )
+    plane = [left, right, swap(left, "mp", mps, 1), swap(right, "mp", mps, 2)]
+    parts = [w_uvqk[:, : wide // 2], w_uvqk[:, wide // 2 :], w_out[: depth // 2], w_out[depth // 2 :]]
+    parts = parts + plane + [swap(p, "section", sections, 1) for p in plane]
 
     from_x, from_y = swap(w_in, "mp", mps, 1), swap(w_in, "mp", mps, 2)
     middle = w_in.shape[0] // 32 * 16
@@ -210,11 +214,12 @@
         for i in range(2):
             w_ref[:depth, i * (wide // 2) : (i + 1) * (wide // 2)] = parts[i][...]
             wout_ref[i * (depth // 2) : (i + 1) * (depth // 2)] = parts[2 + i][...]
-        for ref, (first, other_sec, other_half, at) in zip(parts[4:], owners):
-            owner = (sec ^ other_sec) * 2 + (parity(m) ^ other_half)
+        for i, ref in enumerate(parts[4:]):
+            owner = (sec ^ (i // 4)) * 2 + (parity(m) ^ (i // 2 % 2))
+            at = i % 2 * cut
             cols = pl.ds(pl.multiple_of(owner * width + at, cut), cut)
-            for k in range(ref.shape[0]):
-                row = (first + k) * depth
+            for k in range(dps - 1):
+                row = (k + 1) * depth
                 w_ref[row : row + depth, cols] = ref[k, :depth]
                 rows = pl.ds(pl.multiple_of(row + owner * part, part), part)
                 wout_ref[rows, at : at + cut] = ref[k, depth:]
@@ -259,7 +264,8 @@
     send_ref[:, wide:] = two_terms(square)
 
 
-def down_kernel(chunks, half_ref, other_ref, local_ref, w_ref, _, out_ref, part_ref):
+def down_kernel(chunks, sections, mps, take, half_ref, other_ref, local_ref, w_ref, _, own_ref, *refs):
+    *send_refs, part_ref = refs
     units, wide = w_ref.shape
     each = wide // chunks
     square = half_ref[:, units : units + 1] + jnp.sum(other_ref[:, units:].astype(F32), axis=1, keepdims=True)
@@ -273,18 +279,30 @@
     cols = local_ref.shape[1]
     own = pl.ds(pl.multiple_of(m * cols, cols), cols)
     part_ref[:, own] = part_ref[:, own] + local_ref[...]
-    out_ref[...] = part_ref[...].astype(BF16)
-
-
-def finish_kernel(sections, mps, dps, got_ref, bounds_ref, sums_ev_ref, sums_g_ref, wout_ref, out_ref, pooled_ref):
+    for k, ref in enumerate([own_ref, *send_refs]):
+        starts = [pl.multiple_of((s * mps + (m ^ k)) * take, take) for s in range(sections)]
+        mine = [part_ref[pl.ds(start, take), :] for start in starts]
+        ref[...] = jnp.concatenate(mine, axis=0).astype(ref.dtype)
+
+
+def add_kernel(own_ref, *refs):
+    *got_refs, _, keep_ref, send_ref, total_ref = refs
+    total = own_ref[...]
+    for ref in got_refs:
+        total = total + ref[...].astype(F32)
+    total_ref[...] = total
+    sec = lax.axis_index("section")
+    take = keep_ref.shape[0]
+    keep_ref[...] = total_ref[pl.ds(pl.multiple_of(sec * take, take), take), :]
+    send_ref[...] = total_ref[pl.ds(pl.multiple_of((1 - sec) * take, take), take), :]
+
+
+def finish_kernel(dps, keep_ref, got_ref, bounds_ref, sums_ev_ref, sums_g_ref, wout_ref, out_ref, pooled_ref):
     pooled_ref[...] = pool(dps, bounds_ref, sums_ev_ref[...], sums_g_ref, wout_ref).astype(BF16)
-    got = got_ref[...].astype(F32)
-    take, wide = out_ref.shape[0], got.shape[1]
-    for s in range(sections):
-        total = got[s * mps * take : (s * mps + 1) * take]
-        for k in range(s * mps + 1, (s + 1) * mps):
-            total = total + got[k * take : (k + 1) * take]
-        out_ref[:, s * wide : (s + 1) * wide] = total.astype(BF16)
+    sec = lax.axis_index("section")
+    wide = keep_ref.shape[1]
+    out_ref[:, pl.ds(pl.multiple_of(sec * wide, wide), wide)] = keep_ref[...].astype(BF16)
+    out_ref[:, pl.ds(pl.multiple_of((1 - sec) * wide, wide), wide)] = got_ref[...].astype(BF16)
 
 
 def per_device(sections, dps, mps, events, hist_len, sess_len, w_uvqk, w_out, attn_gain, w_in, ffn_gain, w_up, w_down):
@@ -355,35 +373,50 @@
         6 * 1024 * 1024,
         4 * rest * width,
     )
-    (partial,) = call(
-        functools.partial(down_kernel, 4),
+    pair = sections * take
+    own, *sends = call(
+        functools.partial(down_kernel, 4, sections, mps, take),
         "down_part",
         [half, other, local, w_down, sums_ev],
-        [((rows, half_width), BF16)],
+        [((pair, half_width), F32)] + [((pair, half_width), BF16)] * (mps - 1),
         [pltpu.VMEM((rows, half_width), F32)],
         8,
         2 * rows * w_down.size,
         2 * w_down.size,
         rows * units,
     )
-    arrived = lax.all_to_all(
-        partial.reshape(peers, take, half_width), group, split_axis=0, concat_axis=0, tiled=True
-    ).reshape(rows, half_width)
-    (sums_g,) = call(
-        functools.partial(attend_kernel, first),
-        "attend_rest",
-        [bounds, gain, queries_gate, kv_first, kv_rest, sums_g, partial],
-        [((sess, width), F32)],
-        [pltpu.VMEM((rest, width), F32)],
-        10,
-        4 * rest * length * width,
-        6 * 1024 * 1024,
-        HEADS * rest * length,
-    )
+
+    def attend_part(at, count, sums, after):
+        return call(
+            functools.partial(attend_kernel, first, at, count),
+            f"attend_{at}",
+            [bounds, gain, queries_gate, kv_first, kv_rest, sums, after],
+            [((sess, width), F32)],
+            [pltpu.VMEM((count, width), F32)],
+            10,
+            4 * count * (first + at + count) * width,
+            4 * 1024 * 1024,
+            HEADS * count * (first + at + count),
+        )[0]
+
+    got = [swap(x, "mp", mps, k + 1) for k, x in enumerate(sends)]
+    sums_g = attend_part(0, rest // 2, sums_g, own)
+    keep, send = call(
+        add_kernel,
+        "add_parts",
+        [own, *got, sums_g],
+        [((take, half_width), F32)] * 2,
+        [pltpu.VMEM((pair, half_width), F32)],
+        8,
+        mps * pair * half_width,
+        2 * mps * pair * half_width,
+    )
+    got = swap(send, "section", sections, 1)
+    sums_g = attend_part(rest // 2, rest - rest // 2, sums_g, keep)
     cross_out, pooled = call(
-        functools.partial(finish_kernel, sections, mps, dps),
+        functools.partial(finish_kernel, dps),
         "finish",
-        [arrived, bounds, sums_ev, sums_g, full_wout],
+        [keep, got, bounds, sums_ev, sums_g, full_wout],
         [((take, half_width * sections), BF16), ((sess, width), BF16)],
         [],
         8,

time: 71.6 us -> 59.6 us (0.83)
  waiting for transfers between devices: 20.4 us -> 13.5 us
  starting transfers between devices: 20 us -> 18.5 us
  local copies, waits for them, and re-layouts: 3.3 us -> 2.08 us
  Pallas kernels: 15.4 us -> 14.2 us
  blocking collectives: 8.51 us -> 7.52 us
    ppermute x20 -> x18, waiting for transfers between devices: 20.2 us -> 13.5 us  [swap(): return lax.ppermute(x, axis, [(i, i ^ flip) for i in range(size)])]
    all_to_all x1 -> x0, starting transfers between devices: 3.59 us -> none  [per_device(): lax.all_to_all(partial.reshape(peers, take, half_width), group, split_axi...]
    ppermute x20 -> x18, starting transfers between devices: 16.4 us -> 18.5 us  [swap(): return lax.ppermute(x, axis, [(i, i ^ flip) for i in range(size)])]
    unnamed x20 -> x16, local copies, waits for them, and re-layouts: 1.27 us -> 0.04 us
    pallas_call x8 -> x9, Pallas kernels: 15.4 us -> 14.2 us  [call(): pl.pallas_call(kernel, in_specs=[VMEM] * len(operands), out_specs=[VMEM]...]
    all_to_all x1, blocking collectives: 8.51 us -> 7.52 us  [per_device(): lax.all_to_all(micro_rows.reshape(peers, take, width), group, split_axis=...]
  transfers between devices with their start and end apart: 21 -> 18, of which waited for: 8 -> 4; matrix products, arithmetic and copies ran while one was open for 3% -> 4% of each run, Pallas kernels for 14% -> 16%
where the time goes in v7:
time: 59.6 us; the launch traced here: 59.3 us
  starting transfers between devices  18.5 us (31%)
  Pallas kernels  14.2 us (24%)
  waiting for transfers between devices  13.5 us (23%)
  blocking collectives  7.52 us (13%)
  local copies, waits for them, and re-layouts  2.08 us (3%)
  other arithmetic  1.96 us (3%)
  between operations  1.58 us (3%)
    ppermute x18, starting transfers between devices, swap(): return lax.ppermute(x, axis, [(i, i ^ flip) for i in range(size)])  18.5 us
    pallas_call x9, Pallas kernels, call(): pl.pallas_call(kernel, in_specs=[VMEM] * len(operands), out_specs=[VMEM]...  14.2 us
    ppermute x18, waiting for transfers between devices, swap(): return lax.ppermute(x, axis, [(i, i ^ flip) for i in range(size)])  13.5 us
    all_to_all x1, blocking collectives, per_device(): lax.all_to_all(micro_rows.reshape(peers, take, width), group, split_axis=...  7.52 us
  transfers between devices with their start and end apart: 18, of which 4 were waited for; matrix products, arithmetic and copies ran while one was open for 4% of the time, Pallas kernels for 16%

profile of v7, /device:TPU:0, one launch (start us, length us, event | category | flops | bytes accessed | tf_op | source)
XLA Modules:
  0.0 59.3 jit_solution(3649689136854747708)
XLA Ops:
  0.7 1.0 %constant_dynamic-slice_fusion.1 = bf16[128,512]{1,0:T(8,128)(2,1)S(1)} fusion(bf16[128,2048]{1,0:T(8,128)(2,1)} %param.13, s32[]{:T(128)S(6)} %select_n.11), kind=kLoop, calls=%fused_computation.10 | loop fusion | bytes 262148 | tf_op jit(solution)/shard_map/dynamic_slice | solution.py:188
  1.7 0.8 %constant_dynamic-slice_fusion = bf16[32,512]{1,0:T(8,128)(2,1)S(1)} fusion(bf16[128,512]{1,0:T(8,128)(2,1)} %param.14, s32[]{:T(128)S(6)} %select_n.12), kind=kLoop, calls=%fused_computation.9 | loop fusion | bytes 65540 | tf_op jit(solution)/shard_map/dynamic_slice | solution.py:189
  2.5 4.1 %collective-permute-start = (bf16[160,512]{1,0:T(8,128)(2,1)S(1)}, bf16[160,512]{1,0:T(8,128)(2,1)S(1)}, u32[]{:S(2)}, u32[]{:S(2)}) collective-permute-start(bf16[160,512]{1,0:T(8,128)(2,1)S(1)} %pad_maximum_fusion.1), channel_id=1, source_target_pairs={{0,8},{4,12},{8,0},{12,4},{1,9},{5,13},{9,1},{13,5},{2,10},{6,14},... | collective-permute-start | bytes 491528 | tf_op jit(solution)/shard_map/ppermute | solution.py:22
  6.6 1.3 %collective-permute-start.1 = (bf16[160,512]{1,0:T(8,128)(2,1)S(1)}, bf16[160,512]{1,0:T(8,128)(2,1)S(1)}, u32[]{:S(2)}, u32[]{:S(2)}) collective-permute-start(bf16[160,512]{1,0:T(8,128)(2,1)S(1)} %pad_maximum_fusion.1), channel_id=1, source_target_pairs={{0,12},{4,8},{8,4},{12,0},{1,13},{5,9},{9,5},{13,1},{2,14},{6,10},... | collective-permute-start | bytes 491528 | tf_op jit(solution)/shard_map/ppermute | solution.py:22
  7.9 0.2 collective-permute-start.2
  8.2 0.7 %reduce = bf16[512]{0:T(512)(128)(2,1)S(1)} reduce(bf16[1,512]{1,0:T(2,128)(2,1)} %param.17, bf16[]{:T(256)} %constant.27), dimensions={0}, to_apply=%param.17.reduce_sub_computation | reduce | bytes 2050 | tf_op args[7]
  8.9 1.1 %pad_maximum_fusion.refs_0_ = bf16[528,512]{1,0:T(8,128)(2,1)S(1)} fusion(bf16[16,512]{1,0:T(8,128)(2,1)S(1)} %broadcast_in_dim.36, bf16[512,512]{1,0:T(8,128)(2,1)} %param.16), kind=kLoop, calls=%fused_computation | loop fusion | flops 1081344 | bytes 1081344 | tf_op jit(solution)/shard_map/concatenate | solution.py:171
  10.0 1.6 %collective-permute-start.10 = (bf16[528,512]{1,0:T(8,128)(2,1)S(1)}, bf16[528,512]{1,0:T(8,128)(2,1)S(1)}, u32[]{:S(2)}, u32[]{:S(2)}) collective-permute-start(bf16[528,512]{1,0:T(8,128)(2,1)S(1)} %pad_maximum_fusion.refs_0_), channel_id=1, source_target_pairs={{0,2},{1,3},{2,0},{3,1},{4,6},{5,7},{6,4},{7,5},{8,10},{9,11},{10,... | collective-permute-start | bytes 1622024 | tf_op jit(solution)/shard_map/ppermute | solution.py:22
  11.6 1.5 %collective-permute-start.9 = (bf16[528,512]{1,0:T(8,128)(2,1)S(1)}, bf16[528,512]{1,0:T(8,128)(2,1)S(1)}, u32[]{:S(2)}, u32[]{:S(2)}) collective-permute-start(bf16[528,512]{1,0:T(8,128)(2,1)S(1)} %pad_maximum_fusion.refs_0_), channel_id=1, source_target_pairs={{0,1},{1,0},{2,3},{3,2},{4,5},{5,4},{6,7},{7,6},{8,9},{9,8},{10,11... | collective-permute-start | bytes 1622024 | tf_op jit(solution)/shard_map/ppermute | solution.py:22
  13.2 5.4 %collective-permute-done.refs_0_ = bf16[160,512]{1,0:T(8,128)(2,1)S(1)} collective-permute-done((bf16[160,512]{1,0:T(8,128)(2,1)S(1)}, bf16[160,512]{1,0:T(8,128)(2,1)S(1)}, u32[]{:S(2)}, u32[]{:S(2)}) %collective-permute-start) | collective-permute-done | bytes 163872 | tf_op jit(solution)/shard_map/ppermute | solution.py:22
  18.7 0.5 collective-permute-done.2.refs_2_
  19.2 1.6 %collective-permute-start.3 = (bf16[3,160,256]{2,1,0:T(8,128)(2,1)S(1)}, bf16[3,160,256]{2,1,0:T(8,128)(2,1)S(1)}, u32[]{:S(2)}, u32[]{:S(2)}) collective-permute-start(bf16[3,160,256]{2,1,0:T(8,128)(2,1)S(1)} %get-tuple-element.24.refs_4_), channel_id=1, source_target_pairs={{0,1},{1,0},{2,3},{3,2},{4,5},{5,4},{6,7},{7,6},{8,9},{9,8},{10,11... | collective-permute-start | bytes 737288 | tf_op jit(solution)/shard_map/ppermute | solution.py:22
  20.8 1.5 %collective-permute-start.4 = (bf16[3,160,256]{2,1,0:T(8,128)(2,1)S(1)}, bf16[3,160,256]{2,1,0:T(8,128)(2,1)S(1)}, u32[]{:S(2)}, u32[]{:S(2)}) collective-permute-start(bf16[3,160,256]{2,1,0:T(8,128)(2,1)S(1)} %get-tuple-element.25.refs_5_), channel_id=1, source_target_pairs={{0,2},{1,3},{2,0},{3,1},{4,6},{5,7},{6,4},{7,5},{8,10},{9,11},{10,... | collective-permute-start | bytes 737288 | tf_op jit(solution)/shard_map/ppermute | solution.py:22
  22.5 0.1 select_reduce_fusion
  23.2 6.8 %collective-permute-done.3.refs_6_ = bf16[3,160,256]{2,1,0:T(8,128)(2,1)S(1)} collective-permute-done((bf16[3,160,256]{2,1,0:T(8,128)(2,1)S(1)}, bf16[3,160,256]{2,1,0:T(8,128)(2,1)S(1)}, u32[]{:S(2)}, u32[]{:S(2)}) %collective-permute-start.3) | collective-permute-done | bytes 245792 | tf_op jit(solution)/shard_map/ppermute | solution.py:22
  30.1 0.5 collective-permute-start.7
  30.7 1.6 %collective-permute-start.12 = (bf16[272,512]{1,0:T(8,128)(2,1)S(1)}, bf16[272,512]{1,0:T(8,128)(2,1)S(1)}, u32[]{:S(2)}, u32[]{:S(2)}) collective-permute-start(bf16[272,512]{1,0:T(8,128)(2,1)S(1)} %slice.41), channel_id=1, source_target_pairs={{0,1},{1,0},{2,3},{3,2},{4,5},{5,4},{6,7},{7,6},{8,9},{9,8},{10,11... | collective-permute-start | bytes 835592 | tf_op jit(solution)/shard_map/ppermute | solution.py:22
  32.3 0.6 collective-permute-start.11
  32.9 0.1 broadcast_in_dim.33.bounds_ref
  33.0 3.5 %encode_first.1 = (bf16[64,512]{1,0:T(8,128)(2,1)S(1)}, bf16[512,2048]{1,0:T(8,128)(2,1)S(1)}, bf16[512,512]{1,0:T(8,128)(2,1)S(1)}, bf16[512,1024]{1,0:T(8,128)...) custom-call(f32[3,32,128]{2,1,0:T(8,128)S(1)} %broadcast_in_dim.33.bounds_ref, ...), custom_call_target="tpu_custom_call" | custom-call | flops 1342177280 | bytes 6291456 | tf_op jit(solution)/shard_map/encode_first/pallas_call | solution.py:144
  36.5 7.5 %all_to_all.5 = bf16[8,8,512]{2,1,0:T(8,128)(2,1)S(1)} all-to-all(bf16[8,8,512]{2,1,0:T(8,128)(2,1)S(1)} %bitcast.16), channel_id=1, replica_groups=mesh['section'=2,'dp'=4,'mp'=4] {'section','mp'}, dimensions={0} | all-to-all | bytes 131072 | tf_op jit(solution)/shard_map/all_to_all | solution.py:350
  44.1 2.0 %up_half.1 = (f32[64,512]{1,0:T(8,128)S(1)}, f32[64,2176]{1,0:T(8,128)S(1)}, bf16[64,2176]{1,0:T(8,128)(2,1)S(1)}) custom-call(bf16[64,512]{1,0:T(8,128)(2,1)S(1)} %bitcast.15, bf16[528,512]{1,0:T(8,128)(2,1)S(1)} %pad_maximum_fusion.refs_0_, bf16[528,512]{1,0:T(8,128)(2,1)S(1)} %collective-permute-done.9.refs_1_, ...), custom_call_target="tpu_custom_call" | custom-call | flops 536870912 | bytes 8388608 | tf_op jit(solution)/shard_map/up_half/pallas_call | solution.py:144
  46.1 0.2 collective-permute-start.13
  46.3 1.6 %project_rest.1 = (bf16[512,1024]{1,0:T(8,128)(2,1)S(1)}, bf16[512,1024]{1,0:T(8,128)(2,1)S(1)}, f32[32,512]{1,0:T(8,128)S(1)}) custom-call(f32[3,32,128]{2,1,0:T(8,128)S(1)} %broadcast_in_dim.33.bounds_ref, bf16[512,512]{1,0:T(8,128)(2,1)S(1)} %get-tuple-element.46.ev_ref, bf16[512,2048]{1,0:T(8,128)(2,1)S(1)} %get-tuple-element.30.w_ref, ...), custom_call_target="tpu_custom_call" | custom-call | flops 1073741824 | bytes 6291456 | tf_op jit(solution)/shard_map/project_rest/pallas_call | solution.py:144
  47.9 1.8 %down_part.1 = (f32[16,2048]{1,0:T(8,128)S(1)}, bf16[16,2048]{1,0:T(8,128)(2,1)S(1)}, bf16[16,2048]{1,0:T(8,128)(2,1)S(1)}, bf16[16,2048]{1,0:T(8,128)(2,1)S(1)}) custom-call(f32[64,2176]{1,0:T(8,128)S(1)} %get-tuple-element.27.half_ref, bf16[64,2176]{1,0:T(8,128)(2,1)S(1)} %collective-permute-done.13.other_ref, ...), custom_call_target="tpu_custom_call" | custom-call | flops 536870912 | bytes 8388608 | tf_op jit(solution)/shard_map/down_part/pallas_call | solution.py:144
  49.7 0.6 %collective-permute-start.14 = (bf16[16,2048]{1,0:T(8,128)(2,1)S(1)}, bf16[16,2048]{1,0:T(8,128)(2,1)S(1)}, u32[]{:S(2)}, u32[]{:S(2)}) collective-permute-start(bf16[16,2048]{1,0:T(8,128)(2,1)S(1)} %get-tuple-element.34), channel_id=1, source_target_pairs={{0,1},{1,0},{2,3},{3,2},{4,5},{5,4},{6,7},{7,6},{8,9},{9,8},{10,11... | collective-permute-start | bytes 196616 | tf_op jit(solution)/shard_map/ppermute | solution.py:22
  50.3 0.6 collective-permute-start.15
  50.9 2.4 %collective-permute-start.16 = (bf16[16,2048]{1,0:T(8,128)(2,1)S(1)}, bf16[16,2048]{1,0:T(8,128)(2,1)S(1)}, u32[]{:S(2)}, u32[]{:S(2)}) collective-permute-start(bf16[16,2048]{1,0:T(8,128)(2,1)S(1)} %get-tuple-element.36), channel_id=1, source_target_pairs={{0,3},{1,2},{2,1},{3,0},{4,7},{5,6},{6,5},{7,4},{8,11},{9,10},{10,... | collective-permute-start | bytes 196616 | tf_op jit(solution)/shard_map/ppermute | solution.py:22
  53.3 2.1 %attend_0.1.refs_3_.sums_ref = f32[32,512]{1,0:T(8,128)S(1)} custom-call(f32[3,32,128]{2,1,0:T(8,128)S(1)} %broadcast_in_dim.33.bounds_ref, f32[8,512]{1,0:T(8,128)S(1)} %broadcast_in_dim.34.gain_ref, bf16[512,1024]{1,0:T(8,128)(2,1)S(1)} %get-tuple-element.37.qg_ref, bf16[512,1024]{1,0:T(8,128)(2,1)S(1)} %get-tuple-element.38.kv_first, ...), custom_call_target="tpu_custom_call" | custom-call | flops 402653184 | bytes 4194304 | tf_op jit(solution)/shard_map/attend_0/pallas_call | solution.py:144
  55.4 0.7 %collective-permute-done.16.refs_2_ = bf16[16,2048]{1,0:T(8,128)(2,1)S(1)} collective-permute-done((bf16[16,2048]{1,0:T(8,128)(2,1)S(1)}, bf16[16,2048]{1,0:T(8,128)(2,1)S(1)}, u32[]{:S(2)}, u32[]{:S(2)}) %collective-permute-start.16) | collective-permute-done | bytes 65568 | tf_op jit(solution)/shard_map/ppermute | solution.py:22
  56.2 2.3 %attend_256.1.sums_g_ref = f32[32,512]{1,0:T(8,128)S(1)} custom-call(f32[3,32,128]{2,1,0:T(8,128)S(1)} %broadcast_in_dim.33.bounds_ref, f32[8,512]{1,0:T(8,128)S(1)} %broadcast_in_dim.34.gain_ref, bf16[512,1024]{1,0:T(8,128)(2,1)S(1)} %get-tuple-element.37.qg_ref, bf16[512,1024]{1,0:T(8,128)(2,1)S(1)} %get-tuple-element.38.kv_first, ...), custom_call_target="tpu_custom_call" | custom-call | flops 536870912 | bytes 4194304 | tf_op jit(solution)/shard_map/attend_256/pallas_call | solution.py:144
  58.5 0.8 %finish.1 = (bf16[8,4096]{1,0:T(8,128)(2,1)}, bf16[32,512]{1,0:T(8,128)(2,1)}) custom-call(f32[8,2048]{1,0:T(8,128)S(1)} %get-tuple-element.41._.keep_ref, f32[8,2048]{1,0:T(8,128)S(1)} %collective-permute-done.17.got_ref, f32[3,32,128]{2,1,0:T(8,128)S(1)} %broadcast_in_dim.33.bounds_ref, f32[32,512]{1,0:T(8,128)S(1)} %get-tuple-element.32._.sums_ev_ref, ...), custom_call_target="tpu_custom_call" | custom-call | flops 50331648 | bytes 2097152 | tf_op jit(solution)/shard_map/finish/pallas_call | solution.py:144
  (48 shorter events, 0.6 us)
Async XLA Ops:
  0.6 12.6 %copy-start.2 = (bf16[128,2048]{1,0:T(8,128)(2,1)S(1)}, bf16[128,2048]{1,0:T(8,128)(2,1)}, u32[]{:S(2)}) copy-start(bf16[128,2048]{1,0:T(8,128)(2,1)} %param.13) | copy-start | bytes 1572868
  0.6 12.5 %copy-start.1 = (bf16[1,1024,512]{2,1,0:T(8,128)(2,1)S(1)}, bf16[1,1024,512]{2,1,0:T(8,128)(2,1)}, u32[]{:S(2)}) copy-start(bf16[1,1024,512]{2,1,0:T(8,128)(2,1)} %param.10) | copy-start | bytes 3145732
  2.5 16.2 %collective-permute-start = (bf16[160,512]{1,0:T(8,128)(2,1)S(1)}, bf16[160,512]{1,0:T(8,128)(2,1)S(1)}, u32[]{:S(2)}, u32[]{:S(2)}) collective-permute-start(bf16[160,512]{1,0:T(8,128)(2,1)S(1)} %pad_maximum_fusion.1), channel_id=1, source_target_pairs={{0,8},{4,12},{8,0},{12,4},{1,9},{5,13},{9,1},{13,5},{2,10},{6,14},... | collective-permute-start | bytes 491528 | tf_op jit(solution)/shard_map/ppermute | solution.py:22
  6.6 12.1 %collective-permute-start.1 = (bf16[160,512]{1,0:T(8,128)(2,1)S(1)}, bf16[160,512]{1,0:T(8,128)(2,1)S(1)}, u32[]{:S(2)}, u32[]{:S(2)}) collective-permute-start(bf16[160,512]{1,0:T(8,128)(2,1)S(1)} %pad_maximum_fusion.1), channel_id=1, source_target_pairs={{0,12},{4,8},{8,4},{12,0},{1,13},{5,9},{9,5},{13,1},{2,14},{6,10},... | collective-permute-start | bytes 491528 | tf_op jit(solution)/shard_map/ppermute | solution.py:22
  7.9 11.3 %collective-permute-start.2 = (bf16[160,512]{1,0:T(8,128)(2,1)S(1)}, bf16[160,512]{1,0:T(8,128)(2,1)S(1)}, u32[]{:S(2)}, u32[]{:S(2)}) collective-permute-start(bf16[160,512]{1,0:T(8,128)(2,1)S(1)} %pad_maximum_fusion.1), channel_id=1, source_target_pairs={{0,4},{4,0},{8,12},{12,8},{1,5},{5,1},{9,13},{13,9},{2,6},{6,2},{1... | collective-permute-start | bytes 491528 | tf_op jit(solution)/shard_map/ppermute | solution.py:22
  8.9 13.5 %copy-start.3 = (bf16[128,512]{1,0:T(8,128)(2,1)S(1)}, bf16[128,512]{1,0:T(8,128)(2,1)}, u32[]{:S(2)}) copy-start(bf16[128,512]{1,0:T(8,128)(2,1)} %param.14) | copy-start | bytes 393220
  10.0 12.5 %copy-start.5 = (s32[1,32]{1,0:T(1,128)S(1)}, s32[1,32]{1,0:T(1,128)}, u32[]{:S(2)}) copy-start(s32[1,32]{1,0:T(1,128)} %param.12) | copy-start | bytes 388
  10.0 22.9 %copy-start.4 = (f32[512]{0:T(512)S(1)}, f32[512]{0:T(512)}, u32[]{:S(2)}) copy-start(f32[512]{0:T(512)} %param.15) | copy-start | bytes 6148
  10.0 20.5 %collective-permute-start.10 = (bf16[528,512]{1,0:T(8,128)(2,1)S(1)}, bf16[528,512]{1,0:T(8,128)(2,1)S(1)}, u32[]{:S(2)}, u32[]{:S(2)}) collective-permute-start(bf16[528,512]{1,0:T(8,128)(2,1)S(1)} %pad_maximum_fusion.refs_0_), channel_id=1, source_target_pairs={{0,2},{1,3},{2,0},{3,1},{4,6},{5,7},{6,4},{7,5},{8,10},{9,11},{10,... | collective-permute-start | bytes 1622024 | tf_op jit(solution)/shard_map/ppermute | solution.py:22
  11.6 19.1 %collective-permute-start.9 = (bf16[528,512]{1,0:T(8,128)(2,1)S(1)}, bf16[528,512]{1,0:T(8,128)(2,1)S(1)}, u32[]{:S(2)}, u32[]{:S(2)}) collective-permute-start(bf16[528,512]{1,0:T(8,128)(2,1)S(1)} %pad_maximum_fusion.refs_0_), channel_id=1, source_target_pairs={{0,1},{1,0},{2,3},{3,2},{4,5},{5,4},{6,7},{7,6},{8,9},{9,8},{10,11... | collective-permute-start | bytes 1622024 | tf_op jit(solution)/shard_map/ppermute | solution.py:22
  13.1 30.9 %copy-start = (bf16[2048,2048]{1,0:T(8,128)(2,1)S(1)}, bf16[2048,2048]{1,0:T(8,128)(2,1)}, u32[]{:S(2)}) copy-start(bf16[2048,2048]{1,0:T(8,128)(2,1)} %refs_5_.1) | copy-start | bytes 25165828
  19.2 10.8 %collective-permute-start.3 = (bf16[3,160,256]{2,1,0:T(8,128)(2,1)S(1)}, bf16[3,160,256]{2,1,0:T(8,128)(2,1)S(1)}, u32[]{:S(2)}, u32[]{:S(2)}) collective-permute-start(bf16[3,160,256]{2,1,0:T(8,128)(2,1)S(1)} %get-tuple-element.24.refs_4_), channel_id=1, source_target_pairs={{0,1},{1,0},{2,3},{3,2},{4,5},{5,4},{6,7},{7,6},{8,9},{9,8},{10,11... | collective-permute-start | bytes 737288 | tf_op jit(solution)/shard_map/ppermute | solution.py:22
  20.8 9.2 %collective-permute-start.4 = (bf16[3,160,256]{2,1,0:T(8,128)(2,1)S(1)}, bf16[3,160,256]{2,1,0:T(8,128)(2,1)S(1)}, u32[]{:S(2)}, u32[]{:S(2)}) collective-permute-start(bf16[3,160,256]{2,1,0:T(8,128)(2,1)S(1)} %get-tuple-element.25.refs_5_), channel_id=1, source_target_pairs={{0,2},{1,3},{2,0},{3,1},{4,6},{5,7},{6,4},{7,5},{8,10},{9,11},{10,... | collective-permute-start | bytes 737288 | tf_op jit(solution)/shard_map/ppermute | solution.py:22
  22.4 9.9 %collective-permute-start.5 = (bf16[3,160,256]{2,1,0:T(8,128)(2,1)S(1)}, bf16[3,160,256]{2,1,0:T(8,128)(2,1)S(1)}, u32[]{:S(2)}, u32[]{:S(2)}) collective-permute-start(bf16[3,160,256]{2,1,0:T(8,128)(2,1)S(1)} %get-tuple-element.24.refs_4_), channel_id=1, source_target_pairs={{0,16},{16,0},{1,17},{17,1},{2,18},{18,2},{3,19},{19,3},{4,20},{20... | collective-permute-start | bytes 737288 | tf_op jit(solution)/shard_map/ppermute | solution.py:22
  30.1 2.8 %collective-permute-start.6 = (bf16[3,160,256]{2,1,0:T(8,128)(2,1)S(1)}, bf16[3,160,256]{2,1,0:T(8,128)(2,1)S(1)}, u32[]{:S(2)}, u32[]{:S(2)}) collective-permute-start(bf16[3,160,256]{2,1,0:T(8,128)(2,1)S(1)} %get-tuple-element.25.refs_5_), channel_id=1, source_target_pairs={{0,16},{16,0},{1,17},{17,1},{2,18},{18,2},{3,19},{19,3},{4,20},{20... | collective-permute-start | bytes 737288 | tf_op jit(solution)/shard_map/ppermute | solution.py:22
  30.1 2.8 %collective-permute-start.7 = (bf16[3,160,256]{2,1,0:T(8,128)(2,1)S(1)}, bf16[3,160,256]{2,1,0:T(8,128)(2,1)S(1)}, u32[]{:S(2)}, u32[]{:S(2)}) collective-permute-start(bf16[3,160,256]{2,1,0:T(8,128)(2,1)S(1)} %collective-permute-done.3.refs_6_), channel_id=1, source_target_pairs={{0,16},{16,0},{1,17},{17,1},{2,18},{18,2},{3,19},{19,3},{4,20},{20... | collective-permute-start | bytes 737288 | tf_op jit(solution)/shard_map/ppermute | solution.py:22
  30.6 2.3 %collective-permute-start.8 = (bf16[3,160,256]{2,1,0:T(8,128)(2,1)S(1)}, bf16[3,160,256]{2,1,0:T(8,128)(2,1)S(1)}, u32[]{:S(2)}, u32[]{:S(2)}) collective-permute-start(bf16[3,160,256]{2,1,0:T(8,128)(2,1)S(1)} %collective-permute-done.4.refs_7_), channel_id=1, source_target_pairs={{0,16},{16,0},{1,17},{17,1},{2,18},{18,2},{3,19},{19,3},{4,20},{20... | collective-permute-start | bytes 737288 | tf_op jit(solution)/shard_map/ppermute | solution.py:22
  30.7 13.4 %collective-permute-start.12 = (bf16[272,512]{1,0:T(8,128)(2,1)S(1)}, bf16[272,512]{1,0:T(8,128)(2,1)S(1)}, u32[]{:S(2)}, u32[]{:S(2)}) collective-permute-start(bf16[272,512]{1,0:T(8,128)(2,1)S(1)} %slice.41), channel_id=1, source_target_pairs={{0,1},{1,0},{2,3},{3,2},{4,5},{5,4},{6,7},{7,6},{8,9},{9,8},{10,11... | collective-permute-start | bytes 835592 | tf_op jit(solution)/shard_map/ppermute | solution.py:22
  32.3 11.8 %collective-permute-start.11 = (bf16[256,512]{1,0:T(8,128)(2,1)S(1)}, bf16[256,512]{1,0:T(8,128)(2,1)S(1)}, u32[]{:S(2)}, u32[]{:S(2)}) collective-permute-start(bf16[256,512]{1,0:T(8,128)(2,1)S(1)} %slice.40), channel_id=1, source_target_pairs={{0,2},{1,3},{2,0},{3,1},{4,6},{5,7},{6,4},{7,5},{8,10},{9,11},{10,... | collective-permute-start | bytes 786440 | tf_op jit(solution)/shard_map/ppermute | solution.py:22
  33.0 14.9 %slice-start = ((s8[8388608]{0:T(1024)(128)(4,1)}), s8[4194304]{0:T(1024)(128)(4,1)S(1)}, s32[]{:S(2)}) async-start(s8[8388608]{0:T(1024)(128)(4,1)} %bitcast.13), calls=%async_computation.1 | async-start | bytes 8388608
  44.0 3.8 %slice-start.1 = ((s8[8388608]{0:T(1024)(128)(4,1)}), s8[4194304]{0:T(1024)(128)(4,1)S(1)}, s32[]{:S(2)}) async-start(s8[8388608]{0:T(1024)(128)(4,1)} %bitcast.13), calls=%async_computation.2 | async-start | bytes 8388608
  46.1 1.7 %collective-permute-start.13 = (bf16[64,2176]{1,0:T(8,128)(2,1)S(1)}, bf16[64,2176]{1,0:T(8,128)(2,1)S(1)}, u32[]{:S(2)}, u32[]{:S(2)}) collective-permute-start(bf16[64,2176]{1,0:T(8,128)(2,1)S(1)} %get-tuple-element.28), channel_id=1, source_target_pairs={{0,16},{16,0},{1,17},{17,1},{2,18},{18,2},{3,19},{19,3},{4,20},{20... | collective-permute-start | bytes 835592 | tf_op jit(solution)/shard_map/ppermute | solution.py:22
  49.7 5.7 %collective-permute-start.14 = (bf16[16,2048]{1,0:T(8,128)(2,1)S(1)}, bf16[16,2048]{1,0:T(8,128)(2,1)S(1)}, u32[]{:S(2)}, u32[]{:S(2)}) collective-permute-start(bf16[16,2048]{1,0:T(8,128)(2,1)S(1)} %get-tuple-element.34), channel_id=1, source_target_pairs={{0,1},{1,0},{2,3},{3,2},{4,5},{5,4},{6,7},{7,6},{8,9},{9,8},{10,11... | collective-permute-start | bytes 196616 | tf_op jit(solution)/shard_map/ppermute | solution.py:22
  50.3 5.1 %collective-permute-start.15 = (bf16[16,2048]{1,0:T(8,128)(2,1)S(1)}, bf16[16,2048]{1,0:T(8,128)(2,1)S(1)}, u32[]{:S(2)}, u32[]{:S(2)}) collective-permute-start(bf16[16,2048]{1,0:T(8,128)(2,1)S(1)} %get-tuple-element.35), channel_id=1, source_target_pairs={{0,2},{1,3},{2,0},{3,1},{4,6},{5,7},{6,4},{7,5},{8,10},{9,11},{10,... | collective-permute-start | bytes 196616 | tf_op jit(solution)/shard_map/ppermute | solution.py:22
  50.9 5.2 %collective-permute-start.16 = (bf16[16,2048]{1,0:T(8,128)(2,1)S(1)}, bf16[16,2048]{1,0:T(8,128)(2,1)S(1)}, u32[]{:S(2)}, u32[]{:S(2)}) collective-permute-start(bf16[16,2048]{1,0:T(8,128)(2,1)S(1)} %get-tuple-element.36), channel_id=1, source_target_pairs={{0,3},{1,2},{2,1},{3,0},{4,7},{5,6},{6,5},{7,4},{8,11},{9,10},{10,... | collective-permute-start | bytes 196616 | tf_op jit(solution)/shard_map/ppermute | solution.py:22
  56.1 2.4 %collective-permute-start.17 = (f32[8,2048]{1,0:T(8,128)S(1)}, f32[8,2048]{1,0:T(8,128)S(1)}, u32[]{:S(2)}, u32[]{:S(2)}) collective-permute-start(f32[8,2048]{1,0:T(8,128)S(1)} %get-tuple-element.42), channel_id=1, source_target_pairs={{0,16},{16,0},{1,17},{17,1},{2,18},{18,2},{3,19},{19,3},{4,20},{20... | collective-permute-start | bytes 196616 | tf_op jit(solution)/shard_map/ppermute | solution.py:22

commit v8 on v7

--- a/solution.py
+++ b/solution.py
@@ -153,23 +153,19 @@
     )(*operands)
 
 
-def parity(m):
-    return (m & 1) ^ ((m >> 1) & 1)
-
-
-def split_kernel(*refs):
-    *parts, left_ref, right_ref = refs
-    half = left_ref.shape[2]
+def stack_kernel(*refs):
+    *parts, out_ref = refs
     for k, part in enumerate(parts):
-        left_ref[k] = part[:, :half]
-        right_ref[k] = part[:, half:]
+        out_ref[k] = part[...]
 
 
 def gather_weights(w_uvqk, w_out, w_in, ffn_gain, sections, dps, mps):
     depth, wide = w_uvqk.shape
     width = w_out.shape[1]
     w_in = jnp.concatenate([w_in, jnp.broadcast_to(ffn_gain, (16, w_in.shape[1]))], axis=0)
-    if (sections, mps) != (2, 4) or wide != 4 * width or depth % 128:
+    peers = sections * mps
+    cut, part = wide // peers, depth // peers
+    if (sections, mps) != (2, 4) or width != 2 * cut or depth % 128:
         ws = [lax.all_gather(x, "dp", axis=0, tiled=True) for x in (w_uvqk, w_out)]
         blocks = [[w_in]] + [[swap(w_in, "mp", mps, k)] for k in range(1, mps)]
 
@@ -179,29 +175,17 @@
 
         return place_whole, ws, blocks, 1
 
-    part = depth // 4
-    cut = width // 2
     sec, m = lax.axis_index("section"), lax.axis_index("mp")
-    share = sec * 2 + parity(m)
+    share = sec * mps + m
+    rows = lax.dynamic_slice_in_dim(w_out, share * part, part, 0)
     mine = jnp.concatenate(
-        [
-            lax.dynamic_slice_in_dim(w_uvqk, share * width, width, 1),
-            lax.dynamic_slice_in_dim(w_out, share * part, part, 0),
-        ],
-        axis=0,
+        [lax.dynamic_slice_in_dim(w_uvqk, share * cut, cut, 1), rows[:, :cut], rows[:, cut:]], axis=0
     )
     got = [swap(mine, "dp", dps, k) for k in order_of(dps)[1:]]
-    left, right = call(
-        split_kernel,
-        "split",
-        got,
-        [((len(got), depth + part, cut), BF16)] * 2,
-        [],
-        8,
-        0,
-        16 * 1024 * 1024,
-    )
-    plane = [left, right, swap(left, "mp", mps, 1), swap(right, "mp", mps, 2)]
+    (stacked,) = call(
+        stack_kernel, "stack", got, [((len(got), *mine.shape), BF16)], [], 8, 0, 16 * 1024 * 1024
+    )
+    plane = [stacked] + [swap(stacked, "mp", mps, k) for k in range(1, mps)]
     parts = [w_uvqk[:, : wide // 2], w_uvqk[:, wide // 2 :], w_out[: depth // 2], w_out[depth // 2 :]]
     parts = parts + plane + [swap(p, "section", sections, 1) for p in plane]
 
@@ -215,14 +199,14 @@
             w_ref[:depth, i * (wide // 2) : (i + 1) * (wide // 2)] = parts[i][...]
             wout_ref[i * (depth // 2) : (i + 1) * (depth // 2)] = parts[2 + i][...]
         for i, ref in enumerate(parts[4:]):
-            owner = (sec ^ (i // 4)) * 2 + (parity(m) ^ (i // 2 % 2))
-            at = i % 2 * cut
-            cols = pl.ds(pl.multiple_of(owner * width + at, cut), cut)
+            owner = (sec ^ (i // mps)) * mps + (m ^ (i % mps))
+            cols = pl.ds(pl.multiple_of(owner * cut, cut), cut)
             for k in range(dps - 1):
                 row = (k + 1) * depth
                 w_ref[row : row + depth, cols] = ref[k, :depth]
                 rows = pl.ds(pl.multiple_of(row + owner * part, part), part)
-                wout_ref[rows, at : at + cut] = ref[k, depth:]
+                wout_ref[rows, :cut] = ref[k, depth : depth + part]
+                wout_ref[rows, cut:] = ref[k, depth + part :]
 
     return place, parts, [[w_in], [from_x], [from_y], diagonal], dps
 

time: 59.6 us -> 65.4 us (1.097)
  waiting for transfers between devices: 13.5 us -> 17.7 us
  starting transfers between devices: 18.5 us -> 20.4 us
    ppermute x18 -> x19, waiting for transfers between devices: 13.5 us -> 17.7 us  [swap(): return lax.ppermute(x, axis, [(i, i ^ flip) for i in range(size)])]
    ppermute x18 -> x19, starting transfers between devices: 18.5 us -> 20.4 us  [swap(): return lax.ppermute(x, axis, [(i, i ^ flip) for i in range(size)])]
    dynamic_slice x2 -> x1, local copies, waits for them, and re-layouts: 1.8 us -> 0.96 us  [gather_weights(): lax.dynamic_slice_in_dim(w_uvqk, share * cut, cut, 1)]
    slice x0 -> x1, local copies, waits for them, and re-layouts: none -> 0.72 us  [gather_weights(): rows[:, :cut]]
  transfers between devices with their start and end apart: 18 -> 19, of which waited for: 4 -> 5; matrix products, arithmetic and copies ran while one was open for 4% -> 3% of each run, Pallas kernels for 16% -> 15%
where the time goes in v8:
time: 65.4 us; the launch traced here: 65.1 us
  starting transfers between devices  20.4 us (31%)
  waiting for transfers between devices  17.7 us (27%)
  Pallas kernels  14.2 us (22%)
  blocking collectives  7.3 us (11%)
  local copies, waits for them, and re-layouts  1.96 us (3%)
  other arithmetic  1.95 us (3%)
  between operations  1.56 us (2%)
    ppermute x19, starting transfers between devices, swap(): return lax.ppermute(x, axis, [(i, i ^ flip) for i in range(size)])  20.4 us
    ppermute x19, waiting for transfers between devices, swap(): return lax.ppermute(x, axis, [(i, i ^ flip) for i in range(size)])  17.7 us
    pallas_call x9, Pallas kernels, call(): pl.pallas_call(kernel, in_specs=[VMEM] * len(operands), out_specs=[VMEM]...  14.2 us
    all_to_all x1, blocking collectives, per_device(): lax.all_to_all(micro_rows.reshape(peers, take, width), group, split_axis=...  7.3 us
  transfers between devices with their start and end apart: 19, of which 5 were waited for; matrix products, arithmetic and copies ran while one was open for 3% of the time, Pallas kernels for 15%

profile of v8, /device:TPU:0, one launch (start us, length us, event | category | flops | bytes accessed | tf_op | source)
XLA Modules:
  0.0 65.1 jit_solution(12898853291715086575)
XLA Ops:
  0.7 1.0 %constant_dynamic-slice_fusion = bf16[128,256]{1,0:T(8,128)(2,1)S(1)} fusion(bf16[128,2048]{1,0:T(8,128)(2,1)} %param.13, s32[]{:T(128)S(6)} %select_n.11), kind=kLoop, calls=%fused_computation.9 | loop fusion | bytes 131076 | tf_op jit(solution)/shard_map/dynamic_slice | solution.py:182
  1.6 0.7 %constant_dynamic-slice_fusion.1 = (bf16[16,256]{1,0:T(8,128)(2,1)S(1)}, bf16[16,256]{1,0:T(8,128)(2,1)S(1)}) fusion(bf16[128,512]{1,0:T(8,128)(2,1)} %param.14, s32[]{:T(128)S(6)} %select_n.12, s32[]{:T(128)S(6)} %add.15), kind=kLoop, calls=%fused_computation.10 | loop fusion | bytes 32776 | tf_op jit(solution)/shard_map/slice | solution.py:182
  2.3 4.1 %collective-permute-start = (bf16[160,256]{1,0:T(8,128)(2,1)S(1)}, bf16[160,256]{1,0:T(8,128)(2,1)S(1)}, u32[]{:S(2)}, u32[]{:S(2)}) collective-permute-start(bf16[160,256]{1,0:T(8,128)(2,1)S(1)} %pad_maximum_fusion.1), channel_id=1, source_target_pairs={{0,8},{4,12},{8,0},{12,4},{1,9},{5,13},{9,1},{13,5},{2,10},{6,14},... | collective-permute-start | bytes 245768 | tf_op jit(solution)/shard_map/ppermute | solution.py:22
  6.4 1.3 %collective-permute-start.1 = (bf16[160,256]{1,0:T(8,128)(2,1)S(1)}, bf16[160,256]{1,0:T(8,128)(2,1)S(1)}, u32[]{:S(2)}, u32[]{:S(2)}) collective-permute-start(bf16[160,256]{1,0:T(8,128)(2,1)S(1)} %pad_maximum_fusion.1), channel_id=1, source_target_pairs={{0,12},{4,8},{8,4},{12,0},{1,13},{5,9},{9,5},{13,1},{2,14},{6,10},... | collective-permute-start | bytes 245768 | tf_op jit(solution)/shard_map/ppermute | solution.py:22
  7.8 0.2 collective-permute-start.2
  8.0 0.7 %reduce = bf16[512]{0:T(512)(128)(2,1)S(1)} reduce(bf16[1,512]{1,0:T(2,128)(2,1)} %param.17, bf16[]{:T(256)} %constant.25), dimensions={0}, to_apply=%param.17.reduce_sub_computation | reduce | bytes 2050 | tf_op args[7]
  8.7 1.1 %pad_maximum_fusion.refs_0_ = bf16[528,512]{1,0:T(8,128)(2,1)S(1)} fusion(bf16[16,512]{1,0:T(8,128)(2,1)S(1)} %broadcast_in_dim.36, bf16[512,512]{1,0:T(8,128)(2,1)} %param.16), kind=kLoop, calls=%fused_computation | loop fusion | flops 1081344 | bytes 1081344 | tf_op jit(solution)/shard_map/concatenate | solution.py:165
  9.9 1.6 %collective-permute-start.11 = (bf16[528,512]{1,0:T(8,128)(2,1)S(1)}, bf16[528,512]{1,0:T(8,128)(2,1)S(1)}, u32[]{:S(2)}, u32[]{:S(2)}) collective-permute-start(bf16[528,512]{1,0:T(8,128)(2,1)S(1)} %pad_maximum_fusion.refs_0_), channel_id=1, source_target_pairs={{0,2},{1,3},{2,0},{3,1},{4,6},{5,7},{6,4},{7,5},{8,10},{9,11},{10,... | collective-permute-start | bytes 1622024 | tf_op jit(solution)/shard_map/ppermute | solution.py:22
  11.5 1.5 %collective-permute-start.10 = (bf16[528,512]{1,0:T(8,128)(2,1)S(1)}, bf16[528,512]{1,0:T(8,128)(2,1)S(1)}, u32[]{:S(2)}, u32[]{:S(2)}) collective-permute-start(bf16[528,512]{1,0:T(8,128)(2,1)S(1)} %pad_maximum_fusion.refs_0_), channel_id=1, source_target_pairs={{0,1},{1,0},{2,3},{3,2},{4,5},{5,4},{6,7},{7,6},{8,9},{9,8},{10,11... | collective-permute-start | bytes 1622024 | tf_op jit(solution)/shard_map/ppermute | solution.py:22
  13.2 0.4 collective-permute-done.2.refs_2_
  13.7 1.7 %collective-permute-start.3 = (bf16[3,160,256]{2,1,0:T(8,128)(2,1)S(1)}, bf16[3,160,256]{2,1,0:T(8,128)(2,1)S(1)}, u32[]{:S(2)}, u32[]{:S(2)}) collective-permute-start(bf16[3,160,256]{2,1,0:T(8,128)(2,1)S(1)} %stack.7.refs_4_), channel_id=1, source_target_pairs={{0,1},{1,0},{2,3},{3,2},{4,5},{5,4},{6,7},{7,6},{8,9},{9,8},{10,11... | collective-permute-start | bytes 737288 | tf_op jit(solution)/shard_map/ppermute | solution.py:22
  15.4 1.6 %collective-permute-start.4 = (bf16[3,160,256]{2,1,0:T(8,128)(2,1)S(1)}, bf16[3,160,256]{2,1,0:T(8,128)(2,1)S(1)}, u32[]{:S(2)}, u32[]{:S(2)}) collective-permute-start(bf16[3,160,256]{2,1,0:T(8,128)(2,1)S(1)} %stack.7.refs_4_), channel_id=1, source_target_pairs={{0,2},{1,3},{2,0},{3,1},{4,6},{5,7},{6,4},{7,5},{8,10},{9,11},{10,... | collective-permute-start | bytes 737288 | tf_op jit(solution)/shard_map/ppermute | solution.py:22
  17.0 0.3 collective-permute-start.5
  17.3 14.6 %collective-permute-done.3.refs_5_ = bf16[3,160,256]{2,1,0:T(8,128)(2,1)S(1)} collective-permute-done((bf16[3,160,256]{2,1,0:T(8,128)(2,1)S(1)}, bf16[3,160,256]{2,1,0:T(8,128)(2,1)S(1)}, u32[]{:S(2)}, u32[]{:S(2)}) %collective-permute-start.3) | collective-permute-done | bytes 245792 | tf_op jit(solution)/shard_map/ppermute | solution.py:22
  32.7 0.6 collective-permute-start.7
  33.3 1.8 %collective-permute-done.5.refs_7_ = bf16[3,160,256]{2,1,0:T(8,128)(2,1)S(1)} collective-permute-done((bf16[3,160,256]{2,1,0:T(8,128)(2,1)S(1)}, bf16[3,160,256]{2,1,0:T(8,128)(2,1)S(1)}, u32[]{:S(2)}, u32[]{:S(2)}) %collective-permute-start.5) | collective-permute-done | bytes 245792 | tf_op jit(solution)/shard_map/ppermute | solution.py:22
  35.1 0.5 collective-permute-start.9
  35.7 1.6 %collective-permute-start.13 = (bf16[272,512]{1,0:T(8,128)(2,1)S(1)}, bf16[272,512]{1,0:T(8,128)(2,1)S(1)}, u32[]{:S(2)}, u32[]{:S(2)}) collective-permute-start(bf16[272,512]{1,0:T(8,128)(2,1)S(1)} %slice.49), channel_id=1, source_target_pairs={{0,1},{1,0},{2,3},{3,2},{4,5},{5,4},{6,7},{7,6},{8,9},{9,8},{10,11... | collective-permute-start | bytes 835592 | tf_op jit(solution)/shard_map/ppermute | solution.py:22
  37.3 1.6 %collective-permute-start.12 = (bf16[256,512]{1,0:T(8,128)(2,1)S(1)}, bf16[256,512]{1,0:T(8,128)(2,1)S(1)}, u32[]{:S(2)}, u32[]{:S(2)}) collective-permute-start(bf16[256,512]{1,0:T(8,128)(2,1)S(1)} %slice.48), channel_id=1, source_target_pairs={{0,2},{1,3},{2,0},{3,1},{4,6},{5,7},{6,4},{7,5},{8,10},{9,11},{10,... | collective-permute-start | bytes 786440 | tf_op jit(solution)/shard_map/ppermute | solution.py:22
  39.0 3.5 %encode_first.1 = (bf16[64,512]{1,0:T(8,128)(2,1)S(1)}, bf16[512,2048]{1,0:T(8,128)(2,1)S(1)}, bf16[512,512]{1,0:T(8,128)(2,1)S(1)}, bf16[512,1024]{1,0:T(8,128)...) custom-call(f32[3,32,128]{2,1,0:T(8,128)S(1)} %broadcast_in_dim.33.bounds_ref, ...), custom_call_target="tpu_custom_call" | custom-call | flops 1342177280 | bytes 6291456 | tf_op jit(solution)/shard_map/encode_first/pallas_call | solution.py:144
  42.5 7.3 %all_to_all.5 = bf16[8,8,512]{2,1,0:T(8,128)(2,1)S(1)} all-to-all(bf16[8,8,512]{2,1,0:T(8,128)(2,1)S(1)} %bitcast.16), channel_id=1, replica_groups=mesh['section'=2,'dp'=4,'mp'=4] {'section','mp'}, dimensions={0} | all-to-all | bytes 131072 | tf_op jit(solution)/shard_map/all_to_all | solution.py:334
  49.8 2.0 %up_half.1 = (f32[64,512]{1,0:T(8,128)S(1)}, f32[64,2176]{1,0:T(8,128)S(1)}, bf16[64,2176]{1,0:T(8,128)(2,1)S(1)}) custom-call(bf16[64,512]{1,0:T(8,128)(2,1)S(1)} %bitcast.15, bf16[528,512]{1,0:T(8,128)(2,1)S(1)} %pad_maximum_fusion.refs_0_, bf16[528,512]{1,0:T(8,128)(2,1)S(1)} %collective-permute-done.10.refs_1_, ...), custom_call_target="tpu_custom_call" | custom-call | flops 536870912 | bytes 8388608 | tf_op jit(solution)/shard_map/up_half/pallas_call | solution.py:144
  51.9 0.2 collective-permute-start.14
  52.1 1.6 %project_rest.1 = (bf16[512,1024]{1,0:T(8,128)(2,1)S(1)}, bf16[512,1024]{1,0:T(8,128)(2,1)S(1)}, f32[32,512]{1,0:T(8,128)S(1)}) custom-call(f32[3,32,128]{2,1,0:T(8,128)S(1)} %broadcast_in_dim.33.bounds_ref, bf16[512,512]{1,0:T(8,128)(2,1)S(1)} %get-tuple-element.42.ev_ref, bf16[512,2048]{1,0:T(8,128)(2,1)S(1)} %get-tuple-element.26.w_ref, ...), custom_call_target="tpu_custom_call" | custom-call | flops 1073741824 | bytes 6291456 | tf_op jit(solution)/shard_map/project_rest/pallas_call | solution.py:144
  53.7 1.8 %down_part.1 = (f32[16,2048]{1,0:T(8,128)S(1)}, bf16[16,2048]{1,0:T(8,128)(2,1)S(1)}, bf16[16,2048]{1,0:T(8,128)(2,1)S(1)}, bf16[16,2048]{1,0:T(8,128)(2,1)S(1)}) custom-call(f32[64,2176]{1,0:T(8,128)S(1)} %get-tuple-element.23.half_ref, bf16[64,2176]{1,0:T(8,128)(2,1)S(1)} %collective-permute-done.14.other_ref, ...), custom_call_target="tpu_custom_call" | custom-call | flops 536870912 | bytes 8388608 | tf_op jit(solution)/shard_map/down_part/pallas_call | solution.py:144
  55.5 0.7 %collective-permute-start.15 = (bf16[16,2048]{1,0:T(8,128)(2,1)S(1)}, bf16[16,2048]{1,0:T(8,128)(2,1)S(1)}, u32[]{:S(2)}, u32[]{:S(2)}) collective-permute-start(bf16[16,2048]{1,0:T(8,128)(2,1)S(1)} %get-tuple-element.30), channel_id=1, source_target_pairs={{0,1},{1,0},{2,3},{3,2},{4,5},{5,4},{6,7},{7,6},{8,9},{9,8},{10,11... | collective-permute-start | bytes 196616 | tf_op jit(solution)/shard_map/ppermute | solution.py:22
  56.2 0.5 collective-permute-start.16
  56.7 2.4 %collective-permute-start.17 = (bf16[16,2048]{1,0:T(8,128)(2,1)S(1)}, bf16[16,2048]{1,0:T(8,128)(2,1)S(1)}, u32[]{:S(2)}, u32[]{:S(2)}) collective-permute-start(bf16[16,2048]{1,0:T(8,128)(2,1)S(1)} %get-tuple-element.32), channel_id=1, source_target_pairs={{0,3},{1,2},{2,1},{3,0},{4,7},{5,6},{6,5},{7,4},{8,11},{9,10},{10,... | collective-permute-start | bytes 196616 | tf_op jit(solution)/shard_map/ppermute | solution.py:22
  59.0 2.1 %attend_0.1.refs_3_.sums_ref = f32[32,512]{1,0:T(8,128)S(1)} custom-call(f32[3,32,128]{2,1,0:T(8,128)S(1)} %broadcast_in_dim.33.bounds_ref, f32[8,512]{1,0:T(8,128)S(1)} %broadcast_in_dim.34.gain_ref, bf16[512,1024]{1,0:T(8,128)(2,1)S(1)} %get-tuple-element.33.qg_ref, bf16[512,1024]{1,0:T(8,128)(2,1)S(1)} %get-tuple-element.34.kv_first, ...), custom_call_target="tpu_custom_call" | custom-call | flops 402653184 | bytes 4194304 | tf_op jit(solution)/shard_map/attend_0/pallas_call | solution.py:144
  61.1 0.7 %collective-permute-done.17.refs_2_ = bf16[16,2048]{1,0:T(8,128)(2,1)S(1)} collective-permute-done((bf16[16,2048]{1,0:T(8,128)(2,1)S(1)}, bf16[16,2048]{1,0:T(8,128)(2,1)S(1)}, u32[]{:S(2)}, u32[]{:S(2)}) %collective-permute-start.17) | collective-permute-done | bytes 65568 | tf_op jit(solution)/shard_map/ppermute | solution.py:22
  62.0 2.3 %attend_256.1.sums_g_ref = f32[32,512]{1,0:T(8,128)S(1)} custom-call(f32[3,32,128]{2,1,0:T(8,128)S(1)} %broadcast_in_dim.33.bounds_ref, f32[8,512]{1,0:T(8,128)S(1)} %broadcast_in_dim.34.gain_ref, bf16[512,1024]{1,0:T(8,128)(2,1)S(1)} %get-tuple-element.33.qg_ref, bf16[512,1024]{1,0:T(8,128)(2,1)S(1)} %get-tuple-element.34.kv_first, ...), custom_call_target="tpu_custom_call" | custom-call | flops 536870912 | bytes 4194304 | tf_op jit(solution)/shard_map/attend_256/pallas_call | solution.py:144
  64.3 0.8 %finish.1 = (bf16[8,4096]{1,0:T(8,128)(2,1)}, bf16[32,512]{1,0:T(8,128)(2,1)}) custom-call(f32[8,2048]{1,0:T(8,128)S(1)} %get-tuple-element.37._.keep_ref, f32[8,2048]{1,0:T(8,128)S(1)} %collective-permute-done.18.got_ref, f32[3,32,128]{2,1,0:T(8,128)S(1)} %broadcast_in_dim.33.bounds_ref, f32[32,512]{1,0:T(8,128)S(1)} %get-tuple-element.28._.sums_ev_ref, ...), custom_call_target="tpu_custom_call" | custom-call | flops 50331648 | bytes 2097152 | tf_op jit(solution)/shard_map/finish/pallas_call | solution.py:144
  (50 shorter events, 0.7 us)
Async XLA Ops:
  0.6 12.3 %copy-start.1 = (bf16[1,1024,512]{2,1,0:T(8,128)(2,1)S(1)}, bf16[1,1024,512]{2,1,0:T(8,128)(2,1)}, u32[]{:S(2)}) copy-start(bf16[1,1024,512]{2,1,0:T(8,128)(2,1)} %param.10) | copy-start | bytes 3145732
  0.6 14.8 %copy-start.2 = (bf16[128,2048]{1,0:T(8,128)(2,1)S(1)}, bf16[128,2048]{1,0:T(8,128)(2,1)}, u32[]{:S(2)}) copy-start(bf16[128,2048]{1,0:T(8,128)(2,1)} %param.13) | copy-start | bytes 1572868
  2.3 10.7 %collective-permute-start = (bf16[160,256]{1,0:T(8,128)(2,1)S(1)}, bf16[160,256]{1,0:T(8,128)(2,1)S(1)}, u32[]{:S(2)}, u32[]{:S(2)}) collective-permute-start(bf16[160,256]{1,0:T(8,128)(2,1)S(1)} %pad_maximum_fusion.1), channel_id=1, source_target_pairs={{0,8},{4,12},{8,0},{12,4},{1,9},{5,13},{9,1},{13,5},{2,10},{6,14},... | collective-permute-start | bytes 245768 | tf_op jit(solution)/shard_map/ppermute | solution.py:22
  6.4 6.7 %collective-permute-start.1 = (bf16[160,256]{1,0:T(8,128)(2,1)S(1)}, bf16[160,256]{1,0:T(8,128)(2,1)S(1)}, u32[]{:S(2)}, u32[]{:S(2)}) collective-permute-start(bf16[160,256]{1,0:T(8,128)(2,1)S(1)} %pad_maximum_fusion.1), channel_id=1, source_target_pairs={{0,12},{4,8},{8,4},{12,0},{1,13},{5,9},{9,5},{13,1},{2,14},{6,10},... | collective-permute-start | bytes 245768 | tf_op jit(solution)/shard_map/ppermute | solution.py:22
  7.8 5.8 %collective-permute-start.2 = (bf16[160,256]{1,0:T(8,128)(2,1)S(1)}, bf16[160,256]{1,0:T(8,128)(2,1)S(1)}, u32[]{:S(2)}, u32[]{:S(2)}) collective-permute-start(bf16[160,256]{1,0:T(8,128)(2,1)S(1)} %pad_maximum_fusion.1), channel_id=1, source_target_pairs={{0,4},{4,0},{8,12},{12,8},{1,5},{5,1},{9,13},{13,9},{2,6},{6,2},{1... | collective-permute-start | bytes 245768 | tf_op jit(solution)/shard_map/ppermute | solution.py:22
  8.7 8.6 %copy-start.3 = (bf16[128,512]{1,0:T(8,128)(2,1)S(1)}, bf16[128,512]{1,0:T(8,128)(2,1)}, u32[]{:S(2)}) copy-start(bf16[128,512]{1,0:T(8,128)(2,1)} %param.14) | copy-start | bytes 393220
  9.9 22.1 %copy-start.5 = (s32[1,32]{1,0:T(1,128)S(1)}, s32[1,32]{1,0:T(1,128)}, u32[]{:S(2)}) copy-start(s32[1,32]{1,0:T(1,128)} %param.12) | copy-start | bytes 388
  9.9 29.1 %copy-start.4 = (f32[512]{0:T(512)S(1)}, f32[512]{0:T(512)}, u32[]{:S(2)}) copy-start(f32[512]{0:T(512)} %param.15) | copy-start | bytes 6148
  9.9 25.2 %collective-permute-start.11 = (bf16[528,512]{1,0:T(8,128)(2,1)S(1)}, bf16[528,512]{1,0:T(8,128)(2,1)S(1)}, u32[]{:S(2)}, u32[]{:S(2)}) collective-permute-start(bf16[528,512]{1,0:T(8,128)(2,1)S(1)} %pad_maximum_fusion.refs_0_), channel_id=1, source_target_pairs={{0,2},{1,3},{2,0},{3,1},{4,6},{5,7},{6,4},{7,5},{8,10},{9,11},{10,... | collective-permute-start | bytes 1622024 | tf_op jit(solution)/shard_map/ppermute | solution.py:22
  11.5 24.2 %collective-permute-start.10 = (bf16[528,512]{1,0:T(8,128)(2,1)S(1)}, bf16[528,512]{1,0:T(8,128)(2,1)S(1)}, u32[]{:S(2)}, u32[]{:S(2)}) collective-permute-start(bf16[528,512]{1,0:T(8,128)(2,1)S(1)} %pad_maximum_fusion.refs_0_), channel_id=1, source_target_pairs={{0,1},{1,0},{2,3},{3,2},{4,5},{5,4},{6,7},{7,6},{8,9},{9,8},{10,11... | collective-permute-start | bytes 1622024 | tf_op jit(solution)/shard_map/ppermute | solution.py:22
  13.0 36.9 %copy-start = (bf16[2048,2048]{1,0:T(8,128)(2,1)S(1)}, bf16[2048,2048]{1,0:T(8,128)(2,1)}, u32[]{:S(2)}) copy-start(bf16[2048,2048]{1,0:T(8,128)(2,1)} %refs_5_.1) | copy-start | bytes 25165828
  13.7 18.3 %collective-permute-start.3 = (bf16[3,160,256]{2,1,0:T(8,128)(2,1)S(1)}, bf16[3,160,256]{2,1,0:T(8,128)(2,1)S(1)}, u32[]{:S(2)}, u32[]{:S(2)}) collective-permute-start(bf16[3,160,256]{2,1,0:T(8,128)(2,1)S(1)} %stack.7.refs_4_), channel_id=1, source_target_pairs={{0,1},{1,0},{2,3},{3,2},{4,5},{5,4},{6,7},{7,6},{8,9},{9,8},{10,11... | collective-permute-start | bytes 737288 | tf_op jit(solution)/shard_map/ppermute | solution.py:22
  15.4 17.3 %collective-permute-start.4 = (bf16[3,160,256]{2,1,0:T(8,128)(2,1)S(1)}, bf16[3,160,256]{2,1,0:T(8,128)(2,1)S(1)}, u32[]{:S(2)}, u32[]{:S(2)}) collective-permute-start(bf16[3,160,256]{2,1,0:T(8,128)(2,1)S(1)} %stack.7.refs_4_), channel_id=1, source_target_pairs={{0,2},{1,3},{2,0},{3,1},{4,6},{5,7},{6,4},{7,5},{8,10},{9,11},{10,... | collective-permute-start | bytes 737288 | tf_op jit(solution)/shard_map/ppermute | solution.py:22
  17.0 18.1 %collective-permute-start.5 = (bf16[3,160,256]{2,1,0:T(8,128)(2,1)S(1)}, bf16[3,160,256]{2,1,0:T(8,128)(2,1)S(1)}, u32[]{:S(2)}, u32[]{:S(2)}) collective-permute-start(bf16[3,160,256]{2,1,0:T(8,128)(2,1)S(1)} %stack.7.refs_4_), channel_id=1, source_target_pairs={{0,3},{1,2},{2,1},{3,0},{4,7},{5,6},{6,5},{7,4},{8,11},{9,10},{10,... | collective-permute-start | bytes 737288 | tf_op jit(solution)/shard_map/ppermute | solution.py:22
  32.0 5.3 %collective-permute-start.6 = (bf16[3,160,256]{2,1,0:T(8,128)(2,1)S(1)}, bf16[3,160,256]{2,1,0:T(8,128)(2,1)S(1)}, u32[]{:S(2)}, u32[]{:S(2)}) collective-permute-start(bf16[3,160,256]{2,1,0:T(8,128)(2,1)S(1)} %stack.7.refs_4_), channel_id=1, source_target_pairs={{0,16},{16,0},{1,17},{17,1},{2,18},{18,2},{3,19},{19,3},{4,20},{20... | collective-permute-start | bytes 737288 | tf_op jit(solution)/shard_map/ppermute | solution.py:22
  32.7 6.1 %collective-permute-start.7 = (bf16[3,160,256]{2,1,0:T(8,128)(2,1)S(1)}, bf16[3,160,256]{2,1,0:T(8,128)(2,1)S(1)}, u32[]{:S(2)}, u32[]{:S(2)}) collective-permute-start(bf16[3,160,256]{2,1,0:T(8,128)(2,1)S(1)} %collective-permute-done.3.refs_5_), channel_id=1, source_target_pairs={{0,16},{16,0},{1,17},{17,1},{2,18},{18,2},{3,19},{19,3},{4,20},{20... | collective-permute-start | bytes 737288 | tf_op jit(solution)/shard_map/ppermute | solution.py:22
  35.1 3.8 %collective-permute-start.8 = (bf16[3,160,256]{2,1,0:T(8,128)(2,1)S(1)}, bf16[3,160,256]{2,1,0:T(8,128)(2,1)S(1)}, u32[]{:S(2)}, u32[]{:S(2)}) collective-permute-start(bf16[3,160,256]{2,1,0:T(8,128)(2,1)S(1)} %collective-permute-done.4.refs_6_), channel_id=1, source_target_pairs={{0,16},{16,0},{1,17},{17,1},{2,18},{18,2},{3,19},{19,3},{4,20},{20... | collective-permute-start | bytes 737288 | tf_op jit(solution)/shard_map/ppermute | solution.py:22
  35.1 3.8 %collective-permute-start.9 = (bf16[3,160,256]{2,1,0:T(8,128)(2,1)S(1)}, bf16[3,160,256]{2,1,0:T(8,128)(2,1)S(1)}, u32[]{:S(2)}, u32[]{:S(2)}) collective-permute-start(bf16[3,160,256]{2,1,0:T(8,128)(2,1)S(1)} %collective-permute-done.5.refs_7_), channel_id=1, source_target_pairs={{0,16},{16,0},{1,17},{17,1},{2,18},{18,2},{3,19},{19,3},{4,20},{20... | collective-permute-start | bytes 737288 | tf_op jit(solution)/shard_map/ppermute | solution.py:22
  35.7 14.1 %collective-permute-start.13 = (bf16[272,512]{1,0:T(8,128)(2,1)S(1)}, bf16[272,512]{1,0:T(8,128)(2,1)S(1)}, u32[]{:S(2)}, u32[]{:S(2)}) collective-permute-start(bf16[272,512]{1,0:T(8,128)(2,1)S(1)} %slice.49), channel_id=1, source_target_pairs={{0,1},{1,0},{2,3},{3,2},{4,5},{5,4},{6,7},{7,6},{8,9},{9,8},{10,11... | collective-permute-start | bytes 835592 | tf_op jit(solution)/shard_map/ppermute | solution.py:22
  37.3 12.6 %collective-permute-start.12 = (bf16[256,512]{1,0:T(8,128)(2,1)S(1)}, bf16[256,512]{1,0:T(8,128)(2,1)S(1)}, u32[]{:S(2)}, u32[]{:S(2)}) collective-permute-start(bf16[256,512]{1,0:T(8,128)(2,1)S(1)} %slice.48), channel_id=1, source_target_pairs={{0,2},{1,3},{2,0},{3,1},{4,6},{5,7},{6,4},{7,5},{8,10},{9,11},{10,... | collective-permute-start | bytes 786440 | tf_op jit(solution)/shard_map/ppermute | solution.py:22
  39.0 14.7 %slice-start = ((s8[8388608]{0:T(1024)(128)(4,1)}), s8[4194304]{0:T(1024)(128)(4,1)S(1)}, s32[]{:S(2)}) async-start(s8[8388608]{0:T(1024)(128)(4,1)} %bitcast.13), calls=%async_computation.1 | async-start | bytes 8388608
  49.8 3.8 %slice-start.1 = ((s8[8388608]{0:T(1024)(128)(4,1)}), s8[4194304]{0:T(1024)(128)(4,1)S(1)}, s32[]{:S(2)}) async-start(s8[8388608]{0:T(1024)(128)(4,1)} %bitcast.13), calls=%async_computation.2 | async-start | bytes 8388608
  51.9 1.7 %collective-permute-start.14 = (bf16[64,2176]{1,0:T(8,128)(2,1)S(1)}, bf16[64,2176]{1,0:T(8,128)(2,1)S(1)}, u32[]{:S(2)}, u32[]{:S(2)}) collective-permute-start(bf16[64,2176]{1,0:T(8,128)(2,1)S(1)} %get-tuple-element.24), channel_id=1, source_target_pairs={{0,16},{16,0},{1,17},{17,1},{2,18},{18,2},{3,19},{19,3},{4,20},{20... | collective-permute-start | bytes 835592 | tf_op jit(solution)/shard_map/ppermute | solution.py:22
  55.5 5.6 %collective-permute-start.15 = (bf16[16,2048]{1,0:T(8,128)(2,1)S(1)}, bf16[16,2048]{1,0:T(8,128)(2,1)S(1)}, u32[]{:S(2)}, u32[]{:S(2)}) collective-permute-start(bf16[16,2048]{1,0:T(8,128)(2,1)S(1)} %get-tuple-element.30), channel_id=1, source_target_pairs={{0,1},{1,0},{2,3},{3,2},{4,5},{5,4},{6,7},{7,6},{8,9},{9,8},{10,11... | collective-permute-start | bytes 196616 | tf_op jit(solution)/shard_map/ppermute | solution.py:22
  56.2 5.0 %collective-permute-start.16 = (bf16[16,2048]{1,0:T(8,128)(2,1)S(1)}, bf16[16,2048]{1,0:T(8,128)(2,1)S(1)}, u32[]{:S(2)}, u32[]{:S(2)}) collective-permute-start(bf16[16,2048]{1,0:T(8,128)(2,1)S(1)} %get-tuple-element.31), channel_id=1, source_target_pairs={{0,2},{1,3},{2,0},{3,1},{4,6},{5,7},{6,4},{7,5},{8,10},{9,11},{10,... | collective-permute-start | bytes 196616 | tf_op jit(solution)/shard_map/ppermute | solution.py:22
  56.7 5.2 %collective-permute-start.17 = (bf16[16,2048]{1,0:T(8,128)(2,1)S(1)}, bf16[16,2048]{1,0:T(8,128)(2,1)S(1)}, u32[]{:S(2)}, u32[]{:S(2)}) collective-permute-start(bf16[16,2048]{1,0:T(8,128)(2,1)S(1)} %get-tuple-element.32), channel_id=1, source_target_pairs={{0,3},{1,2},{2,1},{3,0},{4,7},{5,6},{6,5},{7,4},{8,11},{9,10},{10,... | collective-permute-start | bytes 196616 | tf_op jit(solution)/shard_map/ppermute | solution.py:22
  61.9 2.4 %collective-permute-start.18 = (f32[8,2048]{1,0:T(8,128)S(1)}, f32[8,2048]{1,0:T(8,128)S(1)}, u32[]{:S(2)}, u32[]{:S(2)}) collective-permute-start(f32[8,2048]{1,0:T(8,128)S(1)} %get-tuple-element.38), channel_id=1, source_target_pairs={{0,16},{16,0},{1,17},{17,1},{2,18},{18,2},{3,19},{19,3},{4,20},{20... | collective-permute-start | bytes 196616 | tf_op jit(solution)/shard_map/ppermute | solution.py:22

commit v9 on v7

--- a/solution.py
+++ b/solution.py
@@ -56,34 +56,42 @@
         kv_ref[at, width:] = act(3).astype(BF16)
 
 
-def attend(q_ref, kv_refs, gate_ref, gain_ref, att_ref):
+STEP = 256
+
+
+def attend(q_ref, kv_refs, att_ref, pairs):
     rows, width = q_ref.shape
     head = width // HEADS
-    step = min(rows, 256)
+    step = min(rows, STEP)
     blocks = [(ref, r) for ref in kv_refs for r in range(0, ref.shape[0], step)]
     tri = lax.broadcasted_iota(jnp.int32, (step, step), 1) <= lax.broadcasted_iota(
         jnp.int32, (step, step), 0
     )
     before = len(blocks) - rows // step
-    for i in range(rows // step):
+    for i, h in pairs:
         at = slice(i * step, (i + 1) * step)
-        for h in range(HEADS):
-            q = q_ref[at, h * head : (h + 1) * head]
-            total = None
-            for j in range(before + i + 1):
-                ref, r = blocks[j]
-                k = ref[r : r + step, width + h * head : width + (h + 1) * head]
-                v = ref[r : r + step, h * head : (h + 1) * head]
-                s = lax.dot_general(q, k, (((1,), (1,)), ((), ())), preferred_element_type=F32)
-                wts = silu_half(s * (0.5 * head**-0.5))
-                if j == before + i:
-                    wts = jnp.where(tri, wts, 0.0)
-                mixed = jnp.dot(wts.astype(BF16), v, preferred_element_type=F32)
-                total = mixed if total is None else total + mixed
-            att_ref[at, h * head : (h + 1) * head] = total
-    att = att_ref[...]
+        q = q_ref[at, h * head : (h + 1) * head]
+        total = None
+        for j in range(before + i + 1):
+            ref, r = blocks[j]
+            k = ref[r : r + step, width + h * head : width + (h + 1) * head]
+            v = ref[r : r + step, h * head : (h + 1) * head]
+            s = lax.dot_general(q, k, (((1,), (1,)), ((), ())), preferred_element_type=F32)
+            wts = silu_half(s * (0.5 * head**-0.5))
+            if j == before + i:
+                wts = jnp.where(tri, wts, 0.0)
+            mixed = jnp.dot(wts.astype(BF16), v, preferred_element_type=F32)
+            total = mixed if total is None else total + mixed
+        att_ref[at, h * head : (h + 1) * head] = total
+
+
+def all_pairs(rows):
+    return [(i, h) for i in range(max(rows // STEP, 1)) for h in range(HEADS)]
+
+
+def gated_rows(att, gain_ref, gate):
     inv = lax.rsqrt(jnp.mean(att * att, axis=1, keepdims=True) + EPSILON)
-    return (att * inv * gain_ref[:1] * gate_ref[...].astype(F32)).astype(BF16)
+    return (att * inv * gain_ref[:1] * gate.astype(F32)).astype(BF16)
 
 
 def membership(bounds_ref, row0, rows):
@@ -104,7 +112,7 @@
     return (terms[:sess] + terms[sess : 2 * sess] + terms[2 * sess :] + sums_ev) / n_valid
 
 
-def first_kernel(place, dps, copies_out, n_parts, bounds_ref, ev_ref, gain_ref, *refs):
+def first_kernel(place, dps, n_parts, bounds_ref, ev_ref, gain_ref, *refs):
     parts, refs = refs[:n_parts], refs[n_parts:]
     pooled_ref, w_ref, wout_ref, kv_ref, sums_ev_ref, sums_g_ref, q_ref, gate_ref, att_ref = refs
     place(parts, w_ref, wout_ref)
@@ -112,11 +120,11 @@
     sums_ev = jnp.dot(member, ev_ref[...], preferred_element_type=F32)
     sums_ev_ref[...] = sums_ev
     project(dps, 0, bounds_ref[2, :1, :1], ev_ref, w_ref, gate_ref, q_ref, kv_ref)
-    gated = attend(q_ref, [kv_ref], gate_ref, gain_ref, att_ref)
+    attend(q_ref, [kv_ref], att_ref, all_pairs(q_ref.shape[0]))
+    gated = gated_rows(att_ref[...], gain_ref, gate_ref[...])
     sums_g_ref[...] = jnp.dot(member, gated, preferred_element_type=F32)
     out = pool(dps, bounds_ref, sums_ev, sums_g_ref, wout_ref)
-    peers, take = copies_out
-    pooled_ref[...] = jnp.concatenate([out[:take]] * peers, axis=0).astype(BF16)
+    pooled_ref[...] = out[: pooled_ref.shape[0]]
 
 
 def halves(ref):
@@ -131,13 +139,29 @@
     out_ref[...] = sums_ev_ref[...] + jnp.dot(member, ev_ref[...], preferred_element_type=F32)
 
 
-def attend_kernel(row0, at, rows, bounds_ref, gain_ref, qg_ref, kv_first, kv_ref, sums_ref, _, out_ref, att_ref):
-    here = pl.ds(at, rows)
+def attend_kernel(pairs, qg_ref, kv_first, kv_ref, _, att_ref):
+    attend(halves(qg_ref)[0], [kv_first, kv_ref], att_ref, pairs)
+
+
+def attend_rest_kernel(row0, done, bounds_ref, gain_ref, qg_ref, kv_first, kv_ref, sums_ref, *refs):
+    *before_refs, _, out_ref, att_ref = refs
     q_ref, gate_ref = halves(qg_ref)
-    member = membership(bounds_ref, row0 + at, rows)
-    kv_refs = [kv_first, kv_ref.at[: at + rows]]
-    gated = attend(q_ref.at[here], kv_refs, gate_ref.at[here], gain_ref, att_ref)
-    out_ref[...] = sums_ref[...] + jnp.dot(member, gated, preferred_element_type=F32)
+    rows, width = q_ref.shape
+    here = [pair for pair in all_pairs(rows) if not any(pair in pairs for pairs in done)]
+    attend(q_ref, [kv_first, kv_ref], att_ref, here)
+    head = width // HEADS
+    step = min(rows, STEP)
+    total = sums_ref[...]
+    for i in range(rows // step):
+        at = slice(i * step, (i + 1) * step)
+        att = []
+        for h in range(HEADS):
+            ref = next((ref for ref, pairs in zip(before_refs, done) if (i, h) in pairs), att_ref)
+            att.append(ref[at, h * head : (h + 1) * head])
+        gated = gated_rows(jnp.concatenate(att, axis=1), gain_ref, gate_ref[at])
+        member = membership(bounds_ref, row0 + i * step, step)
+        total = total + jnp.dot(member, gated, preferred_element_type=F32)
+    out_ref[...] = total
 
 
 def call(kernel, name, operands, out_shape, scratch, mib, flops, size, transcendentals=0):
@@ -208,6 +232,7 @@
     from_x, from_y = swap(w_in, "mp", mps, 1), swap(w_in, "mp", mps, 2)
     middle = w_in.shape[0] // 32 * 16
     diagonal = [swap(from_x[:middle], "mp", mps, 2), swap(from_y[middle:], "mp", mps, 1)]
+    blocks = [[w_in], [from_x], [from_y], diagonal]
 
     def place(parts, w_ref, wout_ref):
         sec, m = lax.axis_index("section"), lax.axis_index("mp")
@@ -224,7 +249,7 @@
                 rows = pl.ds(pl.multiple_of(row + owner * part, part), part)
                 wout_ref[rows, at : at + cut] = ref[k, depth:]
 
-    return place, parts, [[w_in], [from_x], [from_y], diagonal], dps
+    return place, parts, blocks, dps
 
 
 def two_terms(square):
@@ -233,12 +258,13 @@
     return jnp.where(lane == 0, hi, jnp.where(lane == 1, square - hi, 0.0)).astype(BF16)
 
 
-def up_kernel(chunks, pieces, x_ref, *refs):
+def up_kernel(chunks, pieces, *refs):
+    x_refs, refs = refs[: len(pieces)], refs[len(pieces) :]
     w_in_refs, refs = refs[: sum(pieces)], refs[sum(pieces) :]
     w_ref, local_ref, half_ref, send_ref, normed_ref = refs
     m = lax.axis_index("mp")
-    depth = x_ref.shape[1]
-    x = x_ref[...]
+    x = jnp.concatenate([ref[...] for ref in x_refs], axis=0)
+    depth = x.shape[1]
     square = None
     at = 0
     for k, n in enumerate(pieces):
@@ -264,7 +290,7 @@
     send_ref[:, wide:] = two_terms(square)
 
 
-def down_kernel(chunks, sections, mps, take, half_ref, other_ref, local_ref, w_ref, _, own_ref, *refs):
+def down_kernel(chunks, half_ref, other_ref, local_ref, w_ref, _, own_ref, *refs):
     *send_refs, part_ref = refs
     units, wide = w_ref.shape
     each = wide // chunks
@@ -280,9 +306,16 @@
     own = pl.ds(pl.multiple_of(m * cols, cols), cols)
     part_ref[:, own] = part_ref[:, own] + local_ref[...]
     for k, ref in enumerate([own_ref, *send_refs]):
-        starts = [pl.multiple_of((s * mps + (m ^ k)) * take, take) for s in range(sections)]
-        mine = [part_ref[pl.ds(start, take), :] for start in starts]
-        ref[...] = jnp.concatenate(mine, axis=0).astype(ref.dtype)
+        count = ref.shape[0]
+        ref[...] = part_ref[k * count : (k + 1) * count, :].astype(ref.dtype)
+
+
+def pair_kernel(own_ref, got_ref, _, out_ref, pair_ref):
+    sec = lax.axis_index("section")
+    take = own_ref.shape[0]
+    pair_ref[pl.ds(pl.multiple_of(sec * take, take), take), :] = own_ref[...]
+    pair_ref[pl.ds(pl.multiple_of((1 - sec) * take, take), take), :] = got_ref[...]
+    out_ref[...] = pair_ref[...].astype(BF16)
 
 
 def add_kernel(own_ref, *refs):
@@ -315,7 +348,6 @@
     cols = w_in.shape[1]
     units = w_up.shape[1]
     half_width = w_down.shape[1]
-    group = ("section", "mp")
     first = take * SESS_MAX
     rest = length - first
 
@@ -326,11 +358,11 @@
     place, parts, w_in_blocks, dps = gather_weights(w_uvqk, w_out, w_in, ffn_gain, sections, dps, mps)
 
     micro_rows, full_w, full_wout, kv_first, sums_ev, sums_g = call(
-        functools.partial(first_kernel, place, dps, (peers, take), len(parts)),
+        functools.partial(first_kernel, place, dps, len(parts)),
         "encode_first",
         [bounds, events[:first], gain, *parts],
         [
-            ((rows, width), BF16),
+            ((take, width), F32),
             ((width, 4 * width), BF16),
             ((width, width), BF16),
             ((first, 2 * width), BF16),
@@ -347,25 +379,11 @@
         6 * 1024 * 1024,
         4 * first * width + HEADS * first * first,
     )
-    arrived = lax.all_to_all(
-        micro_rows.reshape(peers, take, width), group, split_axis=0, concat_axis=0, tiled=True
-    ).reshape(rows, width)
-    blocks = [piece for block in w_in_blocks for piece in block]
-    local, half, half_send = call(
-        functools.partial(up_kernel, 4, [len(block) for block in w_in_blocks]),
-        "up_half",
-        [arrived, *blocks, w_up],
-        [((rows, cols), F32), ((rows, units + 128), F32), ((rows, units + 128), BF16)],
-        [pltpu.VMEM((rows, w_up.shape[0]), BF16)],
-        10,
-        2 * rows * w_up.size,
-        2 * w_up.size,
-    )
-    other = swap(half_send, "section", sections, 1)
+    got = swap(micro_rows, "section", sections, 1)
     queries_gate, kv_rest, sums_ev = call(
         functools.partial(project_kernel, dps, first),
         "project_rest",
-        [bounds, events[first:], full_w, sums_ev, local],
+        [bounds, events[first:], full_w, sums_ev, micro_rows],
         [((rest, 2 * width), BF16), ((rest, 2 * width), BF16), ((sess, width), F32)],
         [],
         10,
@@ -374,10 +392,52 @@
         4 * rest * width,
     )
     pair = sections * take
+    (pair_rows,) = call(
+        pair_kernel,
+        "pair_rows",
+        [micro_rows, got, sums_ev],
+        [((pair, width), BF16)],
+        [pltpu.VMEM((pair, width), F32)],
+        8,
+        0,
+        4 * pair * width,
+    )
+    x = [pair_rows] + [swap(pair_rows, "mp", mps, k) for k in range(1, mps)]
+    blocks = [piece for block in w_in_blocks for piece in block]
+    local, half, half_send = call(
+        functools.partial(up_kernel, 4, [len(block) for block in w_in_blocks]),
+        "up_half",
+        [*x, *blocks, w_up],
+        [((rows, cols), F32), ((rows, units + 128), F32), ((rows, units + 128), BF16)],
+        [pltpu.VMEM((rows, w_up.shape[0]), BF16)],
+        10,
+        2 * rows * w_up.size,
+        2 * w_up.size,
+    )
+
+    pairs = all_pairs(rest)
+    done = [pairs[: HEADS // 2], pairs[HEADS // 2 : -1]]
+
+    def attend_part(which, after):
+        share = len(done[which])
+        return call(
+            functools.partial(attend_kernel, done[which]),
+            f"attend_{which}",
+            [queries_gate, kv_first, kv_rest, after],
+            [((rest, width), F32)],
+            [],
+            10,
+            4 * rest * length * width * share // len(pairs),
+            4 * 1024 * 1024,
+            HEADS * rest * length * share // len(pairs),
+        )[0]
+
+    other = swap(half_send, "section", sections, 1)
+    att = [attend_part(0, local)]
     own, *sends = call(
-        functools.partial(down_kernel, 4, sections, mps, take),
+        functools.partial(down_kernel, 4),
         "down_part",
-        [half, other, local, w_down, sums_ev],
+        [half, other, local, w_down, att[0]],
         [((pair, half_width), F32)] + [((pair, half_width), BF16)] * (mps - 1),
         [pltpu.VMEM((rows, half_width), F32)],
         8,
@@ -385,26 +445,12 @@
         2 * w_down.size,
         rows * units,
     )
-
-    def attend_part(at, count, sums, after):
-        return call(
-            functools.partial(attend_kernel, first, at, count),
-            f"attend_{at}",
-            [bounds, gain, queries_gate, kv_first, kv_rest, sums, after],
-            [((sess, width), F32)],
-            [pltpu.VMEM((count, width), F32)],
-            10,
-            4 * count * (first + at + count) * width,
-            4 * 1024 * 1024,
-            HEADS * count * (first + at + count),
-        )[0]
-
     got = [swap(x, "mp", mps, k + 1) for k, x in enumerate(sends)]
-    sums_g = attend_part(0, rest // 2, sums_g, own)
+    att.append(attend_part(1, own))
     keep, send = call(
         add_kernel,
         "add_parts",
-        [own, *got, sums_g],
+        [own, *got, att[1]],
         [((take, half_width), F32)] * 2,
         [pltpu.VMEM((pair, half_width), F32)],
         8,
@@ -412,7 +458,17 @@
         2 * mps * pair * half_width,
     )
     got = swap(send, "section", sections, 1)
-    sums_g = attend_part(rest // 2, rest - rest // 2, sums_g, keep)
+    (sums_g,) = call(
+        functools.partial(attend_rest_kernel, first, done),
+        "attend_last",
+        [bounds, gain, queries_gate, kv_first, kv_rest, sums_g, *att, keep],
+        [((sess, width), F32)],
+        [pltpu.VMEM((rest, width), F32)],
+        10,
+        rest * length * width // 2,
+        4 * 1024 * 1024,
+        HEADS * rest * length // len(pairs),
+    )
     cross_out, pooled = call(
         functools.partial(finish_kernel, dps),
         "finish",

time: 59.6 us -> 60.3 us (1.012)
  blocking collectives: 7.52 us -> 0 us
  waiting for transfers between devices: 13.5 us -> 18.1 us
  starting transfers between devices: 18.5 us -> 22 us
    all_to_all x1 -> x0, blocking collectives: 7.52 us -> none  [per_device(): lax.all_to_all(micro_rows.reshape(peers, take, width), group, split_axis=...]
    ppermute x18 -> x22, waiting for transfers between devices: 13.5 us -> 18.1 us  [swap(): return lax.ppermute(x, axis, [(i, i ^ flip) for i in range(size)])]
    ppermute x18 -> x22, starting transfers between devices: 18.5 us -> 22 us  [swap(): return lax.ppermute(x, axis, [(i, i ^ flip) for i in range(size)])]
    pallas_call x9 -> x11, Pallas kernels: 14.2 us -> 14.2 us  [call(): pl.pallas_call(kernel, in_specs=[VMEM] * len(operands), out_specs=[VMEM]...]
  transfers between devices with their start and end apart: 18 -> 22, of which waited for: 4 -> 10; matrix products, arithmetic and copies ran while one was open for 4% -> 4% of each run, Pallas kernels for 16% -> 16%
where the time goes in v9:
time: 60.3 us; the launch traced here: 60.1 us
  starting transfers between devices  22 us (36%)
  waiting for transfers between devices  18.1 us (30%)
  Pallas kernels  14.2 us (24%)
  local copies, waits for them, and re-layouts  2.08 us (3%)
  other arithmetic  2.07 us (3%)
  between operations  1.62 us (3%)
    ppermute x22, starting transfers between devices, swap(): return lax.ppermute(x, axis, [(i, i ^ flip) for i in range(size)])  22 us
    ppermute x22, waiting for transfers between devices, swap(): return lax.ppermute(x, axis, [(i, i ^ flip) for i in range(size)])  18.1 us
    pallas_call x11, Pallas kernels, call(): pl.pallas_call(kernel, in_specs=[VMEM] * len(operands), out_specs=[VMEM]...  14.2 us
    concatenate x1, other arithmetic, gather_weights(): jnp.concatenate([w_in, jnp.broadcast_to(ffn_gain, (16, w_in.shape[1]))],...  1.23 us
  transfers between devices with their start and end apart: 22, of which 10 were waited for; matrix products, arithmetic and copies ran while one was open for 4% of the time, Pallas kernels for 16%

profile of v9, /device:TPU:0, one launch (start us, length us, event | category | flops | bytes accessed | tf_op | source)
XLA Modules:
  0.0 60.1 jit_solution(3867852049990784682)
XLA Ops:
  0.7 1.0 %constant_dynamic-slice_fusion.1 = bf16[128,512]{1,0:T(8,128)(2,1)S(1)} fusion(bf16[128,2048]{1,0:T(8,128)(2,1)} %param.13, s32[]{:T(128)S(6)} %select_n.11), kind=kLoop, calls=%fused_computation.10 | loop fusion | bytes 262148 | tf_op jit(solution)/shard_map/dynamic_slice | solution.py:212
  1.7 0.8 %constant_dynamic-slice_fusion = bf16[32,512]{1,0:T(8,128)(2,1)S(1)} fusion(bf16[128,512]{1,0:T(8,128)(2,1)} %param.14, s32[]{:T(128)S(6)} %select_n.12), kind=kLoop, calls=%fused_computation.9 | loop fusion | bytes 65540 | tf_op jit(solution)/shard_map/dynamic_slice | solution.py:213
  2.5 4.1 %collective-permute-start = (bf16[160,512]{1,0:T(8,128)(2,1)S(1)}, bf16[160,512]{1,0:T(8,128)(2,1)S(1)}, u32[]{:S(2)}, u32[]{:S(2)}) collective-permute-start(bf16[160,512]{1,0:T(8,128)(2,1)S(1)} %pad_maximum_fusion.1), channel_id=1, source_target_pairs={{0,8},{4,12},{8,0},{12,4},{1,9},{5,13},{9,1},{13,5},{2,10},{6,14},... | collective-permute-start | bytes 491528 | tf_op jit(solution)/shard_map/ppermute | solution.py:22
  6.6 1.3 %collective-permute-start.1 = (bf16[160,512]{1,0:T(8,128)(2,1)S(1)}, bf16[160,512]{1,0:T(8,128)(2,1)S(1)}, u32[]{:S(2)}, u32[]{:S(2)}) collective-permute-start(bf16[160,512]{1,0:T(8,128)(2,1)S(1)} %pad_maximum_fusion.1), channel_id=1, source_target_pairs={{0,12},{4,8},{8,4},{12,0},{1,13},{5,9},{9,5},{13,1},{2,14},{6,10},... | collective-permute-start | bytes 491528 | tf_op jit(solution)/shard_map/ppermute | solution.py:22
  8.2 0.7 %reduce = bf16[512]{0:T(512)(128)(2,1)S(1)} reduce(bf16[1,512]{1,0:T(2,128)(2,1)} %param.17, bf16[]{:T(256)} %constant.27), dimensions={0}, to_apply=%param.17.reduce_sub_computation | reduce | bytes 2050 | tf_op args[7]
  8.9 1.2 %pad_maximum_fusion.refs_4_ = bf16[528,512]{1,0:T(8,128)(2,1)S(1)} fusion(bf16[16,512]{1,0:T(8,128)(2,1)S(1)} %broadcast_in_dim.36, bf16[512,512]{1,0:T(8,128)(2,1)} %param.16), kind=kLoop, calls=%fused_computation | loop fusion | flops 1081344 | bytes 1081344 | tf_op jit(solution)/shard_map/concatenate | solution.py:195
  10.2 1.6 %collective-permute-start.14 = (bf16[528,512]{1,0:T(8,128)(2,1)S(1)}, bf16[528,512]{1,0:T(8,128)(2,1)S(1)}, u32[]{:S(2)}, u32[]{:S(2)}) collective-permute-start(bf16[528,512]{1,0:T(8,128)(2,1)S(1)} %pad_maximum_fusion.refs_4_), channel_id=1, source_target_pairs={{0,2},{1,3},{2,0},{3,1},{4,6},{5,7},{6,4},{7,5},{8,10},{9,11},{10,... | collective-permute-start | bytes 1622024 | tf_op jit(solution)/shard_map/ppermute | solution.py:22
  11.7 1.5 %collective-permute-start.13 = (bf16[528,512]{1,0:T(8,128)(2,1)S(1)}, bf16[528,512]{1,0:T(8,128)(2,1)S(1)}, u32[]{:S(2)}, u32[]{:S(2)}) collective-permute-start(bf16[528,512]{1,0:T(8,128)(2,1)S(1)} %pad_maximum_fusion.refs_4_), channel_id=1, source_target_pairs={{0,1},{1,0},{2,3},{3,2},{4,5},{5,4},{6,7},{7,6},{8,9},{9,8},{10,11... | collective-permute-start | bytes 1622024 | tf_op jit(solution)/shard_map/ppermute | solution.py:22
  13.4 5.3 %collective-permute-done.refs_0_ = bf16[160,512]{1,0:T(8,128)(2,1)S(1)} collective-permute-done((bf16[160,512]{1,0:T(8,128)(2,1)S(1)}, bf16[160,512]{1,0:T(8,128)(2,1)S(1)}, u32[]{:S(2)}, u32[]{:S(2)}) %collective-permute-start) | collective-permute-done | bytes 163872 | tf_op jit(solution)/shard_map/ppermute | solution.py:22
  19.2 1.6 %collective-permute-start.3 = (bf16[3,160,256]{2,1,0:T(8,128)(2,1)S(1)}, bf16[3,160,256]{2,1,0:T(8,128)(2,1)S(1)}, u32[]{:S(2)}, u32[]{:S(2)}) collective-permute-start(bf16[3,160,256]{2,1,0:T(8,128)(2,1)S(1)} %get-tuple-element.24.refs_4_), channel_id=1, source_target_pairs={{0,1},{1,0},{2,3},{3,2},{4,5},{5,4},{6,7},{7,6},{8,9},{9,8},{10,11... | collective-permute-start | bytes 737288 | tf_op jit(solution)/shard_map/ppermute | solution.py:22
  20.8 1.5 %collective-permute-start.4 = (bf16[3,160,256]{2,1,0:T(8,128)(2,1)S(1)}, bf16[3,160,256]{2,1,0:T(8,128)(2,1)S(1)}, u32[]{:S(2)}, u32[]{:S(2)}) collective-permute-start(bf16[3,160,256]{2,1,0:T(8,128)(2,1)S(1)} %get-tuple-element.25.refs_5_), channel_id=1, source_target_pairs={{0,2},{1,3},{2,0},{3,1},{4,6},{5,7},{6,4},{7,5},{8,10},{9,11},{10,... | collective-permute-start | bytes 737288 | tf_op jit(solution)/shard_map/ppermute | solution.py:22
  23.2 6.9 %collective-permute-done.3.refs_6_ = bf16[3,160,256]{2,1,0:T(8,128)(2,1)S(1)} collective-permute-done((bf16[3,160,256]{2,1,0:T(8,128)(2,1)S(1)}, bf16[3,160,256]{2,1,0:T(8,128)(2,1)S(1)}, u32[]{:S(2)}, u32[]{:S(2)}) %collective-permute-start.3) | collective-permute-done | bytes 245792 | tf_op jit(solution)/shard_map/ppermute | solution.py:22
  30.8 1.6 %collective-permute-start.16 = (bf16[272,512]{1,0:T(8,128)(2,1)S(1)}, bf16[272,512]{1,0:T(8,128)(2,1)S(1)}, u32[]{:S(2)}, u32[]{:S(2)}) collective-permute-start(bf16[272,512]{1,0:T(8,128)(2,1)S(1)} %slice.41), channel_id=1, source_target_pairs={{0,1},{1,0},{2,3},{3,2},{4,5},{5,4},{6,7},{7,6},{8,9},{9,8},{10,11... | collective-permute-start | bytes 835592 | tf_op jit(solution)/shard_map/ppermute | solution.py:22
  32.4 0.6 collective-permute-start.15
  33.1 3.5 %encode_first.1 = (f32[8,512]{1,0:T(8,128)S(1)}, bf16[512,2048]{1,0:T(8,128)(2,1)S(1)}, bf16[512,512]{1,0:T(8,128)(2,1)S(1)}, bf16[512,1024]{1,0:T(8,128)(2,1)S(...) custom-call(f32[3,32,128]{2,1,0:T(8,128)S(1)} %broadcast_in_dim.33.bounds_ref, ...), custom_call_target="tpu_custom_call" | custom-call | flops 1342177280 | bytes 6291456 | tf_op jit(solution)/shard_map/encode_first/pallas_call | solution.py:168
  36.7 1.6 %project_rest.1 = (bf16[512,1024]{1,0:T(8,128)(2,1)S(1)}, bf16[512,1024]{1,0:T(8,128)(2,1)S(1)}, f32[32,512]{1,0:T(8,128)S(1)}) custom-call(f32[3,32,128]{2,1,0:T(8,128)S(1)} %broadcast_in_dim.33.bounds_ref, bf16[512,512]{1,0:T(8,128)(2,1)S(1)} %get-tuple-element.46.ev_ref, bf16[512,2048]{1,0:T(8,128)(2,1)S(1)} %get-tuple-element.27.w_ref, ...), custom_call_target="tpu_custom_call" | custom-call | flops 1073741824 | bytes 6291456 | tf_op jit(solution)/shard_map/project_rest/pallas_call | solution.py:168
  38.4 1.1 %collective-permute-start.10 = (bf16[16,512]{1,0:T(8,128)(2,1)S(1)}, bf16[16,512]{1,0:T(8,128)(2,1)S(1)}, u32[]{:S(2)}, u32[]{:S(2)}) collective-permute-start(bf16[16,512]{1,0:T(8,128)(2,1)S(1)} %pair_rows.1.refs_0_), channel_id=1, source_target_pairs={{0,1},{1,0},{2,3},{3,2},{4,5},{5,4},{6,7},{7,6},{8,9},{9,8},{10,11... | collective-permute-start | bytes 49160 | tf_op jit(solution)/shard_map/ppermute | solution.py:22
  39.4 1.1 %collective-permute-start.11 = (bf16[16,512]{1,0:T(8,128)(2,1)S(1)}, bf16[16,512]{1,0:T(8,128)(2,1)S(1)}, u32[]{:S(2)}, u32[]{:S(2)}) collective-permute-start(bf16[16,512]{1,0:T(8,128)(2,1)S(1)} %pair_rows.1.refs_0_), channel_id=1, source_target_pairs={{0,2},{1,3},{2,0},{3,1},{4,6},{5,7},{6,4},{7,5},{8,10},{9,11},{10,... | collective-permute-start | bytes 49160 | tf_op jit(solution)/shard_map/ppermute | solution.py:22
  40.5 1.4 %collective-permute-start.12 = (bf16[16,512]{1,0:T(8,128)(2,1)S(1)}, bf16[16,512]{1,0:T(8,128)(2,1)S(1)}, u32[]{:S(2)}, u32[]{:S(2)}) collective-permute-start(bf16[16,512]{1,0:T(8,128)(2,1)S(1)} %pair_rows.1.refs_0_), channel_id=1, source_target_pairs={{0,3},{1,2},{2,1},{3,0},{4,7},{5,6},{6,5},{7,4},{8,11},{9,10},{10,... | collective-permute-start | bytes 49160 | tf_op jit(solution)/shard_map/ppermute | solution.py:22
  42.2 1.0 %collective-permute-done.11.refs_2_ = bf16[16,512]{1,0:T(8,128)(2,1)S(1)} collective-permute-done((bf16[16,512]{1,0:T(8,128)(2,1)S(1)}, bf16[16,512]{1,0:T(8,128)(2,1)S(1)}, u32[]{:S(2)}, u32[]{:S(2)}) %collective-permute-start.11) | collective-permute-done | bytes 16416 | tf_op jit(solution)/shard_map/ppermute | solution.py:22
  43.2 2.0 %collective-permute-done.12.refs_3_ = bf16[16,512]{1,0:T(8,128)(2,1)S(1)} collective-permute-done((bf16[16,512]{1,0:T(8,128)(2,1)S(1)}, bf16[16,512]{1,0:T(8,128)(2,1)S(1)}, u32[]{:S(2)}, u32[]{:S(2)}) %collective-permute-start.12) | collective-permute-done | bytes 16416 | tf_op jit(solution)/shard_map/ppermute | solution.py:22
  45.1 2.0 %up_half.1 = (f32[64,512]{1,0:T(8,128)S(1)}, f32[64,2176]{1,0:T(8,128)S(1)}, bf16[64,2176]{1,0:T(8,128)(2,1)S(1)}) custom-call(bf16[16,512]{1,0:T(8,128)(2,1)S(1)} %pair_rows.1.refs_0_, bf16[16,512]{1,0:T(8,128)(2,1)S(1)} %collective-permute-done.10.refs_1_, bf16[16,512]{1,0:T(8,128)(2,1)S(1)} %collective-permute-done.11.refs_2_, ...), custom_call_target="tpu_custom_call" | custom-call | flops 536870912 | bytes 8388608 | tf_op jit(solution)/shard_map/up_half/pallas_call | solution.py:168
  47.3 1.0 %attend_0.1._.refs_0_ = f32[512,512]{1,0:T(8,128)S(1)} custom-call(bf16[512,1024]{1,0:T(8,128)(2,1)S(1)} %get-tuple-element.33.qg_ref, bf16[512,1024]{1,0:T(8,128)(2,1)S(1)} %get-tuple-element.34.kv_first, bf16[512,1024]{1,0:T(8,128)(2,1)S(1)} %get-tuple-element.35.kv_ref, f32[64,512]{1,0:T(8,128)S(1)} %get-tuple-element.32._.local_ref), custom_call_target="tpu_custom_call" | custom-call | flops 268435456 | bytes 4194304 | tf_op jit(solution)/shard_map/attend_0/pallas_call | solution.py:168
  48.3 0.5 collective-permute-done.17.other_ref
  48.8 1.8 %down_part.1 = (f32[16,2048]{1,0:T(8,128)S(1)}, bf16[16,2048]{1,0:T(8,128)(2,1)S(1)}, bf16[16,2048]{1,0:T(8,128)(2,1)S(1)}, bf16[16,2048]{1,0:T(8,128)(2,1)S(1)}) custom-call(f32[64,2176]{1,0:T(8,128)S(1)} %get-tuple-element.30.half_ref, bf16[64,2176]{1,0:T(8,128)(2,1)S(1)} %collective-permute-done.17.other_ref, ...), custom_call_target="tpu_custom_call" | custom-call | flops 536870912 | bytes 8388608 | tf_op jit(solution)/shard_map/down_part/pallas_call | solution.py:168
  50.6 1.6 %collective-permute-start.18 = (bf16[16,2048]{1,0:T(8,128)(2,1)S(1)}, bf16[16,2048]{1,0:T(8,128)(2,1)S(1)}, u32[]{:S(2)}, u32[]{:S(2)}) collective-permute-start(bf16[16,2048]{1,0:T(8,128)(2,1)S(1)} %get-tuple-element.37), channel_id=1, source_target_pairs={{0,1},{1,0},{2,3},{3,2},{4,5},{5,4},{6,7},{7,6},{8,9},{9,8},{10,11... | collective-permute-start | bytes 196616 | tf_op jit(solution)/shard_map/ppermute | solution.py:22
  52.7 1.5 %collective-permute-start.20 = (bf16[16,2048]{1,0:T(8,128)(2,1)S(1)}, bf16[16,2048]{1,0:T(8,128)(2,1)S(1)}, u32[]{:S(2)}, u32[]{:S(2)}) collective-permute-start(bf16[16,2048]{1,0:T(8,128)(2,1)S(1)} %get-tuple-element.39), channel_id=1, source_target_pairs={{0,3},{1,2},{2,1},{3,0},{4,7},{5,6},{6,5},{7,4},{8,11},{9,10},{10,... | collective-permute-start | bytes 196616 | tf_op jit(solution)/shard_map/ppermute | solution.py:22
  54.2 2.4 %attend_1.1.refs_3_.refs_1_ = f32[512,512]{1,0:T(8,128)S(1)} custom-call(bf16[512,1024]{1,0:T(8,128)(2,1)S(1)} %get-tuple-element.33.qg_ref, bf16[512,1024]{1,0:T(8,128)(2,1)S(1)} %get-tuple-element.34.kv_first, bf16[512,1024]{1,0:T(8,128)(2,1)S(1)} %get-tuple-element.35.kv_ref, f32[16,2048]{1,0:T(8,128)S(1)} %get-tuple-element.36._.own_ref), custom_call_target="tpu_custom_call" | custom-call | flops 671088640 | bytes 4194304 | tf_op jit(solution)/shard_map/attend_1/pallas_call | solution.py:168
  56.6 0.6 collective-permute-done.19.refs_1_
  57.2 0.7 %collective-permute-done.20.refs_2_ = bf16[16,2048]{1,0:T(8,128)(2,1)S(1)} collective-permute-done((bf16[16,2048]{1,0:T(8,128)(2,1)S(1)}, bf16[16,2048]{1,0:T(8,128)(2,1)S(1)}, u32[]{:S(2)}, u32[]{:S(2)}) %collective-permute-start.20) | collective-permute-done | bytes 65568 | tf_op jit(solution)/shard_map/ppermute | solution.py:22
  58.0 0.9 %attend_last.1.sums_g_ref = f32[32,512]{1,0:T(8,128)S(1)} custom-call(f32[3,32,128]{2,1,0:T(8,128)S(1)} %broadcast_in_dim.33.bounds_ref, f32[8,512]{1,0:T(8,128)S(1)} %broadcast_in_dim.34.gain_ref, bf16[512,1024]{1,0:T(8,128)(2,1)S(1)} %get-tuple-element.33.qg_ref, bf16[512,1024]{1,0:T(8,128)(2,1)S(1)} %get-tuple-element.34.kv_first, ...), custom_call_target="tpu_custom_call" | custom-call | flops 134217728 | bytes 4194304 | tf_op jit(solution)/shard_map/attend_last/pallas_call | solution.py:168
  59.2 0.8 %finish.1 = (bf16[8,4096]{1,0:T(8,128)(2,1)}, bf16[32,512]{1,0:T(8,128)(2,1)}) custom-call(f32[8,2048]{1,0:T(8,128)S(1)} %get-tuple-element.40.refs_2_.keep_ref, f32[8,2048]{1,0:T(8,128)S(1)} %collective-permute-done.21.got_ref, f32[3,32,128]{2,1,0:T(8,128)S(1)} %broadcast_in_dim.33.bounds_ref, f32[32,512]{1,0:T(8,128)S(1)} %get-tuple-element.29._.sums_ev_ref, ...), custom_call_target="tpu_custom_call" | custom-call | flops 50331648 | bytes 2097152 | tf_op jit(solution)/shard_map/finish/pallas_call | solution.py:168
  (60 shorter events, 3.2 us)
Async XLA Ops:
  0.6 12.7 %copy-start.1 = (bf16[128,2048]{1,0:T(8,128)(2,1)S(1)}, bf16[128,2048]{1,0:T(8,128)(2,1)}, u32[]{:S(2)}) copy-start(bf16[128,2048]{1,0:T(8,128)(2,1)} %param.13) | copy-start | bytes 1572868
  0.6 12.6 %copy-start = (bf16[1,1024,512]{2,1,0:T(8,128)(2,1)S(1)}, bf16[1,1024,512]{2,1,0:T(8,128)(2,1)}, u32[]{:S(2)}) copy-start(bf16[1,1024,512]{2,1,0:T(8,128)(2,1)} %param.10) | copy-start | bytes 3145732
  2.5 16.2 %collective-permute-start = (bf16[160,512]{1,0:T(8,128)(2,1)S(1)}, bf16[160,512]{1,0:T(8,128)(2,1)S(1)}, u32[]{:S(2)}, u32[]{:S(2)}) collective-permute-start(bf16[160,512]{1,0:T(8,128)(2,1)S(1)} %pad_maximum_fusion.1), channel_id=1, source_target_pairs={{0,8},{4,12},{8,0},{12,4},{1,9},{5,13},{9,1},{13,5},{2,10},{6,14},... | collective-permute-start | bytes 491528 | tf_op jit(solution)/shard_map/ppermute | solution.py:22
  6.6 12.1 %collective-permute-start.1 = (bf16[160,512]{1,0:T(8,128)(2,1)S(1)}, bf16[160,512]{1,0:T(8,128)(2,1)S(1)}, u32[]{:S(2)}, u32[]{:S(2)}) collective-permute-start(bf16[160,512]{1,0:T(8,128)(2,1)S(1)} %pad_maximum_fusion.1), channel_id=1, source_target_pairs={{0,12},{4,8},{8,4},{12,0},{1,13},{5,9},{9,5},{13,1},{2,14},{6,10},... | collective-permute-start | bytes 491528 | tf_op jit(solution)/shard_map/ppermute | solution.py:22
  7.9 11.3 %collective-permute-start.2 = (bf16[160,512]{1,0:T(8,128)(2,1)S(1)}, bf16[160,512]{1,0:T(8,128)(2,1)S(1)}, u32[]{:S(2)}, u32[]{:S(2)}) collective-permute-start(bf16[160,512]{1,0:T(8,128)(2,1)S(1)} %pad_maximum_fusion.1), channel_id=1, source_target_pairs={{0,4},{4,0},{8,12},{12,8},{1,5},{5,1},{9,13},{13,9},{2,6},{6,2},{1... | collective-permute-start | bytes 491528 | tf_op jit(solution)/shard_map/ppermute | solution.py:22
  8.9 13.5 %copy-start.2 = (bf16[128,512]{1,0:T(8,128)(2,1)S(1)}, bf16[128,512]{1,0:T(8,128)(2,1)}, u32[]{:S(2)}) copy-start(bf16[128,512]{1,0:T(8,128)(2,1)} %param.14) | copy-start | bytes 393220
  8.9 13.6 %copy-start.4 = (s32[1,32]{1,0:T(1,128)S(1)}, s32[1,32]{1,0:T(1,128)}, u32[]{:S(2)}) copy-start(s32[1,32]{1,0:T(1,128)} %param.12) | copy-start | bytes 388
  8.9 36.2 %slice-start.2 = ((s8[8388608]{0:T(1024)(128)(4,1)}), s8[4194304]{0:T(1024)(128)(4,1)S(1)}, s32[]{:S(2)}) async-start(s8[8388608]{0:T(1024)(128)(4,1)} %bitcast.13), calls=%async_computation.2 | async-start | bytes 8388608
  10.1 22.9 %copy-start.3 = (f32[512]{0:T(512)S(1)}, f32[512]{0:T(512)}, u32[]{:S(2)}) copy-start(f32[512]{0:T(512)} %param.15) | copy-start | bytes 6148
  10.2 20.5 %collective-permute-start.14 = (bf16[528,512]{1,0:T(8,128)(2,1)S(1)}, bf16[528,512]{1,0:T(8,128)(2,1)S(1)}, u32[]{:S(2)}, u32[]{:S(2)}) collective-permute-start(bf16[528,512]{1,0:T(8,128)(2,1)S(1)} %pad_maximum_fusion.refs_4_), channel_id=1, source_target_pairs={{0,2},{1,3},{2,0},{3,1},{4,6},{5,7},{6,4},{7,5},{8,10},{9,11},{10,... | collective-permute-start | bytes 1622024 | tf_op jit(solution)/shard_map/ppermute | solution.py:22
  11.7 19.1 %collective-permute-start.13 = (bf16[528,512]{1,0:T(8,128)(2,1)S(1)}, bf16[528,512]{1,0:T(8,128)(2,1)S(1)}, u32[]{:S(2)}, u32[]{:S(2)}) collective-permute-start(bf16[528,512]{1,0:T(8,128)(2,1)S(1)} %pad_maximum_fusion.refs_4_), channel_id=1, source_target_pairs={{0,1},{1,0},{2,3},{3,2},{4,5},{5,4},{6,7},{7,6},{8,9},{9,8},{10,11... | collective-permute-start | bytes 1622024 | tf_op jit(solution)/shard_map/ppermute | solution.py:22
  19.2 10.9 %collective-permute-start.3 = (bf16[3,160,256]{2,1,0:T(8,128)(2,1)S(1)}, bf16[3,160,256]{2,1,0:T(8,128)(2,1)S(1)}, u32[]{:S(2)}, u32[]{:S(2)}) collective-permute-start(bf16[3,160,256]{2,1,0:T(8,128)(2,1)S(1)} %get-tuple-element.24.refs_4_), channel_id=1, source_target_pairs={{0,1},{1,0},{2,3},{3,2},{4,5},{5,4},{6,7},{7,6},{8,9},{9,8},{10,11... | collective-permute-start | bytes 737288 | tf_op jit(solution)/shard_map/ppermute | solution.py:22
  20.8 9.3 %collective-permute-start.4 = (bf16[3,160,256]{2,1,0:T(8,128)(2,1)S(1)}, bf16[3,160,256]{2,1,0:T(8,128)(2,1)S(1)}, u32[]{:S(2)}, u32[]{:S(2)}) collective-permute-start(bf16[3,160,256]{2,1,0:T(8,128)(2,1)S(1)} %get-tuple-element.25.refs_5_), channel_id=1, source_target_pairs={{0,2},{1,3},{2,0},{3,1},{4,6},{5,7},{6,4},{7,5},{8,10},{9,11},{10,... | collective-permute-start | bytes 737288 | tf_op jit(solution)/shard_map/ppermute | solution.py:22
  22.4 10.0 %collective-permute-start.5 = (bf16[3,160,256]{2,1,0:T(8,128)(2,1)S(1)}, bf16[3,160,256]{2,1,0:T(8,128)(2,1)S(1)}, u32[]{:S(2)}, u32[]{:S(2)}) collective-permute-start(bf16[3,160,256]{2,1,0:T(8,128)(2,1)S(1)} %get-tuple-element.24.refs_4_), channel_id=1, source_target_pairs={{0,16},{16,0},{1,17},{17,1},{2,18},{18,2},{3,19},{19,3},{4,20},{20... | collective-permute-start | bytes 737288 | tf_op jit(solution)/shard_map/ppermute | solution.py:22
  30.2 2.8 %collective-permute-start.6 = (bf16[3,160,256]{2,1,0:T(8,128)(2,1)S(1)}, bf16[3,160,256]{2,1,0:T(8,128)(2,1)S(1)}, u32[]{:S(2)}, u32[]{:S(2)}) collective-permute-start(bf16[3,160,256]{2,1,0:T(8,128)(2,1)S(1)} %get-tuple-element.25.refs_5_), channel_id=1, source_target_pairs={{0,16},{16,0},{1,17},{17,1},{2,18},{18,2},{3,19},{19,3},{4,20},{20... | collective-permute-start | bytes 737288 | tf_op jit(solution)/shard_map/ppermute | solution.py:22
  30.2 2.8 %collective-permute-start.7 = (bf16[3,160,256]{2,1,0:T(8,128)(2,1)S(1)}, bf16[3,160,256]{2,1,0:T(8,128)(2,1)S(1)}, u32[]{:S(2)}, u32[]{:S(2)}) collective-permute-start(bf16[3,160,256]{2,1,0:T(8,128)(2,1)S(1)} %collective-permute-done.3.refs_6_), channel_id=1, source_target_pairs={{0,16},{16,0},{1,17},{17,1},{2,18},{18,2},{3,19},{19,3},{4,20},{20... | collective-permute-start | bytes 737288 | tf_op jit(solution)/shard_map/ppermute | solution.py:22
  30.7 2.3 %collective-permute-start.8 = (bf16[3,160,256]{2,1,0:T(8,128)(2,1)S(1)}, bf16[3,160,256]{2,1,0:T(8,128)(2,1)S(1)}, u32[]{:S(2)}, u32[]{:S(2)}) collective-permute-start(bf16[3,160,256]{2,1,0:T(8,128)(2,1)S(1)} %collective-permute-done.4.refs_7_), channel_id=1, source_target_pairs={{0,16},{16,0},{1,17},{17,1},{2,18},{18,2},{3,19},{19,3},{4,20},{20... | collective-permute-start | bytes 737288 | tf_op jit(solution)/shard_map/ppermute | solution.py:22
  30.8 14.3 %collective-permute-start.16 = (bf16[272,512]{1,0:T(8,128)(2,1)S(1)}, bf16[272,512]{1,0:T(8,128)(2,1)S(1)}, u32[]{:S(2)}, u32[]{:S(2)}) collective-permute-start(bf16[272,512]{1,0:T(8,128)(2,1)S(1)} %slice.41), channel_id=1, source_target_pairs={{0,1},{1,0},{2,3},{3,2},{4,5},{5,4},{6,7},{7,6},{8,9},{9,8},{10,11... | collective-permute-start | bytes 835592 | tf_op jit(solution)/shard_map/ppermute | solution.py:22
  32.4 12.7 %collective-permute-start.15 = (bf16[256,512]{1,0:T(8,128)(2,1)S(1)}, bf16[256,512]{1,0:T(8,128)(2,1)S(1)}, u32[]{:S(2)}, u32[]{:S(2)}) collective-permute-start(bf16[256,512]{1,0:T(8,128)(2,1)S(1)} %slice.40), channel_id=1, source_target_pairs={{0,2},{1,3},{2,0},{3,1},{4,6},{5,7},{6,4},{7,5},{8,10},{9,11},{10,... | collective-permute-start | bytes 786440 | tf_op jit(solution)/shard_map/ppermute | solution.py:22
  33.1 12.0 %slice-start.3 = ((s8[8388608]{0:T(1024)(128)(4,1)}), s8[4194304]{0:T(1024)(128)(4,1)S(1)}, s32[]{:S(2)}) async-start(s8[8388608]{0:T(1024)(128)(4,1)} %bitcast.13), calls=%async_computation.3 | async-start | bytes 8388608
  36.6 1.7 %collective-permute-start.9 = (f32[8,512]{1,0:T(8,128)S(1)}, f32[8,512]{1,0:T(8,128)S(1)}, u32[]{:S(2)}, u32[]{:S(2)}) collective-permute-start(f32[8,512]{1,0:T(8,128)S(1)} %get-tuple-element.26._.own_ref), channel_id=1, source_target_pairs={{0,16},{16,0},{1,17},{17,1},{2,18},{18,2},{3,19},{19,3},{4,20},{20... | collective-permute-start | bytes 49160 | tf_op jit(solution)/shard_map/ppermute | solution.py:22
  36.7 12.1 %slice-start = ((s8[8388608]{0:T(1024)(128)(4,1)}), s8[4194304]{0:T(1024)(128)(4,1)S(1)}, s32[]{:S(2)}) async-start(s8[8388608]{0:T(1024)(128)(4,1)} %bitcast.11), calls=%async_computation | async-start | bytes 8388608
  38.3 10.5 %slice-start.1 = ((s8[8388608]{0:T(1024)(128)(4,1)}), s8[4194304]{0:T(1024)(128)(4,1)S(1)}, s32[]{:S(2)}) async-start(s8[8388608]{0:T(1024)(128)(4,1)} %bitcast.11), calls=%async_computation.1 | async-start | bytes 8388608
  38.4 3.8 %collective-permute-start.10 = (bf16[16,512]{1,0:T(8,128)(2,1)S(1)}, bf16[16,512]{1,0:T(8,128)(2,1)S(1)}, u32[]{:S(2)}, u32[]{:S(2)}) collective-permute-start(bf16[16,512]{1,0:T(8,128)(2,1)S(1)} %pair_rows.1.refs_0_), channel_id=1, source_target_pairs={{0,1},{1,0},{2,3},{3,2},{4,5},{5,4},{6,7},{7,6},{8,9},{9,8},{10,11... | collective-permute-start | bytes 49160 | tf_op jit(solution)/shard_map/ppermute | solution.py:22
  39.4 3.7 %collective-permute-start.11 = (bf16[16,512]{1,0:T(8,128)(2,1)S(1)}, bf16[16,512]{1,0:T(8,128)(2,1)S(1)}, u32[]{:S(2)}, u32[]{:S(2)}) collective-permute-start(bf16[16,512]{1,0:T(8,128)(2,1)S(1)} %pair_rows.1.refs_0_), channel_id=1, source_target_pairs={{0,2},{1,3},{2,0},{3,1},{4,6},{5,7},{6,4},{7,5},{8,10},{9,11},{10,... | collective-permute-start | bytes 49160 | tf_op jit(solution)/shard_map/ppermute | solution.py:22
  40.5 4.6 %collective-permute-start.12 = (bf16[16,512]{1,0:T(8,128)(2,1)S(1)}, bf16[16,512]{1,0:T(8,128)(2,1)S(1)}, u32[]{:S(2)}, u32[]{:S(2)}) collective-permute-start(bf16[16,512]{1,0:T(8,128)(2,1)S(1)} %pair_rows.1.refs_0_), channel_id=1, source_target_pairs={{0,3},{1,2},{2,1},{3,0},{4,7},{5,6},{6,5},{7,4},{8,11},{9,10},{10,... | collective-permute-start | bytes 49160 | tf_op jit(solution)/shard_map/ppermute | solution.py:22
  47.2 1.6 %collective-permute-start.17 = (bf16[64,2176]{1,0:T(8,128)(2,1)S(1)}, bf16[64,2176]{1,0:T(8,128)(2,1)S(1)}, u32[]{:S(2)}, u32[]{:S(2)}) collective-permute-start(bf16[64,2176]{1,0:T(8,128)(2,1)S(1)} %get-tuple-element.31), channel_id=1, source_target_pairs={{0,16},{16,0},{1,17},{17,1},{2,18},{18,2},{3,19},{19,3},{4,20},{20... | collective-permute-start | bytes 835592 | tf_op jit(solution)/shard_map/ppermute | solution.py:22
  50.6 6.0 %collective-permute-start.18 = (bf16[16,2048]{1,0:T(8,128)(2,1)S(1)}, bf16[16,2048]{1,0:T(8,128)(2,1)S(1)}, u32[]{:S(2)}, u32[]{:S(2)}) collective-permute-start(bf16[16,2048]{1,0:T(8,128)(2,1)S(1)} %get-tuple-element.37), channel_id=1, source_target_pairs={{0,1},{1,0},{2,3},{3,2},{4,5},{5,4},{6,7},{7,6},{8,9},{9,8},{10,11... | collective-permute-start | bytes 196616 | tf_op jit(solution)/shard_map/ppermute | solution.py:22
  52.2 5.0 %collective-permute-start.19 = (bf16[16,2048]{1,0:T(8,128)(2,1)S(1)}, bf16[16,2048]{1,0:T(8,128)(2,1)S(1)}, u32[]{:S(2)}, u32[]{:S(2)}) collective-permute-start(bf16[16,2048]{1,0:T(8,128)(2,1)S(1)} %get-tuple-element.38), channel_id=1, source_target_pairs={{0,2},{1,3},{2,0},{3,1},{4,6},{5,7},{6,4},{7,5},{8,10},{9,11},{10,... | collective-permute-start | bytes 196616 | tf_op jit(solution)/shard_map/ppermute | solution.py:22
  52.7 5.2 %collective-permute-start.20 = (bf16[16,2048]{1,0:T(8,128)(2,1)S(1)}, bf16[16,2048]{1,0:T(8,128)(2,1)S(1)}, u32[]{:S(2)}, u32[]{:S(2)}) collective-permute-start(bf16[16,2048]{1,0:T(8,128)(2,1)S(1)} %get-tuple-element.39), channel_id=1, source_target_pairs={{0,3},{1,2},{2,1},{3,0},{4,7},{5,6},{6,5},{7,4},{8,11},{9,10},{10,... | collective-permute-start | bytes 196616 | tf_op jit(solution)/shard_map/ppermute | solution.py:22
  57.9 1.3 %collective-permute-start.21 = (f32[8,2048]{1,0:T(8,128)S(1)}, f32[8,2048]{1,0:T(8,128)S(1)}, u32[]{:S(2)}, u32[]{:S(2)}) collective-permute-start(f32[8,2048]{1,0:T(8,128)S(1)} %get-tuple-element.41), channel_id=1, source_target_pairs={{0,16},{16,0},{1,17},{17,1},{2,18},{18,2},{3,19},{19,3},{4,20},{20... | collective-permute-start | bytes 196616 | tf_op jit(solution)/shard_map/ppermute | solution.py:22

commit v10 on v7

--- a/solution.py
+++ b/solution.py
@@ -56,34 +56,42 @@
         kv_ref[at, width:] = act(3).astype(BF16)
 
 
-def attend(q_ref, kv_refs, gate_ref, gain_ref, att_ref):
+STEP = 256
+
+
+def attend(q_ref, kv_refs, att_ref, pairs):
     rows, width = q_ref.shape
     head = width // HEADS
-    step = min(rows, 256)
+    step = min(rows, STEP)
     blocks = [(ref, r) for ref in kv_refs for r in range(0, ref.shape[0], step)]
     tri = lax.broadcasted_iota(jnp.int32, (step, step), 1) <= lax.broadcasted_iota(
         jnp.int32, (step, step), 0
     )
     before = len(blocks) - rows // step
-    for i in range(rows // step):
+    for i, h in pairs:
         at = slice(i * step, (i + 1) * step)
-        for h in range(HEADS):
-            q = q_ref[at, h * head : (h + 1) * head]
-            total = None
-            for j in range(before + i + 1):
-                ref, r = blocks[j]
-                k = ref[r : r + step, width + h * head : width + (h + 1) * head]
-                v = ref[r : r + step, h * head : (h + 1) * head]
-                s = lax.dot_general(q, k, (((1,), (1,)), ((), ())), preferred_element_type=F32)
-                wts = silu_half(s * (0.5 * head**-0.5))
-                if j == before + i:
-                    wts = jnp.where(tri, wts, 0.0)
-                mixed = jnp.dot(wts.astype(BF16), v, preferred_element_type=F32)
-                total = mixed if total is None else total + mixed
-            att_ref[at, h * head : (h + 1) * head] = total
-    att = att_ref[...]
+        q = q_ref[at, h * head : (h + 1) * head]
+        total = None
+        for j in range(before + i + 1):
+            ref, r = blocks[j]
+            k = ref[r : r + step, width + h * head : width + (h + 1) * head]
+            v = ref[r : r + step, h * head : (h + 1) * head]
+            s = lax.dot_general(q, k, (((1,), (1,)), ((), ())), preferred_element_type=F32)
+            wts = silu_half(s * (0.5 * head**-0.5))
+            if j == before + i:
+                wts = jnp.where(tri, wts, 0.0)
+            mixed = jnp.dot(wts.astype(BF16), v, preferred_element_type=F32)
+            total = mixed if total is None else total + mixed
+        att_ref[at, h * head : (h + 1) * head] = total
+
+
+def all_pairs(rows):
+    return [(i, h) for i in range(max(rows // STEP, 1)) for h in range(HEADS)]
+
+
+def gated_rows(att, gain_ref, gate):
     inv = lax.rsqrt(jnp.mean(att * att, axis=1, keepdims=True) + EPSILON)
-    return (att * inv * gain_ref[:1] * gate_ref[...].astype(F32)).astype(BF16)
+    return (att * inv * gain_ref[:1] * gate.astype(F32)).astype(BF16)
 
 
 def membership(bounds_ref, row0, rows):
@@ -112,7 +120,8 @@
     sums_ev = jnp.dot(member, ev_ref[...], preferred_element_type=F32)
     sums_ev_ref[...] = sums_ev
     project(dps, 0, bounds_ref[2, :1, :1], ev_ref, w_ref, gate_ref, q_ref, kv_ref)
-    gated = attend(q_ref, [kv_ref], gate_ref, gain_ref, att_ref)
+    attend(q_ref, [kv_ref], att_ref, all_pairs(q_ref.shape[0]))
+    gated = gated_rows(att_ref[...], gain_ref, gate_ref[...])
     sums_g_ref[...] = jnp.dot(member, gated, preferred_element_type=F32)
     out = pool(dps, bounds_ref, sums_ev, sums_g_ref, wout_ref)
     peers, take = copies_out
@@ -131,13 +140,30 @@
     out_ref[...] = sums_ev_ref[...] + jnp.dot(member, ev_ref[...], preferred_element_type=F32)
 
 
-def attend_kernel(row0, at, rows, bounds_ref, gain_ref, qg_ref, kv_first, kv_ref, sums_ref, _, out_ref, att_ref):
-    here = pl.ds(at, rows)
+def attend_kernel(pairs, qg_ref, kv_first, kv_ref, _, att_ref):
+    attend(halves(qg_ref)[0], [kv_first, kv_ref], att_ref, pairs)
+
+
+def attend_rest_kernel(
+    row0, pairs, dps, bounds_ref, gain_ref, qg_ref, kv_first, kv_ref, sums_ref, sums_ev_ref, wout_ref, before_ref, _, out_ref,
+    att_ref, total_ref,
+):
     q_ref, gate_ref = halves(qg_ref)
-    member = membership(bounds_ref, row0 + at, rows)
-    kv_refs = [kv_first, kv_ref.at[: at + rows]]
-    gated = attend(q_ref.at[here], kv_refs, gate_ref.at[here], gain_ref, att_ref)
-    out_ref[...] = sums_ref[...] + jnp.dot(member, gated, preferred_element_type=F32)
+    rows, width = q_ref.shape
+    attend(q_ref, [kv_first, kv_ref], att_ref, pairs)
+    head = width // HEADS
+    step = min(rows, STEP)
+    total = sums_ref[...]
+    for i in range(rows // step):
+        at = slice(i * step, (i + 1) * step)
+        att = [
+            (att_ref if (i, h) in pairs else before_ref)[at, h * head : (h + 1) * head] for h in range(HEADS)
+        ]
+        gated = gated_rows(jnp.concatenate(att, axis=1), gain_ref, gate_ref[at])
+        member = membership(bounds_ref, row0 + i * step, step)
+        total = total + jnp.dot(member, gated, preferred_element_type=F32)
+    total_ref[...] = total
+    out_ref[...] = pool(dps, bounds_ref, sums_ev_ref[...], total_ref, wout_ref).astype(BF16)
 
 
 def call(kernel, name, operands, out_shape, scratch, mib, flops, size, transcendentals=0):
@@ -168,7 +194,7 @@
 def gather_weights(w_uvqk, w_out, w_in, ffn_gain, sections, dps, mps):
     depth, wide = w_uvqk.shape
     width = w_out.shape[1]
-    w_in = jnp.concatenate([w_in, jnp.broadcast_to(ffn_gain, (16, w_in.shape[1]))], axis=0)
+    w_in = jnp.concatenate([w_in, ffn_gain, jnp.zeros((15, w_in.shape[1]), BF16)], axis=0)
     if (sections, mps) != (2, 4) or wide != 4 * width or depth % 128:
         ws = [lax.all_gather(x, "dp", axis=0, tiled=True) for x in (w_uvqk, w_out)]
         blocks = [[w_in]] + [[swap(w_in, "mp", mps, k)] for k in range(1, mps)]
@@ -208,6 +234,7 @@
     from_x, from_y = swap(w_in, "mp", mps, 1), swap(w_in, "mp", mps, 2)
     middle = w_in.shape[0] // 32 * 16
     diagonal = [swap(from_x[:middle], "mp", mps, 2), swap(from_y[middle:], "mp", mps, 1)]
+    blocks = [[w_in], [from_x], [from_y], diagonal]
 
     def place(parts, w_ref, wout_ref):
         sec, m = lax.axis_index("section"), lax.axis_index("mp")
@@ -224,7 +251,7 @@
                 rows = pl.ds(pl.multiple_of(row + owner * part, part), part)
                 wout_ref[rows, at : at + cut] = ref[k, depth:]
 
-    return place, parts, [[w_in], [from_x], [from_y], diagonal], dps
+    return place, parts, blocks, dps
 
 
 def two_terms(square):
@@ -297,8 +324,7 @@
     send_ref[...] = total_ref[pl.ds(pl.multiple_of((1 - sec) * take, take), take), :]
 
 
-def finish_kernel(dps, keep_ref, got_ref, bounds_ref, sums_ev_ref, sums_g_ref, wout_ref, out_ref, pooled_ref):
-    pooled_ref[...] = pool(dps, bounds_ref, sums_ev_ref[...], sums_g_ref, wout_ref).astype(BF16)
+def finish_kernel(keep_ref, got_ref, out_ref):
     sec = lax.axis_index("section")
     wide = keep_ref.shape[1]
     out_ref[:, pl.ds(pl.multiple_of(sec * wide, wide), wide)] = keep_ref[...].astype(BF16)
@@ -386,25 +412,25 @@
         rows * units,
     )
 
-    def attend_part(at, count, sums, after):
-        return call(
-            functools.partial(attend_kernel, first, at, count),
-            f"attend_{at}",
-            [bounds, gain, queries_gate, kv_first, kv_rest, sums, after],
-            [((sess, width), F32)],
-            [pltpu.VMEM((count, width), F32)],
-            10,
-            4 * count * (first + at + count) * width,
-            4 * 1024 * 1024,
-            HEADS * count * (first + at + count),
-        )[0]
-
     got = [swap(x, "mp", mps, k + 1) for k, x in enumerate(sends)]
-    sums_g = attend_part(0, rest // 2, sums_g, own)
+    pairs = all_pairs(rest)
+    late = pairs[-1:]
+    pairs = pairs[: -len(late)]
+    (att,) = call(
+        functools.partial(attend_kernel, pairs),
+        "attend_most",
+        [queries_gate, kv_first, kv_rest, own],
+        [((rest, width), F32)],
+        [],
+        10,
+        3 * rest * length * width,
+        4 * 1024 * 1024,
+        HEADS * rest * length,
+    )
     keep, send = call(
         add_kernel,
         "add_parts",
-        [own, *got, sums_g],
+        [own, *got, att],
         [((take, half_width), F32)] * 2,
         [pltpu.VMEM((pair, half_width), F32)],
         8,
@@ -412,16 +438,26 @@
         2 * mps * pair * half_width,
     )
     got = swap(send, "section", sections, 1)
-    sums_g = attend_part(rest // 2, rest - rest // 2, sums_g, keep)
-    cross_out, pooled = call(
-        functools.partial(finish_kernel, dps),
+    (pooled,) = call(
+        functools.partial(attend_rest_kernel, first, late, dps),
+        "attend_last",
+        [bounds, gain, queries_gate, kv_first, kv_rest, sums_g, sums_ev, full_wout, att, keep],
+        [((sess, width), BF16)],
+        [pltpu.VMEM((rest, width), F32), pltpu.VMEM((sess, width), F32)],
+        10,
+        rest * length * width // 2,
+        4 * 1024 * 1024,
+        HEADS * rest * length // 8,
+    )
+    (cross_out,) = call(
+        finish_kernel,
         "finish",
-        [keep, got, bounds, sums_ev, sums_g, full_wout],
-        [((take, half_width * sections), BF16), ((sess, width), BF16)],
+        [keep, got],
+        [((take, half_width * sections), BF16)],
         [],
         8,
-        6 * sess * width * width,
-        2 * 1024 * 1024,
+        0,
+        16 * take * half_width,
     )
     return (pooled, cross_out)
 

time: 59.6 us -> 59 us (0.990)
  waiting for transfers between devices: 13.5 us -> 12.8 us
    unnamed x2 -> x1, other arithmetic: 0.7 us -> 0.01 us
    ppermute x18, waiting for transfers between devices: 13.5 us -> 12.8 us  [swap(): return lax.ppermute(x, axis, [(i, i ^ flip) for i in range(size)])]
  transfers between devices with their start and end apart: 18 -> 18, of which waited for: 4 -> 4; matrix products, arithmetic and copies ran while one was open for 4% -> 3% of each run, Pallas kernels for 16% -> 17%
where the time goes in v10:
time: 59 us; the launch traced here: 58.5 us
  starting transfers between devices  18.5 us (31%)
  Pallas kernels  14.6 us (25%)
  waiting for transfers between devices  12.8 us (22%)
  blocking collectives  7.5 us (13%)
  local copies, waits for them, and re-layouts  2.11 us (4%)
  between operations  1.57 us (3%)
  other arithmetic  1.41 us (2%)
    ppermute x18, starting transfers between devices, swap(): return lax.ppermute(x, axis, [(i, i ^ flip) for i in range(size)])  18.5 us
    pallas_call x9, Pallas kernels, call(): pl.pallas_call(kernel, in_specs=[VMEM] * len(operands), out_specs=[VMEM]...  14.6 us
    ppermute x18, waiting for transfers between devices, swap(): return lax.ppermute(x, axis, [(i, i ^ flip) for i in range(size)])  12.8 us
    all_to_all x1, blocking collectives, per_device(): lax.all_to_all(micro_rows.reshape(peers, take, width), group, split_axis=...  7.5 us
    concatenate x1, other arithmetic, gather_weights(): jnp.concatenate([w_in, ffn_gain, jnp.zeros((15, w_in.shape[1]), BF16)], a...  1.27 us
  transfers between devices with their start and end apart: 18, of which 4 were waited for; matrix products, arithmetic and copies ran while one was open for 3% of the time, Pallas kernels for 17%

profile of v10, /device:TPU:0, one launch (start us, length us, event | category | flops | bytes accessed | tf_op | source)
XLA Modules:
  0.0 58.5 jit_solution(13743478118487247104)
XLA Ops:
  0.7 0.8 %constant_dynamic-slice_fusion = bf16[32,512]{1,0:T(8,128)(2,1)S(1)} fusion(bf16[128,512]{1,0:T(8,128)(2,1)} %param.14, s32[]{:T(128)S(6)} %select_n.12), kind=kLoop, calls=%fused_computation.9 | loop fusion | bytes 65540 | tf_op jit(solution)/shard_map/dynamic_slice | solution.py:215
  1.5 0.9 %constant_dynamic-slice_fusion.1 = bf16[128,512]{1,0:T(8,128)(2,1)S(1)} fusion(bf16[128,2048]{1,0:T(8,128)(2,1)} %param.13, s32[]{:T(128)S(6)} %select_n.11), kind=kLoop, calls=%fused_computation.10 | loop fusion | bytes 262148 | tf_op jit(solution)/shard_map/dynamic_slice | solution.py:214
  2.4 4.1 %collective-permute-start = (bf16[160,512]{1,0:T(8,128)(2,1)S(1)}, bf16[160,512]{1,0:T(8,128)(2,1)S(1)}, u32[]{:S(2)}, u32[]{:S(2)}) collective-permute-start(bf16[160,512]{1,0:T(8,128)(2,1)S(1)} %pad_maximum_fusion), channel_id=1, source_target_pairs={{0,8},{4,12},{8,0},{12,4},{1,9},{5,13},{9,1},{13,5},{2,10},{6,14},... | collective-permute-start | bytes 491528 | tf_op jit(solution)/shard_map/ppermute | solution.py:22
  6.5 1.3 %collective-permute-start.1 = (bf16[160,512]{1,0:T(8,128)(2,1)S(1)}, bf16[160,512]{1,0:T(8,128)(2,1)S(1)}, u32[]{:S(2)}, u32[]{:S(2)}) collective-permute-start(bf16[160,512]{1,0:T(8,128)(2,1)S(1)} %pad_maximum_fusion), channel_id=1, source_target_pairs={{0,12},{4,8},{8,4},{12,0},{1,13},{5,9},{9,5},{13,1},{2,14},{6,10},... | collective-permute-start | bytes 491528 | tf_op jit(solution)/shard_map/ppermute | solution.py:22
  7.9 0.2 collective-permute-start.2
  8.1 0.1 pad.2.clone
  8.2 1.3 %maximum_maximum_fusion.refs_0_ = bf16[528,512]{1,0:T(8,128)(2,1)S(1)} fusion(bf16[1,512]{1,0:T(2,128)(2,1)} %param.17, bf16[512,512]{1,0:T(8,128)(2,1)} %param.16, bf16[528]{0:T(1024)(128)(2,1)S(1)} %pad.2.clone), kind=kLoop, calls=%fused_computation | loop fusion | flops 1622016 | bytes 1067040 | tf_op jit(solution)/shard_map/concatenate | solution.py:197
  9.5 1.6 %collective-permute-start.9 = (bf16[528,512]{1,0:T(8,128)(2,1)S(1)}, bf16[528,512]{1,0:T(8,128)(2,1)S(1)}, u32[]{:S(2)}, u32[]{:S(2)}) collective-permute-start(bf16[528,512]{1,0:T(8,128)(2,1)S(1)} %maximum_maximum_fusion.refs_0_), channel_id=1, source_target_pairs={{0,1},{1,0},{2,3},{3,2},{4,5},{5,4},{6,7},{7,6},{8,9},{9,8},{10,11... | collective-permute-start | bytes 1622024 | tf_op jit(solution)/shard_map/ppermute | solution.py:22
  11.1 1.5 %collective-permute-start.10 = (bf16[528,512]{1,0:T(8,128)(2,1)S(1)}, bf16[528,512]{1,0:T(8,128)(2,1)S(1)}, u32[]{:S(2)}, u32[]{:S(2)}) collective-permute-start(bf16[528,512]{1,0:T(8,128)(2,1)S(1)} %maximum_maximum_fusion.refs_0_), channel_id=1, source_target_pairs={{0,2},{1,3},{2,0},{3,1},{4,6},{5,7},{6,4},{7,5},{8,10},{9,11},{10,... | collective-permute-start | bytes 1622024 | tf_op jit(solution)/shard_map/ppermute | solution.py:22
  12.7 5.9 %collective-permute-done.refs_0_ = bf16[160,512]{1,0:T(8,128)(2,1)S(1)} collective-permute-done((bf16[160,512]{1,0:T(8,128)(2,1)S(1)}, bf16[160,512]{1,0:T(8,128)(2,1)S(1)}, u32[]{:S(2)}, u32[]{:S(2)}) %collective-permute-start) | collective-permute-done | bytes 163872 | tf_op jit(solution)/shard_map/ppermute | solution.py:22
  18.6 0.5 collective-permute-done.2.refs_2_
  19.2 1.6 %collective-permute-start.3 = (bf16[3,160,256]{2,1,0:T(8,128)(2,1)S(1)}, bf16[3,160,256]{2,1,0:T(8,128)(2,1)S(1)}, u32[]{:S(2)}, u32[]{:S(2)}) collective-permute-start(bf16[3,160,256]{2,1,0:T(8,128)(2,1)S(1)} %get-tuple-element.22.refs_4_), channel_id=1, source_target_pairs={{0,1},{1,0},{2,3},{3,2},{4,5},{5,4},{6,7},{7,6},{8,9},{9,8},{10,11... | collective-permute-start | bytes 737288 | tf_op jit(solution)/shard_map/ppermute | solution.py:22
  20.8 1.5 %collective-permute-start.4 = (bf16[3,160,256]{2,1,0:T(8,128)(2,1)S(1)}, bf16[3,160,256]{2,1,0:T(8,128)(2,1)S(1)}, u32[]{:S(2)}, u32[]{:S(2)}) collective-permute-start(bf16[3,160,256]{2,1,0:T(8,128)(2,1)S(1)} %get-tuple-element.23.refs_5_), channel_id=1, source_target_pairs={{0,2},{1,3},{2,0},{3,1},{4,6},{5,7},{6,4},{7,5},{8,10},{9,11},{10,... | collective-permute-start | bytes 737288 | tf_op jit(solution)/shard_map/ppermute | solution.py:22
  22.4 0.1 select_reduce_fusion
  23.2 5.1 %collective-permute-done.3.refs_6_ = bf16[3,160,256]{2,1,0:T(8,128)(2,1)S(1)} collective-permute-done((bf16[3,160,256]{2,1,0:T(8,128)(2,1)S(1)}, bf16[3,160,256]{2,1,0:T(8,128)(2,1)S(1)}, u32[]{:S(2)}, u32[]{:S(2)}) %collective-permute-start.3) | collective-permute-done | bytes 245792 | tf_op jit(solution)/shard_map/ppermute | solution.py:22
  28.3 1.2 %collective-permute-done.4.refs_7_ = bf16[3,160,256]{2,1,0:T(8,128)(2,1)S(1)} collective-permute-done((bf16[3,160,256]{2,1,0:T(8,128)(2,1)S(1)}, bf16[3,160,256]{2,1,0:T(8,128)(2,1)S(1)}, u32[]{:S(2)}, u32[]{:S(2)}) %collective-permute-start.4) | collective-permute-done | bytes 245792 | tf_op jit(solution)/shard_map/ppermute | solution.py:22
  29.5 0.5 collective-permute-start.8
  30.0 1.6 %collective-permute-start.11 = (bf16[256,512]{1,0:T(8,128)(2,1)S(1)}, bf16[256,512]{1,0:T(8,128)(2,1)S(1)}, u32[]{:S(2)}, u32[]{:S(2)}) collective-permute-start(bf16[256,512]{1,0:T(8,128)(2,1)S(1)} %slice.40), channel_id=1, source_target_pairs={{0,2},{1,3},{2,0},{3,1},{4,6},{5,7},{6,4},{7,5},{8,10},{9,11},{10,... | collective-permute-start | bytes 786440 | tf_op jit(solution)/shard_map/ppermute | solution.py:22
  31.7 0.6 %collective-permute-start.12 = (bf16[272,512]{1,0:T(8,128)(2,1)S(1)}, bf16[272,512]{1,0:T(8,128)(2,1)S(1)}, u32[]{:S(2)}, u32[]{:S(2)}) collective-permute-start(bf16[272,512]{1,0:T(8,128)(2,1)S(1)} %slice.41), channel_id=1, source_target_pairs={{0,1},{1,0},{2,3},{3,2},{4,5},{5,4},{6,7},{7,6},{8,9},{9,8},{10,11... | collective-permute-start | bytes 835592 | tf_op jit(solution)/shard_map/ppermute | solution.py:22
  32.3 0.1 broadcast_in_dim.29.bounds_ref
  32.4 3.5 %encode_first.1 = (bf16[64,512]{1,0:T(8,128)(2,1)S(1)}, bf16[512,2048]{1,0:T(8,128)(2,1)S(1)}, bf16[512,512]{1,0:T(8,128)(2,1)S(1)}, bf16[512,1024]{1,0:T(8,128)...) custom-call(f32[3,32,128]{2,1,0:T(8,128)S(1)} %broadcast_in_dim.29.bounds_ref, ...), custom_call_target="tpu_custom_call" | custom-call | flops 1342177280 | bytes 6291456 | tf_op jit(solution)/shard_map/encode_first/pallas_call | solution.py:170
  35.9 7.5 %all_to_all.5 = bf16[8,8,512]{2,1,0:T(8,128)(2,1)S(1)} all-to-all(bf16[8,8,512]{2,1,0:T(8,128)(2,1)S(1)} %bitcast.16), channel_id=1, replica_groups=mesh['section'=2,'dp'=4,'mp'=4] {'section','mp'}, dimensions={0} | all-to-all | bytes 131072 | tf_op jit(solution)/shard_map/all_to_all | solution.py:376
  43.5 2.0 %up_half.1 = (f32[64,512]{1,0:T(8,128)S(1)}, f32[64,2176]{1,0:T(8,128)S(1)}, bf16[64,2176]{1,0:T(8,128)(2,1)S(1)}) custom-call(bf16[64,512]{1,0:T(8,128)(2,1)S(1)} %bitcast.15, bf16[528,512]{1,0:T(8,128)(2,1)S(1)} %maximum_maximum_fusion.refs_0_, bf16[528,512]{1,0:T(8,128)(2,1)S(1)} %collective-permute-done.9.refs_1_, ...), custom_call_target="tpu_custom_call" | custom-call | flops 536870912 | bytes 8388608 | tf_op jit(solution)/shard_map/up_half/pallas_call | solution.py:170
  45.5 0.2 collective-permute-start.13
  45.7 1.6 %project_rest.1 = (bf16[512,1024]{1,0:T(8,128)(2,1)S(1)}, bf16[512,1024]{1,0:T(8,128)(2,1)S(1)}, f32[32,512]{1,0:T(8,128)S(1)}) custom-call(f32[3,32,128]{2,1,0:T(8,128)S(1)} %broadcast_in_dim.29.bounds_ref, bf16[512,512]{1,0:T(8,128)(2,1)S(1)} %get-tuple-element.43.ev_ref, bf16[512,2048]{1,0:T(8,128)(2,1)S(1)} %get-tuple-element.24.w_ref, ...), custom_call_target="tpu_custom_call" | custom-call | flops 1073741824 | bytes 6291456 | tf_op jit(solution)/shard_map/project_rest/pallas_call | solution.py:170
  47.3 1.8 %down_part.1 = (f32[16,2048]{1,0:T(8,128)S(1)}, bf16[16,2048]{1,0:T(8,128)(2,1)S(1)}, bf16[16,2048]{1,0:T(8,128)(2,1)S(1)}, bf16[16,2048]{1,0:T(8,128)(2,1)S(1)}) custom-call(f32[64,2176]{1,0:T(8,128)S(1)} %get-tuple-element.34.half_ref, bf16[64,2176]{1,0:T(8,128)(2,1)S(1)} %collective-permute-done.13.other_ref, ...), custom_call_target="tpu_custom_call" | custom-call | flops 536870912 | bytes 8388608 | tf_op jit(solution)/shard_map/down_part/pallas_call | solution.py:170
  49.1 0.6 %collective-permute-start.14 = (bf16[16,2048]{1,0:T(8,128)(2,1)S(1)}, bf16[16,2048]{1,0:T(8,128)(2,1)S(1)}, u32[]{:S(2)}, u32[]{:S(2)}) collective-permute-start(bf16[16,2048]{1,0:T(8,128)(2,1)S(1)} %get-tuple-element.37), channel_id=1, source_target_pairs={{0,1},{1,0},{2,3},{3,2},{4,5},{5,4},{6,7},{7,6},{8,9},{9,8},{10,11... | collective-permute-start | bytes 196616 | tf_op jit(solution)/shard_map/ppermute | solution.py:22
  49.7 0.6 collective-permute-start.15
  50.3 2.4 %collective-permute-start.16 = (bf16[16,2048]{1,0:T(8,128)(2,1)S(1)}, bf16[16,2048]{1,0:T(8,128)(2,1)S(1)}, u32[]{:S(2)}, u32[]{:S(2)}) collective-permute-start(bf16[16,2048]{1,0:T(8,128)(2,1)S(1)} %get-tuple-element.39), channel_id=1, source_target_pairs={{0,3},{1,2},{2,1},{3,0},{4,7},{5,6},{6,5},{7,4},{8,11},{9,10},{10,... | collective-permute-start | bytes 196616 | tf_op jit(solution)/shard_map/ppermute | solution.py:22
  52.7 3.2 %attend_most.1.refs_3_.before_ref = f32[512,512]{1,0:T(8,128)S(1)} custom-call(bf16[512,1024]{1,0:T(8,128)(2,1)S(1)} %get-tuple-element.28.qg_ref, bf16[512,1024]{1,0:T(8,128)(2,1)S(1)} %get-tuple-element.29.kv_first, bf16[512,1024]{1,0:T(8,128)(2,1)S(1)} %get-tuple-element.30.kv_ref, f32[16,2048]{1,0:T(8,128)S(1)} %get-tuple-element.36._.own_ref), custom_call_target="tpu_custom_call" | custom-call | flops 805306368 | bytes 4194304 | tf_op jit(solution)/shard_map/attend_most/pallas_call | solution.py:170
  56.1 1.8 %attend_last.1 = bf16[32,512]{1,0:T(8,128)(2,1)} custom-call(f32[3,32,128]{2,1,0:T(8,128)S(1)} %broadcast_in_dim.29.bounds_ref, f32[8,512]{1,0:T(8,128)S(1)} %broadcast_in_dim.30.gain_ref, bf16[512,1024]{1,0:T(8,128)(2,1)S(1)} %get-tuple-element.28.qg_ref, bf16[512,1024]{1,0:T(8,128)(2,1)S(1)} %get-tuple-element.29.kv_first, ...), custom_call_target="tpu_custom_call" | custom-call | flops 134217728 | bytes 4194304 | tf_op jit(solution)/shard_map/attend_last/pallas_call | solution.py:170
  57.8 0.6 %finish.1 = bf16[8,4096]{1,0:T(8,128)(2,1)} custom-call(f32[8,2048]{1,0:T(8,128)S(1)} %get-tuple-element.40._.keep_ref, f32[8,2048]{1,0:T(8,128)S(1)} %collective-permute-done.17.got_ref), custom_call_target="tpu_custom_call" | custom-call | bytes 262144 | tf_op jit(solution)/shard_map/finish/pallas_call | solution.py:170
  (48 shorter events, 0.5 us)
Async XLA Ops:
  0.6 12.0 %copy-start.1 = (bf16[1,1024,512]{2,1,0:T(8,128)(2,1)S(1)}, bf16[1,1024,512]{2,1,0:T(8,128)(2,1)}, u32[]{:S(2)}) copy-start(bf16[1,1024,512]{2,1,0:T(8,128)(2,1)} %param.10) | copy-start | bytes 3145732
  2.4 16.2 %collective-permute-start = (bf16[160,512]{1,0:T(8,128)(2,1)S(1)}, bf16[160,512]{1,0:T(8,128)(2,1)S(1)}, u32[]{:S(2)}, u32[]{:S(2)}) collective-permute-start(bf16[160,512]{1,0:T(8,128)(2,1)S(1)} %pad_maximum_fusion), channel_id=1, source_target_pairs={{0,8},{4,12},{8,0},{12,4},{1,9},{5,13},{9,1},{13,5},{2,10},{6,14},... | collective-permute-start | bytes 491528 | tf_op jit(solution)/shard_map/ppermute | solution.py:22
  6.5 12.1 %collective-permute-start.1 = (bf16[160,512]{1,0:T(8,128)(2,1)S(1)}, bf16[160,512]{1,0:T(8,128)(2,1)S(1)}, u32[]{:S(2)}, u32[]{:S(2)}) collective-permute-start(bf16[160,512]{1,0:T(8,128)(2,1)S(1)} %pad_maximum_fusion), channel_id=1, source_target_pairs={{0,12},{4,8},{8,4},{12,0},{1,13},{5,9},{9,5},{13,1},{2,14},{6,10},... | collective-permute-start | bytes 491528 | tf_op jit(solution)/shard_map/ppermute | solution.py:22
  7.9 11.3 %collective-permute-start.2 = (bf16[160,512]{1,0:T(8,128)(2,1)S(1)}, bf16[160,512]{1,0:T(8,128)(2,1)S(1)}, u32[]{:S(2)}, u32[]{:S(2)}) collective-permute-start(bf16[160,512]{1,0:T(8,128)(2,1)S(1)} %pad_maximum_fusion), channel_id=1, source_target_pairs={{0,4},{4,0},{8,12},{12,8},{1,5},{5,1},{9,13},{13,9},{2,6},{6,2},{1... | collective-permute-start | bytes 491528 | tf_op jit(solution)/shard_map/ppermute | solution.py:22
  8.2 14.1 %copy-start.3 = (bf16[128,512]{1,0:T(8,128)(2,1)S(1)}, bf16[128,512]{1,0:T(8,128)(2,1)}, u32[]{:S(2)}) copy-start(bf16[128,512]{1,0:T(8,128)(2,1)} %param.14) | copy-start | bytes 393220
  8.2 14.2 %copy-start.5 = (s32[1,32]{1,0:T(1,128)S(1)}, s32[1,32]{1,0:T(1,128)}, u32[]{:S(2)}) copy-start(s32[1,32]{1,0:T(1,128)} %param.12) | copy-start | bytes 388
  9.5 3.2 %copy-start.2 = (bf16[128,2048]{1,0:T(8,128)(2,1)S(1)}, bf16[128,2048]{1,0:T(8,128)(2,1)}, u32[]{:S(2)}) copy-start(bf16[128,2048]{1,0:T(8,128)(2,1)} %param.13) | copy-start | bytes 1572868
  9.5 20.0 %collective-permute-start.9 = (bf16[528,512]{1,0:T(8,128)(2,1)S(1)}, bf16[528,512]{1,0:T(8,128)(2,1)S(1)}, u32[]{:S(2)}, u32[]{:S(2)}) collective-permute-start(bf16[528,512]{1,0:T(8,128)(2,1)S(1)} %maximum_maximum_fusion.refs_0_), channel_id=1, source_target_pairs={{0,1},{1,0},{2,3},{3,2},{4,5},{5,4},{6,7},{7,6},{8,9},{9,8},{10,11... | collective-permute-start | bytes 1622024 | tf_op jit(solution)/shard_map/ppermute | solution.py:22
  11.1 21.3 %copy-start.4 = (f32[512]{0:T(512)S(1)}, f32[512]{0:T(512)}, u32[]{:S(2)}) copy-start(f32[512]{0:T(512)} %param.15) | copy-start | bytes 6148
  11.1 19.0 %collective-permute-start.10 = (bf16[528,512]{1,0:T(8,128)(2,1)S(1)}, bf16[528,512]{1,0:T(8,128)(2,1)S(1)}, u32[]{:S(2)}, u32[]{:S(2)}) collective-permute-start(bf16[528,512]{1,0:T(8,128)(2,1)S(1)} %maximum_maximum_fusion.refs_0_), channel_id=1, source_target_pairs={{0,2},{1,3},{2,0},{3,1},{4,6},{5,7},{6,4},{7,5},{8,10},{9,11},{10,... | collective-permute-start | bytes 1622024 | tf_op jit(solution)/shard_map/ppermute | solution.py:22
  12.6 30.9 %copy-start = (bf16[2048,2048]{1,0:T(8,128)(2,1)S(1)}, bf16[2048,2048]{1,0:T(8,128)(2,1)}, u32[]{:S(2)}) copy-start(bf16[2048,2048]{1,0:T(8,128)(2,1)} %refs_5_.1) | copy-start | bytes 25165828
  19.2 9.1 %collective-permute-start.3 = (bf16[3,160,256]{2,1,0:T(8,128)(2,1)S(1)}, bf16[3,160,256]{2,1,0:T(8,128)(2,1)S(1)}, u32[]{:S(2)}, u32[]{:S(2)}) collective-permute-start(bf16[3,160,256]{2,1,0:T(8,128)(2,1)S(1)} %get-tuple-element.22.refs_4_), channel_id=1, source_target_pairs={{0,1},{1,0},{2,3},{3,2},{4,5},{5,4},{6,7},{7,6},{8,9},{9,8},{10,11... | collective-permute-start | bytes 737288 | tf_op jit(solution)/shard_map/ppermute | solution.py:22
  20.8 8.7 %collective-permute-start.4 = (bf16[3,160,256]{2,1,0:T(8,128)(2,1)S(1)}, bf16[3,160,256]{2,1,0:T(8,128)(2,1)S(1)}, u32[]{:S(2)}, u32[]{:S(2)}) collective-permute-start(bf16[3,160,256]{2,1,0:T(8,128)(2,1)S(1)} %get-tuple-element.23.refs_5_), channel_id=1, source_target_pairs={{0,2},{1,3},{2,0},{3,1},{4,6},{5,7},{6,4},{7,5},{8,10},{9,11},{10,... | collective-permute-start | bytes 737288 | tf_op jit(solution)/shard_map/ppermute | solution.py:22
  22.3 9.3 %collective-permute-start.5 = (bf16[3,160,256]{2,1,0:T(8,128)(2,1)S(1)}, bf16[3,160,256]{2,1,0:T(8,128)(2,1)S(1)}, u32[]{:S(2)}, u32[]{:S(2)}) collective-permute-start(bf16[3,160,256]{2,1,0:T(8,128)(2,1)S(1)} %get-tuple-element.22.refs_4_), channel_id=1, source_target_pairs={{0,16},{16,0},{1,17},{17,1},{2,18},{18,2},{3,19},{19,3},{4,20},{20... | collective-permute-start | bytes 737288 | tf_op jit(solution)/shard_map/ppermute | solution.py:22
  28.3 4.0 %collective-permute-start.6 = (bf16[3,160,256]{2,1,0:T(8,128)(2,1)S(1)}, bf16[3,160,256]{2,1,0:T(8,128)(2,1)S(1)}, u32[]{:S(2)}, u32[]{:S(2)}) collective-permute-start(bf16[3,160,256]{2,1,0:T(8,128)(2,1)S(1)} %get-tuple-element.23.refs_5_), channel_id=1, source_target_pairs={{0,16},{16,0},{1,17},{17,1},{2,18},{18,2},{3,19},{19,3},{4,20},{20... | collective-permute-start | bytes 737288 | tf_op jit(solution)/shard_map/ppermute | solution.py:22
  29.5 2.8 %collective-permute-start.7 = (bf16[3,160,256]{2,1,0:T(8,128)(2,1)S(1)}, bf16[3,160,256]{2,1,0:T(8,128)(2,1)S(1)}, u32[]{:S(2)}, u32[]{:S(2)}) collective-permute-start(bf16[3,160,256]{2,1,0:T(8,128)(2,1)S(1)} %collective-permute-done.3.refs_6_), channel_id=1, source_target_pairs={{0,16},{16,0},{1,17},{17,1},{2,18},{18,2},{3,19},{19,3},{4,20},{20... | collective-permute-start | bytes 737288 | tf_op jit(solution)/shard_map/ppermute | solution.py:22
  29.5 2.8 %collective-permute-start.8 = (bf16[3,160,256]{2,1,0:T(8,128)(2,1)S(1)}, bf16[3,160,256]{2,1,0:T(8,128)(2,1)S(1)}, u32[]{:S(2)}, u32[]{:S(2)}) collective-permute-start(bf16[3,160,256]{2,1,0:T(8,128)(2,1)S(1)} %collective-permute-done.4.refs_7_), channel_id=1, source_target_pairs={{0,16},{16,0},{1,17},{17,1},{2,18},{18,2},{3,19},{19,3},{4,20},{20... | collective-permute-start | bytes 737288 | tf_op jit(solution)/shard_map/ppermute | solution.py:22
  30.0 13.4 %collective-permute-start.11 = (bf16[256,512]{1,0:T(8,128)(2,1)S(1)}, bf16[256,512]{1,0:T(8,128)(2,1)S(1)}, u32[]{:S(2)}, u32[]{:S(2)}) collective-permute-start(bf16[256,512]{1,0:T(8,128)(2,1)S(1)} %slice.40), channel_id=1, source_target_pairs={{0,2},{1,3},{2,0},{3,1},{4,6},{5,7},{6,4},{7,5},{8,10},{9,11},{10,... | collective-permute-start | bytes 786440 | tf_op jit(solution)/shard_map/ppermute | solution.py:22
  31.7 11.8 %collective-permute-start.12 = (bf16[272,512]{1,0:T(8,128)(2,1)S(1)}, bf16[272,512]{1,0:T(8,128)(2,1)S(1)}, u32[]{:S(2)}, u32[]{:S(2)}) collective-permute-start(bf16[272,512]{1,0:T(8,128)(2,1)S(1)} %slice.41), channel_id=1, source_target_pairs={{0,1},{1,0},{2,3},{3,2},{4,5},{5,4},{6,7},{7,6},{8,9},{9,8},{10,11... | collective-permute-start | bytes 835592 | tf_op jit(solution)/shard_map/ppermute | solution.py:22
  32.4 14.9 %slice-start = ((s8[8388608]{0:T(1024)(128)(4,1)}), s8[4194304]{0:T(1024)(128)(4,1)S(1)}, s32[]{:S(2)}) async-start(s8[8388608]{0:T(1024)(128)(4,1)} %bitcast.13), calls=%async_computation.1 | async-start | bytes 8388608
  43.4 3.8 %slice-start.1 = ((s8[8388608]{0:T(1024)(128)(4,1)}), s8[4194304]{0:T(1024)(128)(4,1)S(1)}, s32[]{:S(2)}) async-start(s8[8388608]{0:T(1024)(128)(4,1)} %bitcast.13), calls=%async_computation.2 | async-start | bytes 8388608
  45.5 1.7 %collective-permute-start.13 = (bf16[64,2176]{1,0:T(8,128)(2,1)S(1)}, bf16[64,2176]{1,0:T(8,128)(2,1)S(1)}, u32[]{:S(2)}, u32[]{:S(2)}) collective-permute-start(bf16[64,2176]{1,0:T(8,128)(2,1)S(1)} %get-tuple-element.35), channel_id=1, source_target_pairs={{0,16},{16,0},{1,17},{17,1},{2,18},{18,2},{3,19},{19,3},{4,20},{20... | collective-permute-start | bytes 835592 | tf_op jit(solution)/shard_map/ppermute | solution.py:22
  49.1 6.8 %collective-permute-start.14 = (bf16[16,2048]{1,0:T(8,128)(2,1)S(1)}, bf16[16,2048]{1,0:T(8,128)(2,1)S(1)}, u32[]{:S(2)}, u32[]{:S(2)}) collective-permute-start(bf16[16,2048]{1,0:T(8,128)(2,1)S(1)} %get-tuple-element.37), channel_id=1, source_target_pairs={{0,1},{1,0},{2,3},{3,2},{4,5},{5,4},{6,7},{7,6},{8,9},{9,8},{10,11... | collective-permute-start | bytes 196616 | tf_op jit(solution)/shard_map/ppermute | solution.py:22
  49.7 6.2 %collective-permute-start.15 = (bf16[16,2048]{1,0:T(8,128)(2,1)S(1)}, bf16[16,2048]{1,0:T(8,128)(2,1)S(1)}, u32[]{:S(2)}, u32[]{:S(2)}) collective-permute-start(bf16[16,2048]{1,0:T(8,128)(2,1)S(1)} %get-tuple-element.38), channel_id=1, source_target_pairs={{0,2},{1,3},{2,0},{3,1},{4,6},{5,7},{6,4},{7,5},{8,10},{9,11},{10,... | collective-permute-start | bytes 196616 | tf_op jit(solution)/shard_map/ppermute | solution.py:22
  50.3 5.6 %collective-permute-start.16 = (bf16[16,2048]{1,0:T(8,128)(2,1)S(1)}, bf16[16,2048]{1,0:T(8,128)(2,1)S(1)}, u32[]{:S(2)}, u32[]{:S(2)}) collective-permute-start(bf16[16,2048]{1,0:T(8,128)(2,1)S(1)} %get-tuple-element.39), channel_id=1, source_target_pairs={{0,3},{1,2},{2,1},{3,0},{4,7},{5,6},{6,5},{7,4},{8,11},{9,10},{10,... | collective-permute-start | bytes 196616 | tf_op jit(solution)/shard_map/ppermute | solution.py:22
  56.0 1.8 %collective-permute-start.17 = (f32[8,2048]{1,0:T(8,128)S(1)}, f32[8,2048]{1,0:T(8,128)S(1)}, u32[]{:S(2)}, u32[]{:S(2)}) collective-permute-start(f32[8,2048]{1,0:T(8,128)S(1)} %get-tuple-element.41), channel_id=1, source_target_pairs={{0,16},{16,0},{1,17},{17,1},{2,18},{18,2},{3,19},{19,3},{4,20},{20... | collective-permute-start | bytes 196616 | tf_op jit(solution)/shard_map/ppermute | solution.py:22

commit v11 on v10

--- a/solution.py
+++ b/solution.py
@@ -40,7 +40,7 @@
 
 def project(dps, row0, hist, ev_ref, w_ref, gate_ref, q_ref, kv_ref):
     rows, width = ev_ref.shape
-    step = min(rows, 256)
+    step = min(rows, 512)
     for r in range(0, rows, step):
         at = slice(r, r + step)
         x = in_order(ev_ref, at, dps)
@@ -63,22 +63,23 @@
     rows, width = q_ref.shape
     head = width // HEADS
     step = min(rows, STEP)
-    blocks = [(ref, r) for ref in kv_refs for r in range(0, ref.shape[0], step)]
     tri = lax.broadcasted_iota(jnp.int32, (step, step), 1) <= lax.broadcasted_iota(
         jnp.int32, (step, step), 0
     )
-    before = len(blocks) - rows // step
+    *earlier, own = kv_refs
     for i, h in pairs:
         at = slice(i * step, (i + 1) * step)
         q = q_ref[at, h * head : (h + 1) * head]
+        runs = [(ref, slice(0, ref.shape[0])) for ref in earlier]
+        if i:
+            runs.append((own, slice(0, i * step)))
         total = None
-        for j in range(before + i + 1):
-            ref, r = blocks[j]
-            k = ref[r : r + step, width + h * head : width + (h + 1) * head]
-            v = ref[r : r + step, h * head : (h + 1) * head]
+        for ref, keys in [*runs, (own, at)]:
+            k = ref[keys, width + h * head : width + (h + 1) * head]
+            v = ref[keys, h * head : (h + 1) * head]
             s = lax.dot_general(q, k, (((1,), (1,)), ((), ())), preferred_element_type=F32)
             wts = silu_half(s * (0.5 * head**-0.5))
-            if j == before + i:
+            if keys is at:
                 wts = jnp.where(tri, wts, 0.0)
             mixed = jnp.dot(wts.astype(BF16), v, preferred_element_type=F32)
             total = mixed if total is None else total + mixed
@@ -184,11 +185,13 @@
 
 
 def split_kernel(*refs):
-    *parts, left_ref, right_ref = refs
+    *parts, left_ref, right_ref, both_ref = refs
     half = left_ref.shape[2]
     for k, part in enumerate(parts):
-        left_ref[k] = part[:, :half]
-        right_ref[k] = part[:, half:]
+        for i, ref in enumerate((left_ref, right_ref)):
+            piece = part[:, i * half : (i + 1) * half]
+            ref[k] = piece
+            both_ref[i, k] = piece
 
 
 def gather_weights(w_uvqk, w_out, w_in, ffn_gain, sections, dps, mps):
@@ -217,19 +220,13 @@
         axis=0,
     )
     got = [swap(mine, "dp", dps, k) for k in order_of(dps)[1:]]
-    left, right = call(
-        split_kernel,
-        "split",
-        got,
-        [((len(got), depth + part, cut), BF16)] * 2,
-        [],
-        8,
-        0,
-        16 * 1024 * 1024,
-    )
-    plane = [left, right, swap(left, "mp", mps, 1), swap(right, "mp", mps, 2)]
+    size = (len(got), depth + part, cut)
+    left, right, both = call(
+        split_kernel, "split", got, [(size, BF16), (size, BF16), ((2, *size), BF16)], [], 8, 0, 16 * 1024 * 1024
+    )
+    others = [swap(left, "mp", mps, 1), swap(right, "mp", mps, 2)]
     parts = [w_uvqk[:, : wide // 2], w_uvqk[:, wide // 2 :], w_out[: depth // 2], w_out[depth // 2 :]]
-    parts = parts + plane + [swap(p, "section", sections, 1) for p in plane]
+    parts = parts + [both, *others] + [swap(p, "section", sections, 1) for p in (both, *others)]
 
     from_x, from_y = swap(w_in, "mp", mps, 1), swap(w_in, "mp", mps, 2)
     middle = w_in.shape[0] // 32 * 16
@@ -242,14 +239,17 @@
             w_ref[:depth, i * (wide // 2) : (i + 1) * (wide // 2)] = parts[i][...]
             wout_ref[i * (depth // 2) : (i + 1) * (depth // 2)] = parts[2 + i][...]
         for i, ref in enumerate(parts[4:]):
-            owner = (sec ^ (i // 4)) * 2 + (parity(m) ^ (i // 2 % 2))
-            at = i % 2 * cut
-            cols = pl.ds(pl.multiple_of(owner * width + at, cut), cut)
-            for k in range(dps - 1):
-                row = (k + 1) * depth
-                w_ref[row : row + depth, cols] = ref[k, :depth]
-                rows = pl.ds(pl.multiple_of(row + owner * part, part), part)
-                wout_ref[rows, at : at + cut] = ref[k, depth:]
+            other_sec, what = i // 3, i % 3
+            owner = (sec ^ other_sec) * 2 + (parity(m) ^ (what > 0))
+            for side in (0, 1) if what == 0 else (what - 1,):
+                at = side * cut
+                cols = pl.ds(pl.multiple_of(owner * width + at, cut), cut)
+                for k in range(dps - 1):
+                    piece = ref[side, k] if what == 0 else ref[k]
+                    row = (k + 1) * depth
+                    w_ref[row : row + depth, cols] = piece[:depth]
+                    rows = pl.ds(pl.multiple_of(row + owner * part, part), part)
+                    wout_ref[rows, at : at + cut] = piece[depth:]
 
     return place, parts, blocks, dps
 

time: 59 us -> 58 us (0.983)
  Pallas kernels: 14.6 us -> 13.4 us
  waiting for transfers between devices: 12.8 us -> 13.6 us
    pallas_call x9, Pallas kernels: 14.6 us -> 13.4 us  [call(): pl.pallas_call(kernel, in_specs=[VMEM] * len(operands), out_specs=[VMEM]...]
    ppermute x18 -> x17, waiting for transfers between devices: 12.8 us -> 13.6 us  [swap(): return lax.ppermute(x, axis, [(i, i ^ flip) for i in range(size)])]
    ppermute x18 -> x17, starting transfers between devices: 18.5 us -> 18.1 us  [swap(): return lax.ppermute(x, axis, [(i, i ^ flip) for i in range(size)])]
  transfers between devices with their start and end apart: 18 -> 17, of which waited for: 4 -> 5; matrix products, arithmetic and copies ran while one was open for 3% -> 3% of each run, Pallas kernels for 17% -> 15%
where the time goes in v11:
time: 58 us; the launch traced here: 57.5 us
  starting transfers between devices  18.1 us (31%)
  waiting for transfers between devices  13.6 us (23%)
  Pallas kernels  13.4 us (23%)
  blocking collectives  7.3 us (13%)
  local copies, waits for them, and re-layouts  2.11 us (4%)
  between operations  1.54 us (3%)
  other arithmetic  1.41 us (2%)
    ppermute x17, starting transfers between devices, swap(): return lax.ppermute(x, axis, [(i, i ^ flip) for i in range(size)])  18.1 us
    ppermute x17, waiting for transfers between devices, swap(): return lax.ppermute(x, axis, [(i, i ^ flip) for i in range(size)])  13.6 us
    pallas_call x9, Pallas kernels, call(): pl.pallas_call(kernel, in_specs=[VMEM] * len(operands), out_specs=[VMEM]...  13.4 us
    all_to_all x1, blocking collectives, per_device(): lax.all_to_all(micro_rows.reshape(peers, take, width), group, split_axis=...  7.3 us
    concatenate x1, other arithmetic, gather_weights(): jnp.concatenate([w_in, ffn_gain, jnp.zeros((15, w_in.shape[1]), BF16)], a...  1.27 us
  transfers between devices with their start and end apart: 17, of which 5 were waited for; matrix products, arithmetic and copies ran while one was open for 3% of the time, Pallas kernels for 15%

profile of v11, /device:TPU:0, one launch (start us, length us, event | category | flops | bytes accessed | tf_op | source)
XLA Modules:
  0.0 57.5 jit_solution(17868804536086043890)
XLA Ops:
  0.7 0.8 %constant_dynamic-slice_fusion = bf16[32,512]{1,0:T(8,128)(2,1)S(1)} fusion(bf16[128,512]{1,0:T(8,128)(2,1)} %param.14, s32[]{:T(128)S(6)} %select_n.12), kind=kLoop, calls=%fused_computation.9 | loop fusion | bytes 65540 | tf_op jit(solution)/shard_map/dynamic_slice | solution.py:218
  1.5 0.9 %constant_dynamic-slice_fusion.1 = bf16[128,512]{1,0:T(8,128)(2,1)S(1)} fusion(bf16[128,2048]{1,0:T(8,128)(2,1)} %param.13, s32[]{:T(128)S(6)} %select_n.11), kind=kLoop, calls=%fused_computation.10 | loop fusion | bytes 262148 | tf_op jit(solution)/shard_map/dynamic_slice | solution.py:217
  2.4 4.1 %collective-permute-start = (bf16[160,512]{1,0:T(8,128)(2,1)S(1)}, bf16[160,512]{1,0:T(8,128)(2,1)S(1)}, u32[]{:S(2)}, u32[]{:S(2)}) collective-permute-start(bf16[160,512]{1,0:T(8,128)(2,1)S(1)} %pad_maximum_fusion), channel_id=1, source_target_pairs={{0,8},{4,12},{8,0},{12,4},{1,9},{5,13},{9,1},{13,5},{2,10},{6,14},... | collective-permute-start | bytes 491528 | tf_op jit(solution)/shard_map/ppermute | solution.py:22
  6.5 1.3 %collective-permute-start.1 = (bf16[160,512]{1,0:T(8,128)(2,1)S(1)}, bf16[160,512]{1,0:T(8,128)(2,1)S(1)}, u32[]{:S(2)}, u32[]{:S(2)}) collective-permute-start(bf16[160,512]{1,0:T(8,128)(2,1)S(1)} %pad_maximum_fusion), channel_id=1, source_target_pairs={{0,12},{4,8},{8,4},{12,0},{1,13},{5,9},{9,5},{13,1},{2,14},{6,10},... | collective-permute-start | bytes 491528 | tf_op jit(solution)/shard_map/ppermute | solution.py:22
  7.9 0.2 collective-permute-start.2
  8.1 0.1 pad.2.clone
  8.2 1.3 %maximum_maximum_fusion.refs_0_ = bf16[528,512]{1,0:T(8,128)(2,1)S(1)} fusion(bf16[1,512]{1,0:T(2,128)(2,1)} %param.17, bf16[512,512]{1,0:T(8,128)(2,1)} %param.16, bf16[528]{0:T(1024)(128)(2,1)S(1)} %pad.2.clone), kind=kLoop, calls=%fused_computation | loop fusion | flops 1622016 | bytes 1067040 | tf_op jit(solution)/shard_map/concatenate | solution.py:200
  9.5 1.6 %collective-permute-start.8 = (bf16[528,512]{1,0:T(8,128)(2,1)S(1)}, bf16[528,512]{1,0:T(8,128)(2,1)S(1)}, u32[]{:S(2)}, u32[]{:S(2)}) collective-permute-start(bf16[528,512]{1,0:T(8,128)(2,1)S(1)} %maximum_maximum_fusion.refs_0_), channel_id=1, source_target_pairs={{0,1},{1,0},{2,3},{3,2},{4,5},{5,4},{6,7},{7,6},{8,9},{9,8},{10,11... | collective-permute-start | bytes 1622024 | tf_op jit(solution)/shard_map/ppermute | solution.py:22
  11.1 1.5 %collective-permute-start.9 = (bf16[528,512]{1,0:T(8,128)(2,1)S(1)}, bf16[528,512]{1,0:T(8,128)(2,1)S(1)}, u32[]{:S(2)}, u32[]{:S(2)}) collective-permute-start(bf16[528,512]{1,0:T(8,128)(2,1)S(1)} %maximum_maximum_fusion.refs_0_), channel_id=1, source_target_pairs={{0,2},{1,3},{2,0},{3,1},{4,6},{5,7},{6,4},{7,5},{8,10},{9,11},{10,... | collective-permute-start | bytes 1622024 | tf_op jit(solution)/shard_map/ppermute | solution.py:22
  12.7 5.9 %collective-permute-done.refs_0_ = bf16[160,512]{1,0:T(8,128)(2,1)S(1)} collective-permute-done((bf16[160,512]{1,0:T(8,128)(2,1)S(1)}, bf16[160,512]{1,0:T(8,128)(2,1)S(1)}, u32[]{:S(2)}, u32[]{:S(2)}) %collective-permute-start) | collective-permute-done | bytes 163872 | tf_op jit(solution)/shard_map/ppermute | solution.py:22
  18.6 0.5 collective-permute-done.2.refs_2_
  19.2 1.6 %collective-permute-start.3 = (bf16[3,160,256]{2,1,0:T(8,128)(2,1)S(1)}, bf16[3,160,256]{2,1,0:T(8,128)(2,1)S(1)}, u32[]{:S(2)}, u32[]{:S(2)}) collective-permute-start(bf16[3,160,256]{2,1,0:T(8,128)(2,1)S(1)} %get-tuple-element.24), channel_id=1, source_target_pairs={{0,1},{1,0},{2,3},{3,2},{4,5},{5,4},{6,7},{7,6},{8,9},{9,8},{10,11... | collective-permute-start | bytes 737288 | tf_op jit(solution)/shard_map/ppermute | solution.py:22
  20.8 1.5 %collective-permute-start.4 = (bf16[3,160,256]{2,1,0:T(8,128)(2,1)S(1)}, bf16[3,160,256]{2,1,0:T(8,128)(2,1)S(1)}, u32[]{:S(2)}, u32[]{:S(2)}) collective-permute-start(bf16[3,160,256]{2,1,0:T(8,128)(2,1)S(1)} %get-tuple-element.25), channel_id=1, source_target_pairs={{0,2},{1,3},{2,0},{3,1},{4,6},{5,7},{6,4},{7,5},{8,10},{9,11},{10,... | collective-permute-start | bytes 737288 | tf_op jit(solution)/shard_map/ppermute | solution.py:22
  23.0 0.1 select_reduce_fusion
  23.1 5.1 %collective-permute-done.3.refs_5_ = bf16[3,160,256]{2,1,0:T(8,128)(2,1)S(1)} collective-permute-done((bf16[3,160,256]{2,1,0:T(8,128)(2,1)S(1)}, bf16[3,160,256]{2,1,0:T(8,128)(2,1)S(1)}, u32[]{:S(2)}, u32[]{:S(2)}) %collective-permute-start.3) | collective-permute-done | bytes 245792 | tf_op jit(solution)/shard_map/ppermute | solution.py:22
  28.3 1.2 %collective-permute-done.4.refs_6_ = bf16[3,160,256]{2,1,0:T(8,128)(2,1)S(1)} collective-permute-done((bf16[3,160,256]{2,1,0:T(8,128)(2,1)S(1)}, bf16[3,160,256]{2,1,0:T(8,128)(2,1)S(1)}, u32[]{:S(2)}, u32[]{:S(2)}) %collective-permute-start.4) | collective-permute-done | bytes 245792 | tf_op jit(solution)/shard_map/ppermute | solution.py:22
  29.5 1.6 %collective-permute-start.10 = (bf16[256,512]{1,0:T(8,128)(2,1)S(1)}, bf16[256,512]{1,0:T(8,128)(2,1)S(1)}, u32[]{:S(2)}, u32[]{:S(2)}) collective-permute-start(bf16[256,512]{1,0:T(8,128)(2,1)S(1)} %slice.40), channel_id=1, source_target_pairs={{0,2},{1,3},{2,0},{3,1},{4,6},{5,7},{6,4},{7,5},{8,10},{9,11},{10,... | collective-permute-start | bytes 786440 | tf_op jit(solution)/shard_map/ppermute | solution.py:22
  31.1 0.8 %collective-permute-start.11 = (bf16[272,512]{1,0:T(8,128)(2,1)S(1)}, bf16[272,512]{1,0:T(8,128)(2,1)S(1)}, u32[]{:S(2)}, u32[]{:S(2)}) collective-permute-start(bf16[272,512]{1,0:T(8,128)(2,1)S(1)} %slice.41), channel_id=1, source_target_pairs={{0,1},{1,0},{2,3},{3,2},{4,5},{5,4},{6,7},{7,6},{8,9},{9,8},{10,11... | collective-permute-start | bytes 835592 | tf_op jit(solution)/shard_map/ppermute | solution.py:22
  32.0 0.1 broadcast_in_dim.29.bounds_ref
  32.1 3.6 %encode_first.1 = (bf16[64,512]{1,0:T(8,128)(2,1)S(1)}, bf16[512,2048]{1,0:T(8,128)(2,1)S(1)}, bf16[512,512]{1,0:T(8,128)(2,1)S(1)}, bf16[512,1024]{1,0:T(8,128)...) custom-call(f32[3,32,128]{2,1,0:T(8,128)S(1)} %broadcast_in_dim.29.bounds_ref, ...), custom_call_target="tpu_custom_call" | custom-call | flops 1342177280 | bytes 6291456 | tf_op jit(solution)/shard_map/encode_first/pallas_call | solution.py:171
  35.7 7.3 %all_to_all.5 = bf16[8,8,512]{2,1,0:T(8,128)(2,1)S(1)} all-to-all(bf16[8,8,512]{2,1,0:T(8,128)(2,1)S(1)} %bitcast.16), channel_id=1, replica_groups=mesh['section'=2,'dp'=4,'mp'=4] {'section','mp'}, dimensions={0} | all-to-all | bytes 131072 | tf_op jit(solution)/shard_map/all_to_all | solution.py:376
  43.1 2.0 %up_half.1 = (f32[64,512]{1,0:T(8,128)S(1)}, f32[64,2176]{1,0:T(8,128)S(1)}, bf16[64,2176]{1,0:T(8,128)(2,1)S(1)}) custom-call(bf16[64,512]{1,0:T(8,128)(2,1)S(1)} %bitcast.15, bf16[528,512]{1,0:T(8,128)(2,1)S(1)} %maximum_maximum_fusion.refs_0_, bf16[528,512]{1,0:T(8,128)(2,1)S(1)} %collective-permute-done.8.refs_1_, ...), custom_call_target="tpu_custom_call" | custom-call | flops 536870912 | bytes 8388608 | tf_op jit(solution)/shard_map/up_half/pallas_call | solution.py:171
  45.1 0.2 collective-permute-start.12
  45.3 1.5 %project_rest.1 = (bf16[512,1024]{1,0:T(8,128)(2,1)S(1)}, bf16[512,1024]{1,0:T(8,128)(2,1)S(1)}, f32[32,512]{1,0:T(8,128)S(1)}) custom-call(f32[3,32,128]{2,1,0:T(8,128)S(1)} %broadcast_in_dim.29.bounds_ref, bf16[512,512]{1,0:T(8,128)(2,1)S(1)} %get-tuple-element.45.ev_ref, bf16[512,2048]{1,0:T(8,128)(2,1)S(1)} %get-tuple-element.26.w_ref, ...), custom_call_target="tpu_custom_call" | custom-call | flops 1073741824 | bytes 6291456 | tf_op jit(solution)/shard_map/project_rest/pallas_call | solution.py:171
  46.9 1.8 %down_part.1 = (f32[16,2048]{1,0:T(8,128)S(1)}, bf16[16,2048]{1,0:T(8,128)(2,1)S(1)}, bf16[16,2048]{1,0:T(8,128)(2,1)S(1)}, bf16[16,2048]{1,0:T(8,128)(2,1)S(1)}) custom-call(f32[64,2176]{1,0:T(8,128)S(1)} %get-tuple-element.36.half_ref, bf16[64,2176]{1,0:T(8,128)(2,1)S(1)} %collective-permute-done.12.other_ref, ...), custom_call_target="tpu_custom_call" | custom-call | flops 536870912 | bytes 8388608 | tf_op jit(solution)/shard_map/down_part/pallas_call | solution.py:171
  48.7 0.7 %collective-permute-start.13 = (bf16[16,2048]{1,0:T(8,128)(2,1)S(1)}, bf16[16,2048]{1,0:T(8,128)(2,1)S(1)}, u32[]{:S(2)}, u32[]{:S(2)}) collective-permute-start(bf16[16,2048]{1,0:T(8,128)(2,1)S(1)} %get-tuple-element.39), channel_id=1, source_target_pairs={{0,1},{1,0},{2,3},{3,2},{4,5},{5,4},{6,7},{7,6},{8,9},{9,8},{10,11... | collective-permute-start | bytes 196616 | tf_op jit(solution)/shard_map/ppermute | solution.py:22
  49.4 0.5 collective-permute-start.14
  49.9 2.4 %collective-permute-start.15 = (bf16[16,2048]{1,0:T(8,128)(2,1)S(1)}, bf16[16,2048]{1,0:T(8,128)(2,1)S(1)}, u32[]{:S(2)}, u32[]{:S(2)}) collective-permute-start(bf16[16,2048]{1,0:T(8,128)(2,1)S(1)} %get-tuple-element.41), channel_id=1, source_target_pairs={{0,3},{1,2},{2,1},{3,0},{4,7},{5,6},{6,5},{7,4},{8,11},{9,10},{10,... | collective-permute-start | bytes 196616 | tf_op jit(solution)/shard_map/ppermute | solution.py:22
  52.3 2.0 %attend_most.1.refs_3_.before_ref = f32[512,512]{1,0:T(8,128)S(1)} custom-call(bf16[512,1024]{1,0:T(8,128)(2,1)S(1)} %get-tuple-element.30.qg_ref, bf16[512,1024]{1,0:T(8,128)(2,1)S(1)} %get-tuple-element.31.kv_first, bf16[512,1024]{1,0:T(8,128)(2,1)S(1)} %get-tuple-element.32.kv_ref, f32[16,2048]{1,0:T(8,128)S(1)} %get-tuple-element.38._.own_ref), custom_call_target="tpu_custom_call" | custom-call | flops 805306368 | bytes 4194304 | tf_op jit(solution)/shard_map/attend_most/pallas_call | solution.py:171
  54.3 0.7 %collective-permute-done.15.refs_2_ = bf16[16,2048]{1,0:T(8,128)(2,1)S(1)} collective-permute-done((bf16[16,2048]{1,0:T(8,128)(2,1)S(1)}, bf16[16,2048]{1,0:T(8,128)(2,1)S(1)}, u32[]{:S(2)}, u32[]{:S(2)}) %collective-permute-start.15) | collective-permute-done | bytes 65568 | tf_op jit(solution)/shard_map/ppermute | solution.py:22
  55.2 1.7 %attend_last.1 = bf16[32,512]{1,0:T(8,128)(2,1)} custom-call(f32[3,32,128]{2,1,0:T(8,128)S(1)} %broadcast_in_dim.29.bounds_ref, f32[8,512]{1,0:T(8,128)S(1)} %broadcast_in_dim.30.gain_ref, bf16[512,1024]{1,0:T(8,128)(2,1)S(1)} %get-tuple-element.30.qg_ref, bf16[512,1024]{1,0:T(8,128)(2,1)S(1)} %get-tuple-element.31.kv_first, ...), custom_call_target="tpu_custom_call" | custom-call | flops 134217728 | bytes 4194304 | tf_op jit(solution)/shard_map/attend_last/pallas_call | solution.py:171
  56.9 0.6 %finish.1 = bf16[8,4096]{1,0:T(8,128)(2,1)} custom-call(f32[8,2048]{1,0:T(8,128)S(1)} %get-tuple-element.42._.keep_ref, f32[8,2048]{1,0:T(8,128)S(1)} %collective-permute-done.16.got_ref), custom_call_target="tpu_custom_call" | custom-call | bytes 262144 | tf_op jit(solution)/shard_map/finish/pallas_call | solution.py:171
  (46 shorter events, 0.5 us)
Async XLA Ops:
  0.6 12.0 %copy-start.1 = (bf16[1,1024,512]{2,1,0:T(8,128)(2,1)S(1)}, bf16[1,1024,512]{2,1,0:T(8,128)(2,1)}, u32[]{:S(2)}) copy-start(bf16[1,1024,512]{2,1,0:T(8,128)(2,1)} %param.10) | copy-start | bytes 3145732
  2.4 16.2 %collective-permute-start = (bf16[160,512]{1,0:T(8,128)(2,1)S(1)}, bf16[160,512]{1,0:T(8,128)(2,1)S(1)}, u32[]{:S(2)}, u32[]{:S(2)}) collective-permute-start(bf16[160,512]{1,0:T(8,128)(2,1)S(1)} %pad_maximum_fusion), channel_id=1, source_target_pairs={{0,8},{4,12},{8,0},{12,4},{1,9},{5,13},{9,1},{13,5},{2,10},{6,14},... | collective-permute-start | bytes 491528 | tf_op jit(solution)/shard_map/ppermute | solution.py:22
  6.5 12.1 %collective-permute-start.1 = (bf16[160,512]{1,0:T(8,128)(2,1)S(1)}, bf16[160,512]{1,0:T(8,128)(2,1)S(1)}, u32[]{:S(2)}, u32[]{:S(2)}) collective-permute-start(bf16[160,512]{1,0:T(8,128)(2,1)S(1)} %pad_maximum_fusion), channel_id=1, source_target_pairs={{0,12},{4,8},{8,4},{12,0},{1,13},{5,9},{9,5},{13,1},{2,14},{6,10},... | collective-permute-start | bytes 491528 | tf_op jit(solution)/shard_map/ppermute | solution.py:22
  7.9 11.3 %collective-permute-start.2 = (bf16[160,512]{1,0:T(8,128)(2,1)S(1)}, bf16[160,512]{1,0:T(8,128)(2,1)S(1)}, u32[]{:S(2)}, u32[]{:S(2)}) collective-permute-start(bf16[160,512]{1,0:T(8,128)(2,1)S(1)} %pad_maximum_fusion), channel_id=1, source_target_pairs={{0,4},{4,0},{8,12},{12,8},{1,5},{5,1},{9,13},{13,9},{2,6},{6,2},{1... | collective-permute-start | bytes 491528 | tf_op jit(solution)/shard_map/ppermute | solution.py:22
  8.2 14.1 %copy-start.3 = (bf16[128,512]{1,0:T(8,128)(2,1)S(1)}, bf16[128,512]{1,0:T(8,128)(2,1)}, u32[]{:S(2)}) copy-start(bf16[128,512]{1,0:T(8,128)(2,1)} %param.14) | copy-start | bytes 393220
  8.2 14.8 %copy-start.5 = (s32[1,32]{1,0:T(1,128)S(1)}, s32[1,32]{1,0:T(1,128)}, u32[]{:S(2)}) copy-start(s32[1,32]{1,0:T(1,128)} %param.12) | copy-start | bytes 388
  9.5 3.2 %copy-start.2 = (bf16[128,2048]{1,0:T(8,128)(2,1)S(1)}, bf16[128,2048]{1,0:T(8,128)(2,1)}, u32[]{:S(2)}) copy-start(bf16[128,2048]{1,0:T(8,128)(2,1)} %param.13) | copy-start | bytes 1572868
  9.5 20.0 %collective-permute-start.8 = (bf16[528,512]{1,0:T(8,128)(2,1)S(1)}, bf16[528,512]{1,0:T(8,128)(2,1)S(1)}, u32[]{:S(2)}, u32[]{:S(2)}) collective-permute-start(bf16[528,512]{1,0:T(8,128)(2,1)S(1)} %maximum_maximum_fusion.refs_0_), channel_id=1, source_target_pairs={{0,1},{1,0},{2,3},{3,2},{4,5},{5,4},{6,7},{7,6},{8,9},{9,8},{10,11... | collective-permute-start | bytes 1622024 | tf_op jit(solution)/shard_map/ppermute | solution.py:22
  11.1 21.1 %copy-start.4 = (f32[512]{0:T(512)S(1)}, f32[512]{0:T(512)}, u32[]{:S(2)}) copy-start(f32[512]{0:T(512)} %param.15) | copy-start | bytes 6148
  11.1 20.1 %collective-permute-start.9 = (bf16[528,512]{1,0:T(8,128)(2,1)S(1)}, bf16[528,512]{1,0:T(8,128)(2,1)S(1)}, u32[]{:S(2)}, u32[]{:S(2)}) collective-permute-start(bf16[528,512]{1,0:T(8,128)(2,1)S(1)} %maximum_maximum_fusion.refs_0_), channel_id=1, source_target_pairs={{0,2},{1,3},{2,0},{3,1},{4,6},{5,7},{6,4},{7,5},{8,10},{9,11},{10,... | collective-permute-start | bytes 1622024 | tf_op jit(solution)/shard_map/ppermute | solution.py:22
  12.6 30.5 %copy-start = (bf16[2048,2048]{1,0:T(8,128)(2,1)S(1)}, bf16[2048,2048]{1,0:T(8,128)(2,1)}, u32[]{:S(2)}) copy-start(bf16[2048,2048]{1,0:T(8,128)(2,1)} %refs_5_.1) | copy-start | bytes 25165828
  19.2 9.1 %collective-permute-start.3 = (bf16[3,160,256]{2,1,0:T(8,128)(2,1)S(1)}, bf16[3,160,256]{2,1,0:T(8,128)(2,1)S(1)}, u32[]{:S(2)}, u32[]{:S(2)}) collective-permute-start(bf16[3,160,256]{2,1,0:T(8,128)(2,1)S(1)} %get-tuple-element.24), channel_id=1, source_target_pairs={{0,1},{1,0},{2,3},{3,2},{4,5},{5,4},{6,7},{7,6},{8,9},{9,8},{10,11... | collective-permute-start | bytes 737288 | tf_op jit(solution)/shard_map/ppermute | solution.py:22
  20.8 8.7 %collective-permute-start.4 = (bf16[3,160,256]{2,1,0:T(8,128)(2,1)S(1)}, bf16[3,160,256]{2,1,0:T(8,128)(2,1)S(1)}, u32[]{:S(2)}, u32[]{:S(2)}) collective-permute-start(bf16[3,160,256]{2,1,0:T(8,128)(2,1)S(1)} %get-tuple-element.25), channel_id=1, source_target_pairs={{0,2},{1,3},{2,0},{3,1},{4,6},{5,7},{6,4},{7,5},{8,10},{9,11},{10,... | collective-permute-start | bytes 737288 | tf_op jit(solution)/shard_map/ppermute | solution.py:22
  22.3 9.7 %collective-permute-start.5 = (bf16[2,3,160,256]{3,2,1,0:T(8,128)(2,1)S(1)}, bf16[2,3,160,256]{3,2,1,0:T(8,128)(2,1)S(1)}, u32[]{:S(2)}, u32[]{:S(2)}) collective-permute-start(bf16[2,3,160,256]{3,2,1,0:T(8,128)(2,1)S(1)} %get-tuple-element.23.refs_4_), channel_id=1, source_target_pairs={{0,16},{16,0},{1,17},{17,1},{2,18},{18,2},{3,19},{19,3},{4,20},{20... | collective-permute-start | bytes 1474568 | tf_op jit(solution)/shard_map/ppermute | solution.py:22
  28.3 3.7 %collective-permute-start.6 = (bf16[3,160,256]{2,1,0:T(8,128)(2,1)S(1)}, bf16[3,160,256]{2,1,0:T(8,128)(2,1)S(1)}, u32[]{:S(2)}, u32[]{:S(2)}) collective-permute-start(bf16[3,160,256]{2,1,0:T(8,128)(2,1)S(1)} %collective-permute-done.3.refs_5_), channel_id=1, source_target_pairs={{0,16},{16,0},{1,17},{17,1},{2,18},{18,2},{3,19},{19,3},{4,20},{20... | collective-permute-start | bytes 737288 | tf_op jit(solution)/shard_map/ppermute | solution.py:22
  29.5 2.5 %collective-permute-start.7 = (bf16[3,160,256]{2,1,0:T(8,128)(2,1)S(1)}, bf16[3,160,256]{2,1,0:T(8,128)(2,1)S(1)}, u32[]{:S(2)}, u32[]{:S(2)}) collective-permute-start(bf16[3,160,256]{2,1,0:T(8,128)(2,1)S(1)} %collective-permute-done.4.refs_6_), channel_id=1, source_target_pairs={{0,16},{16,0},{1,17},{17,1},{2,18},{18,2},{3,19},{19,3},{4,20},{20... | collective-permute-start | bytes 737288 | tf_op jit(solution)/shard_map/ppermute | solution.py:22
  29.5 13.5 %collective-permute-start.10 = (bf16[256,512]{1,0:T(8,128)(2,1)S(1)}, bf16[256,512]{1,0:T(8,128)(2,1)S(1)}, u32[]{:S(2)}, u32[]{:S(2)}) collective-permute-start(bf16[256,512]{1,0:T(8,128)(2,1)S(1)} %slice.40), channel_id=1, source_target_pairs={{0,2},{1,3},{2,0},{3,1},{4,6},{5,7},{6,4},{7,5},{8,10},{9,11},{10,... | collective-permute-start | bytes 786440 | tf_op jit(solution)/shard_map/ppermute | solution.py:22
  31.1 11.9 %collective-permute-start.11 = (bf16[272,512]{1,0:T(8,128)(2,1)S(1)}, bf16[272,512]{1,0:T(8,128)(2,1)S(1)}, u32[]{:S(2)}, u32[]{:S(2)}) collective-permute-start(bf16[272,512]{1,0:T(8,128)(2,1)S(1)} %slice.41), channel_id=1, source_target_pairs={{0,1},{1,0},{2,3},{3,2},{4,5},{5,4},{6,7},{7,6},{8,9},{9,8},{10,11... | collective-permute-start | bytes 835592 | tf_op jit(solution)/shard_map/ppermute | solution.py:22
  32.1 14.7 %slice-start = ((s8[8388608]{0:T(1024)(128)(4,1)}), s8[4194304]{0:T(1024)(128)(4,1)S(1)}, s32[]{:S(2)}) async-start(s8[8388608]{0:T(1024)(128)(4,1)} %bitcast.13), calls=%async_computation.1 | async-start | bytes 8388608
  43.1 3.8 %slice-start.1 = ((s8[8388608]{0:T(1024)(128)(4,1)}), s8[4194304]{0:T(1024)(128)(4,1)S(1)}, s32[]{:S(2)}) async-start(s8[8388608]{0:T(1024)(128)(4,1)} %bitcast.13), calls=%async_computation.2 | async-start | bytes 8388608
  45.1 1.7 %collective-permute-start.12 = (bf16[64,2176]{1,0:T(8,128)(2,1)S(1)}, bf16[64,2176]{1,0:T(8,128)(2,1)S(1)}, u32[]{:S(2)}, u32[]{:S(2)}) collective-permute-start(bf16[64,2176]{1,0:T(8,128)(2,1)S(1)} %get-tuple-element.37), channel_id=1, source_target_pairs={{0,16},{16,0},{1,17},{17,1},{2,18},{18,2},{3,19},{19,3},{4,20},{20... | collective-permute-start | bytes 835592 | tf_op jit(solution)/shard_map/ppermute | solution.py:22
  48.7 5.6 %collective-permute-start.13 = (bf16[16,2048]{1,0:T(8,128)(2,1)S(1)}, bf16[16,2048]{1,0:T(8,128)(2,1)S(1)}, u32[]{:S(2)}, u32[]{:S(2)}) collective-permute-start(bf16[16,2048]{1,0:T(8,128)(2,1)S(1)} %get-tuple-element.39), channel_id=1, source_target_pairs={{0,1},{1,0},{2,3},{3,2},{4,5},{5,4},{6,7},{7,6},{8,9},{9,8},{10,11... | collective-permute-start | bytes 196616 | tf_op jit(solution)/shard_map/ppermute | solution.py:22
  49.4 5.0 %collective-permute-start.14 = (bf16[16,2048]{1,0:T(8,128)(2,1)S(1)}, bf16[16,2048]{1,0:T(8,128)(2,1)S(1)}, u32[]{:S(2)}, u32[]{:S(2)}) collective-permute-start(bf16[16,2048]{1,0:T(8,128)(2,1)S(1)} %get-tuple-element.40), channel_id=1, source_target_pairs={{0,2},{1,3},{2,0},{3,1},{4,6},{5,7},{6,4},{7,5},{8,10},{9,11},{10,... | collective-permute-start | bytes 196616 | tf_op jit(solution)/shard_map/ppermute | solution.py:22
  49.9 5.2 %collective-permute-start.15 = (bf16[16,2048]{1,0:T(8,128)(2,1)S(1)}, bf16[16,2048]{1,0:T(8,128)(2,1)S(1)}, u32[]{:S(2)}, u32[]{:S(2)}) collective-permute-start(bf16[16,2048]{1,0:T(8,128)(2,1)S(1)} %get-tuple-element.41), channel_id=1, source_target_pairs={{0,3},{1,2},{2,1},{3,0},{4,7},{5,6},{6,5},{7,4},{8,11},{9,10},{10,... | collective-permute-start | bytes 196616 | tf_op jit(solution)/shard_map/ppermute | solution.py:22
  55.1 1.8 %collective-permute-start.16 = (f32[8,2048]{1,0:T(8,128)S(1)}, f32[8,2048]{1,0:T(8,128)S(1)}, u32[]{:S(2)}, u32[]{:S(2)}) collective-permute-start(f32[8,2048]{1,0:T(8,128)S(1)} %get-tuple-element.43), channel_id=1, source_target_pairs={{0,16},{16,0},{1,17},{17,1},{2,18},{18,2},{3,19},{19,3},{4,20},{20... | collective-permute-start | bytes 196616 | tf_op jit(solution)/shard_map/ppermute | solution.py:22

commit v12 on v11

--- a/solution.py
+++ b/solution.py
@@ -59,35 +59,29 @@
 STEP = 256
 
 
-def attend(q_ref, kv_refs, att_ref, pairs):
+def attend(q_ref, kv_refs, att_ref):
     rows, width = q_ref.shape
     head = width // HEADS
     step = min(rows, STEP)
-    tri = lax.broadcasted_iota(jnp.int32, (step, step), 1) <= lax.broadcasted_iota(
-        jnp.int32, (step, step), 0
-    )
     *earlier, own = kv_refs
-    for i, h in pairs:
+    for i in range(rows // step):
         at = slice(i * step, (i + 1) * step)
-        q = q_ref[at, h * head : (h + 1) * head]
-        runs = [(ref, slice(0, ref.shape[0])) for ref in earlier]
-        if i:
-            runs.append((own, slice(0, i * step)))
-        total = None
-        for ref, keys in [*runs, (own, at)]:
-            k = ref[keys, width + h * head : width + (h + 1) * head]
-            v = ref[keys, h * head : (h + 1) * head]
-            s = lax.dot_general(q, k, (((1,), (1,)), ((), ())), preferred_element_type=F32)
-            wts = silu_half(s * (0.5 * head**-0.5))
-            if keys is at:
-                wts = jnp.where(tri, wts, 0.0)
-            mixed = jnp.dot(wts.astype(BF16), v, preferred_element_type=F32)
-            total = mixed if total is None else total + mixed
-        att_ref[at, h * head : (h + 1) * head] = total
-
-
-def all_pairs(rows):
-    return [(i, h) for i in range(max(rows // STEP, 1)) for h in range(HEADS)]
+        upto = slice(0, (i + 1) * step)
+        row = lax.broadcasted_iota(jnp.int32, (step, (i + 1) * step), 0) + i * step
+        seen = lax.broadcasted_iota(jnp.int32, (step, (i + 1) * step), 1) <= row
+        for h in range(HEADS):
+            q = q_ref[at, h * head : (h + 1) * head]
+            total = None
+            for ref, keys in [*[(ref, slice(0, ref.shape[0])) for ref in earlier], (own, upto)]:
+                k = ref[keys, width + h * head : width + (h + 1) * head]
+                v = ref[keys, h * head : (h + 1) * head]
+                s = lax.dot_general(q, k, (((1,), (1,)), ((), ())), preferred_element_type=F32)
+                wts = silu_half(s * (0.5 * head**-0.5))
+                if ref is own:
+                    wts = jnp.where(seen, wts, 0.0)
+                mixed = jnp.dot(wts.astype(BF16), v, preferred_element_type=F32)
+                total = mixed if total is None else total + mixed
+            att_ref[at, h * head : (h + 1) * head] = total
 
 
 def gated_rows(att, gain_ref, gate):
@@ -121,7 +115,7 @@
     sums_ev = jnp.dot(member, ev_ref[...], preferred_element_type=F32)
     sums_ev_ref[...] = sums_ev
     project(dps, 0, bounds_ref[2, :1, :1], ev_ref, w_ref, gate_ref, q_ref, kv_ref)
-    attend(q_ref, [kv_ref], att_ref, all_pairs(q_ref.shape[0]))
+    attend(q_ref, [kv_ref], att_ref)
     gated = gated_rows(att_ref[...], gain_ref, gate_ref[...])
     sums_g_ref[...] = jnp.dot(member, gated, preferred_element_type=F32)
     out = pool(dps, bounds_ref, sums_ev, sums_g_ref, wout_ref)
@@ -141,30 +135,16 @@
     out_ref[...] = sums_ev_ref[...] + jnp.dot(member, ev_ref[...], preferred_element_type=F32)
 
 
-def attend_kernel(pairs, qg_ref, kv_first, kv_ref, _, att_ref):
-    attend(halves(qg_ref)[0], [kv_first, kv_ref], att_ref, pairs)
-
-
-def attend_rest_kernel(
-    row0, pairs, dps, bounds_ref, gain_ref, qg_ref, kv_first, kv_ref, sums_ref, sums_ev_ref, wout_ref, before_ref, _, out_ref,
-    att_ref, total_ref,
-):
+def attend_kernel(row0, bounds_ref, gain_ref, qg_ref, kv_first, kv_ref, sums_ref, _, out_ref, att_ref):
     q_ref, gate_ref = halves(qg_ref)
-    rows, width = q_ref.shape
-    attend(q_ref, [kv_first, kv_ref], att_ref, pairs)
-    head = width // HEADS
-    step = min(rows, STEP)
-    total = sums_ref[...]
-    for i in range(rows // step):
-        at = slice(i * step, (i + 1) * step)
-        att = [
-            (att_ref if (i, h) in pairs else before_ref)[at, h * head : (h + 1) * head] for h in range(HEADS)
-        ]
-        gated = gated_rows(jnp.concatenate(att, axis=1), gain_ref, gate_ref[at])
-        member = membership(bounds_ref, row0 + i * step, step)
-        total = total + jnp.dot(member, gated, preferred_element_type=F32)
-    total_ref[...] = total
-    out_ref[...] = pool(dps, bounds_ref, sums_ev_ref[...], total_ref, wout_ref).astype(BF16)
+    attend(q_ref, [kv_first, kv_ref], att_ref)
+    gated = gated_rows(att_ref[...], gain_ref, gate_ref[...])
+    member = membership(bounds_ref, row0, q_ref.shape[0])
+    out_ref[...] = sums_ref[...] + jnp.dot(member, gated, preferred_element_type=F32)
+
+
+def pool_kernel(dps, bounds_ref, sums_ev_ref, sums_ref, wout_ref, _, out_ref):
+    out_ref[...] = pool(dps, bounds_ref, sums_ev_ref[...], sums_ref, wout_ref).astype(BF16)
 
 
 def call(kernel, name, operands, out_shape, scratch, mib, flops, size, transcendentals=0):
@@ -413,24 +393,21 @@
     )
 
     got = [swap(x, "mp", mps, k + 1) for k, x in enumerate(sends)]
-    pairs = all_pairs(rest)
-    late = pairs[-1:]
-    pairs = pairs[: -len(late)]
-    (att,) = call(
-        functools.partial(attend_kernel, pairs),
-        "attend_most",
-        [queries_gate, kv_first, kv_rest, own],
-        [((rest, width), F32)],
-        [],
+    (sums_g,) = call(
+        functools.partial(attend_kernel, first),
+        "attend_rest",
+        [bounds, gain, queries_gate, kv_first, kv_rest, sums_g, own],
+        [((sess, width), F32)],
+        [pltpu.VMEM((rest, width), F32)],
         10,
-        3 * rest * length * width,
+        4 * rest * length * width,
         4 * 1024 * 1024,
         HEADS * rest * length,
     )
     keep, send = call(
         add_kernel,
         "add_parts",
-        [own, *got, att],
+        [own, *got, sums_g],
         [((take, half_width), F32)] * 2,
         [pltpu.VMEM((pair, half_width), F32)],
         8,
@@ -439,15 +416,14 @@
     )
     got = swap(send, "section", sections, 1)
     (pooled,) = call(
-        functools.partial(attend_rest_kernel, first, late, dps),
-        "attend_last",
-        [bounds, gain, queries_gate, kv_first, kv_rest, sums_g, sums_ev, full_wout, att, keep],
+        functools.partial(pool_kernel, dps),
+        "pool_rows",
+        [bounds, sums_ev, sums_g, full_wout, keep],
         [((sess, width), BF16)],
-        [pltpu.VMEM((rest, width), F32), pltpu.VMEM((sess, width), F32)],
-        10,
-        rest * length * width // 2,
-        4 * 1024 * 1024,
-        HEADS * rest * length // 8,
+        [],
+        8,
+        6 * sess * width * width,
+        1024 * 1024,
     )
     (cross_out,) = call(
         finish_kernel,

time: 58 us -> 57.4 us (0.990)
  transfers between devices with their start and end apart: 17 -> 17, of which waited for: 5 -> 5; matrix products, arithmetic and copies ran while one was open for 3% -> 3% of each run, Pallas kernels for 15% -> 16%
where the time goes in v12:
time: 57.4 us; the launch traced here: 57.2 us
  starting transfers between devices  18.1 us (32%)
  Pallas kernels  13.5 us (24%)
  waiting for transfers between devices  13.2 us (23%)
  blocking collectives  7.3 us (13%)
  local copies, waits for them, and re-layouts  2.11 us (4%)
  between operations  1.55 us (3%)
  other arithmetic  1.41 us (2%)
    ppermute x17, starting transfers between devices, swap(): return lax.ppermute(x, axis, [(i, i ^ flip) for i in range(size)])  18.1 us
    pallas_call x9, Pallas kernels, call(): pl.pallas_call(kernel, in_specs=[VMEM] * len(operands), out_specs=[VMEM]...  13.5 us
    ppermute x17, waiting for transfers between devices, swap(): return lax.ppermute(x, axis, [(i, i ^ flip) for i in range(size)])  13.2 us
    all_to_all x1, blocking collectives, per_device(): lax.all_to_all(micro_rows.reshape(peers, take, width), group, split_axis=...  7.3 us
    concatenate x1, other arithmetic, gather_weights(): jnp.concatenate([w_in, ffn_gain, jnp.zeros((15, w_in.shape[1]), BF16)], a...  1.27 us
  transfers between devices with their start and end apart: 17, of which 5 were waited for; matrix products, arithmetic and copies ran while one was open for 3% of the time, Pallas kernels for 16%

profile of v12, /device:TPU:0, one launch (start us, length us, event | category | flops | bytes accessed | tf_op | source)
XLA Modules:
  0.0 57.2 jit_solution(5478459901774947099)
XLA Ops:
  0.7 0.8 %constant_dynamic-slice_fusion = bf16[32,512]{1,0:T(8,128)(2,1)S(1)} fusion(bf16[128,512]{1,0:T(8,128)(2,1)} %param.14, s32[]{:T(128)S(6)} %select_n.12), kind=kLoop, calls=%fused_computation.9 | loop fusion | bytes 65540 | tf_op jit(solution)/shard_map/dynamic_slice | solution.py:198
  1.5 0.9 %constant_dynamic-slice_fusion.1 = bf16[128,512]{1,0:T(8,128)(2,1)S(1)} fusion(bf16[128,2048]{1,0:T(8,128)(2,1)} %param.13, s32[]{:T(128)S(6)} %select_n.11), kind=kLoop, calls=%fused_computation.10 | loop fusion | bytes 262148 | tf_op jit(solution)/shard_map/dynamic_slice | solution.py:197
  2.4 4.1 %collective-permute-start = (bf16[160,512]{1,0:T(8,128)(2,1)S(1)}, bf16[160,512]{1,0:T(8,128)(2,1)S(1)}, u32[]{:S(2)}, u32[]{:S(2)}) collective-permute-start(bf16[160,512]{1,0:T(8,128)(2,1)S(1)} %pad_maximum_fusion), channel_id=1, source_target_pairs={{0,8},{4,12},{8,0},{12,4},{1,9},{5,13},{9,1},{13,5},{2,10},{6,14},... | collective-permute-start | bytes 491528 | tf_op jit(solution)/shard_map/ppermute | solution.py:22
  6.5 1.3 %collective-permute-start.1 = (bf16[160,512]{1,0:T(8,128)(2,1)S(1)}, bf16[160,512]{1,0:T(8,128)(2,1)S(1)}, u32[]{:S(2)}, u32[]{:S(2)}) collective-permute-start(bf16[160,512]{1,0:T(8,128)(2,1)S(1)} %pad_maximum_fusion), channel_id=1, source_target_pairs={{0,12},{4,8},{8,4},{12,0},{1,13},{5,9},{9,5},{13,1},{2,14},{6,10},... | collective-permute-start | bytes 491528 | tf_op jit(solution)/shard_map/ppermute | solution.py:22
  7.9 0.2 collective-permute-start.2
  8.1 0.1 pad.2.clone
  8.2 1.3 %maximum_maximum_fusion.refs_0_ = bf16[528,512]{1,0:T(8,128)(2,1)S(1)} fusion(bf16[1,512]{1,0:T(2,128)(2,1)} %param.17, bf16[512,512]{1,0:T(8,128)(2,1)} %param.16, bf16[528]{0:T(1024)(128)(2,1)S(1)} %pad.2.clone), kind=kLoop, calls=%fused_computation | loop fusion | flops 1622016 | bytes 1067040 | tf_op jit(solution)/shard_map/concatenate | solution.py:180
  9.5 1.6 %collective-permute-start.8 = (bf16[528,512]{1,0:T(8,128)(2,1)S(1)}, bf16[528,512]{1,0:T(8,128)(2,1)S(1)}, u32[]{:S(2)}, u32[]{:S(2)}) collective-permute-start(bf16[528,512]{1,0:T(8,128)(2,1)S(1)} %maximum_maximum_fusion.refs_0_), channel_id=1, source_target_pairs={{0,1},{1,0},{2,3},{3,2},{4,5},{5,4},{6,7},{7,6},{8,9},{9,8},{10,11... | collective-permute-start | bytes 1622024 | tf_op jit(solution)/shard_map/ppermute | solution.py:22
  11.1 1.5 %collective-permute-start.9 = (bf16[528,512]{1,0:T(8,128)(2,1)S(1)}, bf16[528,512]{1,0:T(8,128)(2,1)S(1)}, u32[]{:S(2)}, u32[]{:S(2)}) collective-permute-start(bf16[528,512]{1,0:T(8,128)(2,1)S(1)} %maximum_maximum_fusion.refs_0_), channel_id=1, source_target_pairs={{0,2},{1,3},{2,0},{3,1},{4,6},{5,7},{6,4},{7,5},{8,10},{9,11},{10,... | collective-permute-start | bytes 1622024 | tf_op jit(solution)/shard_map/ppermute | solution.py:22
  12.7 5.9 %collective-permute-done.refs_0_ = bf16[160,512]{1,0:T(8,128)(2,1)S(1)} collective-permute-done((bf16[160,512]{1,0:T(8,128)(2,1)S(1)}, bf16[160,512]{1,0:T(8,128)(2,1)S(1)}, u32[]{:S(2)}, u32[]{:S(2)}) %collective-permute-start) | collective-permute-done | bytes 163872 | tf_op jit(solution)/shard_map/ppermute | solution.py:22
  18.6 0.5 collective-permute-done.2.refs_2_
  19.2 1.6 %collective-permute-start.3 = (bf16[3,160,256]{2,1,0:T(8,128)(2,1)S(1)}, bf16[3,160,256]{2,1,0:T(8,128)(2,1)S(1)}, u32[]{:S(2)}, u32[]{:S(2)}) collective-permute-start(bf16[3,160,256]{2,1,0:T(8,128)(2,1)S(1)} %get-tuple-element.24), channel_id=1, source_target_pairs={{0,1},{1,0},{2,3},{3,2},{4,5},{5,4},{6,7},{7,6},{8,9},{9,8},{10,11... | collective-permute-start | bytes 737288 | tf_op jit(solution)/shard_map/ppermute | solution.py:22
  20.8 1.5 %collective-permute-start.4 = (bf16[3,160,256]{2,1,0:T(8,128)(2,1)S(1)}, bf16[3,160,256]{2,1,0:T(8,128)(2,1)S(1)}, u32[]{:S(2)}, u32[]{:S(2)}) collective-permute-start(bf16[3,160,256]{2,1,0:T(8,128)(2,1)S(1)} %get-tuple-element.25), channel_id=1, source_target_pairs={{0,2},{1,3},{2,0},{3,1},{4,6},{5,7},{6,4},{7,5},{8,10},{9,11},{10,... | collective-permute-start | bytes 737288 | tf_op jit(solution)/shard_map/ppermute | solution.py:22
  23.0 0.1 select_reduce_fusion
  23.1 5.1 %collective-permute-done.3.refs_5_ = bf16[3,160,256]{2,1,0:T(8,128)(2,1)S(1)} collective-permute-done((bf16[3,160,256]{2,1,0:T(8,128)(2,1)S(1)}, bf16[3,160,256]{2,1,0:T(8,128)(2,1)S(1)}, u32[]{:S(2)}, u32[]{:S(2)}) %collective-permute-start.3) | collective-permute-done | bytes 245792 | tf_op jit(solution)/shard_map/ppermute | solution.py:22
  28.3 1.2 %collective-permute-done.4.refs_6_ = bf16[3,160,256]{2,1,0:T(8,128)(2,1)S(1)} collective-permute-done((bf16[3,160,256]{2,1,0:T(8,128)(2,1)S(1)}, bf16[3,160,256]{2,1,0:T(8,128)(2,1)S(1)}, u32[]{:S(2)}, u32[]{:S(2)}) %collective-permute-start.4) | collective-permute-done | bytes 245792 | tf_op jit(solution)/shard_map/ppermute | solution.py:22
  29.5 1.6 %collective-permute-start.10 = (bf16[256,512]{1,0:T(8,128)(2,1)S(1)}, bf16[256,512]{1,0:T(8,128)(2,1)S(1)}, u32[]{:S(2)}, u32[]{:S(2)}) collective-permute-start(bf16[256,512]{1,0:T(8,128)(2,1)S(1)} %slice.40), channel_id=1, source_target_pairs={{0,2},{1,3},{2,0},{3,1},{4,6},{5,7},{6,4},{7,5},{8,10},{9,11},{10,... | collective-permute-start | bytes 786440 | tf_op jit(solution)/shard_map/ppermute | solution.py:22
  31.1 0.8 %collective-permute-start.11 = (bf16[272,512]{1,0:T(8,128)(2,1)S(1)}, bf16[272,512]{1,0:T(8,128)(2,1)S(1)}, u32[]{:S(2)}, u32[]{:S(2)}) collective-permute-start(bf16[272,512]{1,0:T(8,128)(2,1)S(1)} %slice.41), channel_id=1, source_target_pairs={{0,1},{1,0},{2,3},{3,2},{4,5},{5,4},{6,7},{7,6},{8,9},{9,8},{10,11... | collective-permute-start | bytes 835592 | tf_op jit(solution)/shard_map/ppermute | solution.py:22
  32.0 0.1 broadcast_in_dim.29.bounds_ref
  32.1 3.6 %encode_first.1 = (bf16[64,512]{1,0:T(8,128)(2,1)S(1)}, bf16[512,2048]{1,0:T(8,128)(2,1)S(1)}, bf16[512,512]{1,0:T(8,128)(2,1)S(1)}, bf16[512,1024]{1,0:T(8,128)...) custom-call(f32[3,32,128]{2,1,0:T(8,128)S(1)} %broadcast_in_dim.29.bounds_ref, ...), custom_call_target="tpu_custom_call" | custom-call | flops 1342177280 | bytes 6291456 | tf_op jit(solution)/shard_map/encode_first/pallas_call | solution.py:151
  35.8 7.3 %all_to_all.5 = bf16[8,8,512]{2,1,0:T(8,128)(2,1)S(1)} all-to-all(bf16[8,8,512]{2,1,0:T(8,128)(2,1)S(1)} %bitcast.16), channel_id=1, replica_groups=mesh['section'=2,'dp'=4,'mp'=4] {'section','mp'}, dimensions={0} | all-to-all | bytes 131072 | tf_op jit(solution)/shard_map/all_to_all | solution.py:356
  43.1 2.0 %up_half.1 = (f32[64,512]{1,0:T(8,128)S(1)}, f32[64,2176]{1,0:T(8,128)S(1)}, bf16[64,2176]{1,0:T(8,128)(2,1)S(1)}) custom-call(bf16[64,512]{1,0:T(8,128)(2,1)S(1)} %bitcast.15, bf16[528,512]{1,0:T(8,128)(2,1)S(1)} %maximum_maximum_fusion.refs_0_, bf16[528,512]{1,0:T(8,128)(2,1)S(1)} %collective-permute-done.8.refs_1_, ...), custom_call_target="tpu_custom_call" | custom-call | flops 536870912 | bytes 8388608 | tf_op jit(solution)/shard_map/up_half/pallas_call | solution.py:151
  45.1 0.2 collective-permute-start.12
  45.3 1.5 %project_rest.1 = (bf16[512,1024]{1,0:T(8,128)(2,1)S(1)}, bf16[512,1024]{1,0:T(8,128)(2,1)S(1)}, f32[32,512]{1,0:T(8,128)S(1)}) custom-call(f32[3,32,128]{2,1,0:T(8,128)S(1)} %broadcast_in_dim.29.bounds_ref, bf16[512,512]{1,0:T(8,128)(2,1)S(1)} %get-tuple-element.45.ev_ref, bf16[512,2048]{1,0:T(8,128)(2,1)S(1)} %get-tuple-element.26.w_ref, ...), custom_call_target="tpu_custom_call" | custom-call | flops 1073741824 | bytes 6291456 | tf_op jit(solution)/shard_map/project_rest/pallas_call | solution.py:151
  46.9 1.8 %down_part.1 = (f32[16,2048]{1,0:T(8,128)S(1)}, bf16[16,2048]{1,0:T(8,128)(2,1)S(1)}, bf16[16,2048]{1,0:T(8,128)(2,1)S(1)}, bf16[16,2048]{1,0:T(8,128)(2,1)S(1)}) custom-call(f32[64,2176]{1,0:T(8,128)S(1)} %get-tuple-element.35.half_ref, bf16[64,2176]{1,0:T(8,128)(2,1)S(1)} %collective-permute-done.12.other_ref, ...), custom_call_target="tpu_custom_call" | custom-call | flops 536870912 | bytes 8388608 | tf_op jit(solution)/shard_map/down_part/pallas_call | solution.py:151
  48.7 0.7 %collective-permute-start.13 = (bf16[16,2048]{1,0:T(8,128)(2,1)S(1)}, bf16[16,2048]{1,0:T(8,128)(2,1)S(1)}, u32[]{:S(2)}, u32[]{:S(2)}) collective-permute-start(bf16[16,2048]{1,0:T(8,128)(2,1)S(1)} %get-tuple-element.39), channel_id=1, source_target_pairs={{0,1},{1,0},{2,3},{3,2},{4,5},{5,4},{6,7},{7,6},{8,9},{9,8},{10,11... | collective-permute-start | bytes 196616 | tf_op jit(solution)/shard_map/ppermute | solution.py:22
  49.4 0.5 collective-permute-start.14
  49.9 2.4 %collective-permute-start.15 = (bf16[16,2048]{1,0:T(8,128)(2,1)S(1)}, bf16[16,2048]{1,0:T(8,128)(2,1)S(1)}, u32[]{:S(2)}, u32[]{:S(2)}) collective-permute-start(bf16[16,2048]{1,0:T(8,128)(2,1)S(1)} %get-tuple-element.41), channel_id=1, source_target_pairs={{0,3},{1,2},{2,1},{3,0},{4,7},{5,6},{6,5},{7,4},{8,11},{9,10},{10,... | collective-permute-start | bytes 196616 | tf_op jit(solution)/shard_map/ppermute | solution.py:22
  52.3 2.9 %attend_rest.1.refs_3_.sums_ref = f32[32,512]{1,0:T(8,128)S(1)} custom-call(f32[3,32,128]{2,1,0:T(8,128)S(1)} %broadcast_in_dim.29.bounds_ref, f32[8,512]{1,0:T(8,128)S(1)} %broadcast_in_dim.30.gain_ref, bf16[512,1024]{1,0:T(8,128)(2,1)S(1)} %get-tuple-element.31.qg_ref, bf16[512,1024]{1,0:T(8,128)(2,1)S(1)} %get-tuple-element.32.kv_first, ...), custom_call_target="tpu_custom_call" | custom-call | flops 1073741824 | bytes 4194304 | tf_op jit(solution)/shard_map/attend_rest/pallas_call | solution.py:151
  55.3 0.8 %pool_rows.1 = bf16[32,512]{1,0:T(8,128)(2,1)} custom-call(f32[3,32,128]{2,1,0:T(8,128)S(1)} %broadcast_in_dim.29.bounds_ref, f32[32,512]{1,0:T(8,128)S(1)} %get-tuple-element.30._.sums_ev_ref, f32[32,512]{1,0:T(8,128)S(1)} %attend_rest.1.refs_3_.sums_ref, bf16[512,512]{1,0:T(8,128)(2,1)S(1)} %get-tuple-element.38.wout_ref, ...), custom_call_target="tpu_custom_call" | custom-call | flops 50331648 | bytes 1048576 | tf_op jit(solution)/shard_map/pool_rows/pallas_call | solution.py:151
  56.2 0.4 collective-permute-done.16.got_ref
  56.6 0.6 %finish.1 = bf16[8,4096]{1,0:T(8,128)(2,1)} custom-call(f32[8,2048]{1,0:T(8,128)S(1)} %get-tuple-element.42._.keep_ref, f32[8,2048]{1,0:T(8,128)S(1)} %collective-permute-done.16.got_ref), custom_call_target="tpu_custom_call" | custom-call | bytes 262144 | tf_op jit(solution)/shard_map/finish/pallas_call | solution.py:151
  (46 shorter events, 0.5 us)
Async XLA Ops:
  0.6 12.0 %copy-start.1 = (bf16[1,1024,512]{2,1,0:T(8,128)(2,1)S(1)}, bf16[1,1024,512]{2,1,0:T(8,128)(2,1)}, u32[]{:S(2)}) copy-start(bf16[1,1024,512]{2,1,0:T(8,128)(2,1)} %param.10) | copy-start | bytes 3145732
  2.4 16.2 %collective-permute-start = (bf16[160,512]{1,0:T(8,128)(2,1)S(1)}, bf16[160,512]{1,0:T(8,128)(2,1)S(1)}, u32[]{:S(2)}, u32[]{:S(2)}) collective-permute-start(bf16[160,512]{1,0:T(8,128)(2,1)S(1)} %pad_maximum_fusion), channel_id=1, source_target_pairs={{0,8},{4,12},{8,0},{12,4},{1,9},{5,13},{9,1},{13,5},{2,10},{6,14},... | collective-permute-start | bytes 491528 | tf_op jit(solution)/shard_map/ppermute | solution.py:22
  6.5 12.1 %collective-permute-start.1 = (bf16[160,512]{1,0:T(8,128)(2,1)S(1)}, bf16[160,512]{1,0:T(8,128)(2,1)S(1)}, u32[]{:S(2)}, u32[]{:S(2)}) collective-permute-start(bf16[160,512]{1,0:T(8,128)(2,1)S(1)} %pad_maximum_fusion), channel_id=1, source_target_pairs={{0,12},{4,8},{8,4},{12,0},{1,13},{5,9},{9,5},{13,1},{2,14},{6,10},... | collective-permute-start | bytes 491528 | tf_op jit(solution)/shard_map/ppermute | solution.py:22
  7.9 11.3 %collective-permute-start.2 = (bf16[160,512]{1,0:T(8,128)(2,1)S(1)}, bf16[160,512]{1,0:T(8,128)(2,1)S(1)}, u32[]{:S(2)}, u32[]{:S(2)}) collective-permute-start(bf16[160,512]{1,0:T(8,128)(2,1)S(1)} %pad_maximum_fusion), channel_id=1, source_target_pairs={{0,4},{4,0},{8,12},{12,8},{1,5},{5,1},{9,13},{13,9},{2,6},{6,2},{1... | collective-permute-start | bytes 491528 | tf_op jit(solution)/shard_map/ppermute | solution.py:22
  8.2 14.1 %copy-start.3 = (bf16[128,512]{1,0:T(8,128)(2,1)S(1)}, bf16[128,512]{1,0:T(8,128)(2,1)}, u32[]{:S(2)}) copy-start(bf16[128,512]{1,0:T(8,128)(2,1)} %param.14) | copy-start | bytes 393220
  8.2 14.8 %copy-start.5 = (s32[1,32]{1,0:T(1,128)S(1)}, s32[1,32]{1,0:T(1,128)}, u32[]{:S(2)}) copy-start(s32[1,32]{1,0:T(1,128)} %param.12) | copy-start | bytes 388
  9.5 3.2 %copy-start.2 = (bf16[128,2048]{1,0:T(8,128)(2,1)S(1)}, bf16[128,2048]{1,0:T(8,128)(2,1)}, u32[]{:S(2)}) copy-start(bf16[128,2048]{1,0:T(8,128)(2,1)} %param.13) | copy-start | bytes 1572868
  9.5 20.0 %collective-permute-start.8 = (bf16[528,512]{1,0:T(8,128)(2,1)S(1)}, bf16[528,512]{1,0:T(8,128)(2,1)S(1)}, u32[]{:S(2)}, u32[]{:S(2)}) collective-permute-start(bf16[528,512]{1,0:T(8,128)(2,1)S(1)} %maximum_maximum_fusion.refs_0_), channel_id=1, source_target_pairs={{0,1},{1,0},{2,3},{3,2},{4,5},{5,4},{6,7},{7,6},{8,9},{9,8},{10,11... | collective-permute-start | bytes 1622024 | tf_op jit(solution)/shard_map/ppermute | solution.py:22
  11.1 21.1 %copy-start.4 = (f32[512]{0:T(512)S(1)}, f32[512]{0:T(512)}, u32[]{:S(2)}) copy-start(f32[512]{0:T(512)} %param.15) | copy-start | bytes 6148
  11.1 20.1 %collective-permute-start.9 = (bf16[528,512]{1,0:T(8,128)(2,1)S(1)}, bf16[528,512]{1,0:T(8,128)(2,1)S(1)}, u32[]{:S(2)}, u32[]{:S(2)}) collective-permute-start(bf16[528,512]{1,0:T(8,128)(2,1)S(1)} %maximum_maximum_fusion.refs_0_), channel_id=1, source_target_pairs={{0,2},{1,3},{2,0},{3,1},{4,6},{5,7},{6,4},{7,5},{8,10},{9,11},{10,... | collective-permute-start | bytes 1622024 | tf_op jit(solution)/shard_map/ppermute | solution.py:22
  12.6 30.5 %copy-start = (bf16[2048,2048]{1,0:T(8,128)(2,1)S(1)}, bf16[2048,2048]{1,0:T(8,128)(2,1)}, u32[]{:S(2)}) copy-start(bf16[2048,2048]{1,0:T(8,128)(2,1)} %refs_5_.1) | copy-start | bytes 25165828
  19.2 9.1 %collective-permute-start.3 = (bf16[3,160,256]{2,1,0:T(8,128)(2,1)S(1)}, bf16[3,160,256]{2,1,0:T(8,128)(2,1)S(1)}, u32[]{:S(2)}, u32[]{:S(2)}) collective-permute-start(bf16[3,160,256]{2,1,0:T(8,128)(2,1)S(1)} %get-tuple-element.24), channel_id=1, source_target_pairs={{0,1},{1,0},{2,3},{3,2},{4,5},{5,4},{6,7},{7,6},{8,9},{9,8},{10,11... | collective-permute-start | bytes 737288 | tf_op jit(solution)/shard_map/ppermute | solution.py:22
  20.8 8.7 %collective-permute-start.4 = (bf16[3,160,256]{2,1,0:T(8,128)(2,1)S(1)}, bf16[3,160,256]{2,1,0:T(8,128)(2,1)S(1)}, u32[]{:S(2)}, u32[]{:S(2)}) collective-permute-start(bf16[3,160,256]{2,1,0:T(8,128)(2,1)S(1)} %get-tuple-element.25), channel_id=1, source_target_pairs={{0,2},{1,3},{2,0},{3,1},{4,6},{5,7},{6,4},{7,5},{8,10},{9,11},{10,... | collective-permute-start | bytes 737288 | tf_op jit(solution)/shard_map/ppermute | solution.py:22
  22.3 9.7 %collective-permute-start.5 = (bf16[2,3,160,256]{3,2,1,0:T(8,128)(2,1)S(1)}, bf16[2,3,160,256]{3,2,1,0:T(8,128)(2,1)S(1)}, u32[]{:S(2)}, u32[]{:S(2)}) collective-permute-start(bf16[2,3,160,256]{3,2,1,0:T(8,128)(2,1)S(1)} %get-tuple-element.23.refs_4_), channel_id=1, source_target_pairs={{0,16},{16,0},{1,17},{17,1},{2,18},{18,2},{3,19},{19,3},{4,20},{20... | collective-permute-start | bytes 1474568 | tf_op jit(solution)/shard_map/ppermute | solution.py:22
  28.3 3.7 %collective-permute-start.6 = (bf16[3,160,256]{2,1,0:T(8,128)(2,1)S(1)}, bf16[3,160,256]{2,1,0:T(8,128)(2,1)S(1)}, u32[]{:S(2)}, u32[]{:S(2)}) collective-permute-start(bf16[3,160,256]{2,1,0:T(8,128)(2,1)S(1)} %collective-permute-done.3.refs_5_), channel_id=1, source_target_pairs={{0,16},{16,0},{1,17},{17,1},{2,18},{18,2},{3,19},{19,3},{4,20},{20... | collective-permute-start | bytes 737288 | tf_op jit(solution)/shard_map/ppermute | solution.py:22
  29.5 2.5 %collective-permute-start.7 = (bf16[3,160,256]{2,1,0:T(8,128)(2,1)S(1)}, bf16[3,160,256]{2,1,0:T(8,128)(2,1)S(1)}, u32[]{:S(2)}, u32[]{:S(2)}) collective-permute-start(bf16[3,160,256]{2,1,0:T(8,128)(2,1)S(1)} %collective-permute-done.4.refs_6_), channel_id=1, source_target_pairs={{0,16},{16,0},{1,17},{17,1},{2,18},{18,2},{3,19},{19,3},{4,20},{20... | collective-permute-start | bytes 737288 | tf_op jit(solution)/shard_map/ppermute | solution.py:22
  29.5 13.5 %collective-permute-start.10 = (bf16[256,512]{1,0:T(8,128)(2,1)S(1)}, bf16[256,512]{1,0:T(8,128)(2,1)S(1)}, u32[]{:S(2)}, u32[]{:S(2)}) collective-permute-start(bf16[256,512]{1,0:T(8,128)(2,1)S(1)} %slice.40), channel_id=1, source_target_pairs={{0,2},{1,3},{2,0},{3,1},{4,6},{5,7},{6,4},{7,5},{8,10},{9,11},{10,... | collective-permute-start | bytes 786440 | tf_op jit(solution)/shard_map/ppermute | solution.py:22
  31.1 11.9 %collective-permute-start.11 = (bf16[272,512]{1,0:T(8,128)(2,1)S(1)}, bf16[272,512]{1,0:T(8,128)(2,1)S(1)}, u32[]{:S(2)}, u32[]{:S(2)}) collective-permute-start(bf16[272,512]{1,0:T(8,128)(2,1)S(1)} %slice.41), channel_id=1, source_target_pairs={{0,1},{1,0},{2,3},{3,2},{4,5},{5,4},{6,7},{7,6},{8,9},{9,8},{10,11... | collective-permute-start | bytes 835592 | tf_op jit(solution)/shard_map/ppermute | solution.py:22
  32.1 14.7 %slice-start = ((s8[8388608]{0:T(1024)(128)(4,1)}), s8[4194304]{0:T(1024)(128)(4,1)S(1)}, s32[]{:S(2)}) async-start(s8[8388608]{0:T(1024)(128)(4,1)} %bitcast.13), calls=%async_computation.1 | async-start | bytes 8388608
  43.1 3.8 %slice-start.1 = ((s8[8388608]{0:T(1024)(128)(4,1)}), s8[4194304]{0:T(1024)(128)(4,1)S(1)}, s32[]{:S(2)}) async-start(s8[8388608]{0:T(1024)(128)(4,1)} %bitcast.13), calls=%async_computation.2 | async-start | bytes 8388608
  45.1 1.7 %collective-permute-start.12 = (bf16[64,2176]{1,0:T(8,128)(2,1)S(1)}, bf16[64,2176]{1,0:T(8,128)(2,1)S(1)}, u32[]{:S(2)}, u32[]{:S(2)}) collective-permute-start(bf16[64,2176]{1,0:T(8,128)(2,1)S(1)} %get-tuple-element.36), channel_id=1, source_target_pairs={{0,16},{16,0},{1,17},{17,1},{2,18},{18,2},{3,19},{19,3},{4,20},{20... | collective-permute-start | bytes 835592 | tf_op jit(solution)/shard_map/ppermute | solution.py:22
  48.7 6.4 %collective-permute-start.13 = (bf16[16,2048]{1,0:T(8,128)(2,1)S(1)}, bf16[16,2048]{1,0:T(8,128)(2,1)S(1)}, u32[]{:S(2)}, u32[]{:S(2)}) collective-permute-start(bf16[16,2048]{1,0:T(8,128)(2,1)S(1)} %get-tuple-element.39), channel_id=1, source_target_pairs={{0,1},{1,0},{2,3},{3,2},{4,5},{5,4},{6,7},{7,6},{8,9},{9,8},{10,11... | collective-permute-start | bytes 196616 | tf_op jit(solution)/shard_map/ppermute | solution.py:22
  49.4 5.8 %collective-permute-start.14 = (bf16[16,2048]{1,0:T(8,128)(2,1)S(1)}, bf16[16,2048]{1,0:T(8,128)(2,1)S(1)}, u32[]{:S(2)}, u32[]{:S(2)}) collective-permute-start(bf16[16,2048]{1,0:T(8,128)(2,1)S(1)} %get-tuple-element.40), channel_id=1, source_target_pairs={{0,2},{1,3},{2,0},{3,1},{4,6},{5,7},{6,4},{7,5},{8,10},{9,11},{10,... | collective-permute-start | bytes 196616 | tf_op jit(solution)/shard_map/ppermute | solution.py:22
  49.9 5.3 %collective-permute-start.15 = (bf16[16,2048]{1,0:T(8,128)(2,1)S(1)}, bf16[16,2048]{1,0:T(8,128)(2,1)S(1)}, u32[]{:S(2)}, u32[]{:S(2)}) collective-permute-start(bf16[16,2048]{1,0:T(8,128)(2,1)S(1)} %get-tuple-element.41), channel_id=1, source_target_pairs={{0,3},{1,2},{2,1},{3,0},{4,7},{5,6},{6,5},{7,4},{8,11},{9,10},{10,... | collective-permute-start | bytes 196616 | tf_op jit(solution)/shard_map/ppermute | solution.py:22
  55.2 1.3 %collective-permute-start.16 = (f32[8,2048]{1,0:T(8,128)S(1)}, f32[8,2048]{1,0:T(8,128)S(1)}, u32[]{:S(2)}, u32[]{:S(2)}) collective-permute-start(f32[8,2048]{1,0:T(8,128)S(1)} %get-tuple-element.43), channel_id=1, source_target_pairs={{0,16},{16,0},{1,17},{17,1},{2,18},{18,2},{3,19},{19,3},{4,20},{20... | collective-permute-start | bytes 196616 | tf_op jit(solution)/shard_map/ppermute | solution.py:22

commit v13 on v12

--- a/solution.py
+++ b/solution.py
@@ -12,6 +12,7 @@
 MICRO = 4
 SESS_MAX = 64
 EPSILON = 1e-06
+STEP = 256
 F32 = jnp.float32
 BF16 = jnp.bfloat16
 
@@ -40,7 +41,7 @@
 
 def project(dps, row0, hist, ev_ref, w_ref, gate_ref, q_ref, kv_ref):
     rows, width = ev_ref.shape
-    step = min(rows, 512)
+    step = min(rows, STEP)
     for r in range(0, rows, step):
         at = slice(r, r + step)
         x = in_order(ev_ref, at, dps)
@@ -54,9 +55,6 @@
         kv_ref[at, :width] = jnp.where(row_pos < hist, act(1), 0.0).astype(BF16)
         q_ref[at, :] = act(2).astype(BF16)
         kv_ref[at, width:] = act(3).astype(BF16)
-
-
-STEP = 256
 
 
 def attend(q_ref, kv_refs, att_ref):
@@ -392,7 +390,7 @@
         rows * units,
     )
 
-    got = [swap(x, "mp", mps, k + 1) for k, x in enumerate(sends)]
+    got = [swap(sends[k - 1], "mp", mps, k) for k in range(mps - 1, 0, -1)]
     (sums_g,) = call(
         functools.partial(attend_kernel, first),
         "attend_rest",

time: 57.4 us -> 57.4 us (level)
  no operation moved by 1% of the time
where the time goes in v13:
time: 57.4 us; the launch traced here: 57.2 us
  starting transfers between devices  18.2 us (32%)
  Pallas kernels  13.4 us (23%)
  waiting for transfers between devices  13.2 us (23%)
  blocking collectives  7.3 us (13%)
  local copies, waits for them, and re-layouts  2.11 us (4%)
  between operations  1.54 us (3%)
  other arithmetic  1.41 us (2%)
    ppermute x17, starting transfers between devices, swap(): return lax.ppermute(x, axis, [(i, i ^ flip) for i in range(size)])  18.2 us
    pallas_call x9, Pallas kernels, call(): pl.pallas_call(kernel, in_specs=[VMEM] * len(operands), out_specs=[VMEM]...  13.4 us
    ppermute x17, waiting for transfers between devices, swap(): return lax.ppermute(x, axis, [(i, i ^ flip) for i in range(size)])  13.2 us
    all_to_all x1, blocking collectives, per_device(): lax.all_to_all(micro_rows.reshape(peers, take, width), group, split_axis=...  7.3 us
    concatenate x1, other arithmetic, gather_weights(): jnp.concatenate([w_in, ffn_gain, jnp.zeros((15, w_in.shape[1]), BF16)], a...  1.27 us
  transfers between devices with their start and end apart: 17, of which 5 were waited for; matrix products, arithmetic and copies ran while one was open for 3% of the time, Pallas kernels for 16%

profile of v13, /device:TPU:0, one launch (start us, length us, event | category | flops | bytes accessed | tf_op | source)
XLA Modules:
  0.0 57.2 jit_solution(13274390737176955955)
XLA Ops:
  0.7 0.8 %constant_dynamic-slice_fusion = bf16[32,512]{1,0:T(8,128)(2,1)S(1)} fusion(bf16[128,512]{1,0:T(8,128)(2,1)} %param.14, s32[]{:T(128)S(6)} %select_n.12), kind=kLoop, calls=%fused_computation.9 | loop fusion | bytes 65540 | tf_op jit(solution)/shard_map/dynamic_slice | solution.py:196
  1.5 0.9 %constant_dynamic-slice_fusion.1 = bf16[128,512]{1,0:T(8,128)(2,1)S(1)} fusion(bf16[128,2048]{1,0:T(8,128)(2,1)} %param.13, s32[]{:T(128)S(6)} %select_n.11), kind=kLoop, calls=%fused_computation.10 | loop fusion | bytes 262148 | tf_op jit(solution)/shard_map/dynamic_slice | solution.py:195
  2.4 4.1 %collective-permute-start = (bf16[160,512]{1,0:T(8,128)(2,1)S(1)}, bf16[160,512]{1,0:T(8,128)(2,1)S(1)}, u32[]{:S(2)}, u32[]{:S(2)}) collective-permute-start(bf16[160,512]{1,0:T(8,128)(2,1)S(1)} %pad_maximum_fusion), channel_id=1, source_target_pairs={{0,8},{4,12},{8,0},{12,4},{1,9},{5,13},{9,1},{13,5},{2,10},{6,14},... | collective-permute-start | bytes 491528 | tf_op jit(solution)/shard_map/ppermute | solution.py:23
  6.5 1.3 %collective-permute-start.1 = (bf16[160,512]{1,0:T(8,128)(2,1)S(1)}, bf16[160,512]{1,0:T(8,128)(2,1)S(1)}, u32[]{:S(2)}, u32[]{:S(2)}) collective-permute-start(bf16[160,512]{1,0:T(8,128)(2,1)S(1)} %pad_maximum_fusion), channel_id=1, source_target_pairs={{0,12},{4,8},{8,4},{12,0},{1,13},{5,9},{9,5},{13,1},{2,14},{6,10},... | collective-permute-start | bytes 491528 | tf_op jit(solution)/shard_map/ppermute | solution.py:23
  7.9 0.2 collective-permute-start.2
  8.1 0.1 pad.2.clone
  8.2 1.3 %maximum_maximum_fusion.refs_0_ = bf16[528,512]{1,0:T(8,128)(2,1)S(1)} fusion(bf16[1,512]{1,0:T(2,128)(2,1)} %param.17, bf16[512,512]{1,0:T(8,128)(2,1)} %param.16, bf16[528]{0:T(1024)(128)(2,1)S(1)} %pad.2.clone), kind=kLoop, calls=%fused_computation | loop fusion | flops 1622016 | bytes 1067040 | tf_op jit(solution)/shard_map/concatenate | solution.py:178
  9.5 1.6 %collective-permute-start.8 = (bf16[528,512]{1,0:T(8,128)(2,1)S(1)}, bf16[528,512]{1,0:T(8,128)(2,1)S(1)}, u32[]{:S(2)}, u32[]{:S(2)}) collective-permute-start(bf16[528,512]{1,0:T(8,128)(2,1)S(1)} %maximum_maximum_fusion.refs_0_), channel_id=1, source_target_pairs={{0,1},{1,0},{2,3},{3,2},{4,5},{5,4},{6,7},{7,6},{8,9},{9,8},{10,11... | collective-permute-start | bytes 1622024 | tf_op jit(solution)/shard_map/ppermute | solution.py:23
  11.1 1.5 %collective-permute-start.9 = (bf16[528,512]{1,0:T(8,128)(2,1)S(1)}, bf16[528,512]{1,0:T(8,128)(2,1)S(1)}, u32[]{:S(2)}, u32[]{:S(2)}) collective-permute-start(bf16[528,512]{1,0:T(8,128)(2,1)S(1)} %maximum_maximum_fusion.refs_0_), channel_id=1, source_target_pairs={{0,2},{1,3},{2,0},{3,1},{4,6},{5,7},{6,4},{7,5},{8,10},{9,11},{10,... | collective-permute-start | bytes 1622024 | tf_op jit(solution)/shard_map/ppermute | solution.py:23
  12.7 5.9 %collective-permute-done.refs_0_ = bf16[160,512]{1,0:T(8,128)(2,1)S(1)} collective-permute-done((bf16[160,512]{1,0:T(8,128)(2,1)S(1)}, bf16[160,512]{1,0:T(8,128)(2,1)S(1)}, u32[]{:S(2)}, u32[]{:S(2)}) %collective-permute-start) | collective-permute-done | bytes 163872 | tf_op jit(solution)/shard_map/ppermute | solution.py:23
  18.6 0.5 collective-permute-done.2.refs_2_
  19.2 1.6 %collective-permute-start.3 = (bf16[3,160,256]{2,1,0:T(8,128)(2,1)S(1)}, bf16[3,160,256]{2,1,0:T(8,128)(2,1)S(1)}, u32[]{:S(2)}, u32[]{:S(2)}) collective-permute-start(bf16[3,160,256]{2,1,0:T(8,128)(2,1)S(1)} %get-tuple-element.24), channel_id=1, source_target_pairs={{0,1},{1,0},{2,3},{3,2},{4,5},{5,4},{6,7},{7,6},{8,9},{9,8},{10,11... | collective-permute-start | bytes 737288 | tf_op jit(solution)/shard_map/ppermute | solution.py:23
  20.8 1.5 %collective-permute-start.4 = (bf16[3,160,256]{2,1,0:T(8,128)(2,1)S(1)}, bf16[3,160,256]{2,1,0:T(8,128)(2,1)S(1)}, u32[]{:S(2)}, u32[]{:S(2)}) collective-permute-start(bf16[3,160,256]{2,1,0:T(8,128)(2,1)S(1)} %get-tuple-element.25), channel_id=1, source_target_pairs={{0,2},{1,3},{2,0},{3,1},{4,6},{5,7},{6,4},{7,5},{8,10},{9,11},{10,... | collective-permute-start | bytes 737288 | tf_op jit(solution)/shard_map/ppermute | solution.py:23
  23.0 0.1 select_reduce_fusion
  23.1 5.1 %collective-permute-done.3.refs_5_ = bf16[3,160,256]{2,1,0:T(8,128)(2,1)S(1)} collective-permute-done((bf16[3,160,256]{2,1,0:T(8,128)(2,1)S(1)}, bf16[3,160,256]{2,1,0:T(8,128)(2,1)S(1)}, u32[]{:S(2)}, u32[]{:S(2)}) %collective-permute-start.3) | collective-permute-done | bytes 245792 | tf_op jit(solution)/shard_map/ppermute | solution.py:23
  28.3 1.2 %collective-permute-done.4.refs_6_ = bf16[3,160,256]{2,1,0:T(8,128)(2,1)S(1)} collective-permute-done((bf16[3,160,256]{2,1,0:T(8,128)(2,1)S(1)}, bf16[3,160,256]{2,1,0:T(8,128)(2,1)S(1)}, u32[]{:S(2)}, u32[]{:S(2)}) %collective-permute-start.4) | collective-permute-done | bytes 245792 | tf_op jit(solution)/shard_map/ppermute | solution.py:23
  29.5 1.6 %collective-permute-start.10 = (bf16[256,512]{1,0:T(8,128)(2,1)S(1)}, bf16[256,512]{1,0:T(8,128)(2,1)S(1)}, u32[]{:S(2)}, u32[]{:S(2)}) collective-permute-start(bf16[256,512]{1,0:T(8,128)(2,1)S(1)} %slice.40), channel_id=1, source_target_pairs={{0,2},{1,3},{2,0},{3,1},{4,6},{5,7},{6,4},{7,5},{8,10},{9,11},{10,... | collective-permute-start | bytes 786440 | tf_op jit(solution)/shard_map/ppermute | solution.py:23
  31.1 0.8 %collective-permute-start.11 = (bf16[272,512]{1,0:T(8,128)(2,1)S(1)}, bf16[272,512]{1,0:T(8,128)(2,1)S(1)}, u32[]{:S(2)}, u32[]{:S(2)}) collective-permute-start(bf16[272,512]{1,0:T(8,128)(2,1)S(1)} %slice.41), channel_id=1, source_target_pairs={{0,1},{1,0},{2,3},{3,2},{4,5},{5,4},{6,7},{7,6},{8,9},{9,8},{10,11... | collective-permute-start | bytes 835592 | tf_op jit(solution)/shard_map/ppermute | solution.py:23
  32.0 0.1 broadcast_in_dim.29.bounds_ref
  32.1 3.5 %encode_first.1 = (bf16[64,512]{1,0:T(8,128)(2,1)S(1)}, bf16[512,2048]{1,0:T(8,128)(2,1)S(1)}, bf16[512,512]{1,0:T(8,128)(2,1)S(1)}, bf16[512,1024]{1,0:T(8,128)...) custom-call(f32[3,32,128]{2,1,0:T(8,128)S(1)} %broadcast_in_dim.29.bounds_ref, ...), custom_call_target="tpu_custom_call" | custom-call | flops 1342177280 | bytes 6291456 | tf_op jit(solution)/shard_map/encode_first/pallas_call | solution.py:149
  35.7 7.3 %all_to_all.5 = bf16[8,8,512]{2,1,0:T(8,128)(2,1)S(1)} all-to-all(bf16[8,8,512]{2,1,0:T(8,128)(2,1)S(1)} %bitcast.16), channel_id=1, replica_groups=mesh['section'=2,'dp'=4,'mp'=4] {'section','mp'}, dimensions={0} | all-to-all | bytes 131072 | tf_op jit(solution)/shard_map/all_to_all | solution.py:354
  43.0 2.0 %up_half.1 = (f32[64,512]{1,0:T(8,128)S(1)}, f32[64,2176]{1,0:T(8,128)S(1)}, bf16[64,2176]{1,0:T(8,128)(2,1)S(1)}) custom-call(bf16[64,512]{1,0:T(8,128)(2,1)S(1)} %bitcast.15, bf16[528,512]{1,0:T(8,128)(2,1)S(1)} %maximum_maximum_fusion.refs_0_, bf16[528,512]{1,0:T(8,128)(2,1)S(1)} %collective-permute-done.8.refs_1_, ...), custom_call_target="tpu_custom_call" | custom-call | flops 536870912 | bytes 8388608 | tf_op jit(solution)/shard_map/up_half/pallas_call | solution.py:149
  45.1 0.2 collective-permute-start.12
  45.2 1.6 %project_rest.1 = (bf16[512,1024]{1,0:T(8,128)(2,1)S(1)}, bf16[512,1024]{1,0:T(8,128)(2,1)S(1)}, f32[32,512]{1,0:T(8,128)S(1)}) custom-call(f32[3,32,128]{2,1,0:T(8,128)S(1)} %broadcast_in_dim.29.bounds_ref, bf16[512,512]{1,0:T(8,128)(2,1)S(1)} %get-tuple-element.45.ev_ref, bf16[512,2048]{1,0:T(8,128)(2,1)S(1)} %get-tuple-element.26.w_ref, ...), custom_call_target="tpu_custom_call" | custom-call | flops 1073741824 | bytes 6291456 | tf_op jit(solution)/shard_map/project_rest/pallas_call | solution.py:149
  46.8 1.8 %down_part.1 = (f32[16,2048]{1,0:T(8,128)S(1)}, bf16[16,2048]{1,0:T(8,128)(2,1)S(1)}, bf16[16,2048]{1,0:T(8,128)(2,1)S(1)}, bf16[16,2048]{1,0:T(8,128)(2,1)S(1)}) custom-call(f32[64,2176]{1,0:T(8,128)S(1)} %get-tuple-element.35.half_ref, bf16[64,2176]{1,0:T(8,128)(2,1)S(1)} %collective-permute-done.12.other_ref, ...), custom_call_target="tpu_custom_call" | custom-call | flops 536870912 | bytes 8388608 | tf_op jit(solution)/shard_map/down_part/pallas_call | solution.py:149
  48.7 0.6 %collective-permute-start.13 = (bf16[16,2048]{1,0:T(8,128)(2,1)S(1)}, bf16[16,2048]{1,0:T(8,128)(2,1)S(1)}, u32[]{:S(2)}, u32[]{:S(2)}) collective-permute-start(bf16[16,2048]{1,0:T(8,128)(2,1)S(1)} %get-tuple-element.39), channel_id=1, source_target_pairs={{0,3},{1,2},{2,1},{3,0},{4,7},{5,6},{6,5},{7,4},{8,11},{9,10},{10,... | collective-permute-start | bytes 196616 | tf_op jit(solution)/shard_map/ppermute | solution.py:23
  49.3 1.5 %collective-permute-start.14 = (bf16[16,2048]{1,0:T(8,128)(2,1)S(1)}, bf16[16,2048]{1,0:T(8,128)(2,1)S(1)}, u32[]{:S(2)}, u32[]{:S(2)}) collective-permute-start(bf16[16,2048]{1,0:T(8,128)(2,1)S(1)} %get-tuple-element.40), channel_id=1, source_target_pairs={{0,2},{1,3},{2,0},{3,1},{4,6},{5,7},{6,4},{7,5},{8,10},{9,11},{10,... | collective-permute-start | bytes 196616 | tf_op jit(solution)/shard_map/ppermute | solution.py:23
  50.7 1.5 %collective-permute-start.15 = (bf16[16,2048]{1,0:T(8,128)(2,1)S(1)}, bf16[16,2048]{1,0:T(8,128)(2,1)S(1)}, u32[]{:S(2)}, u32[]{:S(2)}) collective-permute-start(bf16[16,2048]{1,0:T(8,128)(2,1)S(1)} %get-tuple-element.41), channel_id=1, source_target_pairs={{0,1},{1,0},{2,3},{3,2},{4,5},{5,4},{6,7},{7,6},{8,9},{9,8},{10,11... | collective-permute-start | bytes 196616 | tf_op jit(solution)/shard_map/ppermute | solution.py:23
  52.2 2.9 %attend_rest.1.refs_3_.sums_ref = f32[32,512]{1,0:T(8,128)S(1)} custom-call(f32[3,32,128]{2,1,0:T(8,128)S(1)} %broadcast_in_dim.29.bounds_ref, f32[8,512]{1,0:T(8,128)S(1)} %broadcast_in_dim.30.gain_ref, bf16[512,1024]{1,0:T(8,128)(2,1)S(1)} %get-tuple-element.31.qg_ref, bf16[512,1024]{1,0:T(8,128)(2,1)S(1)} %get-tuple-element.32.kv_first, ...), custom_call_target="tpu_custom_call" | custom-call | flops 1073741824 | bytes 4194304 | tf_op jit(solution)/shard_map/attend_rest/pallas_call | solution.py:149
  55.3 0.8 %pool_rows.1 = bf16[32,512]{1,0:T(8,128)(2,1)} custom-call(f32[3,32,128]{2,1,0:T(8,128)S(1)} %broadcast_in_dim.29.bounds_ref, f32[32,512]{1,0:T(8,128)S(1)} %get-tuple-element.30._.sums_ev_ref, f32[32,512]{1,0:T(8,128)S(1)} %attend_rest.1.refs_3_.sums_ref, bf16[512,512]{1,0:T(8,128)(2,1)S(1)} %get-tuple-element.38.wout_ref, ...), custom_call_target="tpu_custom_call" | custom-call | flops 50331648 | bytes 1048576 | tf_op jit(solution)/shard_map/pool_rows/pallas_call | solution.py:149
  56.1 0.4 collective-permute-done.16.got_ref
  56.5 0.6 %finish.1 = bf16[8,4096]{1,0:T(8,128)(2,1)} custom-call(f32[8,2048]{1,0:T(8,128)S(1)} %get-tuple-element.42._.keep_ref, f32[8,2048]{1,0:T(8,128)S(1)} %collective-permute-done.16.got_ref), custom_call_target="tpu_custom_call" | custom-call | bytes 262144 | tf_op jit(solution)/shard_map/finish/pallas_call | solution.py:149
  (46 shorter events, 0.5 us)
Async XLA Ops:
  0.6 12.0 %copy-start.1 = (bf16[1,1024,512]{2,1,0:T(8,128)(2,1)S(1)}, bf16[1,1024,512]{2,1,0:T(8,128)(2,1)}, u32[]{:S(2)}) copy-start(bf16[1,1024,512]{2,1,0:T(8,128)(2,1)} %param.10) | copy-start | bytes 3145732
  2.4 16.2 %collective-permute-start = (bf16[160,512]{1,0:T(8,128)(2,1)S(1)}, bf16[160,512]{1,0:T(8,128)(2,1)S(1)}, u32[]{:S(2)}, u32[]{:S(2)}) collective-permute-start(bf16[160,512]{1,0:T(8,128)(2,1)S(1)} %pad_maximum_fusion), channel_id=1, source_target_pairs={{0,8},{4,12},{8,0},{12,4},{1,9},{5,13},{9,1},{13,5},{2,10},{6,14},... | collective-permute-start | bytes 491528 | tf_op jit(solution)/shard_map/ppermute | solution.py:23
  6.5 12.1 %collective-permute-start.1 = (bf16[160,512]{1,0:T(8,128)(2,1)S(1)}, bf16[160,512]{1,0:T(8,128)(2,1)S(1)}, u32[]{:S(2)}, u32[]{:S(2)}) collective-permute-start(bf16[160,512]{1,0:T(8,128)(2,1)S(1)} %pad_maximum_fusion), channel_id=1, source_target_pairs={{0,12},{4,8},{8,4},{12,0},{1,13},{5,9},{9,5},{13,1},{2,14},{6,10},... | collective-permute-start | bytes 491528 | tf_op jit(solution)/shard_map/ppermute | solution.py:23
  7.9 11.3 %collective-permute-start.2 = (bf16[160,512]{1,0:T(8,128)(2,1)S(1)}, bf16[160,512]{1,0:T(8,128)(2,1)S(1)}, u32[]{:S(2)}, u32[]{:S(2)}) collective-permute-start(bf16[160,512]{1,0:T(8,128)(2,1)S(1)} %pad_maximum_fusion), channel_id=1, source_target_pairs={{0,4},{4,0},{8,12},{12,8},{1,5},{5,1},{9,13},{13,9},{2,6},{6,2},{1... | collective-permute-start | bytes 491528 | tf_op jit(solution)/shard_map/ppermute | solution.py:23
  8.2 14.1 %copy-start.3 = (bf16[128,512]{1,0:T(8,128)(2,1)S(1)}, bf16[128,512]{1,0:T(8,128)(2,1)}, u32[]{:S(2)}) copy-start(bf16[128,512]{1,0:T(8,128)(2,1)} %param.14) | copy-start | bytes 393220
  8.2 14.8 %copy-start.5 = (s32[1,32]{1,0:T(1,128)S(1)}, s32[1,32]{1,0:T(1,128)}, u32[]{:S(2)}) copy-start(s32[1,32]{1,0:T(1,128)} %param.12) | copy-start | bytes 388
  9.5 3.2 %copy-start.2 = (bf16[128,2048]{1,0:T(8,128)(2,1)S(1)}, bf16[128,2048]{1,0:T(8,128)(2,1)}, u32[]{:S(2)}) copy-start(bf16[128,2048]{1,0:T(8,128)(2,1)} %param.13) | copy-start | bytes 1572868
  9.5 20.0 %collective-permute-start.8 = (bf16[528,512]{1,0:T(8,128)(2,1)S(1)}, bf16[528,512]{1,0:T(8,128)(2,1)S(1)}, u32[]{:S(2)}, u32[]{:S(2)}) collective-permute-start(bf16[528,512]{1,0:T(8,128)(2,1)S(1)} %maximum_maximum_fusion.refs_0_), channel_id=1, source_target_pairs={{0,1},{1,0},{2,3},{3,2},{4,5},{5,4},{6,7},{7,6},{8,9},{9,8},{10,11... | collective-permute-start | bytes 1622024 | tf_op jit(solution)/shard_map/ppermute | solution.py:23
  11.1 21.1 %copy-start.4 = (f32[512]{0:T(512)S(1)}, f32[512]{0:T(512)}, u32[]{:S(2)}) copy-start(f32[512]{0:T(512)} %param.15) | copy-start | bytes 6148
  11.1 20.1 %collective-permute-start.9 = (bf16[528,512]{1,0:T(8,128)(2,1)S(1)}, bf16[528,512]{1,0:T(8,128)(2,1)S(1)}, u32[]{:S(2)}, u32[]{:S(2)}) collective-permute-start(bf16[528,512]{1,0:T(8,128)(2,1)S(1)} %maximum_maximum_fusion.refs_0_), channel_id=1, source_target_pairs={{0,2},{1,3},{2,0},{3,1},{4,6},{5,7},{6,4},{7,5},{8,10},{9,11},{10,... | collective-permute-start | bytes 1622024 | tf_op jit(solution)/shard_map/ppermute | solution.py:23
  12.6 30.4 %copy-start = (bf16[2048,2048]{1,0:T(8,128)(2,1)S(1)}, bf16[2048,2048]{1,0:T(8,128)(2,1)}, u32[]{:S(2)}) copy-start(bf16[2048,2048]{1,0:T(8,128)(2,1)} %refs_5_.1) | copy-start | bytes 25165828
  19.2 9.1 %collective-permute-start.3 = (bf16[3,160,256]{2,1,0:T(8,128)(2,1)S(1)}, bf16[3,160,256]{2,1,0:T(8,128)(2,1)S(1)}, u32[]{:S(2)}, u32[]{:S(2)}) collective-permute-start(bf16[3,160,256]{2,1,0:T(8,128)(2,1)S(1)} %get-tuple-element.24), channel_id=1, source_target_pairs={{0,1},{1,0},{2,3},{3,2},{4,5},{5,4},{6,7},{7,6},{8,9},{9,8},{10,11... | collective-permute-start | bytes 737288 | tf_op jit(solution)/shard_map/ppermute | solution.py:23
  20.8 8.7 %collective-permute-start.4 = (bf16[3,160,256]{2,1,0:T(8,128)(2,1)S(1)}, bf16[3,160,256]{2,1,0:T(8,128)(2,1)S(1)}, u32[]{:S(2)}, u32[]{:S(2)}) collective-permute-start(bf16[3,160,256]{2,1,0:T(8,128)(2,1)S(1)} %get-tuple-element.25), channel_id=1, source_target_pairs={{0,2},{1,3},{2,0},{3,1},{4,6},{5,7},{6,4},{7,5},{8,10},{9,11},{10,... | collective-permute-start | bytes 737288 | tf_op jit(solution)/shard_map/ppermute | solution.py:23
  22.3 9.7 %collective-permute-start.5 = (bf16[2,3,160,256]{3,2,1,0:T(8,128)(2,1)S(1)}, bf16[2,3,160,256]{3,2,1,0:T(8,128)(2,1)S(1)}, u32[]{:S(2)}, u32[]{:S(2)}) collective-permute-start(bf16[2,3,160,256]{3,2,1,0:T(8,128)(2,1)S(1)} %get-tuple-element.23.refs_4_), channel_id=1, source_target_pairs={{0,16},{16,0},{1,17},{17,1},{2,18},{18,2},{3,19},{19,3},{4,20},{20... | collective-permute-start | bytes 1474568 | tf_op jit(solution)/shard_map/ppermute | solution.py:23
  28.3 3.7 %collective-permute-start.6 = (bf16[3,160,256]{2,1,0:T(8,128)(2,1)S(1)}, bf16[3,160,256]{2,1,0:T(8,128)(2,1)S(1)}, u32[]{:S(2)}, u32[]{:S(2)}) collective-permute-start(bf16[3,160,256]{2,1,0:T(8,128)(2,1)S(1)} %collective-permute-done.3.refs_5_), channel_id=1, source_target_pairs={{0,16},{16,0},{1,17},{17,1},{2,18},{18,2},{3,19},{19,3},{4,20},{20... | collective-permute-start | bytes 737288 | tf_op jit(solution)/shard_map/ppermute | solution.py:23
  29.5 2.5 %collective-permute-start.7 = (bf16[3,160,256]{2,1,0:T(8,128)(2,1)S(1)}, bf16[3,160,256]{2,1,0:T(8,128)(2,1)S(1)}, u32[]{:S(2)}, u32[]{:S(2)}) collective-permute-start(bf16[3,160,256]{2,1,0:T(8,128)(2,1)S(1)} %collective-permute-done.4.refs_6_), channel_id=1, source_target_pairs={{0,16},{16,0},{1,17},{17,1},{2,18},{18,2},{3,19},{19,3},{4,20},{20... | collective-permute-start | bytes 737288 | tf_op jit(solution)/shard_map/ppermute | solution.py:23
  29.5 13.5 %collective-permute-start.10 = (bf16[256,512]{1,0:T(8,128)(2,1)S(1)}, bf16[256,512]{1,0:T(8,128)(2,1)S(1)}, u32[]{:S(2)}, u32[]{:S(2)}) collective-permute-start(bf16[256,512]{1,0:T(8,128)(2,1)S(1)} %slice.40), channel_id=1, source_target_pairs={{0,2},{1,3},{2,0},{3,1},{4,6},{5,7},{6,4},{7,5},{8,10},{9,11},{10,... | collective-permute-start | bytes 786440 | tf_op jit(solution)/shard_map/ppermute | solution.py:23
  31.1 11.8 %collective-permute-start.11 = (bf16[272,512]{1,0:T(8,128)(2,1)S(1)}, bf16[272,512]{1,0:T(8,128)(2,1)S(1)}, u32[]{:S(2)}, u32[]{:S(2)}) collective-permute-start(bf16[272,512]{1,0:T(8,128)(2,1)S(1)} %slice.41), channel_id=1, source_target_pairs={{0,1},{1,0},{2,3},{3,2},{4,5},{5,4},{6,7},{7,6},{8,9},{9,8},{10,11... | collective-permute-start | bytes 835592 | tf_op jit(solution)/shard_map/ppermute | solution.py:23
  32.1 14.7 %slice-start = ((s8[8388608]{0:T(1024)(128)(4,1)}), s8[4194304]{0:T(1024)(128)(4,1)S(1)}, s32[]{:S(2)}) async-start(s8[8388608]{0:T(1024)(128)(4,1)} %bitcast.13), calls=%async_computation.1 | async-start | bytes 8388608
  43.0 3.8 %slice-start.1 = ((s8[8388608]{0:T(1024)(128)(4,1)}), s8[4194304]{0:T(1024)(128)(4,1)S(1)}, s32[]{:S(2)}) async-start(s8[8388608]{0:T(1024)(128)(4,1)} %bitcast.13), calls=%async_computation.2 | async-start | bytes 8388608
  45.1 1.8 %collective-permute-start.12 = (bf16[64,2176]{1,0:T(8,128)(2,1)S(1)}, bf16[64,2176]{1,0:T(8,128)(2,1)S(1)}, u32[]{:S(2)}, u32[]{:S(2)}) collective-permute-start(bf16[64,2176]{1,0:T(8,128)(2,1)S(1)} %get-tuple-element.36), channel_id=1, source_target_pairs={{0,16},{16,0},{1,17},{17,1},{2,18},{18,2},{3,19},{19,3},{4,20},{20... | collective-permute-start | bytes 835592 | tf_op jit(solution)/shard_map/ppermute | solution.py:23
  48.7 6.5 %collective-permute-start.13 = (bf16[16,2048]{1,0:T(8,128)(2,1)S(1)}, bf16[16,2048]{1,0:T(8,128)(2,1)S(1)}, u32[]{:S(2)}, u32[]{:S(2)}) collective-permute-start(bf16[16,2048]{1,0:T(8,128)(2,1)S(1)} %get-tuple-element.39), channel_id=1, source_target_pairs={{0,3},{1,2},{2,1},{3,0},{4,7},{5,6},{6,5},{7,4},{8,11},{9,10},{10,... | collective-permute-start | bytes 196616 | tf_op jit(solution)/shard_map/ppermute | solution.py:23
  49.3 5.9 %collective-permute-start.14 = (bf16[16,2048]{1,0:T(8,128)(2,1)S(1)}, bf16[16,2048]{1,0:T(8,128)(2,1)S(1)}, u32[]{:S(2)}, u32[]{:S(2)}) collective-permute-start(bf16[16,2048]{1,0:T(8,128)(2,1)S(1)} %get-tuple-element.40), channel_id=1, source_target_pairs={{0,2},{1,3},{2,0},{3,1},{4,6},{5,7},{6,4},{7,5},{8,10},{9,11},{10,... | collective-permute-start | bytes 196616 | tf_op jit(solution)/shard_map/ppermute | solution.py:23
  50.7 4.4 %collective-permute-start.15 = (bf16[16,2048]{1,0:T(8,128)(2,1)S(1)}, bf16[16,2048]{1,0:T(8,128)(2,1)S(1)}, u32[]{:S(2)}, u32[]{:S(2)}) collective-permute-start(bf16[16,2048]{1,0:T(8,128)(2,1)S(1)} %get-tuple-element.41), channel_id=1, source_target_pairs={{0,1},{1,0},{2,3},{3,2},{4,5},{5,4},{6,7},{7,6},{8,9},{9,8},{10,11... | collective-permute-start | bytes 196616 | tf_op jit(solution)/shard_map/ppermute | solution.py:23
  55.2 1.3 %collective-permute-start.16 = (f32[8,2048]{1,0:T(8,128)S(1)}, f32[8,2048]{1,0:T(8,128)S(1)}, u32[]{:S(2)}, u32[]{:S(2)}) collective-permute-start(f32[8,2048]{1,0:T(8,128)S(1)} %get-tuple-element.43), channel_id=1, source_target_pairs={{0,16},{16,0},{1,17},{17,1},{2,18},{18,2},{3,19},{19,3},{4,20},{20... | collective-permute-start | bytes 196616 | tf_op jit(solution)/shard_map/ppermute | solution.py:23

commit v14 on v13

--- a/solution.py
+++ b/solution.py
@@ -356,7 +356,7 @@
     ).reshape(rows, width)
     blocks = [piece for block in w_in_blocks for piece in block]
     local, half, half_send = call(
-        functools.partial(up_kernel, 4, [len(block) for block in w_in_blocks]),
+        functools.partial(up_kernel, 1, [len(block) for block in w_in_blocks]),
         "up_half",
         [arrived, *blocks, w_up],
         [((rows, cols), F32), ((rows, units + 128), F32), ((rows, units + 128), BF16)],

time: 57.4 us -> 57.4 us (level)
  no operation moved by 1% of the time
where the time goes in v14:
time: 57.4 us; the launch traced here: 57.2 us
  starting transfers between devices  18.2 us (32%)
  Pallas kernels  13.4 us (23%)
  waiting for transfers between devices  13.2 us (23%)
  blocking collectives  7.3 us (13%)
  local copies, waits for them, and re-layouts  2.11 us (4%)
  between operations  1.54 us (3%)
  other arithmetic  1.41 us (2%)
    ppermute x17, starting transfers between devices, swap(): return lax.ppermute(x, axis, [(i, i ^ flip) for i in range(size)])  18.2 us
    pallas_call x9, Pallas kernels, call(): pl.pallas_call(kernel, in_specs=[VMEM] * len(operands), out_specs=[VMEM]...  13.4 us
    ppermute x17, waiting for transfers between devices, swap(): return lax.ppermute(x, axis, [(i, i ^ flip) for i in range(size)])  13.2 us
    all_to_all x1, blocking collectives, per_device(): lax.all_to_all(micro_rows.reshape(peers, take, width), group, split_axis=...  7.3 us
    concatenate x1, other arithmetic, gather_weights(): jnp.concatenate([w_in, ffn_gain, jnp.zeros((15, w_in.shape[1]), BF16)], a...  1.27 us
  transfers between devices with their start and end apart: 17, of which 5 were waited for; matrix products, arithmetic and copies ran while one was open for 3% of the time, Pallas kernels for 16%

profile of v14, /device:TPU:0, one launch (start us, length us, event | category | flops | bytes accessed | tf_op | source)
XLA Modules:
  0.0 57.2 jit_solution(13274390737176955955)
XLA Ops:
  0.7 0.8 %constant_dynamic-slice_fusion = bf16[32,512]{1,0:T(8,128)(2,1)S(1)} fusion(bf16[128,512]{1,0:T(8,128)(2,1)} %param.14, s32[]{:T(128)S(6)} %select_n.12), kind=kLoop, calls=%fused_computation.9 | loop fusion | bytes 65540 | tf_op jit(solution)/shard_map/dynamic_slice | solution.py:196
  1.5 0.9 %constant_dynamic-slice_fusion.1 = bf16[128,512]{1,0:T(8,128)(2,1)S(1)} fusion(bf16[128,2048]{1,0:T(8,128)(2,1)} %param.13, s32[]{:T(128)S(6)} %select_n.11), kind=kLoop, calls=%fused_computation.10 | loop fusion | bytes 262148 | tf_op jit(solution)/shard_map/dynamic_slice | solution.py:195
  2.4 4.1 %collective-permute-start = (bf16[160,512]{1,0:T(8,128)(2,1)S(1)}, bf16[160,512]{1,0:T(8,128)(2,1)S(1)}, u32[]{:S(2)}, u32[]{:S(2)}) collective-permute-start(bf16[160,512]{1,0:T(8,128)(2,1)S(1)} %pad_maximum_fusion), channel_id=1, source_target_pairs={{0,8},{4,12},{8,0},{12,4},{1,9},{5,13},{9,1},{13,5},{2,10},{6,14},... | collective-permute-start | bytes 491528 | tf_op jit(solution)/shard_map/ppermute | solution.py:23
  6.5 1.3 %collective-permute-start.1 = (bf16[160,512]{1,0:T(8,128)(2,1)S(1)}, bf16[160,512]{1,0:T(8,128)(2,1)S(1)}, u32[]{:S(2)}, u32[]{:S(2)}) collective-permute-start(bf16[160,512]{1,0:T(8,128)(2,1)S(1)} %pad_maximum_fusion), channel_id=1, source_target_pairs={{0,12},{4,8},{8,4},{12,0},{1,13},{5,9},{9,5},{13,1},{2,14},{6,10},... | collective-permute-start | bytes 491528 | tf_op jit(solution)/shard_map/ppermute | solution.py:23
  7.9 0.2 collective-permute-start.2
  8.1 0.1 pad.2.clone
  8.2 1.3 %maximum_maximum_fusion.refs_0_ = bf16[528,512]{1,0:T(8,128)(2,1)S(1)} fusion(bf16[1,512]{1,0:T(2,128)(2,1)} %param.17, bf16[512,512]{1,0:T(8,128)(2,1)} %param.16, bf16[528]{0:T(1024)(128)(2,1)S(1)} %pad.2.clone), kind=kLoop, calls=%fused_computation | loop fusion | flops 1622016 | bytes 1067040 | tf_op jit(solution)/shard_map/concatenate | solution.py:178
  9.5 1.6 %collective-permute-start.8 = (bf16[528,512]{1,0:T(8,128)(2,1)S(1)}, bf16[528,512]{1,0:T(8,128)(2,1)S(1)}, u32[]{:S(2)}, u32[]{:S(2)}) collective-permute-start(bf16[528,512]{1,0:T(8,128)(2,1)S(1)} %maximum_maximum_fusion.refs_0_), channel_id=1, source_target_pairs={{0,1},{1,0},{2,3},{3,2},{4,5},{5,4},{6,7},{7,6},{8,9},{9,8},{10,11... | collective-permute-start | bytes 1622024 | tf_op jit(solution)/shard_map/ppermute | solution.py:23
  11.1 1.5 %collective-permute-start.9 = (bf16[528,512]{1,0:T(8,128)(2,1)S(1)}, bf16[528,512]{1,0:T(8,128)(2,1)S(1)}, u32[]{:S(2)}, u32[]{:S(2)}) collective-permute-start(bf16[528,512]{1,0:T(8,128)(2,1)S(1)} %maximum_maximum_fusion.refs_0_), channel_id=1, source_target_pairs={{0,2},{1,3},{2,0},{3,1},{4,6},{5,7},{6,4},{7,5},{8,10},{9,11},{10,... | collective-permute-start | bytes 1622024 | tf_op jit(solution)/shard_map/ppermute | solution.py:23
  12.7 5.9 %collective-permute-done.refs_0_ = bf16[160,512]{1,0:T(8,128)(2,1)S(1)} collective-permute-done((bf16[160,512]{1,0:T(8,128)(2,1)S(1)}, bf16[160,512]{1,0:T(8,128)(2,1)S(1)}, u32[]{:S(2)}, u32[]{:S(2)}) %collective-permute-start) | collective-permute-done | bytes 163872 | tf_op jit(solution)/shard_map/ppermute | solution.py:23
  18.6 0.5 collective-permute-done.2.refs_2_
  19.2 1.6 %collective-permute-start.3 = (bf16[3,160,256]{2,1,0:T(8,128)(2,1)S(1)}, bf16[3,160,256]{2,1,0:T(8,128)(2,1)S(1)}, u32[]{:S(2)}, u32[]{:S(2)}) collective-permute-start(bf16[3,160,256]{2,1,0:T(8,128)(2,1)S(1)} %get-tuple-element.24), channel_id=1, source_target_pairs={{0,1},{1,0},{2,3},{3,2},{4,5},{5,4},{6,7},{7,6},{8,9},{9,8},{10,11... | collective-permute-start | bytes 737288 | tf_op jit(solution)/shard_map/ppermute | solution.py:23
  20.8 1.5 %collective-permute-start.4 = (bf16[3,160,256]{2,1,0:T(8,128)(2,1)S(1)}, bf16[3,160,256]{2,1,0:T(8,128)(2,1)S(1)}, u32[]{:S(2)}, u32[]{:S(2)}) collective-permute-start(bf16[3,160,256]{2,1,0:T(8,128)(2,1)S(1)} %get-tuple-element.25), channel_id=1, source_target_pairs={{0,2},{1,3},{2,0},{3,1},{4,6},{5,7},{6,4},{7,5},{8,10},{9,11},{10,... | collective-permute-start | bytes 737288 | tf_op jit(solution)/shard_map/ppermute | solution.py:23
  23.0 0.1 select_reduce_fusion
  23.1 5.1 %collective-permute-done.3.refs_5_ = bf16[3,160,256]{2,1,0:T(8,128)(2,1)S(1)} collective-permute-done((bf16[3,160,256]{2,1,0:T(8,128)(2,1)S(1)}, bf16[3,160,256]{2,1,0:T(8,128)(2,1)S(1)}, u32[]{:S(2)}, u32[]{:S(2)}) %collective-permute-start.3) | collective-permute-done | bytes 245792 | tf_op jit(solution)/shard_map/ppermute | solution.py:23
  28.3 1.2 %collective-permute-done.4.refs_6_ = bf16[3,160,256]{2,1,0:T(8,128)(2,1)S(1)} collective-permute-done((bf16[3,160,256]{2,1,0:T(8,128)(2,1)S(1)}, bf16[3,160,256]{2,1,0:T(8,128)(2,1)S(1)}, u32[]{:S(2)}, u32[]{:S(2)}) %collective-permute-start.4) | collective-permute-done | bytes 245792 | tf_op jit(solution)/shard_map/ppermute | solution.py:23
  29.5 1.6 %collective-permute-start.10 = (bf16[256,512]{1,0:T(8,128)(2,1)S(1)}, bf16[256,512]{1,0:T(8,128)(2,1)S(1)}, u32[]{:S(2)}, u32[]{:S(2)}) collective-permute-start(bf16[256,512]{1,0:T(8,128)(2,1)S(1)} %slice.40), channel_id=1, source_target_pairs={{0,2},{1,3},{2,0},{3,1},{4,6},{5,7},{6,4},{7,5},{8,10},{9,11},{10,... | collective-permute-start | bytes 786440 | tf_op jit(solution)/shard_map/ppermute | solution.py:23
  31.1 0.8 %collective-permute-start.11 = (bf16[272,512]{1,0:T(8,128)(2,1)S(1)}, bf16[272,512]{1,0:T(8,128)(2,1)S(1)}, u32[]{:S(2)}, u32[]{:S(2)}) collective-permute-start(bf16[272,512]{1,0:T(8,128)(2,1)S(1)} %slice.41), channel_id=1, source_target_pairs={{0,1},{1,0},{2,3},{3,2},{4,5},{5,4},{6,7},{7,6},{8,9},{9,8},{10,11... | collective-permute-start | bytes 835592 | tf_op jit(solution)/shard_map/ppermute | solution.py:23
  32.0 0.1 broadcast_in_dim.29.bounds_ref
  32.1 3.5 %encode_first.1 = (bf16[64,512]{1,0:T(8,128)(2,1)S(1)}, bf16[512,2048]{1,0:T(8,128)(2,1)S(1)}, bf16[512,512]{1,0:T(8,128)(2,1)S(1)}, bf16[512,1024]{1,0:T(8,128)...) custom-call(f32[3,32,128]{2,1,0:T(8,128)S(1)} %broadcast_in_dim.29.bounds_ref, ...), custom_call_target="tpu_custom_call" | custom-call | flops 1342177280 | bytes 6291456 | tf_op jit(solution)/shard_map/encode_first/pallas_call | solution.py:149
  35.7 7.3 %all_to_all.5 = bf16[8,8,512]{2,1,0:T(8,128)(2,1)S(1)} all-to-all(bf16[8,8,512]{2,1,0:T(8,128)(2,1)S(1)} %bitcast.16), channel_id=1, replica_groups=mesh['section'=2,'dp'=4,'mp'=4] {'section','mp'}, dimensions={0} | all-to-all | bytes 131072 | tf_op jit(solution)/shard_map/all_to_all | solution.py:354
  43.0 2.0 %up_half.1 = (f32[64,512]{1,0:T(8,128)S(1)}, f32[64,2176]{1,0:T(8,128)S(1)}, bf16[64,2176]{1,0:T(8,128)(2,1)S(1)}) custom-call(bf16[64,512]{1,0:T(8,128)(2,1)S(1)} %bitcast.15, bf16[528,512]{1,0:T(8,128)(2,1)S(1)} %maximum_maximum_fusion.refs_0_, bf16[528,512]{1,0:T(8,128)(2,1)S(1)} %collective-permute-done.8.refs_1_, ...), custom_call_target="tpu_custom_call" | custom-call | flops 536870912 | bytes 8388608 | tf_op jit(solution)/shard_map/up_half/pallas_call | solution.py:149
  45.1 0.2 collective-permute-start.12
  45.2 1.6 %project_rest.1 = (bf16[512,1024]{1,0:T(8,128)(2,1)S(1)}, bf16[512,1024]{1,0:T(8,128)(2,1)S(1)}, f32[32,512]{1,0:T(8,128)S(1)}) custom-call(f32[3,32,128]{2,1,0:T(8,128)S(1)} %broadcast_in_dim.29.bounds_ref, bf16[512,512]{1,0:T(8,128)(2,1)S(1)} %get-tuple-element.45.ev_ref, bf16[512,2048]{1,0:T(8,128)(2,1)S(1)} %get-tuple-element.26.w_ref, ...), custom_call_target="tpu_custom_call" | custom-call | flops 1073741824 | bytes 6291456 | tf_op jit(solution)/shard_map/project_rest/pallas_call | solution.py:149
  46.8 1.8 %down_part.1 = (f32[16,2048]{1,0:T(8,128)S(1)}, bf16[16,2048]{1,0:T(8,128)(2,1)S(1)}, bf16[16,2048]{1,0:T(8,128)(2,1)S(1)}, bf16[16,2048]{1,0:T(8,128)(2,1)S(1)}) custom-call(f32[64,2176]{1,0:T(8,128)S(1)} %get-tuple-element.35.half_ref, bf16[64,2176]{1,0:T(8,128)(2,1)S(1)} %collective-permute-done.12.other_ref, ...), custom_call_target="tpu_custom_call" | custom-call | flops 536870912 | bytes 8388608 | tf_op jit(solution)/shard_map/down_part/pallas_call | solution.py:149
  48.7 0.6 %collective-permute-start.13 = (bf16[16,2048]{1,0:T(8,128)(2,1)S(1)}, bf16[16,2048]{1,0:T(8,128)(2,1)S(1)}, u32[]{:S(2)}, u32[]{:S(2)}) collective-permute-start(bf16[16,2048]{1,0:T(8,128)(2,1)S(1)} %get-tuple-element.39), channel_id=1, source_target_pairs={{0,3},{1,2},{2,1},{3,0},{4,7},{5,6},{6,5},{7,4},{8,11},{9,10},{10,... | collective-permute-start | bytes 196616 | tf_op jit(solution)/shard_map/ppermute | solution.py:23
  49.3 1.5 %collective-permute-start.14 = (bf16[16,2048]{1,0:T(8,128)(2,1)S(1)}, bf16[16,2048]{1,0:T(8,128)(2,1)S(1)}, u32[]{:S(2)}, u32[]{:S(2)}) collective-permute-start(bf16[16,2048]{1,0:T(8,128)(2,1)S(1)} %get-tuple-element.40), channel_id=1, source_target_pairs={{0,2},{1,3},{2,0},{3,1},{4,6},{5,7},{6,4},{7,5},{8,10},{9,11},{10,... | collective-permute-start | bytes 196616 | tf_op jit(solution)/shard_map/ppermute | solution.py:23
  50.7 1.5 %collective-permute-start.15 = (bf16[16,2048]{1,0:T(8,128)(2,1)S(1)}, bf16[16,2048]{1,0:T(8,128)(2,1)S(1)}, u32[]{:S(2)}, u32[]{:S(2)}) collective-permute-start(bf16[16,2048]{1,0:T(8,128)(2,1)S(1)} %get-tuple-element.41), channel_id=1, source_target_pairs={{0,1},{1,0},{2,3},{3,2},{4,5},{5,4},{6,7},{7,6},{8,9},{9,8},{10,11... | collective-permute-start | bytes 196616 | tf_op jit(solution)/shard_map/ppermute | solution.py:23
  52.2 2.9 %attend_rest.1.refs_3_.sums_ref = f32[32,512]{1,0:T(8,128)S(1)} custom-call(f32[3,32,128]{2,1,0:T(8,128)S(1)} %broadcast_in_dim.29.bounds_ref, f32[8,512]{1,0:T(8,128)S(1)} %broadcast_in_dim.30.gain_ref, bf16[512,1024]{1,0:T(8,128)(2,1)S(1)} %get-tuple-element.31.qg_ref, bf16[512,1024]{1,0:T(8,128)(2,1)S(1)} %get-tuple-element.32.kv_first, ...), custom_call_target="tpu_custom_call" | custom-call | flops 1073741824 | bytes 4194304 | tf_op jit(solution)/shard_map/attend_rest/pallas_call | solution.py:149
  55.3 0.8 %pool_rows.1 = bf16[32,512]{1,0:T(8,128)(2,1)} custom-call(f32[3,32,128]{2,1,0:T(8,128)S(1)} %broadcast_in_dim.29.bounds_ref, f32[32,512]{1,0:T(8,128)S(1)} %get-tuple-element.30._.sums_ev_ref, f32[32,512]{1,0:T(8,128)S(1)} %attend_rest.1.refs_3_.sums_ref, bf16[512,512]{1,0:T(8,128)(2,1)S(1)} %get-tuple-element.38.wout_ref, ...), custom_call_target="tpu_custom_call" | custom-call | flops 50331648 | bytes 1048576 | tf_op jit(solution)/shard_map/pool_rows/pallas_call | solution.py:149
  56.1 0.4 collective-permute-done.16.got_ref
  56.5 0.6 %finish.1 = bf16[8,4096]{1,0:T(8,128)(2,1)} custom-call(f32[8,2048]{1,0:T(8,128)S(1)} %get-tuple-element.42._.keep_ref, f32[8,2048]{1,0:T(8,128)S(1)} %collective-permute-done.16.got_ref), custom_call_target="tpu_custom_call" | custom-call | bytes 262144 | tf_op jit(solution)/shard_map/finish/pallas_call | solution.py:149
  (46 shorter events, 0.5 us)
Async XLA Ops:
  0.6 12.0 %copy-start.1 = (bf16[1,1024,512]{2,1,0:T(8,128)(2,1)S(1)}, bf16[1,1024,512]{2,1,0:T(8,128)(2,1)}, u32[]{:S(2)}) copy-start(bf16[1,1024,512]{2,1,0:T(8,128)(2,1)} %param.10) | copy-start | bytes 3145732
  2.4 16.2 %collective-permute-start = (bf16[160,512]{1,0:T(8,128)(2,1)S(1)}, bf16[160,512]{1,0:T(8,128)(2,1)S(1)}, u32[]{:S(2)}, u32[]{:S(2)}) collective-permute-start(bf16[160,512]{1,0:T(8,128)(2,1)S(1)} %pad_maximum_fusion), channel_id=1, source_target_pairs={{0,8},{4,12},{8,0},{12,4},{1,9},{5,13},{9,1},{13,5},{2,10},{6,14},... | collective-permute-start | bytes 491528 | tf_op jit(solution)/shard_map/ppermute | solution.py:23
  6.5 12.1 %collective-permute-start.1 = (bf16[160,512]{1,0:T(8,128)(2,1)S(1)}, bf16[160,512]{1,0:T(8,128)(2,1)S(1)}, u32[]{:S(2)}, u32[]{:S(2)}) collective-permute-start(bf16[160,512]{1,0:T(8,128)(2,1)S(1)} %pad_maximum_fusion), channel_id=1, source_target_pairs={{0,12},{4,8},{8,4},{12,0},{1,13},{5,9},{9,5},{13,1},{2,14},{6,10},... | collective-permute-start | bytes 491528 | tf_op jit(solution)/shard_map/ppermute | solution.py:23
  7.9 11.3 %collective-permute-start.2 = (bf16[160,512]{1,0:T(8,128)(2,1)S(1)}, bf16[160,512]{1,0:T(8,128)(2,1)S(1)}, u32[]{:S(2)}, u32[]{:S(2)}) collective-permute-start(bf16[160,512]{1,0:T(8,128)(2,1)S(1)} %pad_maximum_fusion), channel_id=1, source_target_pairs={{0,4},{4,0},{8,12},{12,8},{1,5},{5,1},{9,13},{13,9},{2,6},{6,2},{1... | collective-permute-start | bytes 491528 | tf_op jit(solution)/shard_map/ppermute | solution.py:23
  8.2 14.1 %copy-start.3 = (bf16[128,512]{1,0:T(8,128)(2,1)S(1)}, bf16[128,512]{1,0:T(8,128)(2,1)}, u32[]{:S(2)}) copy-start(bf16[128,512]{1,0:T(8,128)(2,1)} %param.14) | copy-start | bytes 393220
  8.2 14.8 %copy-start.5 = (s32[1,32]{1,0:T(1,128)S(1)}, s32[1,32]{1,0:T(1,128)}, u32[]{:S(2)}) copy-start(s32[1,32]{1,0:T(1,128)} %param.12) | copy-start | bytes 388
  9.5 3.2 %copy-start.2 = (bf16[128,2048]{1,0:T(8,128)(2,1)S(1)}, bf16[128,2048]{1,0:T(8,128)(2,1)}, u32[]{:S(2)}) copy-start(bf16[128,2048]{1,0:T(8,128)(2,1)} %param.13) | copy-start | bytes 1572868
  9.5 20.0 %collective-permute-start.8 = (bf16[528,512]{1,0:T(8,128)(2,1)S(1)}, bf16[528,512]{1,0:T(8,128)(2,1)S(1)}, u32[]{:S(2)}, u32[]{:S(2)}) collective-permute-start(bf16[528,512]{1,0:T(8,128)(2,1)S(1)} %maximum_maximum_fusion.refs_0_), channel_id=1, source_target_pairs={{0,1},{1,0},{2,3},{3,2},{4,5},{5,4},{6,7},{7,6},{8,9},{9,8},{10,11... | collective-permute-start | bytes 1622024 | tf_op jit(solution)/shard_map/ppermute | solution.py:23
  11.1 21.1 %copy-start.4 = (f32[512]{0:T(512)S(1)}, f32[512]{0:T(512)}, u32[]{:S(2)}) copy-start(f32[512]{0:T(512)} %param.15) | copy-start | bytes 6148
  11.1 20.1 %collective-permute-start.9 = (bf16[528,512]{1,0:T(8,128)(2,1)S(1)}, bf16[528,512]{1,0:T(8,128)(2,1)S(1)}, u32[]{:S(2)}, u32[]{:S(2)}) collective-permute-start(bf16[528,512]{1,0:T(8,128)(2,1)S(1)} %maximum_maximum_fusion.refs_0_), channel_id=1, source_target_pairs={{0,2},{1,3},{2,0},{3,1},{4,6},{5,7},{6,4},{7,5},{8,10},{9,11},{10,... | collective-permute-start | bytes 1622024 | tf_op jit(solution)/shard_map/ppermute | solution.py:23
  12.6 30.4 %copy-start = (bf16[2048,2048]{1,0:T(8,128)(2,1)S(1)}, bf16[2048,2048]{1,0:T(8,128)(2,1)}, u32[]{:S(2)}) copy-start(bf16[2048,2048]{1,0:T(8,128)(2,1)} %refs_5_.1) | copy-start | bytes 25165828
  19.2 9.1 %collective-permute-start.3 = (bf16[3,160,256]{2,1,0:T(8,128)(2,1)S(1)}, bf16[3,160,256]{2,1,0:T(8,128)(2,1)S(1)}, u32[]{:S(2)}, u32[]{:S(2)}) collective-permute-start(bf16[3,160,256]{2,1,0:T(8,128)(2,1)S(1)} %get-tuple-element.24), channel_id=1, source_target_pairs={{0,1},{1,0},{2,3},{3,2},{4,5},{5,4},{6,7},{7,6},{8,9},{9,8},{10,11... | collective-permute-start | bytes 737288 | tf_op jit(solution)/shard_map/ppermute | solution.py:23
  20.8 8.7 %collective-permute-start.4 = (bf16[3,160,256]{2,1,0:T(8,128)(2,1)S(1)}, bf16[3,160,256]{2,1,0:T(8,128)(2,1)S(1)}, u32[]{:S(2)}, u32[]{:S(2)}) collective-permute-start(bf16[3,160,256]{2,1,0:T(8,128)(2,1)S(1)} %get-tuple-element.25), channel_id=1, source_target_pairs={{0,2},{1,3},{2,0},{3,1},{4,6},{5,7},{6,4},{7,5},{8,10},{9,11},{10,... | collective-permute-start | bytes 737288 | tf_op jit(solution)/shard_map/ppermute | solution.py:23
  22.3 9.7 %collective-permute-start.5 = (bf16[2,3,160,256]{3,2,1,0:T(8,128)(2,1)S(1)}, bf16[2,3,160,256]{3,2,1,0:T(8,128)(2,1)S(1)}, u32[]{:S(2)}, u32[]{:S(2)}) collective-permute-start(bf16[2,3,160,256]{3,2,1,0:T(8,128)(2,1)S(1)} %get-tuple-element.23.refs_4_), channel_id=1, source_target_pairs={{0,16},{16,0},{1,17},{17,1},{2,18},{18,2},{3,19},{19,3},{4,20},{20... | collective-permute-start | bytes 1474568 | tf_op jit(solution)/shard_map/ppermute | solution.py:23
  28.3 3.7 %collective-permute-start.6 = (bf16[3,160,256]{2,1,0:T(8,128)(2,1)S(1)}, bf16[3,160,256]{2,1,0:T(8,128)(2,1)S(1)}, u32[]{:S(2)}, u32[]{:S(2)}) collective-permute-start(bf16[3,160,256]{2,1,0:T(8,128)(2,1)S(1)} %collective-permute-done.3.refs_5_), channel_id=1, source_target_pairs={{0,16},{16,0},{1,17},{17,1},{2,18},{18,2},{3,19},{19,3},{4,20},{20... | collective-permute-start | bytes 737288 | tf_op jit(solution)/shard_map/ppermute | solution.py:23
  29.5 2.5 %collective-permute-start.7 = (bf16[3,160,256]{2,1,0:T(8,128)(2,1)S(1)}, bf16[3,160,256]{2,1,0:T(8,128)(2,1)S(1)}, u32[]{:S(2)}, u32[]{:S(2)}) collective-permute-start(bf16[3,160,256]{2,1,0:T(8,128)(2,1)S(1)} %collective-permute-done.4.refs_6_), channel_id=1, source_target_pairs={{0,16},{16,0},{1,17},{17,1},{2,18},{18,2},{3,19},{19,3},{4,20},{20... | collective-permute-start | bytes 737288 | tf_op jit(solution)/shard_map/ppermute | solution.py:23
  29.5 13.5 %collective-permute-start.10 = (bf16[256,512]{1,0:T(8,128)(2,1)S(1)}, bf16[256,512]{1,0:T(8,128)(2,1)S(1)}, u32[]{:S(2)}, u32[]{:S(2)}) collective-permute-start(bf16[256,512]{1,0:T(8,128)(2,1)S(1)} %slice.40), channel_id=1, source_target_pairs={{0,2},{1,3},{2,0},{3,1},{4,6},{5,7},{6,4},{7,5},{8,10},{9,11},{10,... | collective-permute-start | bytes 786440 | tf_op jit(solution)/shard_map/ppermute | solution.py:23
  31.1 11.8 %collective-permute-start.11 = (bf16[272,512]{1,0:T(8,128)(2,1)S(1)}, bf16[272,512]{1,0:T(8,128)(2,1)S(1)}, u32[]{:S(2)}, u32[]{:S(2)}) collective-permute-start(bf16[272,512]{1,0:T(8,128)(2,1)S(1)} %slice.41), channel_id=1, source_target_pairs={{0,1},{1,0},{2,3},{3,2},{4,5},{5,4},{6,7},{7,6},{8,9},{9,8},{10,11... | collective-permute-start | bytes 835592 | tf_op jit(solution)/shard_map/ppermute | solution.py:23
  32.1 14.7 %slice-start = ((s8[8388608]{0:T(1024)(128)(4,1)}), s8[4194304]{0:T(1024)(128)(4,1)S(1)}, s32[]{:S(2)}) async-start(s8[8388608]{0:T(1024)(128)(4,1)} %bitcast.13), calls=%async_computation.1 | async-start | bytes 8388608
  43.0 3.8 %slice-start.1 = ((s8[8388608]{0:T(1024)(128)(4,1)}), s8[4194304]{0:T(1024)(128)(4,1)S(1)}, s32[]{:S(2)}) async-start(s8[8388608]{0:T(1024)(128)(4,1)} %bitcast.13), calls=%async_computation.2 | async-start | bytes 8388608
  45.1 1.8 %collective-permute-start.12 = (bf16[64,2176]{1,0:T(8,128)(2,1)S(1)}, bf16[64,2176]{1,0:T(8,128)(2,1)S(1)}, u32[]{:S(2)}, u32[]{:S(2)}) collective-permute-start(bf16[64,2176]{1,0:T(8,128)(2,1)S(1)} %get-tuple-element.36), channel_id=1, source_target_pairs={{0,16},{16,0},{1,17},{17,1},{2,18},{18,2},{3,19},{19,3},{4,20},{20... | collective-permute-start | bytes 835592 | tf_op jit(solution)/shard_map/ppermute | solution.py:23
  48.7 6.5 %collective-permute-start.13 = (bf16[16,2048]{1,0:T(8,128)(2,1)S(1)}, bf16[16,2048]{1,0:T(8,128)(2,1)S(1)}, u32[]{:S(2)}, u32[]{:S(2)}) collective-permute-start(bf16[16,2048]{1,0:T(8,128)(2,1)S(1)} %get-tuple-element.39), channel_id=1, source_target_pairs={{0,3},{1,2},{2,1},{3,0},{4,7},{5,6},{6,5},{7,4},{8,11},{9,10},{10,... | collective-permute-start | bytes 196616 | tf_op jit(solution)/shard_map/ppermute | solution.py:23
  49.3 5.9 %collective-permute-start.14 = (bf16[16,2048]{1,0:T(8,128)(2,1)S(1)}, bf16[16,2048]{1,0:T(8,128)(2,1)S(1)}, u32[]{:S(2)}, u32[]{:S(2)}) collective-permute-start(bf16[16,2048]{1,0:T(8,128)(2,1)S(1)} %get-tuple-element.40), channel_id=1, source_target_pairs={{0,2},{1,3},{2,0},{3,1},{4,6},{5,7},{6,4},{7,5},{8,10},{9,11},{10,... | collective-permute-start | bytes 196616 | tf_op jit(solution)/shard_map/ppermute | solution.py:23
  50.7 4.4 %collective-permute-start.15 = (bf16[16,2048]{1,0:T(8,128)(2,1)S(1)}, bf16[16,2048]{1,0:T(8,128)(2,1)S(1)}, u32[]{:S(2)}, u32[]{:S(2)}) collective-permute-start(bf16[16,2048]{1,0:T(8,128)(2,1)S(1)} %get-tuple-element.41), channel_id=1, source_target_pairs={{0,1},{1,0},{2,3},{3,2},{4,5},{5,4},{6,7},{7,6},{8,9},{9,8},{10,11... | collective-permute-start | bytes 196616 | tf_op jit(solution)/shard_map/ppermute | solution.py:23
  55.2 1.3 %collective-permute-start.16 = (f32[8,2048]{1,0:T(8,128)S(1)}, f32[8,2048]{1,0:T(8,128)S(1)}, u32[]{:S(2)}, u32[]{:S(2)}) collective-permute-start(f32[8,2048]{1,0:T(8,128)S(1)} %get-tuple-element.43), channel_id=1, source_target_pairs={{0,16},{16,0},{1,17},{17,1},{2,18},{18,2},{3,19},{19,3},{4,20},{20... | collective-permute-start | bytes 196616 | tf_op jit(solution)/shard_map/ppermute | solution.py:23
